TPU v7x, 32 devices: a whole 2x2x4 slice. The times are simulated.
32 devices in a mesh: dp: 16 (over z, y, x), tensor: 2 (over core).
Axes of the slice: x: 2, y: 2, z: 4, core: 2. Of those that a mesh axis runs over, the one named last changes fastest.
Arguments:
- tokens: bfloat16 [4096, 2048], P(('dp', 'tensor')), may hold values from -6 to 6
- segment_ids: int32 [4096], P('dp'), may hold values from 0 to 2, as said below
- ln1_gain: float32 [2048], replicated, may hold values from 0.5 to 1.5
- ln1_bias: float32 [2048], replicated, may hold values from -1.75 to 1.75
- qkv_weight: bfloat16 [3, 2048, 2048], P(None, 'dp', 'tensor'), may hold values from -0.125 to 0.125
- qkv_bias: float32 [3, 2048], P(None, 'tensor'), may hold values from -3 to 3
- out_weight: bfloat16 [2048, 2048], P('tensor', 'dp'), may hold values from -0.75 to 0.75
- ln2_gain: float32 [2048], replicated, may hold values from 0.5 to 1.5
- ln2_bias: float32 [2048], replicated, may hold values from -1.75 to 1.75
- gate_up_weight: bfloat16 [2, 2048, 5632], P(None, 'dp', 'tensor'), may hold values from -0.125 to 0.125
- down_weight: bfloat16 [5632, 2048], P('tensor', 'dp'), may hold values from -0.078125 to 0.078125
- out_grad: bfloat16 [4096, 2048], P(('dp', 'tensor')), may hold values from -12 to 12
Outputs:
- output: bfloat16 [4096, 2048], P(('dp', 'tensor'))
- tokens_grad: float32 [4096, 2048], P(('dp', 'tensor'))
- ln1_gain_grad: float32 [2048], replicated
- ln1_bias_grad: float32 [2048], replicated
- qkv_weight_grad: float32 [3, 2048, 2048], P(None, 'dp', 'tensor')
- qkv_bias_grad: float32 [3, 2048], replicated
- out_weight_grad: float32 [2048, 2048], P('tensor', 'dp')
- ln2_gain_grad: float32 [2048], replicated
- ln2_bias_grad: float32 [2048], replicated
- gate_up_weight_grad: float32 [2, 2048, 5632], P(None, 'dp', 'tensor')
- down_weight_grad: float32 [5632, 2048], P('tensor', 'dp')
Inputs may be any that keep to these rules, and one draw needn't show every extreme that they name: `segment_ids`: numbers the documents of each sequence of 256 tokens 0, 1, ... in order; every sequence holds exactly 3 documents, and no document begins at the middle token (index 128) of its sequence.
All inputs are finite; a program needn't handle non-finite values.
Results may differ from a plain program's by a relative error of at most 0.014.
Values may be sent and summed in bfloat16 or wider, within the bound.
No kernel may reach another device: no remote copies, remote signals or barrier semaphores. Data moves between devices by JAX's collectives and lax.ppermute only.
A program may use at most 256 MiB of HBM per device.

v0:
```python
import math

import jax
import jax.numpy as jnp
from jax import lax
from jax.sharding import PartitionSpec as P

HD = 64
ROT = 16


norm_eps = 1e-05
rope_base = 10000.0
score_scale = 0.125
masked_score = -1e30


def doc_positions(segment):
    token_index = jnp.arange(segment.shape[0], dtype=jnp.int32)
    begins = jnp.concatenate([jnp.ones((1,), dtype=jnp.bool_), segment[1:] != segment[:-1]])
    starts = lax.cummax(jnp.where(begins, token_index, jnp.zeros_like(token_index)), axis=0)
    return token_index - starts


def rotary_tables(positions):
    half_rot = ROT // 2
    frequency = rope_base ** (-(2.0 * jnp.arange(half_rot, dtype=jnp.float32)) / ROT)
    angles = positions.astype(jnp.float32)[:, None] * frequency[None, :]
    return (jnp.cos(angles), jnp.sin(angles))


def rotate(heads_in, cosine, sine, turn_sign):
    half_rot = cosine.shape[-1]
    lead_half = heads_in[..., :half_rot]
    tail_half = heads_in[..., half_rot : 2 * half_rot]
    remainder = heads_in[..., 2 * half_rot :]
    cos_b = cosine[:, None, :]
    sin_b = sine[:, None, :] * turn_sign
    return jnp.concatenate(
        [lead_half * cos_b - tail_half * sin_b, tail_half * cos_b + lead_half * sin_b, remainder],
        axis=-1,
    )


def norm_parts(values, gain, shift):
    row_mean = jnp.mean(values, axis=-1, keepdims=True)
    centred = values - row_mean
    inv_std = lax.rsqrt(jnp.mean(centred * centred, axis=-1, keepdims=True) + norm_eps)
    normed = centred * inv_std
    return (normed * gain + shift, normed, inv_std)


def norm_back(incoming, normed, inv_std, gain):
    scaled = incoming * gain
    adjusted = (
        scaled
        - jnp.mean(scaled, axis=-1, keepdims=True)
        - normed * jnp.mean(scaled * normed, axis=-1, keepdims=True)
    )
    return adjusted * inv_std


def attend(queries, keys_rot, values, allowed):
    scores = (
        jnp.einsum("hqd,hkd->hqk", queries, keys_rot, preferred_element_type=jnp.float32)
        * score_scale
    )
    scores = jnp.where(allowed, scores, masked_score)
    row_top = jnp.max(scores, axis=-1, keepdims=True)
    weights = jnp.exp(scores - row_top)
    row_total = jnp.sum(weights, axis=-1, keepdims=True)
    attn_probs = (weights / row_total).astype(jnp.bfloat16)
    mixed = jnp.einsum("hqk,hkd->hqd", attn_probs, values, preferred_element_type=jnp.float32)
    return (mixed.astype(jnp.bfloat16), (row_top + jnp.log(row_total))[..., 0])


def attend_back(queries, keys_rot, values, log_total, mixed_grad, allowed):
    scores = (
        jnp.einsum("hqd,hkd->hqk", queries, keys_rot, preferred_element_type=jnp.float32)
        * score_scale
    )
    scores = jnp.where(allowed, scores, masked_score)
    attn_probs = jnp.exp(scores - log_total[..., None])
    prob_grad = jnp.einsum("hqd,hkd->hqk", mixed_grad, values, preferred_element_type=jnp.float32)
    value_grad = jnp.einsum(
        "hqk,hqd->hkd",
        attn_probs.astype(jnp.bfloat16),
        mixed_grad,
        preferred_element_type=jnp.float32,
    )
    score_grad = (
        attn_probs * (prob_grad - jnp.sum(attn_probs * prob_grad, axis=-1, keepdims=True))
    ).astype(jnp.bfloat16)
    query_grad = (
        jnp.einsum("hqk,hkd->hqd", score_grad, keys_rot, preferred_element_type=jnp.float32)
        * score_scale
    )
    key_grad = (
        jnp.einsum("hqk,hqd->hkd", score_grad, queries, preferred_element_type=jnp.float32)
        * score_scale
    )
    return (query_grad, key_grad, value_grad)


def on_device(
    tokens,
    segment_ids,
    ln1_gain,
    ln1_bias,
    qkv_weight,
    qkv_bias,
    out_weight,
    ln2_gain,
    ln2_bias,
    gate_up_weight,
    down_weight,
    out_grad,
):
    local_count = tokens.shape[0]
    tensor_rank = lax.axis_index("tensor")
    first_row = tensor_rank * local_count
    head_cols = qkv_bias.shape[1]
    head_count = head_cols // HD
    head_group = math.gcd(head_count, 4)
    seq_len = segment_ids.shape[0]
    token_index = jnp.arange(seq_len, dtype=jnp.int32)
    allowed = (segment_ids[:, None] == segment_ids[None, :]) & (
        token_index[None, :] <= token_index[:, None]
    )
    cosine, sine = rotary_tables(doc_positions(segment_ids))

    def split_heads(array):
        return array.reshape(seq_len, head_count // head_group, head_group, HD).transpose(
            1, 2, 0, 3
        )

    def unsplit(array):
        return array.transpose(2, 0, 1, 3).reshape(seq_len, head_count, HD)

    def local_part(array):
        return lax.dynamic_slice_in_dim(array, first_row, local_count, 0)

    attn_w = (
        lax.all_gather(qkv_weight, "dp", axis=1, tiled=True),
        lax.all_gather(out_weight, "dp", axis=1, tiled=True),
    )
    seq_tokens = lax.all_gather(tokens, "tensor", axis=0, tiled=True)
    resid = seq_tokens.astype(jnp.float32)
    normed_in, normed_one, inv_one = norm_parts(resid, ln1_gain, ln1_bias)
    seq_in = normed_in.astype(jnp.bfloat16)
    projected = (
        jnp.einsum("sd,jdc->jsc", seq_in, attn_w[0], preferred_element_type=jnp.float32)
        + qkv_bias[:, None, :]
    )
    shaped = projected.reshape(3, seq_len, head_count, HD)
    queries = rotate(shaped[0], cosine, sine, 1.0).astype(jnp.bfloat16)
    keys_rot = rotate(shaped[1], cosine, sine, 1.0).astype(jnp.bfloat16)
    values = shaped[2].astype(jnp.bfloat16)
    mixed, log_total = lax.map(
        lambda pieces: attend(pieces[0], pieces[1], pieces[2], allowed),
        (split_heads(queries), split_heads(keys_rot), split_heads(values)),
    )
    mixed_rows = unsplit(mixed).reshape(seq_len, head_cols)
    attn_terms = jnp.dot(mixed_rows, attn_w[1], preferred_element_type=jnp.float32)
    resid_local = local_part(resid) + lax.psum_scatter(
        attn_terms, "tensor", scatter_dimension=0, tiled=True
    )
    normed_mid, normed_two_local, inv_two_local = norm_parts(resid_local, ln2_gain, ln2_bias)
    seq_mid = lax.all_gather(normed_mid.astype(jnp.bfloat16), "tensor", axis=0, tiled=True)
    mlp_w = (
        lax.all_gather(gate_up_weight, "dp", axis=1, tiled=True),
        lax.all_gather(down_weight, "dp", axis=1, tiled=True),
    )
    gate_up = jnp.einsum("sd,jdf->jsf", seq_mid, mlp_w[0], preferred_element_type=jnp.float32)
    gate_pre = gate_up[0]
    up_values = gate_up[1]
    gate_sig = jax.nn.sigmoid(gate_pre)
    smooth = gate_pre * gate_sig
    hidden = (smooth * up_values).astype(jnp.bfloat16)
    mlp_terms = jnp.dot(hidden, mlp_w[1], preferred_element_type=jnp.float32)
    result = (
        resid_local
        + lax.psum_scatter(
            mlp_terms.astype(jnp.bfloat16), "tensor", scatter_dimension=0, tiled=True
        ).astype(jnp.float32)
    ).astype(jnp.bfloat16)
    gate_up_back, down_back = mlp_w
    grad_rows = lax.all_gather(out_grad, "tensor", axis=0, tiled=True)
    hidden_grad = jnp.einsum("sd,fd->sf", grad_rows, down_back, preferred_element_type=jnp.float32)
    down_grad = jnp.einsum("sf,sd->fd", hidden, grad_rows, preferred_element_type=jnp.float32)
    gate_grad = (hidden_grad * up_values * gate_sig * (1.0 + gate_pre * (1.0 - gate_sig))).astype(
        jnp.bfloat16
    )
    up_grad = (hidden_grad * smooth).astype(jnp.bfloat16)
    pair_grad = jnp.stack([gate_grad, up_grad])
    gate_up_grad = jnp.einsum("sd,jsf->djf", seq_mid, pair_grad, preferred_element_type=jnp.float32)
    mlp_shards = (
        lax.psum_scatter(gate_up_grad, "dp", scatter_dimension=0, tiled=True),
        lax.psum_scatter(down_grad, "dp", scatter_dimension=1, tiled=True),
    )
    mid_terms = jnp.einsum(
        "jsf,jdf->sd", pair_grad, gate_up_back, preferred_element_type=jnp.float32
    )
    mid_local = lax.psum_scatter(mid_terms, "tensor", scatter_dimension=0, tiled=True)
    resid_grad_local = out_grad.astype(jnp.float32) + norm_back(
        mid_local, normed_two_local, inv_two_local, ln2_gain
    )
    attn_grad = lax.all_gather(resid_grad_local.astype(jnp.bfloat16), "tensor", axis=0, tiled=True)
    qkv_back, out_back = attn_w
    out_w_grad = jnp.einsum("sc,sd->cd", mixed_rows, attn_grad, preferred_element_type=jnp.float32)
    mixed_grad = jnp.einsum(
        "sd,cd->sc", attn_grad, out_back, preferred_element_type=jnp.float32
    ).astype(jnp.bfloat16)
    query_grad, key_grad, value_grad = lax.map(
        lambda pieces: attend_back(pieces[0], pieces[1], pieces[2], pieces[3], pieces[4], allowed),
        (
            split_heads(queries),
            split_heads(keys_rot),
            split_heads(values),
            log_total,
            split_heads(mixed_grad.reshape(seq_len, head_count, HD)),
        ),
    )
    lin_grad = (
        jnp.stack(
            [
                rotate(unsplit(query_grad), cosine, sine, -1.0),
                rotate(unsplit(key_grad), cosine, sine, -1.0),
                unsplit(value_grad),
            ]
        )
        .reshape(3, seq_len, head_cols)
        .astype(jnp.bfloat16)
    )
    qkv_grad = jnp.einsum("sd,jsc->djc", seq_in, lin_grad, preferred_element_type=jnp.float32)
    attn_shards = (
        lax.psum_scatter(qkv_grad, "dp", scatter_dimension=0, tiled=True),
        lax.psum_scatter(out_w_grad, "dp", scatter_dimension=1, tiled=True),
    )
    in_terms = jnp.einsum("jsc,jdc->sd", lin_grad, qkv_back, preferred_element_type=jnp.float32)
    in_grad = lax.psum_scatter(
        in_terms.astype(jnp.bfloat16), "tensor", scatter_dimension=0, tiled=True
    ).astype(jnp.float32)
    normed_local = local_part(normed_one)
    token_grad = resid_grad_local + norm_back(in_grad, normed_local, local_part(inv_one), ln1_gain)
    bias_rows = jnp.sum(lin_grad.astype(jnp.float32), axis=1)
    bias_full = lax.dynamic_update_slice(
        jnp.zeros((3, head_cols * lax.axis_size("tensor")), jnp.float32),
        bias_rows,
        (jnp.int32(0), tensor_rank * head_cols),
    )
    small_sums = lax.psum(
        (
            jnp.sum(in_grad * normed_local, axis=0),
            jnp.sum(in_grad, axis=0),
            jnp.sum(mid_local * normed_two_local, axis=0),
            jnp.sum(mid_local, axis=0),
            bias_full,
        ),
        ("dp", "tensor"),
    )
    return (
        result,
        token_grad,
        small_sums[0],
        small_sums[1],
        attn_shards[0].transpose(1, 0, 2),
        small_sums[4],
        attn_shards[1],
        small_sums[2],
        small_sums[3],
        mlp_shards[0].transpose(1, 0, 2),
        mlp_shards[1],
    )


def solution(mesh):
    return jax.shard_map(
        on_device,
        mesh=mesh,
        in_specs=(
            P(("dp", "tensor"), None),
            P("dp"),
            P(),
            P(),
            P(None, "dp", "tensor"),
            P(None, "tensor"),
            P("tensor", "dp"),
            P(),
            P(),
            P(None, "dp", "tensor"),
            P("tensor", "dp"),
            P(("dp", "tensor"), None),
        ),
        out_specs=(
            P(("dp", "tensor"), None),
            P(("dp", "tensor"), None),
            P(),
            P(),
            P(None, "dp", "tensor"),
            P(),
            P("tensor", "dp"),
            P(),
            P(),
            P(None, "dp", "tensor"),
            P("tensor", "dp"),
        ),
        check_vma=False,
    )
```

profile of v0, /device:TPU:0, one launch (start us, length us, event | category | flops | bytes accessed | tf_op | source)
XLA Modules:
  0.0 2996.3 jit_solution(8058608783959168736)
XLA Ops:
  9.5 0.8 slice_compare_fusion
  11.7 9.6 all-gather.9.cloned.1.call-done
  21.4 1.4 convert_reduce_fusion.2
  22.8 1.6 multiply_reduce_fusion.1
  24.5 152.7 %all-gather.11.cloned.1.call-done = bf16[3,2048,1024]{2,1,0:T(8,128)(2,1)} async-done(((bf16[3,128,1024]{2,1,0:T(8,128)(2,1)}), bf16[3,2048,1024]{2,1,0:T(8,128)(2,1)}) %all-gather.11.cloned.1.call-update) | async-done | bytes 12582928 | tf_op jit(solution)/shard_map/all_gather | solution.py:144
  177.2 6.8 add_bitcast_fusion
  184.0 0.9 slice.152
  185.8 2.1 copy.50
  187.9 0.8 subtract_convert_fusion.2
  188.9 12.5 while.28
  189.5 1.9 fusion.117
  192.6 1.9 fusion.117
  195.8 1.9 fusion.117
  198.9 1.9 fusion.117
  201.4 65.9 %all-gather.13.cloned.1.call-done = bf16[1024,2048]{1,0:T(8,128)(2,1)} async-done(((bf16[1024,128]{1,0:T(8,128)(2,1)}), bf16[1024,2048]{1,0:T(8,128)(2,1)}) %all-gather.13.cloned.1.call-update) | async-done | bytes 4194320 | tf_op jit(solution)/shard_map/all_gather | solution.py:145
  267.3 5.0 fusion.74
  272.4 1.6 convert_element_type.74
  274.0 6.3 reduce-scatter.9.cloned.1.call-done
  280.3 1.7 fusion.71
  282.3 1.0 add_convert_fusion.2
  285.7 8.1 all-gather.15.cloned.1.call-done
  293.8 255.5 %all-gather.17.cloned.1.call-done = bf16[2,2048,2816]{2,1,0:T(8,128)(2,1)} async-done(((bf16[2,128,2816]{2,1,0:T(8,128)(2,1)}), bf16[2,2048,2816]{2,1,0:T(8,128)(2,1)}) %all-gather.17.cloned.1.call-update) | async-done | bytes 23068688 | tf_op jit(solution)/shard_map/all_gather | solution.py:171
  549.3 13.1 convolution_bitcast_fusion.1
  562.4 182.6 %all-gather.19.cloned.1.call-done = bf16[2816,2048]{1,0:T(8,128)(2,1)} async-done(((bf16[2816,128]{1,0:T(8,128)(2,1)}), bf16[2816,2048]{1,0:T(8,128)(2,1)}) %all-gather.19.cloned.1.call-update) | async-done | bytes 11534352 | tf_op jit(solution)/shard_map/all_gather | solution.py:172
  745.0 12.4 fusion.54
  757.4 12.5 convolution_bitcast_fusion.3
  770.0 9.3 convolution_convert_fusion.1
  779.6 2.3 multiply_reduce_fusion.2
  781.9 8.4 reduce-scatter.11.cloned.1.call-done
  790.3 3.4 fusion.70
  793.8 10.3 all-gather.23.cloned.1.call-done
  804.1 4.6 convolution_convert_fusion.2
  808.7 1.2 copy.51
  809.9 19.8 while.29
  809.9 1.3 fusion.126
  812.7 0.9 fusion.128
  813.6 1.0 fusion.129
  814.9 1.3 fusion.126
  817.6 0.9 fusion.128
  818.5 1.0 fusion.129
  819.8 1.2 fusion.126
  822.5 0.9 fusion.128
  823.5 1.0 fusion.129
  824.7 1.2 fusion.126
  827.5 0.9 fusion.128
  828.4 1.0 fusion.129
  829.9 1.4 slice.153
  831.3 1.2 slice.154
  832.5 1.8 subtract_convert_fusion.1
  834.6 1.1 pad_maximum_fusion.4
  835.9 9.2 fusion.48
  845.2 5.8 fusion.75
  851.3 12.9 fusion.76
  864.9 10.5 fusion.63
  875.5 1.1 copy-done.1
  877.1 19.4 fusion.49
  897.0 1.7 convert_reduce_fusion
  898.8 1.4 fusion.59
  900.3 45.5 %all-reduce = (f32[2048]{0:T(1024)}, f32[2048]{0:T(1024)}, f32[3,2048]{1,0:T(4,128)}, f32[2048]{0:T(1024)}, f32[2048]{0:T(1024)}) all-reduce(f32[2048]{0:T(1024)S(1)} %get-tuple-element.148, f32[2048]{0:T(1024)S(1)} %get-tuple-element.155, ...), channel_id=1, replica_groups=mesh['dp'=16,'tensor'=2] {'dp','tensor'}, use_global_device_ids=true, to_apply=%region_22.23 | all-reduce | flops 14336 | bytes 114688 | tf_op jit(solution)/shard_map/psum | solution.py:252
  945.7 2.3 fusion.57
  948.0 90.2 %reduce-scatter.19.cloned.1.call-done = f32[1024,128]{1,0:T(8,128)} async-done(((f32[1024,2048]{1,0:T(8,128)}), f32[1024,128]{1,0:T(8,128)}) %reduce-scatter.19.cloned.1.call-update) | async-done | bytes 524304 | tf_op jit(solution)/shard_map/reduce_scatter | solution.py:238
  1038.3 478.2 %reduce-scatter.23.cloned.1.call-done = f32[2816,128]{1,0:T(8,128)} async-done(((f32[2816,2048]{1,0:T(8,128)}), f32[2816,128]{1,0:T(8,128)}) %reduce-scatter.23.cloned.1.call-update) | async-done | bytes 1441808 | tf_op jit(solution)/shard_map/reduce_scatter | solution.py:199
  1516.4 526.5 %reduce-scatter.17.cloned.1.call-done = f32[128,3,1024]{2,0,1:T(8,128)} async-done(((f32[2048,3,1024]{2,0,1:T(8,128)}), f32[128,3,1024]{2,0,1:T(8,128)}) %reduce-scatter.17.cloned.1.call-update) | async-done | bytes 1572880 | tf_op jit(solution)/shard_map/reduce_scatter | solution.py:237
  2042.9 946.4 %reduce-scatter.21.cloned.1.call-done = f32[128,2,2816]{2,0,1:T(8,128)} async-done(((f32[2048,2,2816]{2,0,1:T(8,128)}), f32[128,2,2816]{2,0,1:T(8,128)}) %reduce-scatter.21.cloned.1.call-update) | async-done | bytes 2883600 | tf_op jit(solution)/shard_map/reduce_scatter | solution.py:198
  (144 shorter events, 22.4 us)
Async XLA Ops:
  7.2 170.0 %copy-start.18 = (f32[3,1024]{1,0:T(4,128)S(1)}, f32[3,1024]{1,0:T(4,128)}, u32[]{:S(2)}) copy-start(f32[3,1024]{1,0:T(4,128)} %param.21) | copy-start | bytes 36868
  7.2 170.0 %copy-start.15 = (f32[2048]{0:T(1024)S(1)}, f32[2048]{0:T(1024)}, u32[]{:S(2)}) copy-start(f32[2048]{0:T(1024)} %param.19) | copy-start | bytes 24580
  7.2 170.0 %copy-start.9 = (f32[2048]{0:T(1024)S(1)}, f32[2048]{0:T(1024)}, u32[]{:S(2)}) copy-start(f32[2048]{0:T(1024)} %param.18) | copy-start | bytes 24580
  7.2 14.1 all-gather.9.cloned.1.call-start
  7.9 169.2 %all-gather.11.cloned.1.call-start = ((), (), s32[]{:S(2)}) async-start(), calls=%async_computation.9 | async-start | bytes 13369344 | tf_op jit(solution)/shard_map/all_gather | solution.py:144
  8.7 258.6 %all-gather.13.cloned.1.call-start = ((), (), s32[]{:S(2)}) async-start(), calls=%async_computation.10 | async-start | bytes 4456448 | tf_op jit(solution)/shard_map/all_gather | solution.py:145
  9.4 270.9 %reduce-scatter.9.cloned.1.call-start = ((), (), s32[]{:S(2)}) async-start(), calls=%async_computation.11 | async-start | bytes 3145728 | tf_op jit(solution)/shard_map/reduce_scatter | solution.py:165
  24.5 159.5 %copy-start.13 = (f32[256]{0:T(256)}, f32[256]{0:T(256)S(1)}, u32[]{:S(2)}) copy-start(f32[256]{0:T(256)S(1)} %add_rsqrt_fusion) | copy-start | bytes 3076
  185.8 3.1 copy-start.8
  267.3 5.1 copy-start
  272.3 21.4 all-gather.15.cloned.1.call-start
  274.0 8.3 copy-start.10
  274.0 8.3 copy-start.17
  283.4 265.9 %all-gather.17.cloned.1.call-start = ((), (), s32[]{:S(2)}) async-start(), calls=%async_computation.13 | async-start | bytes 24510464 | tf_op jit(solution)/shard_map/all_gather | solution.py:171
  284.0 278.4 %all-gather.21.cloned.1.call-start = ((), (), s32[]{:S(2)}) async-start(), calls=%async_computation.16 | async-start | bytes 1572864 | tf_op jit(solution)/shard_map/all_gather | solution.py:188
  284.7 460.2 %all-gather.19.cloned.1.call-start = ((), (), s32[]{:S(2)}) async-start(), calls=%async_computation.14 | async-start | bytes 12255232 | tf_op jit(solution)/shard_map/all_gather | solution.py:172
  285.5 494.1 %reduce-scatter.13.cloned.1.call-start = ((), (), s32[]{:S(2)}) async-start(), calls=%async_computation.17 | async-start | bytes 3145728 | tf_op jit(solution)/shard_map/reduce_scatter | solution.py:204
  769.9 20.4 reduce-scatter.11.cloned.1.call-start
  779.3 24.8 all-gather.23.cloned.1.call-start
  793.7 105.1 %reduce-scatter.15.cloned.1.call-start = ((), (), s32[]{:S(2)}) async-start(), calls=%async_computation.19 | async-start | bytes 1572864 | tf_op jit(solution)/shard_map/reduce_scatter | solution.py:241
  829.9 34.4 %copy-start.2 = (bf16[1,256,1024]{2,1,0:T(8,128)(2,1)}, bf16[1,256,1024]{2,1,0:T(8,128)(2,1)S(1)}, u32[]{:S(2)}) copy-start(bf16[1,256,1024]{2,1,0:T(8,128)(2,1)S(1)} %copy.54) | copy-start | bytes 1572868
  834.6 29.7 copy-start.3
  835.9 28.5 copy-start.4
  835.9 9.3 copy-start.7
  845.1 193.2 %reduce-scatter.19.cloned.1.call-start = ((), (), s32[]{:S(2)}) async-start(), calls=%async_computation.21 | async-start | bytes 8912896 | tf_op jit(solution)/shard_map/reduce_scatter | solution.py:238
  851.0 665.4 %reduce-scatter.23.cloned.1.call-start = ((), (), s32[]{:S(2)}) async-start(), calls=%async_computation.23 | async-start | bytes 24510464 | tf_op jit(solution)/shard_map/reduce_scatter | solution.py:199
  864.2 0.7 copy-start.14
  864.2 0.7 copy-start.16
  864.3 1178.7 %reduce-scatter.17.cloned.1.call-start = ((), (), s32[]{:S(2)}) async-start(), calls=%async_computation.20 | async-start | bytes 26738688 | tf_op jit(solution)/shard_map/reduce_scatter | solution.py:237
  875.4 1.2 copy-start.1
  875.5 1.7 copy-start.6
  875.5 2113.8 %reduce-scatter.21.cloned.1.call-start = ((), (), s32[]{:S(2)}) async-start(), calls=%async_computation.22 | async-start | bytes 49020928 | tf_op jit(solution)/shard_map/reduce_scatter | solution.py:198
  896.7 3.6 copy-start.11
  896.7 3.6 copy-start.12
  897.0 48.7 %copy-start.5 = (f32[128,2048]{1,0:T(8,128)S(1)}, f32[128,2048]{1,0:T(8,128)}, u32[]{:S(2)}) copy-start(f32[128,2048]{1,0:T(8,128)} %get-tuple-element.196) | copy-start | bytes 3145732
Sparse Core Ops, SparseCore 0:
  9.6 11.7 all-gather.8
  24.1 153.0 all-gather.10
  179.9 87.3 all-gather.12
  272.5 7.7 reduce-scatter.8
  283.5 10.2 all-gather.14
  296.8 252.4 all-gather.16
  550.9 7.2 all-gather.20
  561.2 183.7 all-gather.18
  770.0 7.7 reduce-scatter.12
  780.5 9.6 reduce-scatter.10
  793.9 10.1 all-gather.22
  845.2 9.6 reduce-scatter.14
  857.8 180.3 reduce-scatter.18
  1041.0 475.3 reduce-scatter.22
  1519.2 523.7 reduce-scatter.16
  2045.7 943.5 reduce-scatter.20
where the time goes:
time: 3010 us; the launch traced here: 3000 us
  waiting for transfers between devices  2740 us (91%)
  matrix products  146 us (5%)
  blocking collectives  45.5 us (2%)
    reduce_scatter x1, waiting for transfers between devices, on_device(): lax.psum_scatter(gate_up_grad, 'dp', scatter_dimension=0, tiled=True)  946 us
    reduce_scatter x1, waiting for transfers between devices, on_device(): lax.psum_scatter(qkv_grad, 'dp', scatter_dimension=0, tiled=True)  527 us
    reduce_scatter x1, waiting for transfers between devices, on_device(): lax.psum_scatter(down_grad, 'dp', scatter_dimension=1, tiled=True)  478 us
    all_gather x1, waiting for transfers between devices, on_device(): lax.all_gather(gate_up_weight, 'dp', axis=1, tiled=True)  256 us
    all_gather x1, waiting for transfers between devices, on_device(): lax.all_gather(down_weight, 'dp', axis=1, tiled=True)  183 us
    all_gather x1, waiting for transfers between devices, on_device(): lax.all_gather(qkv_weight, 'dp', axis=1, tiled=True)  153 us
    reduce_scatter x1, waiting for transfers between devices, on_device(): lax.psum_scatter(out_w_grad, 'dp', scatter_dimension=1, tiled=True)  90.2 us
    all_gather x1, waiting for transfers between devices, on_device(): lax.all_gather(out_weight, 'dp', axis=1, tiled=True)  65.9 us
  transfers between devices with their start and end apart: 16, of which 13 were waited for; matrix products, arithmetic and copies ran while one was open for 4% of the time, Pallas kernels for 0%

commit v1 on v0

v1 whole, which is shorter than its diff:
```python
import jax
import jax.numpy as jnp
from jax import lax
from jax.sharding import PartitionSpec as P

HD = 64
ROT = 16

norm_eps = 1e-05
rope_base = 10000.0
score_scale = 0.125
masked_score = -1e30

GROUP_BITS = (1, 2)
BF = jnp.bfloat16
F32 = jnp.float32


def doc_positions(segment):
    token_index = jnp.arange(segment.shape[0], dtype=jnp.int32)
    begins = jnp.concatenate([jnp.ones((1,), dtype=jnp.bool_), segment[1:] != segment[:-1]])
    starts = lax.cummax(jnp.where(begins, token_index, jnp.zeros_like(token_index)), axis=0)
    return token_index - starts


def rotary_tables(positions):
    half_rot = ROT // 2
    frequency = rope_base ** (-(2.0 * jnp.arange(half_rot, dtype=F32)) / ROT)
    angles = positions.astype(F32)[:, None] * frequency[None, :]
    return (jnp.cos(angles), jnp.sin(angles))


def rotate(heads_in, cosine, sine, turn_sign):
    half_rot = cosine.shape[-1]
    lead_half = heads_in[..., :half_rot]
    tail_half = heads_in[..., half_rot : 2 * half_rot]
    remainder = heads_in[..., 2 * half_rot :]
    cos_b = cosine[:, None, :]
    sin_b = sine[:, None, :] * turn_sign
    return jnp.concatenate(
        [lead_half * cos_b - tail_half * sin_b, tail_half * cos_b + lead_half * sin_b, remainder],
        axis=-1,
    )


def norm_parts(values, gain, shift):
    row_mean = jnp.mean(values, axis=-1, keepdims=True)
    centred = values - row_mean
    inv_std = lax.rsqrt(jnp.mean(centred * centred, axis=-1, keepdims=True) + norm_eps)
    normed = centred * inv_std
    return (normed * gain + shift, normed, inv_std)


def norm_back(incoming, normed, inv_std, gain):
    scaled = incoming * gain
    adjusted = (
        scaled
        - jnp.mean(scaled, axis=-1, keepdims=True)
        - normed * jnp.mean(scaled * normed, axis=-1, keepdims=True)
    )
    return adjusted * inv_std


def attend(queries, keys_rot, values, allowed):
    scores = (
        jnp.einsum("qhd,khd->hqk", queries, keys_rot, preferred_element_type=F32) * score_scale
    )
    scores = jnp.where(allowed, scores, masked_score)
    row_top = jnp.max(scores, axis=-1, keepdims=True)
    weights = jnp.exp(scores - row_top)
    row_total = jnp.sum(weights, axis=-1, keepdims=True)
    attn_probs = (weights / row_total).astype(BF)
    mixed = jnp.einsum("hqk,khd->qhd", attn_probs, values, preferred_element_type=F32)
    return (mixed.astype(BF), row_top + jnp.log(row_total))


def attend_back(queries, keys_rot, values, log_total, mixed_grad, allowed):
    scores = (
        jnp.einsum("qhd,khd->hqk", queries, keys_rot, preferred_element_type=F32) * score_scale
    )
    scores = jnp.where(allowed, scores, masked_score)
    attn_probs = jnp.exp(scores - log_total)
    prob_grad = jnp.einsum("qhd,khd->hqk", mixed_grad, values, preferred_element_type=F32)
    value_grad = jnp.einsum(
        "hqk,qhd->khd", attn_probs.astype(BF), mixed_grad, preferred_element_type=F32
    )
    score_grad = (
        attn_probs * (prob_grad - jnp.sum(attn_probs * prob_grad, axis=-1, keepdims=True))
    ).astype(BF)
    query_grad = (
        jnp.einsum("hqk,khd->qhd", score_grad, keys_rot, preferred_element_type=F32) * score_scale
    )
    key_grad = (
        jnp.einsum("hqk,qhd->khd", score_grad, queries, preferred_element_type=F32) * score_scale
    )
    return (query_grad, key_grad, value_grad)


def dot(a, b, dims):
    return lax.dot_general(a, b, (dims, ((), ())), preferred_element_type=F32)


def on_device(
    tokens,
    segment_ids,
    ln1_gain,
    ln1_bias,
    qkv_weight,
    qkv_bias,
    out_weight,
    ln2_gain,
    ln2_bias,
    gate_up_weight,
    down_weight,
    out_grad,
):
    dp_size = lax.axis_size("dp")
    bits = dp_size.bit_length() - 1
    me = lax.axis_index("dp")
    core = lax.axis_index("tensor")
    rows, width = tokens.shape
    seq_len = segment_ids.shape[0]
    group = 1 << len(GROUP_BITS)
    far_bits = [b for b in reversed(range(bits)) if b not in GROUP_BITS]
    masks = [
        sum(1 << b for i, b in enumerate(GROUP_BITS) if (k >> i) & 1) for k in range(group)
    ]
    my_bit = [(me >> b) & 1 for b in range(bits)]
    rank = sum(my_bit[b] << i for i, b in enumerate(GROUP_BITS))
    heads = qkv_bias.shape[1] // HD // group
    head_cols = heads * HD
    hidden_cols = down_weight.shape[0] // group

    def swap(array, mask):
        if mask == 0:
            return array
        return lax.ppermute(array, "dp", [(d, d ^ mask) for d in range(dp_size)])

    def sibling(array):
        return lax.ppermute(array, "tensor", [(0, 1), (1, 0)])

    order = [bits - 1 - b for b in reversed(far_bits)]
    order += [bits - 1 - b for b in reversed(GROUP_BITS)]

    def to_rel(array):
        lead = array.ndim - 1
        cut = array.reshape(array.shape[:-1] + (2,) * bits + (width // dp_size,))
        cut = cut.transpose(list(range(lead)) + [lead + o for o in order] + [lead + bits])
        for i, b in enumerate(reversed(far_bits)):
            cut = jnp.where(my_bit[b] == 1, jnp.flip(cut, lead + i), cut)
        return cut.reshape(array.shape)

    def from_rel(array):
        lead = array.ndim - 1
        cut = array.reshape(array.shape[:-1] + (2,) * bits + (width // dp_size,))
        for i, b in enumerate(reversed(far_bits)):
            cut = jnp.where(my_bit[b] == 1, jnp.flip(cut, lead + i), cut)
        back = [order.index(i) for i in range(bits)]
        cut = cut.transpose(list(range(lead)) + [lead + o for o in back] + [lead + bits])
        return cut.reshape(array.shape)

    def natural(parts):
        cut = jnp.stack(parts)
        whole = cut.shape
        cut = cut.reshape((2,) * len(GROUP_BITS) + whole[1:])
        for i, b in enumerate(reversed(GROUP_BITS)):
            cut = jnp.where(my_bit[b] == 1, jnp.flip(cut, i), cut)
        return cut.reshape(whole)

    def to_group(pieces):
        return natural(
            [swap(lax.dynamic_index_in_dim(pieces, rank ^ k, 0, False), masks[k]) for k in range(group)]
        )

    def gather_rows(shard):
        for b in far_bits:
            shard = jnp.concatenate([shard, swap(shard, 1 << b)], axis=0)
        return shard

    def gather_cols(shard):
        for b in far_bits:
            shard = jnp.concatenate([shard, swap(shard, 1 << b)], axis=1)
        return shard

    def scatter_rows(grad):
        for b in reversed(far_bits):
            half = grad.shape[0] // 2
            grad = grad[:half] + swap(grad[half:].astype(BF), 1 << b).astype(F32)
        return grad

    def scatter_cols(grad):
        for b in reversed(far_bits):
            half = grad.shape[1] // 2
            grad = grad[:, :half] + swap(grad[:, half:].astype(BF), 1 << b).astype(F32)
        return grad

    def cut_cols(array, cols):
        return jnp.stack([array[:, i * cols : (i + 1) * cols] for i in range(group)])

    def spread(local):
        mine = jnp.stack([swap(local, m) for m in masks])
        return jnp.concatenate([mine, sibling(mine)], axis=1)

    def collect(blocks):
        both = blocks[:, :rows] + sibling(blocks[:, rows:].astype(BF)).astype(F32)
        total = both[0]
        for k in range(1, group):
            total = total + swap(both[k].astype(BF), masks[k]).astype(F32)
        return total

    block = width // dp_size

    q_cols = [cut_cols(qkv_weight[j], head_cols) for j in range(3)]
    w_qkv = gather_rows(to_group(jnp.concatenate(q_cols, axis=2)).reshape(group * block, -1))
    out_cut = to_group(out_weight.reshape(group, head_cols, block))
    w_out = gather_cols(out_cut.transpose(1, 0, 2).reshape(head_cols, group * block))
    g_cols = [cut_cols(gate_up_weight[j], hidden_cols) for j in range(2)]
    g_cut = jnp.concatenate(g_cols, axis=2)
    w_gate_up = gather_rows(to_group(g_cut).reshape(group * block, -1))
    d_cut = to_group(down_weight.reshape(group, hidden_cols, block))
    w_down = gather_cols(d_cut.transpose(1, 0, 2).reshape(hidden_cols, group * block))

    gains = to_rel(jnp.stack([ln1_gain, ln1_bias, ln2_gain, ln2_bias]))
    resid = to_rel(tokens).astype(F32)
    normed_in, normed_one, inv_one = norm_parts(resid, gains[0], gains[1])
    seq_in = spread(normed_in.astype(BF)).reshape(group * seq_len, width)
    grad_local = to_rel(out_grad)
    grad_rows = spread(grad_local).reshape(group * seq_len, width)

    positions = doc_positions(segment_ids)
    token_index = jnp.arange(seq_len, dtype=jnp.int32)
    facts = jnp.stack([segment_ids, positions, token_index])
    facts = jnp.stack([swap(facts, m) for m in masks])
    facts = jnp.where(core == 1, jnp.roll(facts, rows, axis=2), facts)
    segs, spots, index = facts[:, 0], facts[:, 1], facts[:, 2]
    allowed = (segs[:, :, None] == segs[:, None, :]) & (index[:, None, :] <= index[:, :, None])
    allowed = allowed[:, None]
    cosine, sine = rotary_tables(spots.reshape(-1))

    bias = lax.dynamic_slice_in_dim(qkv_bias, rank * head_cols, head_cols, 1).reshape(-1)
    projected = dot(seq_in, w_qkv, ((1,), (0,))) + bias
    shaped = projected.reshape(group * seq_len, 3, heads, HD)
    by_seq = (group, seq_len, heads, HD)
    queries = rotate(shaped[:, 0], cosine, sine, 1.0).astype(BF).reshape(by_seq)
    keys_rot = rotate(shaped[:, 1], cosine, sine, 1.0).astype(BF).reshape(by_seq)
    values = shaped[:, 2].astype(BF).reshape(by_seq)
    mixed, log_total = jax.vmap(attend)(queries, keys_rot, values, allowed)
    mixed_rows = mixed.reshape(group * seq_len, head_cols)
    attn_terms = dot(mixed_rows, w_out, ((1,), (0,)))
    resid_two = resid + collect(attn_terms.reshape(group, seq_len, width))
    normed_mid, normed_two, inv_two = norm_parts(resid_two, gains[2], gains[3])
    seq_mid = spread(normed_mid.astype(BF)).reshape(group * seq_len, width)

    gate_up = dot(seq_mid, w_gate_up, ((1,), (0,)))
    gate_pre = gate_up[:, :hidden_cols]
    up_values = gate_up[:, hidden_cols:]
    gate_sig = jax.nn.sigmoid(gate_pre)
    smooth = gate_pre * gate_sig
    hidden = (smooth * up_values).astype(BF)
    hidden_grad = dot(grad_rows, w_down, ((1,), (1,)))
    gate_grad = (hidden_grad * up_values * gate_sig * (1.0 + gate_pre * (1.0 - gate_sig))).astype(BF)
    up_grad = (hidden_grad * smooth).astype(BF)
    pair_grad = jnp.concatenate([gate_grad, up_grad], axis=1)
    mid_terms = dot(pair_grad, w_gate_up, ((1,), (1,)))
    mid_local = collect(mid_terms.reshape(group, seq_len, width))
    resid_grad = grad_local.astype(F32) + norm_back(mid_local, normed_two, inv_two, gains[2])
    attn_grad = spread(resid_grad.astype(BF)).reshape(group * seq_len, width)

    mlp_terms = dot(hidden, w_down, ((1,), (0,)))
    result = from_rel((resid_two + collect(mlp_terms.reshape(group, seq_len, width))).astype(BF))

    def final_rows(grad, parts):
        mine = scatter_rows(grad).reshape(group, block, -1)
        return to_group(mine.astype(BF)).reshape(group, block, parts, -1).transpose(2, 1, 0, 3).reshape(
            parts, block, -1
        ).astype(F32)

    def final_cols(grad):
        mine = scatter_cols(grad)
        mine = mine.reshape(grad.shape[0], group, block).transpose(1, 0, 2)
        return to_group(mine.astype(BF)).reshape(-1, block).astype(F32)

    down_grad = final_cols(dot(hidden, grad_rows, ((0,), (0,))))
    gate_up_grad = final_rows(dot(seq_mid, pair_grad, ((0,), (0,))), 2)

    mixed_grad = dot(attn_grad, w_out, ((1,), (1,))).astype(BF).reshape(by_seq)
    query_grad, key_grad, value_grad = jax.vmap(attend_back)(
        queries, keys_rot, values, log_total, mixed_grad, allowed
    )
    flat = (group * seq_len, heads, HD)
    lin_grad = jnp.stack(
        [
            rotate(query_grad.reshape(flat), cosine, sine, -1.0),
            rotate(key_grad.reshape(flat), cosine, sine, -1.0),
            value_grad.reshape(flat),
        ],
        axis=1,
    )
    lin_grad = lin_grad.reshape(group * seq_len, 3 * head_cols).astype(BF)
    qkv_grad = final_rows(dot(seq_in, lin_grad, ((0,), (0,))), 3)
    out_w_grad = final_cols(dot(mixed_rows, attn_grad, ((0,), (0,))))

    in_terms = dot(lin_grad, w_qkv, ((1,), (1,)))
    in_grad = collect(in_terms.reshape(group, seq_len, width))
    token_grad = from_rel(resid_grad + norm_back(in_grad, normed_one, inv_one, gains[0]))

    norm_sums = from_rel(
        jnp.stack(
            [
                jnp.sum(in_grad * normed_one, axis=0),
                jnp.sum(in_grad, axis=0),
                jnp.sum(mid_local * normed_two, axis=0),
                jnp.sum(mid_local, axis=0),
            ]
        )
    )
    bias_rows = jnp.sum(lin_grad.astype(F32), axis=0).reshape(3, head_cols)
    bias_full = lax.dynamic_update_slice(
        jnp.zeros((3, head_cols * group * lax.axis_size("tensor")), F32),
        bias_rows,
        (jnp.int32(0), (core * group + rank) * head_cols),
    )
    sums = jnp.concatenate([norm_sums.reshape(-1), bias_full.reshape(-1)])
    sums = sums + sibling(sums)
    for b in range(bits):
        sums = sums + swap(sums, 1 << b)
    norm_sums = sums[: 4 * width].reshape(4, width)
    return (
        result,
        token_grad,
        norm_sums[0],
        norm_sums[1],
        qkv_grad,
        sums[4 * width :].reshape(3, -1),
        out_w_grad,
        norm_sums[2],
        norm_sums[3],
        gate_up_grad,
        down_grad,
    )


def solution(mesh):
    return jax.shard_map(
        on_device,
        mesh=mesh,
        in_specs=(
            P(("dp", "tensor"), None),
            P("dp"),
            P(),
            P(),
            P(None, "dp", "tensor"),
            P(None, "tensor"),
            P("tensor", "dp"),
            P(),
            P(),
            P(None, "dp", "tensor"),
            P("tensor", "dp"),
            P(("dp", "tensor"), None),
        ),
        out_specs=(
            P(("dp", "tensor"), None),
            P(("dp", "tensor"), None),
            P(),
            P(),
            P(None, "dp", "tensor"),
            P(),
            P("tensor", "dp"),
            P(),
            P(),
            P(None, "dp", "tensor"),
            P("tensor", "dp"),
        ),
        check_vma=False,
    )
```

time: 3010 us -> 823 us (0.27)
  waiting for transfers between devices: 2740 us -> 481 us
  matrix products: 146 us -> 67.5 us
  starting transfers between devices: 1.28 us -> 76.9 us
  local copies, waits for them, and re-layouts: 13.7 us -> 87.9 us
  other arithmetic: 29.7 us -> 96.5 us
  blocking collectives: 45.5 us -> 0 us
    reduce_scatter x8 -> x0, waiting for transfers between devices: 2060 us -> none  [the longest x1 946 us: on_device(): lax.psum_scatter(gate_up_grad, 'dp', scatter_dimension=0, tiled=True)]
    all_gather x8 -> x0, waiting for transfers between devices: 685 us -> none  [the longest x1 256 us: on_device(): lax.all_gather(gate_up_weight, 'dp', axis=1, tiled=True)]
    ppermute x0 -> x80, waiting for transfers between devices: none -> 481 us  [the longest x71 479 us: swap(): return lax.ppermute(array, 'dp', [(d, d ^ mask) for d in range(dp_size)])]
    dot_general x40 -> x18, matrix products: 146 us -> 67.5 us  [the longest x12 60.4 us: dot(): return lax.dot_general(a, b, (dims, ((), ())), preferred_element_type=F32)]
    ppermute x0 -> x80, starting transfers between devices: none -> 76.9 us  [the longest x71 76.6 us: swap(): return lax.ppermute(array, 'dp', [(d, d ^ mask) for d in range(dp_size)])]
    psum x1 -> x0, blocking collectives: 45.5 us -> none  [on_device(): lax.psum((jnp.sum(in_grad * normed_local, axis=0), jnp.sum(in_grad, axis=...]
    another operation x7 -> x25, other arithmetic: 2.98 us -> 33.3 us
  transfers between devices with their start and end apart: 16 -> 80, of which waited for: 13 -> 42; matrix products, arithmetic and copies ran while one was open for 4% -> 23% of each run, Pallas kernels for 0% -> 0%
where the time goes in v1:
time: 823 us; the launch traced here: 813 us
  waiting for transfers between devices  481 us (58%)
  other arithmetic  96.5 us (12%)
  local copies, waits for them, and re-layouts  87.9 us (11%)
  starting transfers between devices  76.9 us (9%)
  matrix products  67.5 us (8%)
    ppermute x71, waiting for transfers between devices, swap(): return lax.ppermute(array, 'dp', [(d, d ^ mask) for d in range(dp_size)])  479 us
    ppermute x71, starting transfers between devices, swap(): return lax.ppermute(array, 'dp', [(d, d ^ mask) for d in range(dp_size)])  76.6 us
    dot_general x12, matrix products, dot(): return lax.dot_general(a, b, (dims, ((), ())), preferred_element_type=F32)  60.4 us
    unnamed x233, local copies, waits for them, and re-layouts  24.3 us
    another operation x7, other arithmetic  18.1 us
  transfers between devices with their start and end apart: 80, of which 42 were waited for; matrix products, arithmetic and copies ran while one was open for 23% of the time, Pallas kernels for 0%

profile of v1, /device:TPU:0, one launch (start us, length us, event | category | flops | bytes accessed | tf_op | source)
XLA Modules:
  0.0 812.7 jit_solution(6015363204037098096)
XLA Ops:
  3.5 3.0 collective-permute-start.10
  19.9 2.9 collective-permute-start.2
  41.1 10.2 %collective-permute-done.6 = bf16[128,768]{1,0:T(8,128)(2,1)S(1)} collective-permute-done((bf16[128,768]{1,0:T(8,128)(2,1)}, bf16[128,768]{1,0:T(8,128)(2,1)S(1)}, u32[]{:S(2)}, u32[]{:S(2)}) %collective-permute-start.6) | collective-permute-done | bytes 196640 | tf_op jit(solution)/shard_map/ppermute | solution.py:137
  57.7 2.3 copy.86
  62.8 2.3 copy.87
  66.8 2.6 collective-permute-start.7
  75.0 33.3 %collective-permute-done.7 = bf16[512,768]{1,0:T(8,128)(2,1)S(1)} collective-permute-done((bf16[512,768]{1,0:T(8,128)(2,1)}, bf16[512,768]{1,0:T(8,128)(2,1)S(1)}, u32[]{:S(2)}, u32[]{:S(2)}) %collective-permute-start.7) | collective-permute-done | bytes 786464 | tf_op jit(solution)/shard_map/ppermute | solution.py:137
  115.2 35.8 %collective-permute-done.16 = bf16[256,1024]{1,0:T(8,128)(2,1)S(1)} collective-permute-done((bf16[256,1024]{1,0:T(8,128)(2,1)S(1)}, bf16[256,1024]{1,0:T(8,128)(2,1)S(1)}, u32[]{:S(2)}, u32[]{:S(2)}) %collective-permute-start.16) | collective-permute-done | bytes 524320 | tf_op jit(solution)/shard_map/ppermute | solution.py:137
  151.1 4.6 collective-permute-start.31
  158.8 3.6 convolution_add_fusion
  182.8 6.4 collective-permute-done.27
  189.3 7.8 collective-permute-done.26
  197.5 3.3 collective-permute-start.33
  204.2 14.1 %collective-permute-done.40 = bf16[128,2048]{1,0:T(8,128)(2,1)S(1)} collective-permute-done((bf16[128,2048]{1,0:T(8,128)(2,1)}, bf16[128,2048]{1,0:T(8,128)(2,1)S(1)}, u32[]{:S(2)}, u32[]{:S(2)}) %collective-permute-start.40) | collective-permute-done | bytes 524320 | tf_op jit(solution)/shard_map/ppermute | solution.py:137
  218.6 3.0 pad_maximum_fusion.12
  221.6 11.8 %collective-permute-done.33 = bf16[704,512]{1,0:T(8,128)(2,1)S(1)} collective-permute-done((bf16[704,512]{1,0:T(8,128)(2,1)S(1)}, bf16[704,512]{1,0:T(8,128)(2,1)S(1)}, u32[]{:S(2)}, u32[]{:S(2)}) %collective-permute-start.33) | collective-permute-done | bytes 720928 | tf_op jit(solution)/shard_map/ppermute | solution.py:137
  234.7 16.1 %collective-permute-done.20 = bf16[128,2048]{1,0:T(8,128)(2,1)S(1)} collective-permute-done((bf16[128,2048]{1,0:T(8,128)(2,1)S(1)}, bf16[128,2048]{1,0:T(8,128)(2,1)S(1)}, u32[]{:S(2)}, u32[]{:S(2)}) %collective-permute-start.20) | collective-permute-done | bytes 524320 | tf_op jit(solution)/shard_map/ppermute | solution.py:137
  250.9 10.9 %collective-permute-done.19 = bf16[128,2048]{1,0:T(8,128)(2,1)S(1)} collective-permute-done((bf16[128,2048]{1,0:T(8,128)(2,1)S(1)}, bf16[128,2048]{1,0:T(8,128)(2,1)S(1)}, u32[]{:S(2)}, u32[]{:S(2)}) %collective-permute-start.19) | collective-permute-done | bytes 524320 | tf_op jit(solution)/shard_map/ppermute | solution.py:137
  263.0 3.4 collective-permute-start.23
  266.4 26.1 %collective-permute-done.28 = bf16[512,1408]{1,0:T(8,128)(2,1)S(1)} collective-permute-done((bf16[512,1408]{1,0:T(8,128)(2,1)S(1)}, bf16[512,1408]{1,0:T(8,128)(2,1)S(1)}, u32[]{:S(2)}, u32[]{:S(2)}) %collective-permute-start.28) | collective-permute-done | bytes 1441824 | tf_op jit(solution)/shard_map/ppermute | solution.py:137
  296.9 3.5 collective-permute-done.23
  303.5 84.0 %collective-permute-done.34 = bf16[704,1024]{1,0:T(8,128)(2,1)} collective-permute-done((bf16[704,1024]{1,0:T(8,128)(2,1)}, bf16[704,1024]{1,0:T(8,128)(2,1)}, u32[]{:S(2)}, u32[]{:S(2)}) %collective-permute-start.34) | collective-permute-done | bytes 1441824 | tf_op jit(solution)/shard_map/ppermute | solution.py:137
  395.2 9.5 %fusion.7 = f32[1024,1408]{1,0:T(8,128)S(1)} fusion(bf16[1024,2048]{1,0:T(8,128)(2,1)S(1)} %bitcast.422, bf16[1024,1408]{1,0:T(8,128)(2,1)} %collective-permute-done.29, bf16[512,1408]{1,0:T(8,128)(2,1)S(1)} %copy-done.52, bf16[512,1408]{1,0:T(8,128)(2,1)S(1)} %bitcast.411), kind=kOutput, calls=%fused_computation.43 | convolution fusion | flops 5922881536 | bytes 15728640 | tf_op jit(solution)/shard_map/dot_general | solution.py:100
  404.8 5.9 multiply_convert_fusion.2
  410.7 5.0 fusion.73
  415.7 8.5 %fusion.6 = f32[1024,2048]{1,0:T(8,128)S(1)} fusion(bf16[1024,1408]{1,0:T(8,128)(2,1)} %collective-permute-done.29, bf16[512,1408]{1,0:T(8,128)(2,1)S(1)} %copy-done.52, bf16[512,1408]{1,0:T(8,128)(2,1)S(1)} %bitcast.412, bf16[1024,704]{1,0:T(8,128)(2,1)S(1)} %copy-done.103, bf16[1024,704]{1,0:T(8,128)(2,1)S(1)} %copy-done.102), kind=kOutput, calls=%fused_computation.42 | convolution fusion | flops 5928648704 | bytes 17039360 | tf_op jit(solution)/shard_map/dot_general | solution.py:100
  426.8 4.8 fusion.70
  431.6 3.1 slice.689
  437.8 10.2 %fusion.12 = f32[2048,1408]{1,0:T(8,128)S(1)} fusion(bf16[1024,2048]{1,0:T(8,128)(2,1)} %bitcast.423, bf16[1024,704]{1,0:T(8,128)(2,1)} %get-tuple-element.58, bf16[1024,704]{1,0:T(8,128)(2,1)} %get-tuple-element.57), kind=kOutput, calls=%fused_computation.55 | convolution fusion | flops 5911347200 | bytes 18612224 | tf_op jit(solution)/shard_map/dot_general | solution.py:100
  450.7 2.4 copy-done.7
  453.2 16.3 %collective-permute-done.75 = bf16[704,1024]{1,0:T(8,128)(2,1)S(1)} collective-permute-done((bf16[704,1024]{1,0:T(8,128)(2,1)}, bf16[704,1024]{1,0:T(8,128)(2,1)S(1)}, u32[]{:S(2)}, u32[]{:S(2)}) %collective-permute-start.75) | collective-permute-done | bytes 1441824 | tf_op jit(solution)/shard_map/ppermute | solution.py:137
  471.9 4.5 fusion.60
  479.1 5.1 fusion.61
  484.2 19.3 %collective-permute-done.76 = bf16[704,512]{1,0:T(8,128)(2,1)S(1)} collective-permute-done((bf16[704,512]{1,0:T(8,128)(2,1)S(1)}, bf16[704,512]{1,0:T(8,128)(2,1)S(1)}, u32[]{:S(2)}, u32[]{:S(2)}) %collective-permute-start.76) | collective-permute-done | bytes 720928 | tf_op jit(solution)/shard_map/ppermute | solution.py:137
  506.6 2.5 collective-permute-start.78
  509.3 4.7 collective-permute-done.79
  520.1 9.7 %collective-permute-done.46 = bf16[128,2048]{1,0:T(8,128)(2,1)S(1)} collective-permute-done((bf16[128,2048]{1,0:T(8,128)(2,1)S(1)}, bf16[128,2048]{1,0:T(8,128)(2,1)S(1)}, u32[]{:S(2)}, u32[]{:S(2)}) %collective-permute-start.46) | collective-permute-done | bytes 524320 | tf_op jit(solution)/shard_map/ppermute | solution.py:137
  529.8 10.6 %collective-permute-done.45 = bf16[128,2048]{1,0:T(8,128)(2,1)S(1)} collective-permute-done((bf16[128,2048]{1,0:T(8,128)(2,1)S(1)}, bf16[128,2048]{1,0:T(8,128)(2,1)S(1)}, u32[]{:S(2)}, u32[]{:S(2)}) %collective-permute-start.45) | collective-permute-done | bytes 524320 | tf_op jit(solution)/shard_map/ppermute | solution.py:137
  542.4 4.0 slice_add_fusion
  547.9 17.2 %collective-permute-done.38 = bf16[128,2048]{1,0:T(8,128)(2,1)S(1)} collective-permute-done((bf16[128,2048]{1,0:T(8,128)(2,1)S(1)}, bf16[128,2048]{1,0:T(8,128)(2,1)S(1)}, u32[]{:S(2)}, u32[]{:S(2)}) %collective-permute-start.38) | collective-permute-done | bytes 524320 | tf_op jit(solution)/shard_map/ppermute | solution.py:137
  565.0 8.7 %collective-permute-done.37 = bf16[128,2048]{1,0:T(8,128)(2,1)S(1)} collective-permute-done((bf16[128,2048]{1,0:T(8,128)(2,1)S(1)}, bf16[128,2048]{1,0:T(8,128)(2,1)S(1)}, u32[]{:S(2)}, u32[]{:S(2)}) %collective-permute-start.37) | collective-permute-done | bytes 524320 | tf_op jit(solution)/shard_map/ppermute | solution.py:137
  573.7 3.2 fusion.58
  577.4 2.5 collective-permute-start.48
  582.0 20.3 %collective-permute-done.49 = bf16[128,2048]{1,0:T(8,128)(2,1)S(1)} collective-permute-done((bf16[128,2048]{1,0:T(8,128)(2,1)S(1)}, bf16[128,2048]{1,0:T(8,128)(2,1)S(1)}, u32[]{:S(2)}, u32[]{:S(2)}) %collective-permute-start.49) | collective-permute-done | bytes 524320 | tf_op jit(solution)/shard_map/ppermute | solution.py:137
  602.4 17.8 %collective-permute-done.48 = bf16[128,2048]{1,0:T(8,128)(2,1)S(1)} collective-permute-done((bf16[128,2048]{1,0:T(8,128)(2,1)S(1)}, bf16[128,2048]{1,0:T(8,128)(2,1)S(1)}, u32[]{:S(2)}, u32[]{:S(2)}) %collective-permute-start.48) | collective-permute-done | bytes 524320 | tf_op jit(solution)/shard_map/ppermute | solution.py:137
  622.8 2.5 fusion.5
  632.8 6.0 collective-permute-done.74
  638.8 6.0 collective-permute-done.73
  655.2 3.1 fusion.17
  670.4 5.5 fusion.71
  677.3 2.4 copy-done.18
  680.2 3.5 fusion.2
  696.7 5.8 collective-permute-done.66
  710.7 5.3 collective-permute-done.60
  716.0 2.7 slice_add_fusion.5
  719.7 6.0 fusion.57
  725.6 28.2 %collective-permute-done.61 = bf16[512,768]{1,0:T(8,128)(2,1)S(1)} collective-permute-done((bf16[512,768]{1,0:T(8,128)(2,1)S(1)}, bf16[512,768]{1,0:T(8,128)(2,1)S(1)}, u32[]{:S(2)}, u32[]{:S(2)}) %collective-permute-start.61) | collective-permute-done | bytes 786464 | tf_op jit(solution)/shard_map/ppermute | solution.py:137
  754.2 2.4 collective-permute-start.63
  760.3 2.5 collective-permute-done.64
  762.9 3.7 collective-permute-done.63
  769.9 18.7 %collective-permute-done.52 = bf16[128,2048]{1,0:T(8,128)(2,1)S(1)} collective-permute-done((bf16[128,2048]{1,0:T(8,128)(2,1)}, bf16[128,2048]{1,0:T(8,128)(2,1)S(1)}, u32[]{:S(2)}, u32[]{:S(2)}) %collective-permute-start.52) | collective-permute-done | bytes 524320 | tf_op jit(solution)/shard_map/ppermute | solution.py:137
  788.6 2.9 multiply_reduce_fusion.2
  793.7 3.6 collective-permute-done.56
  802.2 3.6 collective-permute-done.58
  (552 shorter events, 208.0 us)
Async XLA Ops:
  3.5 32.7 %collective-permute-start.10 = (s32[3,256]{1,0:T(4,128)}, s32[3,256]{1,0:T(4,128)}, u32[]{:S(2)}, u32[]{:S(2)}) collective-permute-start(s32[3,256]{1,0:T(4,128)} %get-tuple-element.161), channel_id=1, source_target_pairs={{0,8},{2,10},{4,12},{6,14},{8,0},{10,2},{12,4},{14,6},{16,24},{18,... | collective-permute-start | bytes 9224 | tf_op jit(solution)/shard_map/ppermute | solution.py:137
  6.5 31.2 %collective-permute-start.9 = (s32[3,256]{1,0:T(4,128)}, s32[3,256]{1,0:T(4,128)}, u32[]{:S(2)}, u32[]{:S(2)}) collective-permute-start(s32[3,256]{1,0:T(4,128)} %get-tuple-element.161), channel_id=1, source_target_pairs={{0,4},{2,6},{4,0},{6,2},{8,12},{10,14},{12,8},{14,10},{16,20},{18,... | collective-permute-start | bytes 9224 | tf_op jit(solution)/shard_map/ppermute | solution.py:137
  8.0 29.8 %collective-permute-start.11 = (s32[3,256]{1,0:T(4,128)}, s32[3,256]{1,0:T(4,128)}, u32[]{:S(2)}, u32[]{:S(2)}) collective-permute-start(s32[3,256]{1,0:T(4,128)} %get-tuple-element.161), channel_id=1, source_target_pairs={{0,12},{2,14},{4,8},{6,10},{8,4},{10,6},{12,0},{14,2},{16,28},{18,... | collective-permute-start | bytes 9224 | tf_op jit(solution)/shard_map/ppermute | solution.py:137
  19.9 45.3 %collective-permute-start.2 = (bf16[128,2048]{1,0:T(8,128)(2,1)}, bf16[128,2048]{1,0:T(8,128)(2,1)}, u32[]{:S(2)}, u32[]{:S(2)}) collective-permute-start(bf16[128,2048]{1,0:T(8,128)(2,1)} %add_convert_fusion.1), channel_id=1, source_target_pairs={{0,12},{2,14},{4,8},{6,10},{8,4},{10,6},{12,0},{14,2},{16,28},{18,... | collective-permute-start | bytes 1572872 | tf_op jit(solution)/shard_map/ppermute | solution.py:137
  22.8 44.0 %collective-permute-start.1 = (bf16[128,2048]{1,0:T(8,128)(2,1)}, bf16[128,2048]{1,0:T(8,128)(2,1)}, u32[]{:S(2)}, u32[]{:S(2)}) collective-permute-start(bf16[128,2048]{1,0:T(8,128)(2,1)} %add_convert_fusion.1), channel_id=1, source_target_pairs={{0,8},{2,10},{4,12},{6,14},{8,0},{10,2},{12,4},{14,6},{16,24},{18,... | collective-permute-start | bytes 1572872 | tf_op jit(solution)/shard_map/ppermute | solution.py:137
  36.2 15.1 %collective-permute-start.6 = (bf16[128,768]{1,0:T(8,128)(2,1)}, bf16[128,768]{1,0:T(8,128)(2,1)S(1)}, u32[]{:S(2)}, u32[]{:S(2)}) collective-permute-start(bf16[128,768]{1,0:T(8,128)(2,1)} %get-tuple-element.98), channel_id=1, source_target_pairs={{0,12},{2,14},{4,8},{6,10},{8,4},{10,6},{12,0},{14,2},{16,28},{18,... | collective-permute-start | bytes 589832 | tf_op jit(solution)/shard_map/ppermute | solution.py:137
  37.7 16.2 %collective-permute-start.5 = (bf16[128,768]{1,0:T(8,128)(2,1)}, bf16[128,768]{1,0:T(8,128)(2,1)S(1)}, u32[]{:S(2)}, u32[]{:S(2)}) collective-permute-start(bf16[128,768]{1,0:T(8,128)(2,1)} %get-tuple-element.99), channel_id=1, source_target_pairs={{0,8},{2,10},{4,12},{6,14},{8,0},{10,2},{12,4},{14,6},{16,24},{18,... | collective-permute-start | bytes 589832 | tf_op jit(solution)/shard_map/ppermute | solution.py:137
  37.9 17.6 %collective-permute-start.4 = (bf16[128,768]{1,0:T(8,128)(2,1)}, bf16[128,768]{1,0:T(8,128)(2,1)S(1)}, u32[]{:S(2)}, u32[]{:S(2)}) collective-permute-start(bf16[128,768]{1,0:T(8,128)(2,1)} %get-tuple-element.100), channel_id=1, source_target_pairs={{0,4},{2,6},{4,0},{6,2},{8,12},{10,14},{12,8},{14,10},{16,20},{18,... | collective-permute-start | bytes 589832 | tf_op jit(solution)/shard_map/ppermute | solution.py:137
  51.3 18.1 %collective-permute-start = (bf16[128,2048]{1,0:T(8,128)(2,1)}, bf16[128,2048]{1,0:T(8,128)(2,1)S(1)}, u32[]{:S(2)}, u32[]{:S(2)}) collective-permute-start(bf16[128,2048]{1,0:T(8,128)(2,1)} %add_convert_fusion.1), channel_id=1, source_target_pairs={{0,4},{2,6},{4,0},{6,2},{8,12},{10,14},{12,8},{14,10},{16,20},{18,... | collective-permute-start | bytes 1572872 | tf_op jit(solution)/shard_map/ppermute | solution.py:137
  53.9 17.1 %collective-permute-start.14 = (bf16[256,128]{1,0:T(8,128)(2,1)}, bf16[256,128]{1,0:T(8,128)(2,1)S(1)}, u32[]{:S(2)}, u32[]{:S(2)}) collective-permute-start(bf16[256,128]{1,0:T(8,128)(2,1)} %get-tuple-element.125), channel_id=1, source_target_pairs={{0,12},{2,14},{4,8},{6,10},{8,4},{10,6},{12,0},{14,2},{16,28},{18,... | collective-permute-start | bytes 196616 | tf_op jit(solution)/shard_map/ppermute | solution.py:137
  55.4 17.2 %collective-permute-start.13 = (bf16[256,128]{1,0:T(8,128)(2,1)}, bf16[256,128]{1,0:T(8,128)(2,1)S(1)}, u32[]{:S(2)}, u32[]{:S(2)}) collective-permute-start(bf16[256,128]{1,0:T(8,128)(2,1)} %get-tuple-element.126), channel_id=1, source_target_pairs={{0,8},{2,10},{4,12},{6,14},{8,0},{10,2},{12,4},{14,6},{16,24},{18,... | collective-permute-start | bytes 196616 | tf_op jit(solution)/shard_map/ppermute | solution.py:137
  66.8 41.5 %collective-permute-start.7 = (bf16[512,768]{1,0:T(8,128)(2,1)}, bf16[512,768]{1,0:T(8,128)(2,1)S(1)}, u32[]{:S(2)}, u32[]{:S(2)}) collective-permute-start(bf16[512,768]{1,0:T(8,128)(2,1)} %bitcast.432), channel_id=1, source_target_pairs={{0,16},{2,18},{4,20},{6,22},{8,24},{10,26},{12,28},{14,30},{16,0},... | collective-permute-start | bytes 2359304 | tf_op jit(solution)/shard_map/ppermute | solution.py:137
  70.9 84.7 %collective-permute-start.3 = (bf16[4,128,2048]{2,1,0:T(8,128)(2,1)S(1)}, bf16[4,128,2048]{2,1,0:T(8,128)(2,1)S(1)}, u32[]{:S(2)}, u32[]{:S(2)}) collective-permute-start(bf16[4,128,2048]{2,1,0:T(8,128)(2,1)S(1)} %pad_maximum_fusion.10), channel_id=1, source_target_pairs={{0,1},{1,0},{2,3},{3,2},{4,5},{5,4},{6,7},{7,6},{8,9},{9,8},{10,11... | collective-permute-start | bytes 6291464 | tf_op jit(solution)/shard_map/ppermute | solution.py:140
  71.1 133.1 %collective-permute-start.41 = (bf16[128,2048]{1,0:T(8,128)(2,1)}, bf16[128,2048]{1,0:T(8,128)(2,1)}, u32[]{:S(2)}, u32[]{:S(2)}) collective-permute-start(bf16[128,2048]{1,0:T(8,128)(2,1)} %reshape.571), channel_id=1, source_target_pairs={{0,12},{2,14},{4,8},{6,10},{8,4},{10,6},{12,0},{14,2},{16,28},{18,... | collective-permute-start | bytes 1572872 | tf_op jit(solution)/shard_map/ppermute | solution.py:137
  72.6 104.2 %collective-permute-start.32 = (bf16[704,128]{1,0:T(8,128)(2,1)}, bf16[704,128]{1,0:T(8,128)(2,1)}, u32[]{:S(2)}, u32[]{:S(2)}) collective-permute-start(bf16[704,128]{1,0:T(8,128)(2,1)} %get-tuple-element.109), channel_id=1, source_target_pairs={{0,12},{2,14},{4,8},{6,10},{8,4},{10,6},{12,0},{14,2},{16,28},{18,... | collective-permute-start | bytes 540680 | tf_op jit(solution)/shard_map/ppermute | solution.py:137
  74.6 38.2 %collective-permute-start.15 = (bf16[256,512]{1,0:T(8,128)(2,1)S(1)}, bf16[256,512]{1,0:T(8,128)(2,1)S(1)}, u32[]{:S(2)}, u32[]{:S(2)}) collective-permute-start(bf16[256,512]{1,0:T(8,128)(2,1)S(1)} %bitcast.475), channel_id=1, source_target_pairs={{0,16},{2,18},{4,20},{6,22},{8,24},{10,26},{12,28},{14,30},{16,0},... | collective-permute-start | bytes 786440 | tf_op jit(solution)/shard_map/ppermute | solution.py:137
  108.4 50.4 %collective-permute-start.8 = (bf16[1024,768]{1,0:T(8,128)(2,1)S(1)}, bf16[1024,768]{1,0:T(8,128)(2,1)S(1)}, u32[]{:S(2)}, u32[]{:S(2)}) collective-permute-start(bf16[1024,768]{1,0:T(8,128)(2,1)S(1)} %pad_maximum_fusion.16), channel_id=1, source_target_pairs={{0,2},{2,0},{4,6},{6,4},{8,10},{10,8},{12,14},{14,12},{16,18},{18,... | collective-permute-start | bytes 4718600 | tf_op jit(solution)/shard_map/ppermute | solution.py:137
  112.8 38.3 %collective-permute-start.16 = (bf16[256,1024]{1,0:T(8,128)(2,1)S(1)}, bf16[256,1024]{1,0:T(8,128)(2,1)S(1)}, u32[]{:S(2)}, u32[]{:S(2)}) collective-permute-start(bf16[256,1024]{1,0:T(8,128)(2,1)S(1)} %pad_maximum_fusion.26), channel_id=1, source_target_pairs={{0,2},{2,0},{4,6},{6,4},{8,10},{10,8},{12,14},{14,12},{16,18},{18,... | collective-permute-start | bytes 1572872 | tf_op jit(solution)/shard_map/ppermute | solution.py:137
  151.1 26.9 %collective-permute-start.31 = (bf16[704,128]{1,0:T(8,128)(2,1)}, bf16[704,128]{1,0:T(8,128)(2,1)}, u32[]{:S(2)}, u32[]{:S(2)}) collective-permute-start(bf16[704,128]{1,0:T(8,128)(2,1)} %get-tuple-element.110), channel_id=1, source_target_pairs={{0,8},{2,10},{4,12},{6,14},{8,0},{10,2},{12,4},{14,6},{16,24},{18,... | collective-permute-start | bytes 540680 | tf_op jit(solution)/shard_map/ppermute | solution.py:137
  156.6 23.3 %collective-permute-start.30 = (bf16[704,128]{1,0:T(8,128)(2,1)S(1)}, bf16[704,128]{1,0:T(8,128)(2,1)}, u32[]{:S(2)}, u32[]{:S(2)}) collective-permute-start(bf16[704,128]{1,0:T(8,128)(2,1)S(1)} %copy-done.80), channel_id=1, source_target_pairs={{0,4},{2,6},{4,0},{6,2},{8,12},{10,14},{12,8},{14,10},{16,20},{18,... | collective-permute-start | bytes 540680 | tf_op jit(solution)/shard_map/ppermute | solution.py:137
  173.8 27.5 %collective-permute-start.17 = (bf16[4,128,2048]{2,1,0:T(8,128)(2,1)S(1)}, bf16[4,128,2048]{2,1,0:T(8,128)(2,1)S(1)}, u32[]{:S(2)}, u32[]{:S(2)}) collective-permute-start(bf16[4,128,2048]{2,1,0:T(8,128)(2,1)S(1)} %slice.687), channel_id=1, source_target_pairs={{0,1},{1,0},{2,3},{3,2},{4,5},{5,4},{6,7},{7,6},{8,9},{9,8},{10,11... | collective-permute-start | bytes 6291464 | tf_op jit(solution)/shard_map/ppermute | solution.py:140
  177.9 19.1 %collective-permute-start.26 = (bf16[128,1408]{1,0:T(8,128)(2,1)S(1)}, bf16[128,1408]{1,0:T(8,128)(2,1)S(1)}, u32[]{:S(2)}, u32[]{:S(2)}) collective-permute-start(bf16[128,1408]{1,0:T(8,128)(2,1)S(1)} %get-tuple-element.80), channel_id=1, source_target_pairs={{0,8},{2,10},{4,12},{6,14},{8,0},{10,2},{12,4},{14,6},{16,24},{18,... | collective-permute-start | bytes 1081352 | tf_op jit(solution)/shard_map/ppermute | solution.py:137
  180.0 17.6 %collective-permute-start.25 = (bf16[128,1408]{1,0:T(8,128)(2,1)S(1)}, bf16[128,1408]{1,0:T(8,128)(2,1)S(1)}, u32[]{:S(2)}, u32[]{:S(2)}) collective-permute-start(bf16[128,1408]{1,0:T(8,128)(2,1)S(1)} %get-tuple-element.81), channel_id=1, source_target_pairs={{0,4},{2,6},{4,0},{6,2},{8,12},{10,14},{12,8},{14,10},{16,20},{18,... | collective-permute-start | bytes 1081352 | tf_op jit(solution)/shard_map/ppermute | solution.py:137
  189.2 29.0 %collective-permute-start.40 = (bf16[128,2048]{1,0:T(8,128)(2,1)}, bf16[128,2048]{1,0:T(8,128)(2,1)S(1)}, u32[]{:S(2)}, u32[]{:S(2)}) collective-permute-start(bf16[128,2048]{1,0:T(8,128)(2,1)} %reshape.571), channel_id=1, source_target_pairs={{0,8},{2,10},{4,12},{6,14},{8,0},{10,2},{12,4},{14,6},{16,24},{18,... | collective-permute-start | bytes 1572872 | tf_op jit(solution)/shard_map/ppermute | solution.py:137
  197.0 21.5 %collective-permute-start.39 = (bf16[128,2048]{1,0:T(8,128)(2,1)}, bf16[128,2048]{1,0:T(8,128)(2,1)S(1)}, u32[]{:S(2)}, u32[]{:S(2)}) collective-permute-start(bf16[128,2048]{1,0:T(8,128)(2,1)} %reshape.571), channel_id=1, source_target_pairs={{0,4},{2,6},{4,0},{6,2},{8,12},{10,14},{12,8},{14,10},{16,20},{18,... | collective-permute-start | bytes 1572872 | tf_op jit(solution)/shard_map/ppermute | solution.py:137
  197.5 35.9 %collective-permute-start.33 = (bf16[704,512]{1,0:T(8,128)(2,1)S(1)}, bf16[704,512]{1,0:T(8,128)(2,1)S(1)}, u32[]{:S(2)}, u32[]{:S(2)}) collective-permute-start(bf16[704,512]{1,0:T(8,128)(2,1)S(1)} %bitcast.438), channel_id=1, source_target_pairs={{0,16},{2,18},{4,20},{6,22},{8,24},{10,26},{12,28},{14,30},{16,0},... | collective-permute-start | bytes 2162696 | tf_op jit(solution)/shard_map/ppermute | solution.py:137
  202.6 32.2 %collective-permute-start.18 = (bf16[128,2048]{1,0:T(8,128)(2,1)S(1)}, bf16[128,2048]{1,0:T(8,128)(2,1)S(1)}, u32[]{:S(2)}, u32[]{:S(2)}) collective-permute-start(bf16[128,2048]{1,0:T(8,128)(2,1)S(1)} %get-tuple-element.71), channel_id=1, source_target_pairs={{0,4},{2,6},{4,0},{6,2},{8,12},{10,14},{12,8},{14,10},{16,20},{18,... | collective-permute-start | bytes 1572872 | tf_op jit(solution)/shard_map/ppermute | solution.py:137
  204.2 46.7 %collective-permute-start.20 = (bf16[128,2048]{1,0:T(8,128)(2,1)S(1)}, bf16[128,2048]{1,0:T(8,128)(2,1)S(1)}, u32[]{:S(2)}, u32[]{:S(2)}) collective-permute-start(bf16[128,2048]{1,0:T(8,128)(2,1)S(1)} %get-tuple-element.72), channel_id=1, source_target_pairs={{0,12},{2,14},{4,8},{6,10},{8,4},{10,6},{12,0},{14,2},{16,28},{18,... | collective-permute-start | bytes 1572872 | tf_op jit(solution)/shard_map/ppermute | solution.py:137
  218.2 43.6 %collective-permute-start.19 = (bf16[128,2048]{1,0:T(8,128)(2,1)S(1)}, bf16[128,2048]{1,0:T(8,128)(2,1)S(1)}, u32[]{:S(2)}, u32[]{:S(2)}) collective-permute-start(bf16[128,2048]{1,0:T(8,128)(2,1)S(1)} %get-tuple-element.73), channel_id=1, source_target_pairs={{0,8},{2,10},{4,12},{6,14},{8,0},{10,2},{12,4},{14,6},{16,24},{18,... | collective-permute-start | bytes 1572872 | tf_op jit(solution)/shard_map/ppermute | solution.py:137
  218.5 74.0 %collective-permute-start.28 = (bf16[512,1408]{1,0:T(8,128)(2,1)S(1)}, bf16[512,1408]{1,0:T(8,128)(2,1)S(1)}, u32[]{:S(2)}, u32[]{:S(2)}) collective-permute-start(bf16[512,1408]{1,0:T(8,128)(2,1)S(1)} %bitcast.409), channel_id=1, source_target_pairs={{0,16},{2,18},{4,20},{6,22},{8,24},{10,26},{12,28},{14,30},{16,0},... | collective-permute-start | bytes 4325384 | tf_op jit(solution)/shard_map/ppermute | solution.py:137
  233.4 157.3 %collective-permute-start.42 = (bf16[4,128,2048]{2,1,0:T(8,128)(2,1)}, bf16[4,128,2048]{2,1,0:T(8,128)(2,1)}, u32[]{:S(2)}, u32[]{:S(2)}) collective-permute-start(bf16[4,128,2048]{2,1,0:T(8,128)(2,1)} %pad_maximum_fusion.12), channel_id=1, source_target_pairs={{0,1},{1,0},{2,3},{3,2},{4,5},{5,4},{6,7},{7,6},{8,9},{9,8},{10,11... | collective-permute-start | bytes 6291464 | tf_op jit(solution)/shard_map/ppermute | solution.py:140
  262.8 33.5 %collective-permute-start.22 = (bf16[128,2048]{1,0:T(8,128)(2,1)S(1)}, bf16[128,2048]{1,0:T(8,128)(2,1)S(1)}, u32[]{:S(2)}, u32[]{:S(2)}) collective-permute-start(bf16[128,2048]{1,0:T(8,128)(2,1)S(1)} %add_convert_fusion), channel_id=1, source_target_pairs={{0,8},{2,10},{4,12},{6,14},{8,0},{10,2},{12,4},{14,6},{16,24},{18,... | collective-permute-start | bytes 1572872 | tf_op jit(solution)/shard_map/ppermute | solution.py:137
  262.9 34.0 %collective-permute-start.21 = (bf16[128,2048]{1,0:T(8,128)(2,1)S(1)}, bf16[128,2048]{1,0:T(8,128)(2,1)S(1)}, u32[]{:S(2)}, u32[]{:S(2)}) collective-permute-start(bf16[128,2048]{1,0:T(8,128)(2,1)S(1)} %add_convert_fusion), channel_id=1, source_target_pairs={{0,4},{2,6},{4,0},{6,2},{8,12},{10,14},{12,8},{14,10},{16,20},{18,... | collective-permute-start | bytes 1572872 | tf_op jit(solution)/shard_map/ppermute | solution.py:137
  263.0 37.5 %collective-permute-start.23 = (bf16[128,2048]{1,0:T(8,128)(2,1)S(1)}, bf16[128,2048]{1,0:T(8,128)(2,1)S(1)}, u32[]{:S(2)}, u32[]{:S(2)}) collective-permute-start(bf16[128,2048]{1,0:T(8,128)(2,1)S(1)} %add_convert_fusion), channel_id=1, source_target_pairs={{0,12},{2,14},{4,8},{6,10},{8,4},{10,6},{12,0},{14,2},{16,28},{18,... | collective-permute-start | bytes 1572872 | tf_op jit(solution)/shard_map/ppermute | solution.py:137
  294.6 100.2 %collective-permute-start.29 = (bf16[1024,1408]{1,0:T(8,128)(2,1)}, bf16[1024,1408]{1,0:T(8,128)(2,1)}, u32[]{:S(2)}, u32[]{:S(2)}) collective-permute-start(bf16[1024,1408]{1,0:T(8,128)(2,1)} %pad_maximum_fusion.6), channel_id=1, source_target_pairs={{0,2},{2,0},{4,6},{6,4},{8,10},{10,8},{12,14},{14,12},{16,18},{18,... | collective-permute-start | bytes 8650760 | tf_op jit(solution)/shard_map/ppermute | solution.py:137
  296.3 91.1 %collective-permute-start.34 = (bf16[704,1024]{1,0:T(8,128)(2,1)}, bf16[704,1024]{1,0:T(8,128)(2,1)}, u32[]{:S(2)}, u32[]{:S(2)}) collective-permute-start(bf16[704,1024]{1,0:T(8,128)(2,1)} %pad_maximum_fusion.18), channel_id=1, source_target_pairs={{0,2},{2,0},{4,6},{6,4},{8,10},{10,8},{12,14},{14,12},{16,18},{18,... | collective-permute-start | bytes 4325384 | tf_op jit(solution)/shard_map/ppermute | solution.py:137
  302.0 90.8 %collective-permute-start.24 = (bf16[4,128,2048]{2,1,0:T(8,128)(2,1)}, bf16[4,128,2048]{2,1,0:T(8,128)(2,1)}, u32[]{:S(2)}, u32[]{:S(2)}) collective-permute-start(bf16[4,128,2048]{2,1,0:T(8,128)(2,1)} %pad_maximum_fusion.11), channel_id=1, source_target_pairs={{0,1},{1,0},{2,3},{3,2},{4,5},{5,4},{6,7},{7,6},{8,9},{9,8},{10,11... | collective-permute-start | bytes 6291464 | tf_op jit(solution)/shard_map/ppermute | solution.py:140
  425.9 46.0 %collective-permute-start.43 = (bf16[4,128,2048]{2,1,0:T(8,128)(2,1)}, bf16[4,128,2048]{2,1,0:T(8,128)(2,1)}, u32[]{:S(2)}, u32[]{:S(2)}) collective-permute-start(bf16[4,128,2048]{2,1,0:T(8,128)(2,1)} %slice.685), channel_id=1, source_target_pairs={{0,1},{1,0},{2,3},{3,2},{4,5},{5,4},{6,7},{7,6},{8,9},{9,8},{10,11... | collective-permute-start | bytes 6291464 | tf_op jit(solution)/shard_map/ppermute | solution.py:140
  434.7 34.7 %collective-permute-start.75 = (bf16[704,1024]{1,0:T(8,128)(2,1)}, bf16[704,1024]{1,0:T(8,128)(2,1)S(1)}, u32[]{:S(2)}, u32[]{:S(2)}) collective-permute-start(bf16[704,1024]{1,0:T(8,128)(2,1)} %slice.689), channel_id=1, source_target_pairs={{0,2},{2,0},{4,6},{6,4},{8,10},{10,8},{12,14},{14,12},{16,18},{18,... | collective-permute-start | bytes 4325384 | tf_op jit(solution)/shard_map/ppermute | solution.py:137
  437.8 41.3 %collective-permute-start.35 = (bf16[4,128,2048]{2,1,0:T(8,128)(2,1)}, bf16[4,128,2048]{2,1,0:T(8,128)(2,1)}, u32[]{:S(2)}, u32[]{:S(2)}) collective-permute-start(bf16[4,128,2048]{2,1,0:T(8,128)(2,1)} %slice.686), channel_id=1, source_target_pairs={{0,1},{1,0},{2,3},{3,2},{4,5},{5,4},{6,7},{7,6},{8,9},{9,8},{10,11... | collective-permute-start | bytes 6291464 | tf_op jit(solution)/shard_map/ppermute | solution.py:140
  450.2 92.1 %collective-permute-start.70 = (bf16[1024,1408]{1,0:T(8,128)(2,1)}, bf16[1024,1408]{1,0:T(8,128)(2,1)}, u32[]{:S(2)}, u32[]{:S(2)}) collective-permute-start(bf16[1024,1408]{1,0:T(8,128)(2,1)} %slice.683), channel_id=1, source_target_pairs={{0,2},{2,0},{4,6},{6,4},{8,10},{10,8},{12,14},{14,12},{16,18},{18,... | collective-permute-start | bytes 8650760 | tf_op jit(solution)/shard_map/ppermute | solution.py:137
  471.8 31.7 %collective-permute-start.76 = (bf16[704,512]{1,0:T(8,128)(2,1)S(1)}, bf16[704,512]{1,0:T(8,128)(2,1)S(1)}, u32[]{:S(2)}, u32[]{:S(2)}) collective-permute-start(bf16[704,512]{1,0:T(8,128)(2,1)S(1)} %slice.692), channel_id=1, source_target_pairs={{0,16},{2,18},{4,20},{6,22},{8,24},{10,26},{12,28},{14,30},{16,0},... | collective-permute-start | bytes 2162696 | tf_op jit(solution)/shard_map/ppermute | solution.py:137
  477.6 41.3 %collective-permute-start.44 = (bf16[128,2048]{1,0:T(8,128)(2,1)}, bf16[128,2048]{1,0:T(8,128)(2,1)S(1)}, u32[]{:S(2)}, u32[]{:S(2)}) collective-permute-start(bf16[128,2048]{1,0:T(8,128)(2,1)} %get-tuple-element.65), channel_id=1, source_target_pairs={{0,4},{2,6},{4,0},{6,2},{8,12},{10,14},{12,8},{14,10},{16,20},{18,... | collective-permute-start | bytes 1572872 | tf_op jit(solution)/shard_map/ppermute | solution.py:137
  514.0 15.8 %collective-permute-start.46 = (bf16[128,2048]{1,0:T(8,128)(2,1)S(1)}, bf16[128,2048]{1,0:T(8,128)(2,1)S(1)}, u32[]{:S(2)}, u32[]{:S(2)}) collective-permute-start(bf16[128,2048]{1,0:T(8,128)(2,1)S(1)} %copy-done.69), channel_id=1, source_target_pairs={{0,12},{2,14},{4,8},{6,10},{8,4},{10,6},{12,0},{14,2},{16,28},{18,... | collective-permute-start | bytes 1572872 | tf_op jit(solution)/shard_map/ppermute | solution.py:137
  516.2 24.3 %collective-permute-start.45 = (bf16[128,2048]{1,0:T(8,128)(2,1)S(1)}, bf16[128,2048]{1,0:T(8,128)(2,1)S(1)}, u32[]{:S(2)}, u32[]{:S(2)}) collective-permute-start(bf16[128,2048]{1,0:T(8,128)(2,1)S(1)} %copy-done.68), channel_id=1, source_target_pairs={{0,8},{2,10},{4,12},{6,14},{8,0},{10,2},{12,4},{14,6},{16,24},{18,... | collective-permute-start | bytes 1572872 | tf_op jit(solution)/shard_map/ppermute | solution.py:137
  517.3 30.6 %collective-permute-start.36 = (bf16[128,2048]{1,0:T(8,128)(2,1)S(1)}, bf16[128,2048]{1,0:T(8,128)(2,1)S(1)}, u32[]{:S(2)}, u32[]{:S(2)}) collective-permute-start(bf16[128,2048]{1,0:T(8,128)(2,1)S(1)} %get-tuple-element.68), channel_id=1, source_target_pairs={{0,4},{2,6},{4,0},{6,2},{8,12},{10,14},{12,8},{14,10},{16,20},{18,... | collective-permute-start | bytes 1572872 | tf_op jit(solution)/shard_map/ppermute | solution.py:137
  518.9 46.2 %collective-permute-start.38 = (bf16[128,2048]{1,0:T(8,128)(2,1)S(1)}, bf16[128,2048]{1,0:T(8,128)(2,1)S(1)}, u32[]{:S(2)}, u32[]{:S(2)}) collective-permute-start(bf16[128,2048]{1,0:T(8,128)(2,1)S(1)} %get-tuple-element.69), channel_id=1, source_target_pairs={{0,12},{2,14},{4,8},{6,10},{8,4},{10,6},{12,0},{14,2},{16,28},{18,... | collective-permute-start | bytes 1572872 | tf_op jit(solution)/shard_map/ppermute | solution.py:137
  529.8 43.9 %collective-permute-start.37 = (bf16[128,2048]{1,0:T(8,128)(2,1)S(1)}, bf16[128,2048]{1,0:T(8,128)(2,1)S(1)}, u32[]{:S(2)}, u32[]{:S(2)}) collective-permute-start(bf16[128,2048]{1,0:T(8,128)(2,1)S(1)} %get-tuple-element.70), channel_id=1, source_target_pairs={{0,8},{2,10},{4,12},{6,14},{8,0},{10,2},{12,4},{14,6},{16,24},{18,... | collective-permute-start | bytes 1572872 | tf_op jit(solution)/shard_map/ppermute | solution.py:137
  547.7 75.1 %collective-permute-start.71 = (bf16[512,1408]{1,0:T(8,128)(2,1)}, bf16[512,1408]{1,0:T(8,128)(2,1)}, u32[]{:S(2)}, u32[]{:S(2)}) collective-permute-start(bf16[512,1408]{1,0:T(8,128)(2,1)} %slice.690), channel_id=1, source_target_pairs={{0,16},{2,18},{4,20},{6,22},{8,24},{10,26},{12,28},{14,30},{16,0},... | collective-permute-start | bytes 4325384 | tf_op jit(solution)/shard_map/ppermute | solution.py:137
  576.9 25.4 %collective-permute-start.49 = (bf16[128,2048]{1,0:T(8,128)(2,1)S(1)}, bf16[128,2048]{1,0:T(8,128)(2,1)S(1)}, u32[]{:S(2)}, u32[]{:S(2)}) collective-permute-start(bf16[128,2048]{1,0:T(8,128)(2,1)S(1)} %get-tuple-element.46), channel_id=1, source_target_pairs={{0,12},{2,14},{4,8},{6,10},{8,4},{10,6},{12,0},{14,2},{16,28},{18,... | collective-permute-start | bytes 1572872 | tf_op jit(solution)/shard_map/ppermute | solution.py:137
  577.4 42.7 %collective-permute-start.48 = (bf16[128,2048]{1,0:T(8,128)(2,1)S(1)}, bf16[128,2048]{1,0:T(8,128)(2,1)S(1)}, u32[]{:S(2)}, u32[]{:S(2)}) collective-permute-start(bf16[128,2048]{1,0:T(8,128)(2,1)S(1)} %get-tuple-element.46), channel_id=1, source_target_pairs={{0,8},{2,10},{4,12},{6,14},{8,0},{10,2},{12,4},{14,6},{16,24},{18,... | collective-permute-start | bytes 1572872 | tf_op jit(solution)/shard_map/ppermute | solution.py:137
  579.9 40.2 %collective-permute-start.47 = (bf16[128,2048]{1,0:T(8,128)(2,1)S(1)}, bf16[128,2048]{1,0:T(8,128)(2,1)S(1)}, u32[]{:S(2)}, u32[]{:S(2)}) collective-permute-start(bf16[128,2048]{1,0:T(8,128)(2,1)S(1)} %get-tuple-element.46), channel_id=1, source_target_pairs={{0,4},{2,6},{4,0},{6,2},{8,12},{10,14},{12,8},{14,10},{16,20},{18,... | collective-permute-start | bytes 1572872 | tf_op jit(solution)/shard_map/ppermute | solution.py:137
  622.7 26.3 %collective-permute-start.50 = (bf16[4,128,2048]{2,1,0:T(8,128)(2,1)S(1)}, bf16[4,128,2048]{2,1,0:T(8,128)(2,1)}, u32[]{:S(2)}, u32[]{:S(2)}) collective-permute-start(bf16[4,128,2048]{2,1,0:T(8,128)(2,1)S(1)} %pad_maximum_fusion.13), channel_id=1, source_target_pairs={{0,1},{1,0},{2,3},{3,2},{4,5},{5,4},{6,7},{7,6},{8,9},{9,8},{10,11... | collective-permute-start | bytes 6291464 | tf_op jit(solution)/shard_map/ppermute | solution.py:140
  626.3 12.5 %collective-permute-start.74 = (bf16[128,1408]{1,0:T(8,128)(2,1)}, bf16[128,1408]{1,0:T(8,128)(2,1)}, u32[]{:S(2)}, u32[]{:S(2)}) collective-permute-start(bf16[128,1408]{1,0:T(8,128)(2,1)} %get-tuple-element.75), channel_id=1, source_target_pairs={{0,12},{2,14},{4,8},{6,10},{8,4},{10,6},{12,0},{14,2},{16,28},{18,... | collective-permute-start | bytes 1081352 | tf_op jit(solution)/shard_map/ppermute | solution.py:137
  626.3 18.4 %collective-permute-start.73 = (bf16[128,1408]{1,0:T(8,128)(2,1)}, bf16[128,1408]{1,0:T(8,128)(2,1)}, u32[]{:S(2)}, u32[]{:S(2)}) collective-permute-start(bf16[128,1408]{1,0:T(8,128)(2,1)} %get-tuple-element.76), channel_id=1, source_target_pairs={{0,8},{2,10},{4,12},{6,14},{8,0},{10,2},{12,4},{14,6},{16,24},{18,... | collective-permute-start | bytes 1081352 | tf_op jit(solution)/shard_map/ppermute | solution.py:137
  627.9 18.2 %collective-permute-start.72 = (bf16[128,1408]{1,0:T(8,128)(2,1)}, bf16[128,1408]{1,0:T(8,128)(2,1)}, u32[]{:S(2)}, u32[]{:S(2)}) collective-permute-start(bf16[128,1408]{1,0:T(8,128)(2,1)} %get-tuple-element.77), channel_id=1, source_target_pairs={{0,4},{2,6},{4,0},{6,2},{8,12},{10,14},{12,8},{14,10},{16,20},{18,... | collective-permute-start | bytes 1081352 | tf_op jit(solution)/shard_map/ppermute | solution.py:137
  666.8 18.6 %collective-permute-start.65 = (bf16[256,1024]{1,0:T(8,128)(2,1)}, bf16[256,1024]{1,0:T(8,128)(2,1)}, u32[]{:S(2)}, u32[]{:S(2)}) collective-permute-start(bf16[256,1024]{1,0:T(8,128)(2,1)} %slice.693), channel_id=1, source_target_pairs={{0,2},{2,0},{4,6},{6,4},{8,10},{10,8},{12,14},{14,12},{16,18},{18,... | collective-permute-start | bytes 1572872 | tf_op jit(solution)/shard_map/ppermute | solution.py:137
  679.6 36.4 %collective-permute-start.60 = (bf16[1024,768]{1,0:T(8,128)(2,1)}, bf16[1024,768]{1,0:T(8,128)(2,1)}, u32[]{:S(2)}, u32[]{:S(2)}) collective-permute-start(bf16[1024,768]{1,0:T(8,128)(2,1)} %slice.688), channel_id=1, source_target_pairs={{0,2},{2,0},{4,6},{6,4},{8,10},{10,8},{12,14},{14,12},{16,18},{18,... | collective-permute-start | bytes 4718600 | tf_op jit(solution)/shard_map/ppermute | solution.py:137
  685.4 34.3 %collective-permute-start.51 = (bf16[4,128,2048]{2,1,0:T(8,128)(2,1)}, bf16[4,128,2048]{2,1,0:T(8,128)(2,1)}, u32[]{:S(2)}, u32[]{:S(2)}) collective-permute-start(bf16[4,128,2048]{2,1,0:T(8,128)(2,1)} %slice.684), channel_id=1, source_target_pairs={{0,1},{1,0},{2,3},{3,2},{4,5},{5,4},{6,7},{7,6},{8,9},{9,8},{10,11... | collective-permute-start | bytes 6291464 | tf_op jit(solution)/shard_map/ppermute | solution.py:140
  689.0 13.5 %collective-permute-start.66 = (bf16[256,512]{1,0:T(8,128)(2,1)S(1)}, bf16[256,512]{1,0:T(8,128)(2,1)S(1)}, u32[]{:S(2)}, u32[]{:S(2)}) collective-permute-start(bf16[256,512]{1,0:T(8,128)(2,1)S(1)} %slice.697), channel_id=1, source_target_pairs={{0,16},{2,18},{4,20},{6,22},{8,24},{10,26},{12,28},{14,30},{16,0},... | collective-permute-start | bytes 786440 | tf_op jit(solution)/shard_map/ppermute | solution.py:137
  718.7 35.1 %collective-permute-start.61 = (bf16[512,768]{1,0:T(8,128)(2,1)S(1)}, bf16[512,768]{1,0:T(8,128)(2,1)S(1)}, u32[]{:S(2)}, u32[]{:S(2)}) collective-permute-start(bf16[512,768]{1,0:T(8,128)(2,1)S(1)} %slice.691), channel_id=1, source_target_pairs={{0,16},{2,18},{4,20},{6,22},{8,24},{10,26},{12,28},{14,30},{16,0},... | collective-permute-start | bytes 2359304 | tf_op jit(solution)/shard_map/ppermute | solution.py:137
  758.9 29.7 %collective-permute-start.52 = (bf16[128,2048]{1,0:T(8,128)(2,1)}, bf16[128,2048]{1,0:T(8,128)(2,1)S(1)}, u32[]{:S(2)}, u32[]{:S(2)}) collective-permute-start(bf16[128,2048]{1,0:T(8,128)(2,1)} %get-tuple-element.62), channel_id=1, source_target_pairs={{0,4},{2,6},{4,0},{6,2},{8,12},{10,14},{12,8},{14,10},{16,20},{18,... | collective-permute-start | bytes 1572872 | tf_op jit(solution)/shard_map/ppermute | solution.py:137
  759.8 28.8 %collective-permute-start.54 = (bf16[128,2048]{1,0:T(8,128)(2,1)}, bf16[128,2048]{1,0:T(8,128)(2,1)}, u32[]{:S(2)}, u32[]{:S(2)}) collective-permute-start(bf16[128,2048]{1,0:T(8,128)(2,1)} %get-tuple-element.63), channel_id=1, source_target_pairs={{0,12},{2,14},{4,8},{6,10},{8,4},{10,6},{12,0},{14,2},{16,28},{18,... | collective-permute-start | bytes 1572872 | tf_op jit(solution)/shard_map/ppermute | solution.py:137
  762.9 25.7 %collective-permute-start.53 = (bf16[128,2048]{1,0:T(8,128)(2,1)}, bf16[128,2048]{1,0:T(8,128)(2,1)}, u32[]{:S(2)}, u32[]{:S(2)}) collective-permute-start(bf16[128,2048]{1,0:T(8,128)(2,1)} %get-tuple-element.64), channel_id=1, source_target_pairs={{0,8},{2,10},{4,12},{6,14},{8,0},{10,2},{12,4},{14,6},{16,24},{18,... | collective-permute-start | bytes 1572872 | tf_op jit(solution)/shard_map/ppermute | solution.py:137
  (120 other events, 1974.0 us)

commit v2 on v1

v2 whole, which is shorter than its diff:
```python
import functools

import jax
import jax.numpy as jnp
from jax import lax
from jax.experimental import pallas as pl
from jax.experimental.pallas import tpu as pltpu
from jax.sharding import PartitionSpec as P

HD = 64
ROT = 16
LANES = 128

norm_eps = 1e-05
rope_base = 10000.0
score_scale = 0.125
masked_score = -1e30

GROUP_BITS = (1, 2)
BF = jnp.bfloat16
F32 = jnp.float32
COST = 30
VMEM_LIMIT = 60 * 1024 * 1024


def doc_positions(segment):
    token_index = jnp.arange(segment.shape[0], dtype=jnp.int32)
    begins = jnp.concatenate([jnp.ones((1,), dtype=jnp.bool_), segment[1:] != segment[:-1]])
    starts = lax.cummax(jnp.where(begins, token_index, jnp.zeros_like(token_index)), axis=0)
    return token_index - starts


def norm_parts(values, gain, shift):
    row_mean = jnp.mean(values, axis=-1, keepdims=True)
    centred = values - row_mean
    inv_std = lax.rsqrt(jnp.mean(centred * centred, axis=-1, keepdims=True) + norm_eps)
    normed = centred * inv_std
    return (normed * gain + shift, normed, inv_std)


def norm_back(incoming, normed, inv_std, gain):
    scaled = incoming * gain
    adjusted = (
        scaled
        - jnp.mean(scaled, axis=-1, keepdims=True)
        - normed * jnp.mean(scaled * normed, axis=-1, keepdims=True)
    )
    return adjusted * inv_std


def dot(a, b, a_dim, b_dim):
    return lax.dot_general(
        a, b, (((a_dim,), (b_dim,)), ((), ())), preferred_element_type=F32
    )


def whole(shape, once=False):
    zeros = (0,) * len(shape)
    return pl.BlockSpec(
        shape, lambda *_: zeros, pipeline_mode=pl.Buffered(buffer_count=1) if once else None
    )


def each(shape):
    zeros = (0,) * (len(shape) - 1)
    return pl.BlockSpec((None,) + shape[1:], lambda k, *_: (k,) + zeros)


def call(kernel, ins, out_shapes, flops, in_specs=None, out_specs=None, grid=(1,), scratch=()):
    moved = sum(v.size * v.dtype.itemsize for v in ins)
    moved += sum(s.size * s.dtype.itemsize for s in out_shapes)
    return pl.pallas_call(
        kernel,
        grid=grid,
        in_specs=in_specs or [whole(v.shape) for v in ins],
        out_specs=out_specs or [whole(s.shape) for s in out_shapes],
        out_shape=list(out_shapes),
        scratch_shapes=list(scratch),
        compiler_params=pltpu.CompilerParams(vmem_limit_bytes=VMEM_LIMIT),
        cost_estimate=pl.CostEstimate(flops=COST * flops, bytes_accessed=COST * moved, transcendentals=0),
    )(*ins)


def shaped(shape, dtype):
    return jax.ShapeDtypeStruct(shape, dtype)


def deal(cols, group):
    full = cols // (LANES * group) * LANES
    share = (cols - full * group) // group
    return full, share


def pack_attn_kernel(group, qkv_ref, out_ref, sent_ref):
    cols = qkv_ref.shape[2] // group
    block = qkv_ref.shape[1]
    for k in range(group):
        at, here = slice(k * cols, (k + 1) * cols), slice(k * block, (k + 1) * block)
        for j in range(3):
            sent_ref[here, j * cols : (j + 1) * cols] = qkv_ref[j, :, at]
        sent_ref[here, 3 * cols :] = out_ref[at, :].T


TILE = 2 * LANES


def column(j, at):
    return at // TILE * 3 * TILE + j * TILE + at % TILE


def pack_mlp_kernel(group, gate_up_ref, down_ref, sent_ref):
    full, share = deal(gate_up_ref.shape[2], group)
    block = gate_up_ref.shape[1]
    per = LANES // share
    lane = lax.broadcasted_iota(jnp.int32, (1, LANES), 1) // share
    for k in range(group):
        here = slice(k * block, (k + 1) * block)
        for at in range(0, full + LANES, LANES):
            own = at < full
            start = k * full + at if own else group * full + k // per * LANES
            take = slice(start, start + LANES)
            for j in range(3):
                value = gate_up_ref[j, :, take] if j < 2 else down_ref[take, :].T
                if not own:
                    value = jnp.where(lane == k % per, value, 0).astype(BF)
                to = column(j, at)
                sent_ref[here, to : to + LANES] = value


def finish_mlp_kernel(group, *refs):
    got, (gate_up_ref, down_ref) = refs[:-2], refs[-2:]
    full, share = deal(gate_up_ref.shape[2], group)
    block = gate_up_ref.shape[1]
    per = LANES // share

    def taken(k, j, at):
        to = column(j, at % TILE)
        return got[at // TILE][k * block : (k + 1) * block, to : to + LANES].astype(F32)

    for j in range(3):
        for at in range(0, full + LANES, LANES):
            own = at < full
            for k in range(0, group, 1 if own else per):
                start = k * full + at if own else group * full + k // per * LANES
                take = slice(start, start + LANES)
                value = sum(taken(k + i, j, at) for i in range(1 if own else per))
                if j < 2:
                    gate_up_ref[j, :, take] = value
                else:
                    down_ref[take, :] = value.T


def finish_attn_kernel(group, got_ref, qkv_ref, out_ref):
    cols = qkv_ref.shape[2] // group
    block = qkv_ref.shape[1]
    for k in range(group):
        here, at = slice(k * block, (k + 1) * block), slice(k * cols, (k + 1) * cols)
        for j in range(3):
            qkv_ref[j, :, at] = got_ref[here, j * cols : (j + 1) * cols].astype(F32)
        out_ref[at, :] = got_ref[here, 3 * cols :].astype(F32).T


def spans(weights):
    at = 0
    for w in weights:
        yield slice(at, at + w.shape[0]), w
        at += w.shape[0]


def turn(value, tables, sign):
    cosine, lead, tail = tables
    ahead = pltpu.roll(value, LANES - ROT // 2, 1)
    behind = pltpu.roll(value, ROT // 2, 1)
    return value * cosine + (ahead * lead + behind * tail) * sign


def soft(queries, keys, mask):
    scores = dot(queries, keys, 1, 1) * score_scale + mask
    weights = jnp.exp(scores - jnp.max(scores, axis=-1, keepdims=True))
    return weights * (1.0 / jnp.sum(weights, axis=-1, keepdims=True))


def own_head(half):
    return lax.broadcasted_iota(jnp.int32, (1, LANES), 1) // HD == half


def attend_kernel(far, own_ref, sib_ref, bias_ref, mask_ref, cos_ref, lead_ref, tail_ref, *refs):
    weights, refs = refs[:far], refs[far:]
    qkv_ref, mixed_own, mixed_sib, mine_ref, other_ref, lines, mixed_ref = refs
    rows = mine_ref.shape[0]
    lines[:rows] = own_ref[:rows]
    lines[rows:] = sib_ref[:rows]
    cols = mixed_ref.shape[1]
    tables = (cos_ref[...], lead_ref[...], tail_ref[...])
    lin = bias_ref[...]
    for at, w in spans(weights):
        lin = lin + dot(lines[:, at], w[:, : 3 * cols], 1, 0)
    mask = mask_ref[...]
    for i in range(cols // LANES):
        at = [slice(j * cols + i * LANES, j * cols + (i + 1) * LANES) for j in range(3)]
        queries = turn(lin[:, at[0]], tables, 1.0).astype(BF)
        keys = turn(lin[:, at[1]], tables, 1.0).astype(BF)
        values = lin[:, at[2]].astype(BF)
        qkv_ref[:, at[0]] = queries
        qkv_ref[:, at[1]] = keys
        qkv_ref[:, at[2]] = values
        mixed = None
        for half in range(LANES // HD):
            here = own_head(half)
            probs = soft(jnp.where(here, queries, 0).astype(BF), keys, mask).astype(BF)
            part = dot(probs, values, 1, 0)
            mixed = part if mixed is None else jnp.where(here, part, mixed)
        mixed_ref[:, i * LANES : (i + 1) * LANES] = mixed.astype(BF)
    mixed_own[...] = mixed_ref[:rows]
    mixed_sib[...] = mixed_ref[rows:]
    for at, w in spans(weights):
        term = dot(mixed_ref[...], w[:, 3 * cols :], 1, 1)
        mine_ref[:, at] = term[:rows]
        other_ref[:, at] = term[rows:].astype(BF)


def attend_back_kernel(far, own_ref, sib_ref, qkv_ref, mask_ref, cos_ref, lead_ref, tail_ref, *refs):
    weights, refs = refs[:far], refs[far:]
    lin_own, lin_sib, sums_ref, mine_ref, other_ref, lines, lin_ref = refs
    rows = own_ref.shape[0]
    lines[:rows] = own_ref[...]
    lines[rows:] = sib_ref[...]
    cols = qkv_ref.shape[1] // 3
    tables = (cos_ref[...], lead_ref[...], tail_ref[...])
    mixed_grad = sum(dot(lines[:, at], w[:, 3 * cols :], 1, 0) for at, w in spans(weights))
    mixed_grad = mixed_grad.astype(BF)
    mask = mask_ref[...]
    for i in range(cols // LANES):
        at = [slice(j * cols + i * LANES, j * cols + (i + 1) * LANES) for j in range(3)]
        queries, keys, values = (qkv_ref[:, a] for a in at)
        grad = mixed_grad[:, i * LANES : (i + 1) * LANES]
        found = [None] * 3
        for half in range(LANES // HD):
            here = own_head(half)
            probs = soft(jnp.where(here, queries, 0).astype(BF), keys, mask)
            value_grad = dot(probs.astype(BF), grad, 0, 0)
            prob_grad = dot(jnp.where(here, grad, 0).astype(BF), values, 1, 1)
            score_grad = (
                probs * (prob_grad - jnp.sum(probs * prob_grad, axis=-1, keepdims=True))
            ).astype(BF)
            query_grad = dot(score_grad, keys, 1, 0)
            key_grad = dot(score_grad, queries, 0, 0)
            parts = (query_grad, key_grad, value_grad)
            found = [p if f is None else jnp.where(here, p, f) for p, f in zip(parts, found)]
        lin_ref[:, at[0]] = turn(found[0] * score_scale, tables, -1.0).astype(BF)
        lin_ref[:, at[1]] = turn(found[1] * score_scale, tables, -1.0).astype(BF)
        lin_ref[:, at[2]] = found[2].astype(BF)
    lin_own[...] = lin_ref[:rows]
    lin_sib[...] = lin_ref[rows:]
    sums_ref[...] = jnp.sum(lin_ref[...].astype(F32), axis=0, keepdims=True)
    for at, w in spans(weights):
        term = dot(lin_ref[...], w[:, : 3 * cols], 1, 1)
        mine_ref[:, at] = term[:rows]
        other_ref[:, at] = term[rows:].astype(BF)


def mlp_kernel(far, tiles, first, *refs):
    lines, grads, refs = refs[:2], refs[2:4], refs[4:]
    before, refs = (None, refs) if first else (refs[:2], refs[2:])
    weights, refs = refs[: far * tiles], refs[far * tiles :]
    found, sums, (held, held_grad) = refs[: 4 * tiles], refs[-4:-2], refs[-2:]
    rows = lines[0].shape[0]
    for half in range(2):
        here = slice(half * rows, (half + 1) * rows)
        held[here] = lines[half][...]
        held_grad[here] = grads[half][...]
    inner = []
    for t in range(tiles):
        mine = weights[t * far : (t + 1) * far]
        gate_up = sum(dot(held[:, at], w[:, : 2 * TILE], 1, 0) for at, w in spans(mine))
        hidden_grad = sum(dot(held_grad[:, at], w[:, 2 * TILE :], 1, 0) for at, w in spans(mine))
        gate_pre, up_values = gate_up[:, :TILE], gate_up[:, TILE:]
        gate_sig = jax.nn.sigmoid(gate_pre)
        smooth = gate_pre * gate_sig
        gate_grad = hidden_grad * up_values * gate_sig * (1.0 + gate_pre * (1.0 - gate_sig))
        hidden = (smooth * up_values).astype(BF)
        pair = jnp.concatenate([gate_grad.astype(BF), (hidden_grad * smooth).astype(BF)], axis=1)
        for half in range(2):
            here = slice(half * rows, (half + 1) * rows)
            found[4 * t + half][...] = pair[here]
            found[4 * t + 2 + half][...] = hidden[here]
        inner.append(pair)
    for p, (at, _) in enumerate(spans(weights[:far])):
        term = sum(
            dot(pair, weights[t * far + p][:, : 2 * TILE], 1, 1) for t, pair in enumerate(inner)
        )
        for half in range(2):
            part = term[half * rows : (half + 1) * rows]
            if not first:
                part = part + before[half][:, at]
            sums[half][:, at] = part.astype(sums[half].dtype)


def mlp_out_kernel(far, tiles, *refs):
    hiddens, refs = refs[: 2 * tiles], refs[2 * tiles :]
    weights, outs = refs[: far * tiles], refs[far * tiles :]
    for half in range(2):
        for p, (at, _) in enumerate(spans(weights[:far])):
            term = sum(
                dot(hiddens[2 * t + half][...], weights[t * far + p][...], 1, 1)
                for t in range(tiles)
            )
            outs[half][:, at] = term.astype(outs[half].dtype)


def grad_kernel(kinds, adds, *refs):
    lefts, rights = [], []
    at = 0
    for count in kinds:
        lefts.append(refs[at : at + 2])
        rights.append([refs[at + 2 + 2 * c : at + 4 + 2 * c] for c in range(count)])
        at += 2 + 2 * count
    more = refs[at : at + sum(adds)]
    outs = refs[at + sum(adds) :]
    start = 0
    for left, columns in zip(lefts, rights):
        for right in columns:
            size = right[0].shape[1]
            here = slice(start, start + size)
            start += size
            total = sum(dot(a[...], b[...], 0, 0) for a, b in zip(left, right))
            parts = len(adds)
            depth = total.shape[0] // parts
            used = 0
            for i, count in enumerate(adds):
                part = total[i * depth : (i + 1) * depth]
                for extra in more[used : used + count]:
                    part = part + extra[:, here].astype(F32)
                used += count
                out = outs[i] if len(outs) > 1 else outs[0]
                lines = slice(None) if len(outs) > 1 else slice(i * depth, (i + 1) * depth)
                out[lines, here] = part.astype(BF)


def on_device(
    tokens,
    segment_ids,
    ln1_gain,
    ln1_bias,
    qkv_weight,
    qkv_bias,
    out_weight,
    ln2_gain,
    ln2_bias,
    gate_up_weight,
    down_weight,
    out_grad,
):
    dp_size = lax.axis_size("dp")
    bits = dp_size.bit_length() - 1
    me = lax.axis_index("dp")
    core = lax.axis_index("tensor")
    rows, width = tokens.shape
    seq_len = segment_ids.shape[0]
    group = 1 << len(GROUP_BITS)
    far_bits = [b for b in reversed(range(bits)) if b not in GROUP_BITS]
    my_bit = [(me >> b) & 1 for b in range(bits)]
    rank = sum(my_bit[b] << i for i, b in enumerate(GROUP_BITS))
    heads = qkv_bias.shape[1] // HD // group
    head_cols = heads * HD
    hidden_cols = deal(down_weight.shape[0], group)[0] + LANES

    def swap(array, mask):
        if mask == 0:
            return array
        return lax.ppermute(array, "dp", [(d, d ^ mask) for d in range(dp_size)])

    def sibling(array):
        return lax.ppermute(array, "tensor", [(0, 1), (1, 0)])

    order = [bits - 1 - b for b in reversed(far_bits)]
    order += [bits - 1 - b for b in reversed(GROUP_BITS)]

    def to_rel(array):
        lead = array.ndim - 1
        cut = array.reshape(array.shape[:-1] + (2,) * bits + (width // dp_size,))
        cut = cut.transpose(list(range(lead)) + [lead + o for o in order] + [lead + bits])
        for i, b in enumerate(reversed(far_bits)):
            cut = jnp.where(my_bit[b] == 1, jnp.flip(cut, lead + i), cut)
        return cut.reshape(array.shape)

    def from_rel(array):
        lead = array.ndim - 1
        cut = array.reshape(array.shape[:-1] + (2,) * bits + (width // dp_size,))
        for i, b in enumerate(reversed(far_bits)):
            cut = jnp.where(my_bit[b] == 1, jnp.flip(cut, lead + i), cut)
        back = [order.index(i) for i in range(bits)]
        cut = cut.transpose(list(range(lead)) + [lead + o for o in back] + [lead + bits])
        return cut.reshape(array.shape)

    block = width // dp_size
    shard_rows = group * block
    far = 1 << len(far_bits)
    bands = [
        [d for d in range(dp_size) if all((d ^ first) >> b & 1 == 0 for b in far_bits)]
        for first in range(dp_size)
        if all(first >> b & 1 == 0 for b in GROUP_BITS)
    ]

    def exchange(rows_by_rank):
        return lax.all_to_all(rows_by_rank, "dp", 0, 0, axis_index_groups=bands, tiled=True)

    def tie(value, *after):
        return lax.optimization_barrier((value, *after))[0]

    def pack(kernel, ins, cols):
        return call(
            functools.partial(kernel, group), ins, [shaped((shard_rows, cols), BF)], 0
        )[0]

    def gather(shard, subs, after=()):
        depth = shard_rows // subs
        parts = [tie(shard[i * depth : (i + 1) * depth], *after) for i in range(subs)]
        pieces = [parts]
        for n, b in enumerate(far_bits):
            came = [[swap(p, 1 << b) for p in piece] for piece in pieces[1:]]
            whole_shard = n > 0 and len(pieces) > 1
            first = [swap(shard, 1 << b)] if whole_shard else [swap(p, 1 << b) for p in parts]
            pieces = pieces + [first] + came
        return pieces

    def flat(pieces, shard):
        return [shard] + [p for piece in pieces[1:] for p in piece]

    def spread(local, after=(), then=()):
        mine = exchange(tie(jnp.broadcast_to(local, (group,) + local.shape), *after))
        return mine, sibling(tie(mine, *then))

    def half(array):
        return array.reshape((-1,) + array.shape[2:])

    def by_block(array):
        return array.reshape((group, -1) + array.shape[1:])

    def collect(mine, other, after=(), then=()):
        other = sibling(tie(other, *after))
        both = (by_block(mine) + by_block(other).astype(F32)).astype(BF)
        return jnp.sum(exchange(tie(both, *then)).astype(F32), axis=0)

    def arrived(pieces):
        return [p for piece in pieces for p in piece]

    def weight_grads(kinds, subs):
        cols = sum(c[0].shape[1] for _, sets in kinds for c in sets)
        spec = lambda v, i: pl.BlockSpec((v.shape[0], shard_rows), lambda *_: (0, i))

        def make(i, adds, outs, after):
            ins, specs = [], []
            for left, sets in kinds:
                ins += left
                specs += [spec(v, i) for v in left]
                for s in sets:
                    ins += s
                    specs += [whole(v.shape) for v in s]
            counts = [len(a) for a in adds]
            for a in adds:
                ins += a
                specs += [whole(v.shape) for v in a]
            ins[0] = tie(ins[0], *after)
            return call(
                functools.partial(grad_kernel, [len(s) for _, s in kinds], counts),
                ins,
                [shaped((shard_rows // outs, cols), BF)] * outs,
                2 * group * seq_len * shard_rows * cols,
                in_specs=specs,
            )

        adds = [[[] for _ in range(subs)] for _ in range(far)]
        count = far
        after = ()
        for b in reversed(far_bits):
            count //= 2
            for i in reversed(range(count)):
                parts = make(i + count, adds[i + count], subs, after)
                came = [swap(p, 1 << b) for p in parts]
                for j in range(subs):
                    adds[i][j].append(came[j])
                after = (yield list(parts), came) or ()
        yield make(0, adds[0], 1, after), None

    def finish(kernel, came, shapes):
        return call(functools.partial(kernel, group), came, [shaped(s, F32) for s in shapes], 0)

    gains = to_rel(jnp.stack([ln1_gain, ln1_bias, ln2_gain, ln2_bias]))
    resid = to_rel(tokens).astype(F32)
    normed_in, normed_one, inv_one = norm_parts(resid, gains[0], gains[1])
    note = jnp.pad(segment_ids.astype(BF)[None], ((0, 15), (0, width - seq_len)))
    message = jnp.concatenate([normed_in.astype(BF), note], axis=0)

    attn_pack = pack(pack_attn_kernel, [qkv_weight, out_weight], 4 * head_cols)
    attn_shard = exchange(attn_pack)
    mlp_pack = pack(pack_mlp_kernel, [tie(gate_up_weight, attn_shard), down_weight], 3 * hidden_cols)
    mlp_shard = exchange(tie(mlp_pack, attn_shard))
    attn_pieces = gather(attn_shard, 1)
    w_attn = flat(attn_pieces, attn_shard)
    heard = spread(message, [mlp_shard] + attn_pieces[1], w_attn[1:])
    tiles = hidden_cols // TILE
    mlp_pieces = []
    after = attn_pieces[1]
    for t in range(tiles):
        shard = tie(mlp_shard[:, t * 3 * TILE : (t + 1) * 3 * TILE], *after)
        mlp_pieces.append(gather(shard, 1))
        after = mlp_pieces[t][1]
    w_mlp = [flat(pieces, pieces[0][0]) for pieces in mlp_pieces]
    grad_local = to_rel(out_grad)
    grad_rows = spread(grad_local, [heard[0]])

    segs = heard[0][:, rows, :seq_len].astype(jnp.int32)
    seq_in = [half(h[:, :rows]) for h in heard]
    spots = jax.vmap(doc_positions)(segs)
    segs, spots = (jnp.where(core == 1, jnp.roll(v, rows, axis=1), v) for v in (segs, spots))
    index = jnp.arange(seq_len, dtype=jnp.int32)
    index = jnp.where(core == 1, jnp.roll(index, rows), index)
    allowed = (segs[:, :, None] == segs[:, None, :]) & (index[None, :] <= index[:, None])
    mask = jnp.where(allowed, 0.0, masked_score).astype(F32)
    dim = jnp.arange(LANES, dtype=jnp.int32) % HD
    pair = (dim % (ROT // 2)).astype(F32)
    speed = jnp.where(dim < ROT, rope_base ** (-2.0 * pair / ROT), 0.0)
    angles = spots.astype(F32)[..., None] * speed
    cosine, sine = jnp.cos(angles), jnp.sin(angles)
    lead = jnp.where(dim < ROT // 2, -sine, 0.0)
    tail = jnp.where((dim >= ROT // 2) & (dim < ROT), sine, 0.0)

    bias = lax.dynamic_slice_in_dim(qkv_bias, rank * head_cols, head_cols, 1).reshape(1, -1)
    facts = [mask, cosine, lead, tail]
    lines = pltpu.VMEM((seq_len, width), BF)
    mine, other = shaped((group * rows, width), F32), shaped((group * rows, width), BF)
    mine3, other3 = (shaped((group, rows, width), t) for t in (F32, BF))
    qkv_shape = shaped((group, seq_len, 3 * head_cols), BF)
    mixed_shape = shaped((group, rows, head_cols), BF)
    lin_shape = shaped((group, rows, 3 * head_cols), BF)
    attn_flops = 2 * group * seq_len * width * 4 * head_cols

    ins = [tie(heard[0], *mlp_pieces[0][1]), heard[1], bias] + facts + w_attn
    outs = [qkv_shape, mixed_shape, mixed_shape, mine3, other3]
    qkv, mixed_own, mixed_sib, *terms = call(
        functools.partial(attend_kernel, len(w_attn)),
        ins,
        outs,
        attn_flops,
        in_specs=[each(v.shape) for v in heard]
        + [whole(bias.shape)]
        + [each(v.shape) for v in facts]
        + [whole(v.shape) for v in w_attn],
        out_specs=[each(v.shape) for v in outs],
        grid=(group,),
        scratch=[lines, pltpu.VMEM((seq_len, head_cols), BF)],
    )
    mixed = [half(mixed_own), half(mixed_sib)]
    attn_sum = collect(*map(half, terms), mlp_pieces[0][2], [grad_rows[0]])
    early = arrived(mlp_pieces[0][3:]) + [p for pieces in mlp_pieces[1:2] for p in arrived(pieces[1:3])]
    resid_two = resid + tie(attn_sum, *early)
    normed_mid, normed_two, inv_two = norm_parts(resid_two, gains[2], gains[3])
    late = [p for pieces in mlp_pieces[1:2] for p in arrived(pieces[3:])]
    late += [p for pieces in mlp_pieces[2:] for p in arrived(pieces[1:3])]
    seq_mid = [half(h) for h in spread(normed_mid.astype(BF), (), late)]
    grad_rows = [half(h) for h in grad_rows]

    row_spec = pl.BlockSpec((rows, width), lambda k: (k, 0))
    pair_spec, hidden_spec = (pl.BlockSpec((rows, n * TILE), lambda k: (k, 0)) for n in (2, 1))
    pair_shape, hidden_shape = (shaped((group * rows, n * TILE), BF) for n in (2, 1))
    pairs, hiddens, mlp_steps, mid = [], [], [], []
    parts, came = [], []
    for batch in (range(tiles - 1), range(tiles - 1, tiles)):
        ins = [tie(seq_mid[0], *parts), seq_mid[1], *grad_rows] + mid
        final = batch[-1] == tiles - 1
        weights = [w for t in batch for w in w_mlp[t]]
        *inner, mid_own, mid_sib = call(
            functools.partial(mlp_kernel, far, len(batch), not mid),
            ins + weights,
            ([pair_shape] * 2 + [hidden_shape] * 2) * len(batch) + [mine, other if final else mine],
            10 * group * seq_len * width * TILE * len(batch),
            in_specs=[row_spec] * len(ins) + [whole(w.shape) for w in weights],
            out_specs=([pair_spec] * 2 + [hidden_spec] * 2) * len(batch) + [row_spec] * 2,
            grid=(group,),
            scratch=[lines, lines],
        )
        mid = [mid_own, mid_sib]
        for n, t in enumerate(batch):
            pairs.append(inner[4 * n : 4 * n + 2])
            hiddens.append(inner[4 * n + 2 : 4 * n + 4])
            mlp_steps.append(weight_grads([(seq_mid, [pairs[t]]), (grad_rows, [hiddens[t]])], 1))
            more, came_here = next(mlp_steps[t])
            parts = parts + more
            came.append(came_here)
    came_two = []
    for steps in mlp_steps:
        more, came_here = steps.send(parts)
        parts = parts + more
        came_two.append(came_here)
    mid_local = tie(collect(mid_own, mid_sib, (), came[0]), *parts, *came[1])
    resid_grad = grad_local.astype(F32) + norm_back(mid_local, normed_two, inv_two, gains[2])
    resid_back = resid_grad.astype(BF)
    firsts = [steps.send([resid_back])[0] for steps in mlp_steps]
    attn_grad = spread(resid_back, (), [p for f in firsts[:2] for p in f])

    parts = [p for f in firsts for p in f] + came_two[0]
    out_ins = [h for pair in hiddens for h in pair]
    out_ins[0] = tie(out_ins[0], resid_back)
    out_terms = call(
        functools.partial(mlp_out_kernel, far, tiles),
        out_ins + [w for ws in w_mlp for w in ws],
        [mine, other],
        2 * group * seq_len * width * hidden_cols,
        in_specs=[whole(v.shape) for v in out_ins]
        + [pl.BlockSpec((w.shape[0], TILE), lambda *_: (0, 2)) for ws in w_mlp for w in ws],
    )
    out_sum = collect(*out_terms, [], [attn_grad[0]])
    ins = [tie(attn_grad[0], *parts), attn_grad[1], qkv] + facts + w_attn
    outs = [lin_shape, lin_shape, shaped((group, 1, 3 * head_cols), F32), mine3, other3]
    lin_own, lin_sib, bias_sums, *terms = call(
        functools.partial(attend_back_kernel, len(w_attn)),
        ins,
        outs,
        attn_flops,
        in_specs=[each(v.shape) for v in ins[: 3 + len(facts)]] + [whole(v.shape) for v in w_attn],
        out_specs=[each(v.shape) for v in outs],
        grid=(group,),
        scratch=[lines, pltpu.VMEM((seq_len, 3 * head_cols), BF)],
    )
    bias_sums = jnp.sum(bias_sums, axis=(0, 1))
    in_grad = collect(*map(half, terms), [], [out_sum])
    attn_steps = weight_grads(
        [
            (seq_in, [[half(lin_own), half(lin_sib)]]),
            ([half(h) for h in attn_grad], [mixed]),
        ],
        1,
    )
    parts, _ = attn_steps.send(None)
    more, _ = attn_steps.send(parts + [p for c in came_two for p in c])
    token_grad = from_rel(resid_grad + norm_back(in_grad, normed_one, inv_one, gains[0]))

    def sum_all(array):
        for b in far_bits + list(GROUP_BITS):
            array = array + swap(array, 1 << b)
            yield array
        yield array + sibling(array)

    def both_sums(grad, normed):
        return [jnp.sum(grad * normed, axis=0), jnp.sum(grad, axis=0)]

    norm_sums = jnp.stack(both_sums(in_grad, normed_one) + both_sums(mid_local, normed_two))
    bias_full = lax.dynamic_update_slice(
        jnp.zeros((3, head_cols * group * lax.axis_size("tensor")), F32),
        bias_sums.reshape(3, head_cols),
        (jnp.int32(0), (core * group + rank) * head_cols),
    )
    sums = list(sum_all(jnp.concatenate([from_rel(norm_sums), bias_full])))
    result = from_rel((resid_two + out_sum).astype(BF))
    after = [in_grad]
    mlp_came = []
    for t, steps in enumerate(mlp_steps):
        *_, (mlp_mine, _) = [steps.send(more)] + list(steps)
        mlp_came.append(exchange(tie(mlp_mine[0], *after)))
        after = [mlp_came[-1], sums[t]]
    *_, (attn_mine, _) = list(attn_steps)
    attn_came = exchange(tie(attn_mine[0], *after))
    gate_up_grad, down_grad = finish(
        finish_mlp_kernel, mlp_came, (gate_up_weight.shape, down_weight.shape)
    )
    qkv_grad, out_w_grad = finish(
        finish_attn_kernel, [attn_came], (qkv_weight.shape, out_weight.shape)
    )
    sums = sums[-1]
    return (
        result,
        token_grad,
        sums[0],
        sums[1],
        qkv_grad,
        sums[4:],
        out_w_grad,
        sums[2],
        sums[3],
        gate_up_grad,
        down_grad,
    )


def solution(mesh):
    return jax.shard_map(
        on_device,
        mesh=mesh,
        in_specs=(
            P(("dp", "tensor"), None),
            P("dp"),
            P(),
            P(),
            P(None, "dp", "tensor"),
            P(None, "tensor"),
            P("tensor", "dp"),
            P(),
            P(),
            P(None, "dp", "tensor"),
            P("tensor", "dp"),
            P(("dp", "tensor"), None),
        ),
        out_specs=(
            P(("dp", "tensor"), None),
            P(("dp", "tensor"), None),
            P(),
            P(),
            P(None, "dp", "tensor"),
            P(),
            P("tensor", "dp"),
            P(),
            P(),
            P(None, "dp", "tensor"),
            P("tensor", "dp"),
        ),
        check_vma=False,
    )
```

time: 823 us -> 644 us (0.78)
  waiting for transfers between devices: 481 us -> 280 us
  Pallas kernels: 0 us -> 158 us
  matrix products: 67.5 us -> 0 us
  other arithmetic: 96.5 us -> 40.6 us
  local copies, waits for them, and re-layouts: 87.9 us -> 39.6 us
  blocking collectives: 0 us -> 20.1 us
  starting transfers between devices: 76.9 us -> 93 us
    ppermute x71 -> x28, waiting for transfers between devices: 479 us -> 164 us  [swap(): return lax.ppermute(array, 'dp', [(d, d ^ mask) for d in range(dp_size)])]
    pallas_call x0 -> x25, Pallas kernels: none -> 158 us  [call(): pl.pallas_call(kernel, grid=grid, in_specs=in_specs or [whole(v.shape) fo...]
    all_to_all x0 -> x13, waiting for transfers between devices: none -> 112 us  [exchange(): lax.all_to_all(rows_by_rank, 'dp', 0, 0, axis_index_groups=bands, tiled=T...]
    dot_general x18 -> x0, matrix products: 67.5 us -> none  [the longest x12 60.4 us: dot(): return lax.dot_general(a, b, (dims, ((), ())), preferred_element_type=F32)]
    all_to_all x0 -> x13, starting transfers between devices: none -> 54.7 us  [exchange(): lax.all_to_all(rows_by_rank, 'dp', 0, 0, axis_index_groups=bands, tiled=T...]
    ppermute x71 -> x28, starting transfers between devices: 76.6 us -> 37.7 us  [swap(): return lax.ppermute(array, 'dp', [(d, d ^ mask) for d in range(dp_size)])]
    another operation x25 -> x3, other arithmetic: 33.3 us -> 1.27 us
    all_to_all x0 -> x1, blocking collectives: none -> 20.1 us  [exchange(): lax.all_to_all(rows_by_rank, 'dp', 0, 0, axis_index_groups=bands, tiled=T...]
  transfers between devices with their start and end apart: 80 -> 50, of which waited for: 42 -> 20; matrix products, arithmetic and copies ran while one was open for 23% -> 11% of each run, Pallas kernels for 0% -> 24%
where the time goes in v2:
time: 644 us; the launch traced here: 634 us
  waiting for transfers between devices  280 us (43%)
  Pallas kernels  158 us (25%)
  starting transfers between devices  93 us (14%)
  other arithmetic  40.6 us (6%)
  local copies, waits for them, and re-layouts  39.6 us (6%)
  blocking collectives  20.1 us (3%)
    ppermute x28, waiting for transfers between devices, swap(): return lax.ppermute(array, 'dp', [(d, d ^ mask) for d in range(dp_size)])  164 us
    pallas_call x25, Pallas kernels, call(): pl.pallas_call(kernel, grid=grid, in_specs=in_specs or [whole(v.shape) fo...  158 us
    all_to_all x13, waiting for transfers between devices, exchange(): lax.all_to_all(rows_by_rank, 'dp', 0, 0, axis_index_groups=bands, tiled=T...  112 us
    all_to_all x13, starting transfers between devices, exchange(): lax.all_to_all(rows_by_rank, 'dp', 0, 0, axis_index_groups=bands, tiled=T...  54.7 us
    ppermute x28, starting transfers between devices, swap(): return lax.ppermute(array, 'dp', [(d, d ^ mask) for d in range(dp_size)])  37.7 us
    all_to_all x1, blocking collectives, exchange(): lax.all_to_all(rows_by_rank, 'dp', 0, 0, axis_index_groups=bands, tiled=T...  20.1 us
    convert_element_type x4, other arithmetic, collect(): both = (by_block(mine) + by_block(other).astype(F32)).astype(BF)  17.6 us
  transfers between devices with their start and end apart: 50, of which 20 were waited for; matrix products, arithmetic and copies ran while one was open for 11% of the time, Pallas kernels for 24%

profile of v2, /device:TPU:0, one launch (start us, length us, event | category | flops | bytes accessed | tf_op | source)
XLA Modules:
  0.0 634.1 jit_solution(5225069706660072936)
XLA Ops:
  3.0 20.1 %all_to_all.107 = bf16[4,128,1024]{2,1,0:T(8,128)(2,1)} all-to-all(bf16[4,128,1024]{2,1,0:T(8,128)(2,1)} %bitcast.100), channel_id=1, replica_groups={{0,4,8,12},{2,6,10,14},{16,20,24,28},{18,22,26,30},{1,5,9,13},{3,7,11,1..., dimensions={0} | all-to-all | bytes 2097152 | tf_op jit(solution)/shard_map/all_to_all | solution.py:406
  23.0 3.3 shard_map.204
  26.3 3.8 all-to-all-start.1
  36.2 2.8 collective-permute-start
  43.7 40.3 %collective-permute-done.refs_1_ = bf16[512,1024]{1,0:T(8,128)(2,1)} collective-permute-done((bf16[512,1024]{1,0:T(8,128)(2,1)}, bf16[512,1024]{1,0:T(8,128)(2,1)}, u32[]{:S(2)}, u32[]{:S(2)}) %collective-permute-start) | collective-permute-done | bytes 1048608 | tf_op jit(solution)/shard_map/ppermute | solution.py:371
  84.0 2.8 broadcast_in_dim.68
  86.8 4.5 all-to-all-start.2
  99.4 32.9 %collective-permute-done.1.refs_5_.refs_7_ = bf16[512,768]{1,0:T(8,128)(2,1)S(1)} collective-permute-done((bf16[512,768]{1,0:T(8,128)(2,1)}, bf16[512,768]{1,0:T(8,128)(2,1)S(1)}, u32[]{:S(2)}, u32[]{:S(2)}) %collective-permute-start.1) | collective-permute-done | bytes 786464 | tf_op jit(solution)/shard_map/ppermute | solution.py:371
  134.4 6.5 %collective-permute-done.3.refs_3_ = bf16[512,1024]{1,0:T(8,128)(2,1)} collective-permute-done((bf16[512,1024]{1,0:T(8,128)(2,1)}, bf16[512,1024]{1,0:T(8,128)(2,1)}, u32[]{:S(2)}, u32[]{:S(2)}) %collective-permute-start.3) | collective-permute-done | bytes 1048608 | tf_op jit(solution)/shard_map/ppermute | solution.py:371
  145.7 4.5 all-to-all-start.3
  151.5 3.1 fusion.4
  154.6 17.1 %shard_map.205 = (bf16[4,256,768]{2,1,0:T(8,128)(2,1)}, bf16[4,128,256]{2,1,0:T(8,128)(2,1)}, bf16[4,128,256]{2,1,0:T(8,128)(2,1)}, f32[4,128,2048]{2,1,0:T(8,128)}, bf16[4,128,2048]{2,1,0:T(8,128)(2,1)}) custom-call(bf16[4,144,2048]{2,1,0:T(8,128)(2,1)} %all-to-all-done.2.own_ref, bf16[4,144,2048]{2,1,0:T(8,128)(2,1)} %collective-permute-done.4.sib_ref, ...), custom_call_target="tpu_custom_call" | custom-call | flops 128849018880 | bytes 597780480 | tf_op jit(solution)/shard_map/pallas_call | solution.py:72
  172.3 4.0 collective-permute-done.6
  176.3 4.3 fusion.1
  180.6 4.1 all-to-all-start.4
  188.6 38.4 %all-to-all-done.4 = bf16[4,128,2048]{2,1,0:T(8,128)(2,1)S(1)} async-done(((bf16[4,128,2048]{2,1,0:T(8,128)(2,1)}), bf16[4,128,2048]{2,1,0:T(8,128)(2,1)S(1)}, u32[]{:S(2)}, u32[]{:S(2)}) %all-to-all-start.4) | async-done | bytes 2097184 | tf_op jit(solution)/shard_map/all_to_all | solution.py:406
  230.4 4.3 all-to-all-start.5
  237.7 17.8 %collective-permute-done.10.refs_11_.refs_13_ = bf16[512,768]{1,0:T(8,128)(2,1)S(1)} collective-permute-done((bf16[512,768]{1,0:T(8,128)(2,1)}, bf16[512,768]{1,0:T(8,128)(2,1)S(1)}, u32[]{:S(2)}, u32[]{:S(2)}) %collective-permute-start.10) | collective-permute-done | bytes 786464 | tf_op jit(solution)/shard_map/ppermute | solution.py:371
  255.5 18.3 %collective-permute-done.11.refs_7_.refs_15_ = bf16[512,768]{1,0:T(8,128)(2,1)S(1)} collective-permute-done((bf16[512,768]{1,0:T(8,128)(2,1)S(1)}, bf16[512,768]{1,0:T(8,128)(2,1)S(1)}, u32[]{:S(2)}, u32[]{:S(2)}) %collective-permute-start.11) | collective-permute-done | bytes 786464 | tf_op jit(solution)/shard_map/ppermute | solution.py:371
  277.5 3.1 slice.127
  280.6 3.2 slice.128
  283.8 17.1 %shard_map.206 = (bf16[512,512]{1,0:T(8,128)(2,1)}, bf16[512,512]{1,0:T(8,128)(2,1)}, bf16[512,256]{1,0:T(8,128)(2,1)}, bf16[512,256]{1,0:T(8,128)(2,1)}, bf16[5...) custom-call(bf16[512,2048]{1,0:T(8,128)(2,1)} %bitcast.106, ...), custom_call_target="tpu_custom_call" | custom-call | flops 322122547200 | bytes 786432000 | tf_op jit(solution)/shard_map/pallas_call | solution.py:72
  300.9 3.9 shard_map.207
  305.6 3.9 shard_map.208
  310.8 14.0 %shard_map.209 = (bf16[512,512]{1,0:T(8,128)(2,1)}, bf16[512,512]{1,0:T(8,128)(2,1)}, bf16[512,256]{1,0:T(8,128)(2,1)}, bf16[512,256]{1,0:T(8,128)(2,1)}, f32[51...) custom-call(bf16[512,2048]{1,0:T(8,128)(2,1)} %bitcast.109, bf16[512,2048]{1,0:T(8,128)(2,1)} %bitcast.26.refs_1_, ...), custom_call_target="tpu_custom_call" | custom-call | flops 161061273600 | bytes 833617920 | tf_op jit(solution)/shard_map/pallas_call | solution.py:72
  324.8 3.9 shard_map.210
  329.4 3.9 shard_map.211
  334.6 4.2 add_convert_fusion.1
  338.9 4.2 all-to-all-start.6
  343.1 3.9 shard_map.212
  347.9 3.9 shard_map.213
  353.0 15.3 %all-to-all-done.6 = bf16[4,128,2048]{2,1,0:T(8,128)(2,1)S(1)} async-done(((bf16[4,128,2048]{2,1,0:T(8,128)(2,1)}), bf16[4,128,2048]{2,1,0:T(8,128)(2,1)S(1)}, u32[]{:S(2)}, u32[]{:S(2)}) %all-to-all-start.6) | async-done | bytes 2097184 | tf_op jit(solution)/shard_map/all_to_all | solution.py:406
  371.4 7.2 %shard_map.214 = (f32[512,2048]{1,0:T(8,128)}, bf16[512,2048]{1,0:T(8,128)(2,1)}) custom-call(bf16[512,256]{1,0:T(8,128)(2,1)} %get-tuple-element.111.refs_6_.refs_0_, bf16[512,256]{1,0:T(8,128)(2,1)} %get-tuple-element.92.refs_7_.refs_1_, bf16[512,256]{1,0:T(8,128)(2,1)} %get-tuple-element.95.refs_6_.refs_2_, ...), custom_call_target="tpu_custom_call" | custom-call | flops 96636764160 | bytes 519045120 | tf_op jit(solution)/shard_map/pallas_call | solution.py:72
  380.2 3.6 all-to-all-start.7
  383.8 4.2 shard_map.215
  388.0 4.2 shard_map.216
  392.2 17.4 %all-to-all-done.7.own_ref = bf16[4,128,2048]{2,1,0:T(8,128)(2,1)S(1)} async-done(((bf16[4,128,2048]{2,1,0:T(8,128)(2,1)}), bf16[4,128,2048]{2,1,0:T(8,128)(2,1)S(1)}, u32[]{:S(2)}, u32[]{:S(2)}) %all-to-all-start.7) | async-done | bytes 2097184 | tf_op jit(solution)/shard_map/all_to_all | solution.py:406
  409.6 4.9 shard_map.217
  416.5 4.9 add_convert_fusion
  421.4 4.7 all-to-all-start.8
  429.1 21.5 %shard_map.218 = (bf16[4,128,768]{2,1,0:T(8,128)(2,1)}, bf16[4,128,768]{2,1,0:T(8,128)(2,1)}, f32[4,1,768]{2,1,0:T(1,128)}, f32[4,128,2048]{2,1,0:T(8,128)}, bf16[4,128,2048]{2,1,0:T(8,128)(2,1)}) custom-call(bf16[4,128,2048]{2,1,0:T(8,128)(2,1)} %copy-done.17, bf16[4,128,2048]{2,1,0:T(8,128)(2,1)} %collective-permute-done.22.sib_ref, ...), custom_call_target="tpu_custom_call" | custom-call | flops 128849018880 | bytes 613785600 | tf_op jit(solution)/shard_map/pallas_call | solution.py:72
  450.6 4.5 shard_map.219
  455.1 4.4 shard_map.220
  460.3 13.2 %all-to-all-done.8 = bf16[4,128,2048]{2,1,0:T(8,128)(2,1)} async-done(((bf16[4,128,2048]{2,1,0:T(8,128)(2,1)}), bf16[4,128,2048]{2,1,0:T(8,128)(2,1)}, u32[]{:S(2)}, u32[]{:S(2)}) %all-to-all-start.8) | async-done | bytes 2097184 | tf_op jit(solution)/shard_map/all_to_all | solution.py:406
  473.5 3.0 convert_reduce_fusion.2
  477.2 4.2 fusion
  481.4 3.6 all-to-all-start.9
  485.0 4.5 shard_map.224
  489.6 29.8 %collective-permute-done.36.refs_9_ = bf16[512,768]{1,0:T(8,128)(2,1)} collective-permute-done((bf16[512,768]{1,0:T(8,128)(2,1)}, bf16[512,768]{1,0:T(8,128)(2,1)}, u32[]{:S(2)}, u32[]{:S(2)}) %collective-permute-start.36) | collective-permute-done | bytes 786464 | tf_op jit(solution)/shard_map/ppermute | solution.py:371
  519.4 4.4 shard_map.225
  523.9 11.5 %all-to-all-done.9 = bf16[4,128,2048]{2,1,0:T(8,128)(2,1)S(1)} async-done(((bf16[4,128,2048]{2,1,0:T(8,128)(2,1)}), bf16[4,128,2048]{2,1,0:T(8,128)(2,1)S(1)}, u32[]{:S(2)}, u32[]{:S(2)}) %all-to-all-start.9) | async-done | bytes 2097184 | tf_op jit(solution)/shard_map/all_to_all | solution.py:406
  539.8 4.1 all-to-all-start.10
  543.9 4.8 shard_map.221
  548.7 2.9 collective-permute-start.33
  551.6 5.9 all-to-all-done.10
  558.4 4.2 all-to-all-start.11
  562.6 4.6 shard_map.223
  574.3 6.9 %all-to-all-done.11 = bf16[4,128,768]{2,1,0:T(8,128)(2,1)} async-done(((bf16[4,128,768]{2,1,0:T(8,128)(2,1)}), bf16[4,128,768]{2,1,0:T(8,128)(2,1)}, u32[]{:S(2)}, u32[]{:S(2)}) %all-to-all-start.11) | async-done | bytes 786464 | tf_op jit(solution)/shard_map/all_to_all | solution.py:406
  581.2 5.7 all-to-all-start.12
  586.9 7.8 %collective-permute-done.33.refs_9_ = bf16[512,1024]{1,0:T(8,128)(2,1)} collective-permute-done((bf16[512,1024]{1,0:T(8,128)(2,1)}, bf16[512,1024]{1,0:T(8,128)(2,1)}, u32[]{:S(2)}, u32[]{:S(2)}) %collective-permute-start.33) | collective-permute-done | bytes 1048608 | tf_op jit(solution)/shard_map/ppermute | solution.py:371
  594.7 5.1 shard_map.222
  605.5 3.5 all-to-all-start.13
  615.8 7.1 %collective-permute-done.27 = f32[7,2048]{1,0:T(8,128)S(1)} collective-permute-done((f32[7,2048]{1,0:T(8,128)S(1)}, f32[7,2048]{1,0:T(8,128)S(1)}, u32[]{:S(2)}, u32[]{:S(2)}) %collective-permute-start.27) | collective-permute-done | bytes 57376 | tf_op jit(solution)/shard_map/ppermute | solution.py:371
  626.0 4.0 shard_map.227
  (271 shorter events, 92.3 us)
Async XLA Ops:
  0.6 90.7 %copy-start = (f32[3,1024]{1,0:T(4,128)S(1)}, f32[3,1024]{1,0:T(4,128)}, u32[]{:S(2)}) copy-start(f32[3,1024]{1,0:T(4,128)} %param.17) | copy-start | bytes 36868
  26.3 57.7 %all-to-all-start.1 = ((bf16[4,128,2304]{2,1,0:T(8,128)(2,1)}), bf16[4,128,2304]{2,1,0:T(8,128)(2,1)S(1)}, u32[]{:S(2)}, u32[]{:S(2)}) async-start(bf16[4,128,2304]{2,1,0:T(8,128)(2,1)} %bitcast.94), calls=%async_computation.1 | async-start | bytes 4718592 | tf_op jit(solution)/shard_map/all_to_all | solution.py:406
  35.5 7.1 %copy-start.34 = (f32[128]{0:T(128)}, f32[128]{0:T(128)S(1)}, u32[]{:S(2)}) copy-start(f32[128]{0:T(128)S(1)} %broadcast_multiply_fusion.5) | copy-start | bytes 1540
  36.2 47.8 %collective-permute-start = (bf16[512,1024]{1,0:T(8,128)(2,1)}, bf16[512,1024]{1,0:T(8,128)(2,1)}, u32[]{:S(2)}, u32[]{:S(2)}) collective-permute-start(bf16[512,1024]{1,0:T(8,128)(2,1)} %bitcast.11.refs_0_), channel_id=1, source_target_pairs={{0,16},{2,18},{4,20},{6,22},{8,24},{10,26},{12,28},{14,30},{16,0},... | collective-permute-start | bytes 3145736 | tf_op jit(solution)/shard_map/ppermute | solution.py:371
  41.9 185.5 %copy-start.5 = (f32[128,2048]{1,0:T(8,128)}, f32[128,2048]{1,0:T(8,128)S(1)}, u32[]{:S(2)}) copy-start(f32[128,2048]{1,0:T(8,128)S(1)} %copy.153) | copy-start | bytes 3145732
  42.6 185.3 %copy-start.22 = (f32[1,2,2,2,2,128]{5,4,3,2,1,0:T(2,128)}, f32[1,2,2,2,2,128]{5,4,3,2,1,0:T(2,128)S(1)}, u32[]{:S(2)}) copy-start(f32[1,2,2,2,2,128]{5,4,3,2,1,0:T(2,128)S(1)} %get-tuple-element.191) | copy-start | bytes 24580
  86.8 47.6 %all-to-all-start.2 = ((bf16[4,144,2048]{2,1,0:T(8,128)(2,1)}), bf16[4,144,2048]{2,1,0:T(8,128)(2,1)}, u32[]{:S(2)}, u32[]{:S(2)}) async-start(bf16[4,144,2048]{2,1,0:T(8,128)(2,1)} %broadcast_in_dim.68), calls=%async_computation.2 | async-start | bytes 4718592 | tf_op jit(solution)/shard_map/all_to_all | solution.py:406
  92.0 42.5 %collective-permute-start.2 = (bf16[512,1024]{1,0:T(8,128)(2,1)}, bf16[512,1024]{1,0:T(8,128)(2,1)}, u32[]{:S(2)}, u32[]{:S(2)}) collective-permute-start(bf16[512,1024]{1,0:T(8,128)(2,1)} %bitcast.11.refs_0_), channel_id=1, source_target_pairs={{0,2},{2,0},{4,6},{6,4},{8,10},{10,8},{12,14},{14,12},{16,18},{18,... | collective-permute-start | bytes 3145736 | tf_op jit(solution)/shard_map/ppermute | solution.py:371
  93.1 47.8 %collective-permute-start.3 = (bf16[512,1024]{1,0:T(8,128)(2,1)}, bf16[512,1024]{1,0:T(8,128)(2,1)}, u32[]{:S(2)}, u32[]{:S(2)}) collective-permute-start(bf16[512,1024]{1,0:T(8,128)(2,1)} %collective-permute-done.refs_1_), channel_id=1, source_target_pairs={{0,2},{2,0},{4,6},{6,4},{8,10},{10,8},{12,14},{14,12},{16,18},{18,... | collective-permute-start | bytes 3145736 | tf_op jit(solution)/shard_map/ppermute | solution.py:371
  95.5 36.7 %collective-permute-start.1 = (bf16[512,768]{1,0:T(8,128)(2,1)}, bf16[512,768]{1,0:T(8,128)(2,1)S(1)}, u32[]{:S(2)}, u32[]{:S(2)}) collective-permute-start(bf16[512,768]{1,0:T(8,128)(2,1)} %get-tuple-element.77.refs_4_.refs_6_), channel_id=1, source_target_pairs={{0,16},{2,18},{4,20},{6,22},{8,24},{10,26},{12,28},{14,30},{16,0},... | collective-permute-start | bytes 2359304 | tf_op jit(solution)/shard_map/ppermute | solution.py:371
  97.6 48.0 %copy-start.9 = (bf16[128,2048]{1,0:T(8,128)(2,1)}, bf16[128,2048]{1,0:T(8,128)(2,1)S(1)}, u32[]{:S(2)}) copy-start(bf16[128,2048]{1,0:T(8,128)(2,1)S(1)} %copy.152) | copy-start | bytes 1572868
  97.8 73.9 %collective-permute-start.5 = (bf16[512,768]{1,0:T(8,128)(2,1)}, bf16[512,768]{1,0:T(8,128)(2,1)}, u32[]{:S(2)}, u32[]{:S(2)}) collective-permute-start(bf16[512,768]{1,0:T(8,128)(2,1)} %get-tuple-element.77.refs_4_.refs_6_), channel_id=1, source_target_pairs={{0,2},{2,0},{4,6},{6,4},{8,10},{10,8},{12,14},{14,12},{16,18},{18,... | collective-permute-start | bytes 2359304 | tf_op jit(solution)/shard_map/ppermute | solution.py:371
  132.2 13.4 %copy-start.41 = (bf16[512,768]{1,0:T(8,128)(2,1)}, bf16[512,768]{1,0:T(8,128)(2,1)S(1)}, u32[]{:S(2)}) copy-start(bf16[512,768]{1,0:T(8,128)(2,1)S(1)} %collective-permute-done.1.refs_5_.refs_7_) | copy-start | bytes 2359300
  140.9 13.7 %collective-permute-start.4 = (bf16[4,144,2048]{2,1,0:T(8,128)(2,1)}, bf16[4,144,2048]{2,1,0:T(8,128)(2,1)}, u32[]{:S(2)}, u32[]{:S(2)}) collective-permute-start(bf16[4,144,2048]{2,1,0:T(8,128)(2,1)} %all-to-all-done.2.own_ref), channel_id=1, source_target_pairs={{0,1},{1,0},{2,3},{3,2},{4,5},{5,4},{6,7},{7,6},{8,9},{9,8},{10,11... | collective-permute-start | bytes 7077896 | tf_op jit(solution)/shard_map/ppermute | solution.py:374
  145.7 34.9 %all-to-all-start.3 = ((bf16[4,128,2048]{2,1,0:T(8,128)(2,1)}), bf16[4,128,2048]{2,1,0:T(8,128)(2,1)}, u32[]{:S(2)}, u32[]{:S(2)}) async-start(bf16[4,128,2048]{2,1,0:T(8,128)(2,1)} %broadcast_in_dim.77), calls=%async_computation.3 | async-start | bytes 4194304 | tf_op jit(solution)/shard_map/all_to_all | solution.py:406
  171.7 4.6 collective-permute-start.6
  180.6 46.4 %all-to-all-start.4 = ((bf16[4,128,2048]{2,1,0:T(8,128)(2,1)}), bf16[4,128,2048]{2,1,0:T(8,128)(2,1)S(1)}, u32[]{:S(2)}, u32[]{:S(2)}) async-start(bf16[4,128,2048]{2,1,0:T(8,128)(2,1)} %fusion.1), calls=%async_computation.4 | async-start | bytes 4194304 | tf_op jit(solution)/shard_map/all_to_all | solution.py:406
  184.7 42.6 %collective-permute-start.7 = (bf16[512,768]{1,0:T(8,128)(2,1)}, bf16[512,768]{1,0:T(8,128)(2,1)}, u32[]{:S(2)}, u32[]{:S(2)}) collective-permute-start(bf16[512,768]{1,0:T(8,128)(2,1)} %copy-done.41), channel_id=1, source_target_pairs={{0,2},{2,0},{4,6},{6,4},{8,10},{10,8},{12,14},{14,12},{16,18},{18,... | collective-permute-start | bytes 2359304 | tf_op jit(solution)/shard_map/ppermute | solution.py:371
  185.8 41.6 %collective-permute-start.8 = (bf16[512,768]{1,0:T(8,128)(2,1)}, bf16[512,768]{1,0:T(8,128)(2,1)}, u32[]{:S(2)}, u32[]{:S(2)}) collective-permute-start(bf16[512,768]{1,0:T(8,128)(2,1)} %get-tuple-element.85.refs_8_.refs_10_), channel_id=1, source_target_pairs={{0,16},{2,18},{4,20},{6,22},{8,24},{10,26},{12,28},{14,30},{16,0},... | collective-permute-start | bytes 2359304 | tf_op jit(solution)/shard_map/ppermute | solution.py:371
  188.1 39.3 %collective-permute-start.9 = (bf16[512,768]{1,0:T(8,128)(2,1)}, bf16[512,768]{1,0:T(8,128)(2,1)}, u32[]{:S(2)}, u32[]{:S(2)}) collective-permute-start(bf16[512,768]{1,0:T(8,128)(2,1)} %get-tuple-element.85.refs_8_.refs_10_), channel_id=1, source_target_pairs={{0,2},{2,0},{4,6},{6,4},{8,10},{10,8},{12,14},{14,12},{16,18},{18,... | collective-permute-start | bytes 2359304 | tf_op jit(solution)/shard_map/ppermute | solution.py:371
  230.4 45.6 %all-to-all-start.5 = ((bf16[4,128,2048]{2,1,0:T(8,128)(2,1)}), bf16[4,128,2048]{2,1,0:T(8,128)(2,1)S(1)}, u32[]{:S(2)}, u32[]{:S(2)}) async-start(bf16[4,128,2048]{2,1,0:T(8,128)(2,1)} %broadcast_in_dim.78), calls=%async_computation.5 | async-start | bytes 4194304 | tf_op jit(solution)/shard_map/all_to_all | solution.py:406
  234.7 20.8 %collective-permute-start.10 = (bf16[512,768]{1,0:T(8,128)(2,1)}, bf16[512,768]{1,0:T(8,128)(2,1)S(1)}, u32[]{:S(2)}, u32[]{:S(2)}) collective-permute-start(bf16[512,768]{1,0:T(8,128)(2,1)} %collective-permute-done.8.refs_9_.refs_11_), channel_id=1, source_target_pairs={{0,2},{2,0},{4,6},{6,4},{8,10},{10,8},{12,14},{14,12},{16,18},{18,... | collective-permute-start | bytes 2359304 | tf_op jit(solution)/shard_map/ppermute | solution.py:371
  236.3 37.5 %collective-permute-start.11 = (bf16[512,768]{1,0:T(8,128)(2,1)S(1)}, bf16[512,768]{1,0:T(8,128)(2,1)S(1)}, u32[]{:S(2)}, u32[]{:S(2)}) collective-permute-start(bf16[512,768]{1,0:T(8,128)(2,1)S(1)} %copy-done.18), channel_id=1, source_target_pairs={{0,16},{2,18},{4,20},{6,22},{8,24},{10,26},{12,28},{14,30},{16,0},... | collective-permute-start | bytes 2359304 | tf_op jit(solution)/shard_map/ppermute | solution.py:371
  237.2 37.6 %collective-permute-start.12 = (bf16[512,768]{1,0:T(8,128)(2,1)S(1)}, bf16[512,768]{1,0:T(8,128)(2,1)}, u32[]{:S(2)}, u32[]{:S(2)}) collective-permute-start(bf16[512,768]{1,0:T(8,128)(2,1)S(1)} %copy-done.18), channel_id=1, source_target_pairs={{0,2},{2,0},{4,6},{6,4},{8,10},{10,8},{12,14},{14,12},{16,18},{18,... | collective-permute-start | bytes 2359304 | tf_op jit(solution)/shard_map/ppermute | solution.py:371
  237.7 46.1 %collective-permute-start.14 = (bf16[4,128,2048]{2,1,0:T(8,128)(2,1)}, bf16[4,128,2048]{2,1,0:T(8,128)(2,1)}, u32[]{:S(2)}, u32[]{:S(2)}) collective-permute-start(bf16[4,128,2048]{2,1,0:T(8,128)(2,1)} %all-to-all-done.3), channel_id=1, source_target_pairs={{0,1},{1,0},{2,3},{3,2},{4,5},{5,4},{6,7},{7,6},{8,9},{9,8},{10,11... | collective-permute-start | bytes 6291464 | tf_op jit(solution)/shard_map/ppermute | solution.py:374
  255.5 18.3 %copy-start.42 = (bf16[512,768]{1,0:T(8,128)(2,1)}, bf16[512,768]{1,0:T(8,128)(2,1)S(1)}, u32[]{:S(2)}) copy-start(bf16[512,768]{1,0:T(8,128)(2,1)S(1)} %collective-permute-done.10.refs_11_.refs_13_) | copy-start | bytes 2359300
  276.0 7.8 %collective-permute-start.13 = (bf16[4,128,2048]{2,1,0:T(8,128)(2,1)S(1)}, bf16[4,128,2048]{2,1,0:T(8,128)(2,1)}, u32[]{:S(2)}, u32[]{:S(2)}) collective-permute-start(bf16[4,128,2048]{2,1,0:T(8,128)(2,1)S(1)} %all-to-all-done.5), channel_id=1, source_target_pairs={{0,1},{1,0},{2,3},{3,2},{4,5},{5,4},{6,7},{7,6},{8,9},{9,8},{10,11... | collective-permute-start | bytes 6291464 | tf_op jit(solution)/shard_map/ppermute | solution.py:374
  276.0 34.8 %collective-permute-start.15 = (bf16[512,768]{1,0:T(8,128)(2,1)}, bf16[512,768]{1,0:T(8,128)(2,1)}, u32[]{:S(2)}, u32[]{:S(2)}) collective-permute-start(bf16[512,768]{1,0:T(8,128)(2,1)} %copy-done.43), channel_id=1, source_target_pairs={{0,2},{2,0},{4,6},{6,4},{8,10},{10,8},{12,14},{14,12},{16,18},{18,... | collective-permute-start | bytes 2359304 | tf_op jit(solution)/shard_map/ppermute | solution.py:371
  304.9 34.0 %collective-permute-start.17 = (bf16[512,768]{1,0:T(8,128)(2,1)}, bf16[512,768]{1,0:T(8,128)(2,1)}, u32[]{:S(2)}, u32[]{:S(2)}) collective-permute-start(bf16[512,768]{1,0:T(8,128)(2,1)} %shard_map.207), channel_id=1, source_target_pairs={{0,2},{2,0},{4,6},{6,4},{8,10},{10,8},{12,14},{14,12},{16,18},{18,... | collective-permute-start | bytes 2359304 | tf_op jit(solution)/shard_map/ppermute | solution.py:371
  309.5 59.2 %collective-permute-start.18 = (bf16[512,768]{1,0:T(8,128)(2,1)}, bf16[512,768]{1,0:T(8,128)(2,1)}, u32[]{:S(2)}, u32[]{:S(2)}) collective-permute-start(bf16[512,768]{1,0:T(8,128)(2,1)} %shard_map.208), channel_id=1, source_target_pairs={{0,2},{2,0},{4,6},{6,4},{8,10},{10,8},{12,14},{14,12},{16,18},{18,... | collective-permute-start | bytes 2359304 | tf_op jit(solution)/shard_map/ppermute | solution.py:371
  328.7 80.9 %collective-permute-start.20 = (bf16[512,768]{1,0:T(8,128)(2,1)}, bf16[512,768]{1,0:T(8,128)(2,1)}, u32[]{:S(2)}, u32[]{:S(2)}) collective-permute-start(bf16[512,768]{1,0:T(8,128)(2,1)} %shard_map.210), channel_id=1, source_target_pairs={{0,2},{2,0},{4,6},{6,4},{8,10},{10,8},{12,14},{14,12},{16,18},{18,... | collective-permute-start | bytes 2359304 | tf_op jit(solution)/shard_map/ppermute | solution.py:371
  329.4 5.2 collective-permute-start.16
  333.3 92.8 %collective-permute-start.21 = (bf16[512,768]{1,0:T(8,128)(2,1)}, bf16[512,768]{1,0:T(8,128)(2,1)}, u32[]{:S(2)}, u32[]{:S(2)}) collective-permute-start(bf16[512,768]{1,0:T(8,128)(2,1)} %shard_map.211), channel_id=1, source_target_pairs={{0,2},{2,0},{4,6},{6,4},{8,10},{10,8},{12,14},{14,12},{16,18},{18,... | collective-permute-start | bytes 2359304 | tf_op jit(solution)/shard_map/ppermute | solution.py:371
  338.9 29.5 %all-to-all-start.6 = ((bf16[4,128,2048]{2,1,0:T(8,128)(2,1)}), bf16[4,128,2048]{2,1,0:T(8,128)(2,1)S(1)}, u32[]{:S(2)}, u32[]{:S(2)}) async-start(bf16[4,128,2048]{2,1,0:T(8,128)(2,1)} %bitcast.95), calls=%async_computation.6 | async-start | bytes 4194304 | tf_op jit(solution)/shard_map/all_to_all | solution.py:406
  347.0 108.1 %collective-permute-start.29 = (bf16[512,768]{1,0:T(8,128)(2,1)}, bf16[512,768]{1,0:T(8,128)(2,1)}, u32[]{:S(2)}, u32[]{:S(2)}) collective-permute-start(bf16[512,768]{1,0:T(8,128)(2,1)} %shard_map.212), channel_id=1, source_target_pairs={{0,2},{2,0},{4,6},{6,4},{8,10},{10,8},{12,14},{14,12},{16,18},{18,... | collective-permute-start | bytes 2359304 | tf_op jit(solution)/shard_map/ppermute | solution.py:371
  351.8 16.9 %copy-start.3 = (f32[128,2048]{1,0:T(8,128)S(1)}, f32[128,2048]{1,0:T(8,128)}, u32[]{:S(2)}) copy-start(f32[128,2048]{1,0:T(8,128)} %copy-done.2) | copy-start | bytes 3145732
  351.8 16.9 %copy-start.23 = (f32[1,2,2,2,2,128]{5,4,3,2,1,0:T(2,128)S(1)}, f32[1,2,2,2,2,128]{5,4,3,2,1,0:T(2,128)}, u32[]{:S(2)}) copy-start(f32[1,2,2,2,2,128]{5,4,3,2,1,0:T(2,128)} %copy-done.22) | copy-start | bytes 24580
  351.8 16.9 %copy-start.33 = (f32[128]{0:T(128)S(1)}, f32[128]{0:T(128)}, u32[]{:S(2)}) copy-start(f32[128]{0:T(128)} %copy-done.32) | copy-start | bytes 1540
  351.8 16.9 %copy-start.39 = (f32[128]{0:T(128)S(1)}, f32[128]{0:T(128)}, u32[]{:S(2)}) copy-start(f32[128]{0:T(128)} %copy-done.38) | copy-start | bytes 1540
  351.8 103.2 %collective-permute-start.30 = (bf16[512,768]{1,0:T(8,128)(2,1)}, bf16[512,768]{1,0:T(8,128)(2,1)}, u32[]{:S(2)}, u32[]{:S(2)}) collective-permute-start(bf16[512,768]{1,0:T(8,128)(2,1)} %shard_map.213), channel_id=1, source_target_pairs={{0,2},{2,0},{4,6},{6,4},{8,10},{10,8},{12,14},{14,12},{16,18},{18,... | collective-permute-start | bytes 2359304 | tf_op jit(solution)/shard_map/ppermute | solution.py:371
  378.6 36.0 %collective-permute-start.19 = (bf16[512,2048]{1,0:T(8,128)(2,1)}, bf16[512,2048]{1,0:T(8,128)(2,1)}, u32[]{:S(2)}, u32[]{:S(2)}) collective-permute-start(bf16[512,2048]{1,0:T(8,128)(2,1)} %get-tuple-element.113), channel_id=1, source_target_pairs={{0,1},{1,0},{2,3},{3,2},{4,5},{5,4},{6,7},{7,6},{8,9},{9,8},{10,11... | collective-permute-start | bytes 6291464 | tf_op jit(solution)/shard_map/ppermute | solution.py:374
  380.2 29.4 %all-to-all-start.7 = ((bf16[4,128,2048]{2,1,0:T(8,128)(2,1)}), bf16[4,128,2048]{2,1,0:T(8,128)(2,1)S(1)}, u32[]{:S(2)}, u32[]{:S(2)}) async-start(bf16[4,128,2048]{2,1,0:T(8,128)(2,1)} %broadcast_in_dim.79), calls=%async_computation.7 | async-start | bytes 4194304 | tf_op jit(solution)/shard_map/all_to_all | solution.py:406
  409.6 17.6 %collective-permute-start.22 = (bf16[4,128,2048]{2,1,0:T(8,128)(2,1)S(1)}, bf16[4,128,2048]{2,1,0:T(8,128)(2,1)}, u32[]{:S(2)}, u32[]{:S(2)}) collective-permute-start(bf16[4,128,2048]{2,1,0:T(8,128)(2,1)S(1)} %all-to-all-done.7.own_ref), channel_id=1, source_target_pairs={{0,1},{1,0},{2,3},{3,2},{4,5},{5,4},{6,7},{7,6},{8,9},{9,8},{10,11... | collective-permute-start | bytes 6291464 | tf_op jit(solution)/shard_map/ppermute | solution.py:374
  414.6 70.5 %collective-permute-start.35 = (bf16[512,768]{1,0:T(8,128)(2,1)}, bf16[512,768]{1,0:T(8,128)(2,1)}, u32[]{:S(2)}, u32[]{:S(2)}) collective-permute-start(bf16[512,768]{1,0:T(8,128)(2,1)} %shard_map.216), channel_id=1, source_target_pairs={{0,16},{2,18},{4,20},{6,22},{8,24},{10,26},{12,28},{14,30},{16,0},... | collective-permute-start | bytes 2359304 | tf_op jit(solution)/shard_map/ppermute | solution.py:371
  421.4 52.0 %all-to-all-start.8 = ((bf16[4,128,2048]{2,1,0:T(8,128)(2,1)}), bf16[4,128,2048]{2,1,0:T(8,128)(2,1)}, u32[]{:S(2)}, u32[]{:S(2)}) async-start(bf16[4,128,2048]{2,1,0:T(8,128)(2,1)} %bitcast.30), calls=%async_computation.8 | async-start | bytes 4194304 | tf_op jit(solution)/shard_map/all_to_all | solution.py:406
  426.1 136.5 %collective-permute-start.34 = (bf16[512,768]{1,0:T(8,128)(2,1)}, bf16[512,768]{1,0:T(8,128)(2,1)}, u32[]{:S(2)}, u32[]{:S(2)}) collective-permute-start(bf16[512,768]{1,0:T(8,128)(2,1)} %shard_map.217), channel_id=1, source_target_pairs={{0,16},{2,18},{4,20},{6,22},{8,24},{10,26},{12,28},{14,30},{16,0},... | collective-permute-start | bytes 2359304 | tf_op jit(solution)/shard_map/ppermute | solution.py:371
  427.2 92.3 %collective-permute-start.36 = (bf16[512,768]{1,0:T(8,128)(2,1)}, bf16[512,768]{1,0:T(8,128)(2,1)}, u32[]{:S(2)}, u32[]{:S(2)}) collective-permute-start(bf16[512,768]{1,0:T(8,128)(2,1)} %shard_map.215), channel_id=1, source_target_pairs={{0,16},{2,18},{4,20},{6,22},{8,24},{10,26},{12,28},{14,30},{16,0},... | collective-permute-start | bytes 2359304 | tf_op jit(solution)/shard_map/ppermute | solution.py:371
  455.1 21.4 %collective-permute-start.23 = (bf16[512,2048]{1,0:T(8,128)(2,1)}, bf16[512,2048]{1,0:T(8,128)(2,1)S(1)}, u32[]{:S(2)}, u32[]{:S(2)}) collective-permute-start(bf16[512,2048]{1,0:T(8,128)(2,1)} %bitcast.170), channel_id=1, source_target_pairs={{0,1},{1,0},{2,3},{3,2},{4,5},{5,4},{6,7},{7,6},{8,9},{9,8},{10,11... | collective-permute-start | bytes 6291464 | tf_op jit(solution)/shard_map/ppermute | solution.py:374
  459.5 127.3 %collective-permute-start.31 = (bf16[512,1024]{1,0:T(8,128)(2,1)}, bf16[512,1024]{1,0:T(8,128)(2,1)}, u32[]{:S(2)}, u32[]{:S(2)}) collective-permute-start(bf16[512,1024]{1,0:T(8,128)(2,1)} %shard_map.220), channel_id=1, source_target_pairs={{0,2},{2,0},{4,6},{6,4},{8,10},{10,8},{12,14},{14,12},{16,18},{18,... | collective-permute-start | bytes 3145736 | tf_op jit(solution)/shard_map/ppermute | solution.py:371
  476.5 67.4 %collective-permute-start.32 = (bf16[512,1024]{1,0:T(8,128)(2,1)}, bf16[512,1024]{1,0:T(8,128)(2,1)}, u32[]{:S(2)}, u32[]{:S(2)}) collective-permute-start(bf16[512,1024]{1,0:T(8,128)(2,1)} %shard_map.219), channel_id=1, source_target_pairs={{0,2},{2,0},{4,6},{6,4},{8,10},{10,8},{12,14},{14,12},{16,18},{18,... | collective-permute-start | bytes 3145736 | tf_op jit(solution)/shard_map/ppermute | solution.py:371
  481.4 54.0 %all-to-all-start.9 = ((bf16[4,128,2048]{2,1,0:T(8,128)(2,1)}), bf16[4,128,2048]{2,1,0:T(8,128)(2,1)S(1)}, u32[]{:S(2)}, u32[]{:S(2)}) async-start(bf16[4,128,2048]{2,1,0:T(8,128)(2,1)} %fusion), calls=%async_computation.9 | async-start | bytes 4194304 | tf_op jit(solution)/shard_map/all_to_all | solution.py:406
  539.7 11.8 %collective-permute-start.24 = (f32[7,2048]{1,0:T(8,128)S(1)}, f32[7,2048]{1,0:T(8,128)S(1)}, u32[]{:S(2)}, u32[]{:S(2)}) collective-permute-start(f32[7,2048]{1,0:T(8,128)S(1)} %pad_maximum_fusion), channel_id=1, source_target_pairs={{0,16},{2,18},{4,20},{6,22},{8,24},{10,26},{12,28},{14,30},{16,0},... | collective-permute-start | bytes 172040 | tf_op jit(solution)/shard_map/ppermute | solution.py:371
  539.8 17.7 %all-to-all-start.10 = ((bf16[4,128,768]{2,1,0:T(8,128)(2,1)}), bf16[4,128,768]{2,1,0:T(8,128)(2,1)S(1)}, u32[]{:S(2)}, u32[]{:S(2)}) async-start(bf16[4,128,768]{2,1,0:T(8,128)(2,1)} %bitcast.57), calls=%async_computation.10 | async-start | bytes 1572864 | tf_op jit(solution)/shard_map/all_to_all | solution.py:406
  548.7 46.1 %collective-permute-start.33 = (bf16[512,1024]{1,0:T(8,128)(2,1)}, bf16[512,1024]{1,0:T(8,128)(2,1)}, u32[]{:S(2)}, u32[]{:S(2)}) collective-permute-start(bf16[512,1024]{1,0:T(8,128)(2,1)} %shard_map.221), channel_id=1, source_target_pairs={{0,16},{2,18},{4,20},{6,22},{8,24},{10,26},{12,28},{14,30},{16,0},... | collective-permute-start | bytes 3145736 | tf_op jit(solution)/shard_map/ppermute | solution.py:371
  558.4 22.8 %all-to-all-start.11 = ((bf16[4,128,768]{2,1,0:T(8,128)(2,1)}), bf16[4,128,768]{2,1,0:T(8,128)(2,1)}, u32[]{:S(2)}, u32[]{:S(2)}) async-start(bf16[4,128,768]{2,1,0:T(8,128)(2,1)} %bitcast.59), calls=%async_computation.11 | async-start | bytes 1572864 | tf_op jit(solution)/shard_map/all_to_all | solution.py:406
  570.0 4.3 collective-permute-start.25
  581.2 23.4 %all-to-all-start.12 = ((bf16[4,128,768]{2,1,0:T(8,128)(2,1)}), bf16[4,128,768]{2,1,0:T(8,128)(2,1)S(1)}, u32[]{:S(2)}, u32[]{:S(2)}) async-start(bf16[4,128,768]{2,1,0:T(8,128)(2,1)} %bitcast.140), calls=%async_computation.12 | async-start | bytes 1572864 | tf_op jit(solution)/shard_map/all_to_all | solution.py:406
  586.9 15.5 %copy-start.21 = (f32[1,2,2,2,2,128]{5,4,3,2,1,0:T(2,128)S(1)}, f32[1,2,2,2,2,128]{5,4,3,2,1,0:T(2,128)}, u32[]{:S(2)}) copy-start(f32[1,2,2,2,2,128]{5,4,3,2,1,0:T(2,128)} %copy-done.20) | copy-start | bytes 24580
  599.8 9.2 %copy-start.6 = (f32[128,2048]{1,0:T(8,128)S(1)}, f32[128,2048]{1,0:T(8,128)}, u32[]{:S(2)}) copy-start(f32[128,2048]{1,0:T(8,128)} %copy-done.5) | copy-start | bytes 3145732
  599.8 4.8 collective-permute-start.26
  605.5 24.4 %all-to-all-start.13 = ((bf16[4,128,1024]{2,1,0:T(8,128)(2,1)}), bf16[4,128,1024]{2,1,0:T(8,128)(2,1)S(1)}, u32[]{:S(2)}, u32[]{:S(2)}) async-start(bf16[4,128,1024]{2,1,0:T(8,128)(2,1)} %bitcast.139), calls=%async_computation.13 | async-start | bytes 2097152 | tf_op jit(solution)/shard_map/all_to_all | solution.py:406
  613.7 9.2 %collective-permute-start.27 = (f32[7,2048]{1,0:T(8,128)S(1)}, f32[7,2048]{1,0:T(8,128)S(1)}, u32[]{:S(2)}, u32[]{:S(2)}) collective-permute-start(f32[7,2048]{1,0:T(8,128)S(1)} %add.137), channel_id=1, source_target_pairs={{0,8},{2,10},{4,12},{6,14},{8,0},{10,2},{12,4},{14,6},{16,24},{18,... | collective-permute-start | bytes 172040 | tf_op jit(solution)/shard_map/ppermute | solution.py:371
  622.9 1.8 collective-permute-start.28
  623.4 10.3 %copy-start.1 = (f32[3,1024]{1,0:T(4,128)S(1)}, f32[3,1024]{1,0:T(4,128)}, u32[]{:S(2)}) copy-start(f32[3,1024]{1,0:T(4,128)} %param.17) | copy-start | bytes 36868
  (32 other events, 95.7 us)

commit v3 on v2

--- a/solution.py
+++ b/solution.py
@@ -19,7 +19,6 @@
 GROUP_BITS = (1, 2)
 BF = jnp.bfloat16
 F32 = jnp.float32
-COST = 30
 VMEM_LIMIT = 60 * 1024 * 1024
 
 
@@ -66,9 +65,13 @@
     return pl.BlockSpec((None,) + shape[1:], lambda k, *_: (k,) + zeros)
 
 
-def call(kernel, ins, out_shapes, flops, in_specs=None, out_specs=None, grid=(1,), scratch=()):
-    moved = sum(v.size * v.dtype.itemsize for v in ins)
-    moved += sum(s.size * s.dtype.itemsize for s in out_shapes)
+LONG, SHORT = 30, 0
+
+
+def call(
+    kernel, ins, out_shapes, flops, in_specs=None, out_specs=None, grid=(1,), scratch=(), cost=LONG
+):
+    moved = cost * sum(v.size * v.dtype.itemsize for v in [*ins, *out_shapes])
     return pl.pallas_call(
         kernel,
         grid=grid,
@@ -77,7 +80,7 @@
         out_shape=list(out_shapes),
         scratch_shapes=list(scratch),
         compiler_params=pltpu.CompilerParams(vmem_limit_bytes=VMEM_LIMIT),
-        cost_estimate=pl.CostEstimate(flops=COST * flops, bytes_accessed=COST * moved, transcendentals=0),
+        cost_estimate=pl.CostEstimate(flops=cost * flops, bytes_accessed=moved, transcendentals=0),
     )(*ins)
 
 
@@ -128,14 +131,14 @@
 
 
 def finish_mlp_kernel(group, *refs):
-    got, (gate_up_ref, down_ref) = refs[:-2], refs[-2:]
+    got, gate_up_ref, down_ref = refs
     full, share = deal(gate_up_ref.shape[2], group)
     block = gate_up_ref.shape[1]
     per = LANES // share
 
     def taken(k, j, at):
-        to = column(j, at % TILE)
-        return got[at // TILE][k * block : (k + 1) * block, to : to + LANES].astype(F32)
+        to = column(j, at)
+        return got[k * block : (k + 1) * block, to : to + LANES].astype(F32)
 
     for j in range(3):
         for at in range(0, full + LANES, LANES):
@@ -188,8 +191,8 @@
     weights, refs = refs[:far], refs[far:]
     qkv_ref, mixed_own, mixed_sib, mine_ref, other_ref, lines, mixed_ref = refs
     rows = mine_ref.shape[0]
-    lines[:rows] = own_ref[:rows]
-    lines[rows:] = sib_ref[:rows]
+    lines[:rows] = own_ref[...]
+    lines[rows:] = sib_ref[...]
     cols = mixed_ref.shape[1]
     tables = (cos_ref[...], lead_ref[...], tail_ref[...])
     lin = bias_ref[...]
@@ -315,26 +318,22 @@
         lefts.append(refs[at : at + 2])
         rights.append([refs[at + 2 + 2 * c : at + 4 + 2 * c] for c in range(count)])
         at += 2 + 2 * count
-    more = refs[at : at + sum(adds)]
-    outs = refs[at + sum(adds) :]
+    more, out = refs[at : at + len(adds)], refs[-1]
     start = 0
     for left, columns in zip(lefts, rights):
         for right in columns:
-            size = right[0].shape[1]
-            here = slice(start, start + size)
-            start += size
+            here = slice(start, start + right[0].shape[1])
+            start = here.stop
             total = sum(dot(a[...], b[...], 0, 0) for a, b in zip(left, right))
-            parts = len(adds)
-            depth = total.shape[0] // parts
-            used = 0
-            for i, count in enumerate(adds):
-                part = total[i * depth : (i + 1) * depth]
-                for extra in more[used : used + count]:
-                    part = part + extra[:, here].astype(F32)
-                used += count
-                out = outs[i] if len(outs) > 1 else outs[0]
-                lines = slice(None) if len(outs) > 1 else slice(i * depth, (i + 1) * depth)
-                out[lines, here] = part.astype(BF)
+            for extra, first in zip(more, adds):
+                if first <= here.start < first + extra.shape[1]:
+                    total = total + extra[:, here.start - first : here.stop - first].astype(F32)
+            out[:, here] = total.astype(BF)
+
+
+def copies_kernel(local_ref, out_ref):
+    for k in range(out_ref.shape[0]):
+        out_ref[k] = local_ref[...]
 
 
 def on_device(
@@ -359,6 +358,9 @@
     seq_len = segment_ids.shape[0]
     group = 1 << len(GROUP_BITS)
     far_bits = [b for b in reversed(range(bits)) if b not in GROUP_BITS]
+    masks = [
+        sum(1 << b for i, b in enumerate(GROUP_BITS) if (k >> i) & 1) for k in range(group)
+    ]
     my_bit = [(me >> b) & 1 for b in range(bits)]
     rank = sum(my_bit[b] << i for i, b in enumerate(GROUP_BITS))
     heads = qkv_bias.shape[1] // HD // group
@@ -376,19 +378,24 @@
     order = [bits - 1 - b for b in reversed(far_bits)]
     order += [bits - 1 - b for b in reversed(GROUP_BITS)]
 
+    def swapped(array, axis, bit):
+        low, high = jnp.split(array, 2, axis)
+        low, high = jnp.where(bit == 1, high, low), jnp.where(bit == 1, low, high)
+        return jnp.concatenate([low, high], axis)
+
     def to_rel(array):
         lead = array.ndim - 1
         cut = array.reshape(array.shape[:-1] + (2,) * bits + (width // dp_size,))
         cut = cut.transpose(list(range(lead)) + [lead + o for o in order] + [lead + bits])
         for i, b in enumerate(reversed(far_bits)):
-            cut = jnp.where(my_bit[b] == 1, jnp.flip(cut, lead + i), cut)
+            cut = swapped(cut, lead + i, my_bit[b])
         return cut.reshape(array.shape)
 
     def from_rel(array):
         lead = array.ndim - 1
         cut = array.reshape(array.shape[:-1] + (2,) * bits + (width // dp_size,))
         for i, b in enumerate(reversed(far_bits)):
-            cut = jnp.where(my_bit[b] == 1, jnp.flip(cut, lead + i), cut)
+            cut = swapped(cut, lead + i, my_bit[b])
         back = [order.index(i) for i in range(bits)]
         cut = cut.transpose(list(range(lead)) + [lead + o for o in back] + [lead + bits])
         return cut.reshape(array.shape)
@@ -413,22 +420,18 @@
             functools.partial(kernel, group), ins, [shaped((shard_rows, cols), BF)], 0
         )[0]
 
-    def gather(shard, subs, after=()):
-        depth = shard_rows // subs
-        parts = [tie(shard[i * depth : (i + 1) * depth], *after) for i in range(subs)]
-        pieces = [parts]
+    def gather(shard, after=(), after_own=()):
+        pieces = [shard]
         for n, b in enumerate(far_bits):
-            came = [[swap(p, 1 << b) for p in piece] for piece in pieces[1:]]
-            whole_shard = n > 0 and len(pieces) > 1
-            first = [swap(shard, 1 << b)] if whole_shard else [swap(p, 1 << b) for p in parts]
-            pieces = pieces + [first] + came
+            own = tie(shard, *(after_own if n else after))
+            pieces = pieces + [swap(p, 1 << b) for p in [own] + pieces[1:]]
         return pieces
 
-    def flat(pieces, shard):
-        return [shard] + [p for piece in pieces[1:] for p in piece]
-
-    def spread(local, after=(), then=()):
-        mine = exchange(tie(jnp.broadcast_to(local, (group,) + local.shape), *after))
+    def copies(local):
+        return jnp.broadcast_to(local, (group,) + local.shape)
+
+    def spread(copied, after=(), then=()):
+        mine = exchange(tie(copied, *after))
         return mine, sibling(tie(mine, *then))
 
     def half(array):
@@ -437,51 +440,44 @@
     def by_block(array):
         return array.reshape((group, -1) + array.shape[1:])
 
-    def collect(mine, other, after=(), then=()):
+    def merge(mine, other, after=()):
         other = sibling(tie(other, *after))
-        both = (by_block(mine) + by_block(other).astype(F32)).astype(BF)
-        return jnp.sum(exchange(tie(both, *then)).astype(F32), axis=0)
-
-    def arrived(pieces):
-        return [p for piece in pieces for p in piece]
-
-    def weight_grads(kinds, subs):
+        return (by_block(mine) + by_block(other).astype(F32)).astype(BF)
+
+    def collect(both, after=()):
+        return jnp.sum(exchange(tie(both, *after)).astype(F32), axis=0)
+
+    wide = sorted(range(1, far), key=lambda i: (-i.bit_length(), -i))
+
+    def below(i):
+        bits_left = range(i.bit_length(), len(far_bits))
+        return [c for b in bits_left for c in below(i | 1 << b) + [i | 1 << b]]
+
+    def block_grad(i, kinds, adds, after=()):
         cols = sum(c[0].shape[1] for _, sets in kinds for c in sets)
-        spec = lambda v, i: pl.BlockSpec((v.shape[0], shard_rows), lambda *_: (0, i))
-
-        def make(i, adds, outs, after):
-            ins, specs = [], []
-            for left, sets in kinds:
-                ins += left
-                specs += [spec(v, i) for v in left]
-                for s in sets:
-                    ins += s
-                    specs += [whole(v.shape) for v in s]
-            counts = [len(a) for a in adds]
-            for a in adds:
-                ins += a
-                specs += [whole(v.shape) for v in a]
-            ins[0] = tie(ins[0], *after)
-            return call(
-                functools.partial(grad_kernel, [len(s) for _, s in kinds], counts),
-                ins,
-                [shaped((shard_rows // outs, cols), BF)] * outs,
-                2 * group * seq_len * shard_rows * cols,
-                in_specs=specs,
-            )
-
-        adds = [[[] for _ in range(subs)] for _ in range(far)]
-        count = far
-        after = ()
-        for b in reversed(far_bits):
-            count //= 2
-            for i in reversed(range(count)):
-                parts = make(i + count, adds[i + count], subs, after)
-                came = [swap(p, 1 << b) for p in parts]
-                for j in range(subs):
-                    adds[i][j].append(came[j])
-                after = (yield list(parts), came) or ()
-        yield make(0, adds[0], 1, after), None
+        ins, specs = [], []
+        for left, sets in kinds:
+            ins += left
+            specs += [pl.BlockSpec((v.shape[0], shard_rows), lambda *_: (0, i)) for v in left]
+            for s in sets:
+                ins += s
+                specs += [whole(v.shape) for v in s]
+        ins += [v for v, _ in adds]
+        specs += [whole(v.shape) for v, _ in adds]
+        ins[0] = tie(ins[0], *after)
+        return call(
+            functools.partial(grad_kernel, [len(s) for _, s in kinds], [at for _, at in adds]),
+            ins,
+            [shaped((shard_rows, cols), BF)],
+            2 * group * seq_len * shard_rows * cols,
+            in_specs=specs,
+        )[0]
+
+    def send(i, part):
+        return swap(part, 1 << far_bits[i.bit_length() - 1])
+
+    def parent(i):
+        return i ^ 1 << i.bit_length() - 1
 
     def finish(kernel, came, shapes):
         return call(functools.partial(kernel, group), came, [shaped(s, F32) for s in shapes], 0)
@@ -489,29 +485,18 @@
     gains = to_rel(jnp.stack([ln1_gain, ln1_bias, ln2_gain, ln2_bias]))
     resid = to_rel(tokens).astype(F32)
     normed_in, normed_one, inv_one = norm_parts(resid, gains[0], gains[1])
-    note = jnp.pad(segment_ids.astype(BF)[None], ((0, 15), (0, width - seq_len)))
-    message = jnp.concatenate([normed_in.astype(BF), note], axis=0)
-
+    seq_local = normed_in.astype(BF)
     attn_pack = pack(pack_attn_kernel, [qkv_weight, out_weight], 4 * head_cols)
     attn_shard = exchange(attn_pack)
+    segs = jnp.stack([swap(tie(segment_ids, attn_pack), m) for m in masks])
+    segs = segs.reshape((2,) * len(GROUP_BITS) + segs.shape[1:])
+    for i, b in enumerate(reversed(GROUP_BITS)):
+        segs = swapped(segs, i, my_bit[b])
+    segs = segs.reshape(group, seq_len)
     mlp_pack = pack(pack_mlp_kernel, [tie(gate_up_weight, attn_shard), down_weight], 3 * hidden_cols)
     mlp_shard = exchange(tie(mlp_pack, attn_shard))
-    attn_pieces = gather(attn_shard, 1)
-    w_attn = flat(attn_pieces, attn_shard)
-    heard = spread(message, [mlp_shard] + attn_pieces[1], w_attn[1:])
+    w_attn = gather(attn_shard)
     tiles = hidden_cols // TILE
-    mlp_pieces = []
-    after = attn_pieces[1]
-    for t in range(tiles):
-        shard = tie(mlp_shard[:, t * 3 * TILE : (t + 1) * 3 * TILE], *after)
-        mlp_pieces.append(gather(shard, 1))
-        after = mlp_pieces[t][1]
-    w_mlp = [flat(pieces, pieces[0][0]) for pieces in mlp_pieces]
-    grad_local = to_rel(out_grad)
-    grad_rows = spread(grad_local, [heard[0]])
-
-    segs = heard[0][:, rows, :seq_len].astype(jnp.int32)
-    seq_in = [half(h[:, :rows]) for h in heard]
     spots = jax.vmap(doc_positions)(segs)
     segs, spots = (jnp.where(core == 1, jnp.roll(v, rows, axis=1), v) for v in (segs, spots))
     index = jnp.arange(seq_len, dtype=jnp.int32)
@@ -526,6 +511,22 @@
     lead = jnp.where(dim < ROT // 2, -sine, 0.0)
     tail = jnp.where((dim >= ROT // 2) & (dim < ROT), sine, 0.0)
 
+    w_mlp = []
+    after, after_own = [w_attn[1]], [w_attn[-1]]
+    for t in range(tiles):
+        shard = mlp_shard[:, t * 3 * TILE : (t + 1) * 3 * TILE]
+        w_mlp.append(gather(shard, after, after_own))
+        after, after_own = [w_mlp[t][1]], [w_mlp[t][2]]
+    grad_local = to_rel(out_grad)
+    grad_copies = copies(grad_local)
+    heard = spread(
+        tie(copies(seq_local), grad_copies, cosine, lead, tail, mask),
+        [mlp_shard] + w_attn[1:3],
+        w_attn[3:] + w_mlp[0][1:2],
+    )
+    seq_in = [half(h) for h in heard]
+    grad_rows = spread(grad_copies, [heard[0]])
+
     bias = lax.dynamic_slice_in_dim(qkv_bias, rank * head_cols, head_cols, 1).reshape(1, -1)
     facts = [mask, cosine, lead, tail]
     lines = pltpu.VMEM((seq_len, width), BF)
@@ -536,7 +537,7 @@
     lin_shape = shaped((group, rows, 3 * head_cols), BF)
     attn_flops = 2 * group * seq_len * width * 4 * head_cols
 
-    ins = [tie(heard[0], *mlp_pieces[0][1]), heard[1], bias] + facts + w_attn
+    ins = [*heard, bias] + facts + w_attn
     outs = [qkv_shape, mixed_shape, mixed_shape, mine3, other3]
     qkv, mixed_own, mixed_sib, *terms = call(
         functools.partial(attend_kernel, len(w_attn)),
@@ -552,66 +553,94 @@
         scratch=[lines, pltpu.VMEM((seq_len, head_cols), BF)],
     )
     mixed = [half(mixed_own), half(mixed_sib)]
-    attn_sum = collect(*map(half, terms), mlp_pieces[0][2], [grad_rows[0]])
-    early = arrived(mlp_pieces[0][3:]) + [p for pieces in mlp_pieces[1:2] for p in arrived(pieces[1:3])]
-    resid_two = resid + tie(attn_sum, *early)
+    both = merge(*map(half, terms), w_mlp[0][2:3])
+    attn_sum = collect(both, [grad_rows[0]])
+    resid_two = resid + tie(attn_sum, *w_mlp[0][3:], *w_mlp[1][1:3])
     normed_mid, normed_two, inv_two = norm_parts(resid_two, gains[2], gains[3])
-    late = [p for pieces in mlp_pieces[1:2] for p in arrived(pieces[3:])]
-    late += [p for pieces in mlp_pieces[2:] for p in arrived(pieces[1:3])]
-    seq_mid = [half(h) for h in spread(normed_mid.astype(BF), (), late)]
+    seq_mid = [half(h) for h in spread(copies(normed_mid.astype(BF)), (), w_mlp[1][3:] + [p for w in w_mlp[2:] for p in w[1:3]])]
     grad_rows = [half(h) for h in grad_rows]
 
     row_spec = pl.BlockSpec((rows, width), lambda k: (k, 0))
     pair_spec, hidden_spec = (pl.BlockSpec((rows, n * TILE), lambda k: (k, 0)) for n in (2, 1))
     pair_shape, hidden_shape = (shaped((group * rows, n * TILE), BF) for n in (2, 1))
-    pairs, hiddens, mlp_steps, mid = [], [], [], []
-    parts, came = [], []
+    weights = [[w for w in [mlp_shard] + w_mlp[t][1:]] for t in range(tiles)]
+    inner, mid = [], []
     for batch in (range(tiles - 1), range(tiles - 1, tiles)):
-        ins = [tie(seq_mid[0], *parts), seq_mid[1], *grad_rows] + mid
+        ins = [*seq_mid, *grad_rows] + mid
         final = batch[-1] == tiles - 1
-        weights = [w for t in batch for w in w_mlp[t]]
-        *inner, mid_own, mid_sib = call(
+        *found, mid_own, mid_sib = call(
             functools.partial(mlp_kernel, far, len(batch), not mid),
-            ins + weights,
+            ins + [w for t in batch for w in weights[t]],
             ([pair_shape] * 2 + [hidden_shape] * 2) * len(batch) + [mine, other if final else mine],
             10 * group * seq_len * width * TILE * len(batch),
-            in_specs=[row_spec] * len(ins) + [whole(w.shape) for w in weights],
+            in_specs=[row_spec] * len(ins)
+            + [
+                pl.BlockSpec((w.shape[0], 3 * TILE), lambda *_, t=0 if n else t: (0, t))
+                for t in batch
+                for n, w in enumerate(weights[t])
+            ],
             out_specs=([pair_spec] * 2 + [hidden_spec] * 2) * len(batch) + [row_spec] * 2,
             grid=(group,),
             scratch=[lines, lines],
         )
+        inner += found
         mid = [mid_own, mid_sib]
-        for n, t in enumerate(batch):
-            pairs.append(inner[4 * n : 4 * n + 2])
-            hiddens.append(inner[4 * n + 2 : 4 * n + 4])
-            mlp_steps.append(weight_grads([(seq_mid, [pairs[t]]), (grad_rows, [hiddens[t]])], 1))
-            more, came_here = next(mlp_steps[t])
-            parts = parts + more
-            came.append(came_here)
-    came_two = []
-    for steps in mlp_steps:
-        more, came_here = steps.send(parts)
-        parts = parts + more
-        came_two.append(came_here)
-    mid_local = tie(collect(mid_own, mid_sib, (), came[0]), *parts, *came[1])
+    weights = [w for ws in weights for w in ws]
+    hiddens = [inner[4 * t + 2 : 4 * t + 4] for t in range(tiles)]
+    tile_kinds = [
+        [(seq_mid, [inner[4 * t : 4 * t + 2]]), (grad_rows, [hiddens[t]])] for t in range(tiles)
+    ]
+    all_kinds = [kind for kinds in tile_kinds for kind in kinds]
+    both = merge(mid_own, mid_sib)
+
+    last = far // 2
+    batches = [range(t, t + 1) for t in range(tiles)]
+    batch_kinds = [[kind for t in batch for kind in tile_kinds[t]] for batch in batches]
+    batch_adds = [[[] for _ in range(far)] for _ in batches]
+    first_parts, first_came, later, later_came, held = [], [], [], [], []
+
+    def batch_step(n, i, after):
+        part = block_grad(i, batch_kinds[n], [(v, 0) for v in batch_adds[n][i]], after)
+        if i == 1 and n > 1:
+            held.append((n, i, part))
+            return part, None
+        came = send(i, part)
+        batch_adds[n][parent(i)].append(came)
+        return part, came
+
+    steps = [i for i in below(0) if i != last]
+    for n in range(len(batches)):
+        part, came = batch_step(n, steps[0], [both] + first_parts if n else [])
+        first_parts.append(part)
+        first_came.append(came)
+    last_part = block_grad(last, all_kinds, [], first_parts)
+    last_came = send(last, last_part)
+    mid_local = tie(collect(both), last_part, first_came[0])
     resid_grad = grad_local.astype(F32) + norm_back(mid_local, normed_two, inv_two, gains[2])
     resid_back = resid_grad.astype(BF)
-    firsts = [steps.send([resid_back])[0] for steps in mlp_steps]
-    attn_grad = spread(resid_back, (), [p for f in firsts[:2] for p in f])
-
-    parts = [p for f in firsts for p in f] + came_two[0]
+    copied = copies(resid_back)
+    for i in steps[1:]:
+        for n in range(len(batches)):
+            part, came = batch_step(n, i, [copied] + later)
+            later.append(part)
+            later_came.append(came)
     out_ins = [h for pair in hiddens for h in pair]
-    out_ins[0] = tie(out_ins[0], resid_back)
+    out_ins[0] = tie(out_ins[0], copied)
     out_terms = call(
         functools.partial(mlp_out_kernel, far, tiles),
-        out_ins + [w for ws in w_mlp for w in ws],
+        out_ins + weights,
         [mine, other],
         2 * group * seq_len * width * hidden_cols,
         in_specs=[whole(v.shape) for v in out_ins]
-        + [pl.BlockSpec((w.shape[0], TILE), lambda *_: (0, 2)) for ws in w_mlp for w in ws],
-    )
-    out_sum = collect(*out_terms, [], [attn_grad[0]])
-    ins = [tie(attn_grad[0], *parts), attn_grad[1], qkv] + facts + w_attn
+        + [
+            pl.BlockSpec((w.shape[0], TILE), lambda *_, t=3 * (n // far) if n % far == 0 else 0: (0, t + 2))
+            for n, w in enumerate(weights)
+        ],
+        cost=SHORT,
+    )
+    out_both = merge(*out_terms)
+    attn_grad = spread(copied, [], [out_both, *later, later_came[0], last_came])
+    ins = [*attn_grad, qkv] + facts + w_attn
     outs = [lin_shape, lin_shape, shaped((group, 1, 3 * head_cols), F32), mine3, other3]
     lin_own, lin_sib, bias_sums, *terms = call(
         functools.partial(attend_back_kernel, len(w_attn)),
@@ -624,23 +653,37 @@
         scratch=[lines, pltpu.VMEM((seq_len, 3 * head_cols), BF)],
     )
     bias_sums = jnp.sum(bias_sums, axis=(0, 1))
-    in_grad = collect(*map(half, terms), [], [out_sum])
-    attn_steps = weight_grads(
-        [
-            (seq_in, [[half(lin_own), half(lin_sib)]]),
-            ([half(h) for h in attn_grad], [mixed]),
-        ],
-        1,
-    )
-    parts, _ = attn_steps.send(None)
-    more, _ = attn_steps.send(parts + [p for c in came_two for p in c])
+    for n, i, part in held:
+        came = send(i, tie(part, lin_own))
+        batch_adds[n][parent(i)].append(came)
+        later_came.append(came)
+    later_came = [came for came in later_came if came is not None]
+    both = merge(*map(half, terms), later_came[1:2])
+    out_sum = collect(out_both, [attn_grad[0]])
+    in_grad = tie(collect(both, [out_sum]), *later_came[2:3])
+    attn_kinds = [
+        (seq_in, [[half(lin_own), half(lin_sib)]]),
+        ([half(h) for h in attn_grad], [mixed]),
+    ]
+    attn_adds = [[] for _ in range(far)]
+    parts, attn_sent = [], []
+    for n, i in enumerate(wide):
+        after = ([in_grad] if attn_adds[i] else [both]) + parts if n else []
+        part = block_grad(i, attn_kinds, [(v, 0) for v in attn_adds[i]], after)
+        parts.append(part)
+        attn_sent.append(send(i, part))
+        attn_adds[parent(i)].append(attn_sent[-1])
     token_grad = from_rel(resid_grad + norm_back(in_grad, normed_one, inv_one, gains[0]))
 
     def sum_all(array):
-        for b in far_bits + list(GROUP_BITS):
-            array = array + swap(array, 1 << b)
-            yield array
-        yield array + sibling(array)
+        array = array + sibling(array)
+        yield sum((swap(array, m) for m in masks[1:]), array)
+
+    def far_sum(array):
+        for at in range(0, len(far_bits), 2):
+            pair = [1 << b for b in far_bits[at : at + 2]]
+            array = sum((swap(array, m) for m in pair + [sum(pair)][: len(pair) - 1]), array)
+        return array
 
     def both_sums(grad, normed):
         return [jnp.sum(grad * normed, axis=0), jnp.sum(grad, axis=0)]
@@ -652,17 +695,15 @@
         (jnp.int32(0), (core * group + rank) * head_cols),
     )
     sums = list(sum_all(jnp.concatenate([from_rel(norm_sums), bias_full])))
+    sums.append(far_sum(sums[0]))
     result = from_rel((resid_two + out_sum).astype(BF))
-    after = [in_grad]
-    mlp_came = []
-    for t, steps in enumerate(mlp_steps):
-        *_, (mlp_mine, _) = [steps.send(more)] + list(steps)
-        mlp_came.append(exchange(tie(mlp_mine[0], *after)))
-        after = [mlp_came[-1], sums[t]]
-    *_, (attn_mine, _) = list(attn_steps)
-    attn_came = exchange(tie(attn_mine[0], *after))
+    adds = [(v, 3 * TILE * b[0]) for b, into in zip(batches, batch_adds) for v in into[0]]
+    adds.append((last_came, 0))
+    mlp_came = exchange(tie(block_grad(0, all_kinds, adds, parts), in_grad))
+    attn_mine = block_grad(0, attn_kinds, [(v, 0) for v in attn_adds[0]], sums[1:])
+    attn_came = exchange(tie(attn_mine, mlp_came))
     gate_up_grad, down_grad = finish(
-        finish_mlp_kernel, mlp_came, (gate_up_weight.shape, down_weight.shape)
+        finish_mlp_kernel, [mlp_came], (gate_up_weight.shape, down_weight.shape)
     )
     qkv_grad, out_w_grad = finish(
         finish_attn_kernel, [attn_came], (qkv_weight.shape, out_weight.shape)

time: 644 us -> 621 us (0.964)
  blocking collectives: 20.1 us -> 0 us
  other arithmetic: 40.6 us -> 52.1 us
  local copies, waits for them, and re-layouts: 39.6 us -> 28.9 us
  Pallas kernels: 158 us -> 151 us
    all_to_all x1 -> x0, blocking collectives: 20.1 us -> none  [exchange(): lax.all_to_all(rows_by_rank, 'dp', 0, 0, axis_index_groups=bands, tiled=T...]
    select_n x7 -> x16, other arithmetic: 1.47 us -> 10 us  [swapped(): low, high = (jnp.where(bit == 1, high, low), jnp.where(bit == 1, low, high))]
    pallas_call x25 -> x21, Pallas kernels: 158 us -> 151 us  [call(): pl.pallas_call(kernel, grid=grid, in_specs=in_specs or [whole(v.shape) fo...]
    ppermute x28 -> x31, waiting for transfers between devices: 164 us -> 171 us  [swap(): return lax.ppermute(array, 'dp', [(d, d ^ mask) for d in range(dp_size)])]
    all_to_all x13 -> x12, waiting for transfers between devices: 112 us -> 106 us  [exchange(): lax.all_to_all(rows_by_rank, 'dp', 0, 0, axis_index_groups=bands, tiled=T...]
    all_to_all x13 -> x12, starting transfers between devices: 54.7 us -> 51.3 us  [exchange(): lax.all_to_all(rows_by_rank, 'dp', 0, 0, axis_index_groups=bands, tiled=T...]
    ppermute x28 -> x31, starting transfers between devices: 37.7 us -> 38.7 us  [swap(): return lax.ppermute(array, 'dp', [(d, d ^ mask) for d in range(dp_size)])]
    convert_element_type x8 -> x6, other arithmetic: 18.8 us -> 18.3 us  [the longest x4 17.1 us: merge(): return (by_block(mine) + by_block(other).astype(F32)).astype(BF)]
  transfers between devices with their start and end apart: 50 -> 52, of which waited for: 20 -> 23; matrix products, arithmetic and copies ran while one was open for 11% -> 12% of each run, Pallas kernels for 24% -> 22%
where the time goes in v3:
time: 621 us; the launch traced here: 610 us
  waiting for transfers between devices  286 us (46%)
  Pallas kernels  151 us (24%)
  starting transfers between devices  90.3 us (15%)
  other arithmetic  52.1 us (8%)
  local copies, waits for them, and re-layouts  28.9 us (5%)
    ppermute x31, waiting for transfers between devices, swap(): return lax.ppermute(array, 'dp', [(d, d ^ mask) for d in range(dp_size)])  171 us
    pallas_call x21, Pallas kernels, call(): pl.pallas_call(kernel, grid=grid, in_specs=in_specs or [whole(v.shape) fo...  151 us
    all_to_all x12, waiting for transfers between devices, exchange(): lax.all_to_all(rows_by_rank, 'dp', 0, 0, axis_index_groups=bands, tiled=T...  106 us
    all_to_all x12, starting transfers between devices, exchange(): lax.all_to_all(rows_by_rank, 'dp', 0, 0, axis_index_groups=bands, tiled=T...  51.3 us
    ppermute x31, starting transfers between devices, swap(): return lax.ppermute(array, 'dp', [(d, d ^ mask) for d in range(dp_size)])  38.7 us
    convert_element_type x4, other arithmetic, merge(): return (by_block(mine) + by_block(other).astype(F32)).astype(BF)  17.1 us
  transfers between devices with their start and end apart: 52, of which 23 were waited for; matrix products, arithmetic and copies ran while one was open for 12% of the time, Pallas kernels for 22%

profile of v3, /device:TPU:0, one launch (start us, length us, event | category | flops | bytes accessed | tf_op | source)
XLA Modules:
  0.0 610.2 jit_solution(8489775333629814790)
XLA Ops:
  0.7 2.4 shard_map.203
  3.0 3.0 collective-permute-start.2
  7.6 4.3 all-to-all-start
  25.3 3.5 shard_map.204
  28.8 3.9 all-to-all-start.1
  33.9 2.2 copy.42
  36.1 2.3 reshape.454
  40.3 3.0 collective-permute-start.3
  46.0 3.2 fusion.2
  52.3 35.5 %collective-permute-done.3.refs_1_ = bf16[512,1024]{1,0:T(8,128)(2,1)S(1)} collective-permute-done((bf16[512,1024]{1,0:T(8,128)(2,1)}, bf16[512,1024]{1,0:T(8,128)(2,1)S(1)}, u32[]{:S(2)}, u32[]{:S(2)}) %collective-permute-start.3) | collective-permute-done | bytes 1048608 | tf_op jit(solution)/shard_map/ppermute | solution.py:373
  88.8 4.5 all-to-all-start.2
  99.0 17.6 %collective-permute-done.5.refs_3_ = bf16[512,1024]{1,0:T(8,128)(2,1)} collective-permute-done((bf16[512,1024]{1,0:T(8,128)(2,1)}, bf16[512,1024]{1,0:T(8,128)(2,1)}, u32[]{:S(2)}, u32[]{:S(2)}) %collective-permute-start.5) | collective-permute-done | bytes 1048608 | tf_op jit(solution)/shard_map/ppermute | solution.py:373
  116.6 14.5 %collective-permute-done.6.refs_5_.refs_7_ = bf16[512,768]{1,0:T(8,128)(2,1)} collective-permute-done((bf16[512,768]{1,0:T(8,128)(2,1)S(1)}, bf16[512,768]{1,0:T(8,128)(2,1)}, u32[]{:S(2)}, u32[]{:S(2)}) %collective-permute-start.6) | collective-permute-done | bytes 786464 | tf_op jit(solution)/shard_map/ppermute | solution.py:373
  131.2 2.3 all-to-all-done.2.own_ref
  135.5 4.6 all-to-all-start.3
  140.1 17.1 %shard_map.205 = (bf16[4,256,768]{2,1,0:T(8,128)(2,1)}, bf16[4,128,256]{2,1,0:T(8,128)(2,1)}, bf16[4,128,256]{2,1,0:T(8,128)(2,1)}, f32[4,128,2048]{2,1,0:T(8,128)}, bf16[4,128,2048]{2,1,0:T(8,128)(2,1)}) custom-call(bf16[4,128,2048]{2,1,0:T(8,128)(2,1)} %all-to-all-done.2.own_ref, bf16[4,128,2048]{2,1,0:T(8,128)(2,1)} %collective-permute-done.7.sib_ref, ...), custom_call_target="tpu_custom_call" | custom-call | flops 128849018880 | bytes 582051840 | tf_op jit(solution)/shard_map/pallas_call | solution.py:75
  157.3 4.4 collective-permute-done.9
  161.6 4.3 fusion.1
  167.5 3.9 all-to-all-start.4
  173.5 40.2 %all-to-all-done.4 = bf16[4,128,2048]{2,1,0:T(8,128)(2,1)S(1)} async-done(((bf16[4,128,2048]{2,1,0:T(8,128)(2,1)}), bf16[4,128,2048]{2,1,0:T(8,128)(2,1)S(1)}, u32[]{:S(2)}, u32[]{:S(2)}) %all-to-all-start.4) | async-done | bytes 2097184 | tf_op jit(solution)/shard_map/all_to_all | solution.py:413
  217.2 5.1 all-to-all-start.5
  224.9 18.7 %collective-permute-done.13.refs_11_.refs_13_ = bf16[512,768]{1,0:T(8,128)(2,1)S(1)} collective-permute-done((bf16[512,768]{1,0:T(8,128)(2,1)}, bf16[512,768]{1,0:T(8,128)(2,1)S(1)}, u32[]{:S(2)}, u32[]{:S(2)}) %collective-permute-start.13) | collective-permute-done | bytes 786464 | tf_op jit(solution)/shard_map/ppermute | solution.py:373
  243.6 18.2 %collective-permute-done.14.refs_7_.refs_15_ = bf16[512,768]{1,0:T(8,128)(2,1)S(1)} collective-permute-done((bf16[512,768]{1,0:T(8,128)(2,1)S(1)}, bf16[512,768]{1,0:T(8,128)(2,1)S(1)}, u32[]{:S(2)}, u32[]{:S(2)}) %collective-permute-start.14) | collective-permute-done | bytes 786464 | tf_op jit(solution)/shard_map/ppermute | solution.py:373
  264.5 4.0 collective-permute-done.16
  268.5 17.1 %shard_map.206 = (bf16[512,512]{1,0:T(8,128)(2,1)}, bf16[512,512]{1,0:T(8,128)(2,1)}, bf16[512,256]{1,0:T(8,128)(2,1)}, bf16[512,256]{1,0:T(8,128)(2,1)}, bf16[5...) custom-call(bf16[512,2048]{1,0:T(8,128)(2,1)} %bitcast.22.refs_0_.re, ...), custom_call_target="tpu_custom_call" | custom-call | flops 322122547200 | bytes 880803840 | tf_op jit(solution)/shard_map/pallas_call | solution.py:75
  285.6 14.0 %shard_map.207 = (bf16[512,512]{1,0:T(8,128)(2,1)}, bf16[512,512]{1,0:T(8,128)(2,1)}, bf16[512,256]{1,0:T(8,128)(2,1)}, bf16[512,256]{1,0:T(8,128)(2,1)}, f32[51...) custom-call(bf16[512,2048]{1,0:T(8,128)(2,1)} %bitcast.22.refs_0_.refs_8_.refs_16_, ...), custom_call_target="tpu_custom_call" | custom-call | flops 161061273600 | bytes 880803840 | tf_op jit(solution)/shard_map/pallas_call | solution.py:75
  299.8 3.9 shard_map.208
  304.3 4.2 add_convert_fusion.1
  308.5 3.9 shard_map.209
  313.9 3.9 shard_map.210
  318.4 3.8 all-to-all-start.6
  322.2 8.5 %shard_map.211 = bf16[512,2304]{1,0:T(8,128)(2,1)} custom-call(bf16[512,2048]{1,0:T(8,128)(2,1)} %bitcast.22.refs_0_.refs_8_.refs_16_, bf16[512,2048]{1,0:T(8,128)(2,1)} %bitcast.23.refs_1_.refs_9_.refs_17_, bf16[512,512]{1,0:T(8,128)(2,1)} %get-tuple-element.104.refs_2_, bf16[512,512]{1,0:T(8,128)(2,1)} %get-tuple-element.105.refs_3_, ...), custom_call_target="tpu_custom_call" | custom-call | flops 72477573120 | bytes 967311360 | tf_op jit(solution)/shard_map/pallas_call | solution.py:75
  332.3 14.7 %all-to-all-done.6 = bf16[4,128,2048]{2,1,0:T(8,128)(2,1)S(1)} async-done(((bf16[4,128,2048]{2,1,0:T(8,128)(2,1)}), bf16[4,128,2048]{2,1,0:T(8,128)(2,1)S(1)}, u32[]{:S(2)}, u32[]{:S(2)}) %all-to-all-start.6) | async-done | bytes 2097184 | tf_op jit(solution)/shard_map/all_to_all | solution.py:413
  351.6 4.2 shard_map.213
  357.9 7.1 %shard_map.212 = (f32[512,2048]{1,0:T(8,128)}, bf16[512,2048]{1,0:T(8,128)(2,1)}) custom-call(bf16[512,256]{1,0:T(8,128)(2,1)} %get-tuple-element.119.refs_6_.refs_0_, bf16[512,256]{1,0:T(8,128)(2,1)} %get-tuple-element.106.refs_7_.refs_1_, bf16[512,256]{1,0:T(8,128)(2,1)} %get-tuple-element.110.refs_6_.refs_14_.refs_2_, ...), custom_call_target="tpu_custom_call" | custom-call | tf_op jit(solution)/shard_map/pallas_call | solution.py:75
  365.0 3.6 all-to-all-start.7
  368.7 4.2 shard_map.214
  372.9 4.2 shard_map.215
  377.0 4.9 add_convert_fusion
  381.9 26.2 %collective-permute-done.25.refs_27_ = bf16[512,2304]{1,0:T(8,128)(2,1)} collective-permute-done((bf16[512,2304]{1,0:T(8,128)(2,1)}, bf16[512,2304]{1,0:T(8,128)(2,1)}, u32[]{:S(2)}, u32[]{:S(2)}) %collective-permute-start.25) | collective-permute-done | bytes 2359328 | tf_op jit(solution)/shard_map/ppermute | solution.py:373
  410.8 4.7 all-to-all-start.8
  415.5 21.5 %shard_map.216 = (bf16[4,128,768]{2,1,0:T(8,128)(2,1)}, bf16[4,128,768]{2,1,0:T(8,128)(2,1)}, f32[4,1,768]{2,1,0:T(1,128)}, f32[4,128,2048]{2,1,0:T(8,128)}, bf16[4,128,2048]{2,1,0:T(8,128)(2,1)}) custom-call(bf16[4,128,2048]{2,1,0:T(8,128)(2,1)} %copy-done.14, bf16[4,128,2048]{2,1,0:T(8,128)(2,1)} %collective-permute-done.26.sib_ref, ...), custom_call_target="tpu_custom_call" | custom-call | flops 128849018880 | bytes 613785600 | tf_op jit(solution)/shard_map/pallas_call | solution.py:75
  436.9 10.3 %collective-permute-done.27.refs_25_ = bf16[512,768]{1,0:T(8,128)(2,1)} collective-permute-done((bf16[512,768]{1,0:T(8,128)(2,1)}, bf16[512,768]{1,0:T(8,128)(2,1)}, u32[]{:S(2)}, u32[]{:S(2)}) %collective-permute-start.27) | collective-permute-done | bytes 786464 | tf_op jit(solution)/shard_map/ppermute | solution.py:373
  447.3 4.4 shard_map.217
  453.3 5.8 all-to-all-done.8
  459.2 2.1 convert_reduce_fusion.1
  464.6 3.7 fusion
  468.3 4.7 all-to-all-start.9
  475.2 4.4 shard_map.218
  481.1 26.5 %all-to-all-done.9 = bf16[4,128,2048]{2,1,0:T(8,128)(2,1)} async-done(((bf16[4,128,2048]{2,1,0:T(8,128)(2,1)}), bf16[4,128,2048]{2,1,0:T(8,128)(2,1)}, u32[]{:S(2)}, u32[]{:S(2)}) %all-to-all-start.9) | async-done | bytes 2097184 | tf_op jit(solution)/shard_map/all_to_all | solution.py:413
  510.2 4.8 shard_map.219
  515.5 10.1 %shard_map.221 = bf16[512,2304]{1,0:T(8,128)(2,1)} custom-call(bf16[512,2048]{1,0:T(8,128)(2,1)} %bitcast.22.refs_0_.refs_8_.refs_16_, bf16[512,2048]{1,0:T(8,128)(2,1)} %bitcast.23.refs_1_.refs_9_.refs_17_, bf16[512,512]{1,0:T(8,128)(2,1)} %get-tuple-element.104.refs_2_, bf16[512,512]{1,0:T(8,128)(2,1)} %get-tuple-element.105.refs_3_, ...), custom_call_target="tpu_custom_call" | custom-call | flops 72477573120 | bytes 1108869120 | tf_op jit(solution)/shard_map/pallas_call | solution.py:75
  525.6 3.7 collective-permute-start.33
  530.0 4.5 all-to-all-start.10
  534.5 5.9 collective-permute-done.33
  541.8 3.7 collective-permute-start.36
  546.2 22.1 %collective-permute-done.36 = f32[7,2048]{1,0:T(8,128)S(1)} collective-permute-done((f32[7,2048]{1,0:T(8,128)S(1)}, f32[7,2048]{1,0:T(8,128)S(1)}, u32[]{:S(2)}, u32[]{:S(2)}) %collective-permute-start.36) | collective-permute-done | bytes 57376 | tf_op jit(solution)/shard_map/ppermute | solution.py:373
  569.0 5.1 shard_map.220
  574.2 13.6 %all-to-all-done.10 = bf16[4,128,2304]{2,1,0:T(8,128)(2,1)} async-done(((bf16[4,128,2304]{2,1,0:T(8,128)(2,1)}), bf16[4,128,2304]{2,1,0:T(8,128)(2,1)}, u32[]{:S(2)}, u32[]{:S(2)}) %all-to-all-start.10) | async-done | bytes 2359328 | tf_op jit(solution)/shard_map/all_to_all | solution.py:413
  587.7 3.8 all-to-all-start.11
  591.6 2.7 multiply_add_fusion
  594.3 2.1 reshape.467
  602.0 4.1 shard_map.223
  607.0 2.7 shard_map.222
  (266 shorter events, 80.3 us)
Async XLA Ops:
  0.6 132.8 %copy-start = (f32[3,1024]{1,0:T(4,128)S(1)}, f32[3,1024]{1,0:T(4,128)}, u32[]{:S(2)}) copy-start(f32[3,1024]{1,0:T(4,128)} %param.17) | copy-start | bytes 36868
  3.0 35.3 %collective-permute-start.2 = (s32[256]{0:T(256)S(1)}, s32[256]{0:T(256)S(1)}, u32[]{:S(2)}, u32[]{:S(2)}) collective-permute-start(s32[256]{0:T(256)S(1)} %copy-done.41), channel_id=1, source_target_pairs={{0,4},{2,6},{4,0},{6,2},{8,12},{10,14},{12,8},{14,10},{16,20},{18,... | collective-permute-start | bytes 3080 | tf_op jit(solution)/shard_map/ppermute | solution.py:373
  6.0 32.4 %collective-permute-start.1 = (s32[256]{0:T(256)S(1)}, s32[256]{0:T(256)S(1)}, u32[]{:S(2)}, u32[]{:S(2)}) collective-permute-start(s32[256]{0:T(256)S(1)} %copy-done.41), channel_id=1, source_target_pairs={{0,12},{2,14},{4,8},{6,10},{8,4},{10,6},{12,0},{14,2},{16,28},{18,... | collective-permute-start | bytes 3080 | tf_op jit(solution)/shard_map/ppermute | solution.py:373
  7.5 30.9 %collective-permute-start = (s32[256]{0:T(256)S(1)}, s32[256]{0:T(256)S(1)}, u32[]{:S(2)}, u32[]{:S(2)}) collective-permute-start(s32[256]{0:T(256)S(1)} %copy-done.41), channel_id=1, source_target_pairs={{0,8},{2,10},{4,12},{6,14},{8,0},{10,2},{12,4},{14,6},{16,24},{18,... | collective-permute-start | bytes 3080 | tf_op jit(solution)/shard_map/ppermute | solution.py:373
  7.6 17.7 %all-to-all-start = ((bf16[4,128,1024]{2,1,0:T(8,128)(2,1)}), bf16[4,128,1024]{2,1,0:T(8,128)(2,1)}, u32[]{:S(2)}, u32[]{:S(2)}) async-start(bf16[4,128,1024]{2,1,0:T(8,128)(2,1)} %bitcast.82), calls=%async_computation | async-start | bytes 2097152 | tf_op jit(solution)/shard_map/all_to_all | solution.py:413
  20.2 193.9 %copy-start.6 = (f32[128,2048]{1,0:T(8,128)}, f32[128,2048]{1,0:T(8,128)S(1)}, u32[]{:S(2)}) copy-start(f32[128,2048]{1,0:T(8,128)S(1)} %reshape.479) | copy-start | bytes 3145732
  28.8 60.0 %all-to-all-start.1 = ((bf16[4,128,2304]{2,1,0:T(8,128)(2,1)}), bf16[4,128,2304]{2,1,0:T(8,128)(2,1)S(1)}, u32[]{:S(2)}, u32[]{:S(2)}) async-start(bf16[4,128,2304]{2,1,0:T(8,128)(2,1)} %bitcast.78), calls=%async_computation.1 | async-start | bytes 4718592 | tf_op jit(solution)/shard_map/all_to_all | solution.py:413
  40.3 47.6 %collective-permute-start.3 = (bf16[512,1024]{1,0:T(8,128)(2,1)}, bf16[512,1024]{1,0:T(8,128)(2,1)S(1)}, u32[]{:S(2)}, u32[]{:S(2)}) collective-permute-start(bf16[512,1024]{1,0:T(8,128)(2,1)} %bitcast.15.refs_0_), channel_id=1, source_target_pairs={{0,16},{2,18},{4,20},{6,22},{8,24},{10,26},{12,28},{14,30},{16,0},... | collective-permute-start | bytes 3145736 | tf_op jit(solution)/shard_map/ppermute | solution.py:373
  43.2 45.5 %collective-permute-start.4 = (bf16[512,1024]{1,0:T(8,128)(2,1)}, bf16[512,1024]{1,0:T(8,128)(2,1)}, u32[]{:S(2)}, u32[]{:S(2)}) collective-permute-start(bf16[512,1024]{1,0:T(8,128)(2,1)} %bitcast.15.refs_0_), channel_id=1, source_target_pairs={{0,2},{2,0},{4,6},{6,4},{8,10},{10,8},{12,14},{14,12},{16,18},{18,... | collective-permute-start | bytes 3145736 | tf_op jit(solution)/shard_map/ppermute | solution.py:373
  88.8 44.7 %all-to-all-start.2 = ((bf16[4,128,2048]{2,1,0:T(8,128)(2,1)}), bf16[4,128,2048]{2,1,0:T(8,128)(2,1)}, u32[]{:S(2)}, u32[]{:S(2)}) async-start(bf16[4,128,2048]{2,1,0:T(8,128)(2,1)} %broadcast_in_dim.64), calls=%async_computation.2 | async-start | bytes 4194304 | tf_op jit(solution)/shard_map/all_to_all | solution.py:413
  93.3 23.4 %collective-permute-start.5 = (bf16[512,1024]{1,0:T(8,128)(2,1)}, bf16[512,1024]{1,0:T(8,128)(2,1)}, u32[]{:S(2)}, u32[]{:S(2)}) collective-permute-start(bf16[512,1024]{1,0:T(8,128)(2,1)} %copy-done.42), channel_id=1, source_target_pairs={{0,2},{2,0},{4,6},{6,4},{8,10},{10,8},{12,14},{14,12},{16,18},{18,... | collective-permute-start | bytes 3145736 | tf_op jit(solution)/shard_map/ppermute | solution.py:373
  97.1 34.1 %collective-permute-start.6 = (bf16[512,768]{1,0:T(8,128)(2,1)S(1)}, bf16[512,768]{1,0:T(8,128)(2,1)}, u32[]{:S(2)}, u32[]{:S(2)}) collective-permute-start(bf16[512,768]{1,0:T(8,128)(2,1)S(1)} %get-tuple-element.89), channel_id=1, source_target_pairs={{0,16},{2,18},{4,20},{6,22},{8,24},{10,26},{12,28},{14,30},{16,0},... | collective-permute-start | bytes 2359304 | tf_op jit(solution)/shard_map/ppermute | solution.py:373
  133.5 6.6 %collective-permute-start.7 = (bf16[4,128,2048]{2,1,0:T(8,128)(2,1)}, bf16[4,128,2048]{2,1,0:T(8,128)(2,1)}, u32[]{:S(2)}, u32[]{:S(2)}) collective-permute-start(bf16[4,128,2048]{2,1,0:T(8,128)(2,1)} %all-to-all-done.2.own_ref), channel_id=1, source_target_pairs={{0,1},{1,0},{2,3},{3,2},{4,5},{5,4},{6,7},{7,6},{8,9},{9,8},{10,11... | collective-permute-start | bytes 6291464 | tf_op jit(solution)/shard_map/ppermute | solution.py:376
  134.1 23.1 %collective-permute-start.8 = (bf16[512,768]{1,0:T(8,128)(2,1)}, bf16[512,768]{1,0:T(8,128)(2,1)}, u32[]{:S(2)}, u32[]{:S(2)}) collective-permute-start(bf16[512,768]{1,0:T(8,128)(2,1)} %copy-done.17), channel_id=1, source_target_pairs={{0,2},{2,0},{4,6},{6,4},{8,10},{10,8},{12,14},{14,12},{16,18},{18,... | collective-permute-start | bytes 2359304 | tf_op jit(solution)/shard_map/ppermute | solution.py:373
  135.5 30.7 %all-to-all-start.3 = ((bf16[4,128,2048]{2,1,0:T(8,128)(2,1)}), bf16[4,128,2048]{2,1,0:T(8,128)(2,1)S(1)}, u32[]{:S(2)}, u32[]{:S(2)}) async-start(bf16[4,128,2048]{2,1,0:T(8,128)(2,1)} %broadcast_in_dim.65), calls=%async_computation.3 | async-start | bytes 4194304 | tf_op jit(solution)/shard_map/all_to_all | solution.py:413
  157.2 4.4 collective-permute-start.9
  167.5 46.2 %all-to-all-start.4 = ((bf16[4,128,2048]{2,1,0:T(8,128)(2,1)}), bf16[4,128,2048]{2,1,0:T(8,128)(2,1)S(1)}, u32[]{:S(2)}, u32[]{:S(2)}) async-start(bf16[4,128,2048]{2,1,0:T(8,128)(2,1)} %fusion.1), calls=%async_computation.4 | async-start | bytes 4194304 | tf_op jit(solution)/shard_map/all_to_all | solution.py:413
  171.4 42.7 %collective-permute-start.11 = (bf16[512,768]{1,0:T(8,128)(2,1)}, bf16[512,768]{1,0:T(8,128)(2,1)}, u32[]{:S(2)}, u32[]{:S(2)}) collective-permute-start(bf16[512,768]{1,0:T(8,128)(2,1)} %get-tuple-element.94), channel_id=1, source_target_pairs={{0,16},{2,18},{4,20},{6,22},{8,24},{10,26},{12,28},{14,30},{16,0},... | collective-permute-start | bytes 2359304 | tf_op jit(solution)/shard_map/ppermute | solution.py:373
  171.4 42.7 %collective-permute-start.10 = (bf16[512,768]{1,0:T(8,128)(2,1)}, bf16[512,768]{1,0:T(8,128)(2,1)}, u32[]{:S(2)}, u32[]{:S(2)}) collective-permute-start(bf16[512,768]{1,0:T(8,128)(2,1)} %collective-permute-done.6.refs_5_.refs_7_), channel_id=1, source_target_pairs={{0,2},{2,0},{4,6},{6,4},{8,10},{10,8},{12,14},{14,12},{16,18},{18,... | collective-permute-start | bytes 2359304 | tf_op jit(solution)/shard_map/ppermute | solution.py:373
  172.3 41.9 %collective-permute-start.12 = (bf16[512,768]{1,0:T(8,128)(2,1)}, bf16[512,768]{1,0:T(8,128)(2,1)}, u32[]{:S(2)}, u32[]{:S(2)}) collective-permute-start(bf16[512,768]{1,0:T(8,128)(2,1)} %get-tuple-element.94), channel_id=1, source_target_pairs={{0,2},{2,0},{4,6},{6,4},{8,10},{10,8},{12,14},{14,12},{16,18},{18,... | collective-permute-start | bytes 2359304 | tf_op jit(solution)/shard_map/ppermute | solution.py:373
  173.5 41.2 %copy-start.24 = (f32[1,2,2,2,2,128]{5,4,3,2,1,0:T(2,128)}, f32[1,2,2,2,2,128]{5,4,3,2,1,0:T(2,128)S(1)}, u32[]{:S(2)}) copy-start(f32[1,2,2,2,2,128]{5,4,3,2,1,0:T(2,128)S(1)} %copy.45) | copy-start | bytes 24580
  217.2 46.8 %all-to-all-start.5 = ((bf16[4,128,2048]{2,1,0:T(8,128)(2,1)}), bf16[4,128,2048]{2,1,0:T(8,128)(2,1)}, u32[]{:S(2)}, u32[]{:S(2)}) async-start(bf16[4,128,2048]{2,1,0:T(8,128)(2,1)} %broadcast_in_dim.74), calls=%async_computation.5 | async-start | bytes 4194304 | tf_op jit(solution)/shard_map/all_to_all | solution.py:413
  222.3 39.5 %collective-permute-start.14 = (bf16[512,768]{1,0:T(8,128)(2,1)S(1)}, bf16[512,768]{1,0:T(8,128)(2,1)S(1)}, u32[]{:S(2)}, u32[]{:S(2)}) collective-permute-start(bf16[512,768]{1,0:T(8,128)(2,1)S(1)} %copy-done.16), channel_id=1, source_target_pairs={{0,16},{2,18},{4,20},{6,22},{8,24},{10,26},{12,28},{14,30},{16,0},... | collective-permute-start | bytes 2359304 | tf_op jit(solution)/shard_map/ppermute | solution.py:373
  222.9 20.7 %collective-permute-start.13 = (bf16[512,768]{1,0:T(8,128)(2,1)}, bf16[512,768]{1,0:T(8,128)(2,1)S(1)}, u32[]{:S(2)}, u32[]{:S(2)}) collective-permute-start(bf16[512,768]{1,0:T(8,128)(2,1)} %collective-permute-done.11.refs_9_.refs_11_), channel_id=1, source_target_pairs={{0,2},{2,0},{4,6},{6,4},{8,10},{10,8},{12,14},{14,12},{16,18},{18,... | collective-permute-start | bytes 2359304 | tf_op jit(solution)/shard_map/ppermute | solution.py:373
  223.4 39.2 %collective-permute-start.15 = (bf16[512,768]{1,0:T(8,128)(2,1)S(1)}, bf16[512,768]{1,0:T(8,128)(2,1)}, u32[]{:S(2)}, u32[]{:S(2)}) collective-permute-start(bf16[512,768]{1,0:T(8,128)(2,1)S(1)} %copy-done.16), channel_id=1, source_target_pairs={{0,2},{2,0},{4,6},{6,4},{8,10},{10,8},{12,14},{14,12},{16,18},{18,... | collective-permute-start | bytes 2359304 | tf_op jit(solution)/shard_map/ppermute | solution.py:373
  224.9 39.6 %collective-permute-start.17 = (bf16[4,128,2048]{2,1,0:T(8,128)(2,1)S(1)}, bf16[4,128,2048]{2,1,0:T(8,128)(2,1)}, u32[]{:S(2)}, u32[]{:S(2)}) collective-permute-start(bf16[4,128,2048]{2,1,0:T(8,128)(2,1)S(1)} %copy-done.13), channel_id=1, source_target_pairs={{0,1},{1,0},{2,3},{3,2},{4,5},{5,4},{6,7},{7,6},{8,9},{9,8},{10,11... | collective-permute-start | bytes 6291464 | tf_op jit(solution)/shard_map/ppermute | solution.py:376
  243.6 18.2 %copy-start.19 = (bf16[512,768]{1,0:T(8,128)(2,1)}, bf16[512,768]{1,0:T(8,128)(2,1)S(1)}, u32[]{:S(2)}) copy-start(bf16[512,768]{1,0:T(8,128)(2,1)S(1)} %collective-permute-done.13.refs_11_.refs_13_) | copy-start | bytes 2359300
  264.0 4.5 collective-permute-start.16
  264.0 21.6 %collective-permute-start.18 = (bf16[512,768]{1,0:T(8,128)(2,1)}, bf16[512,768]{1,0:T(8,128)(2,1)}, u32[]{:S(2)}, u32[]{:S(2)}) collective-permute-start(bf16[512,768]{1,0:T(8,128)(2,1)} %copy-done.18), channel_id=1, source_target_pairs={{0,2},{2,0},{4,6},{6,4},{8,10},{10,8},{12,14},{14,12},{16,18},{18,... | collective-permute-start | bytes 2359304 | tf_op jit(solution)/shard_map/ppermute | solution.py:373
  299.6 4.7 collective-permute-start.19
  303.8 43.6 %collective-permute-start.20 = (bf16[512,768]{1,0:T(8,128)(2,1)}, bf16[512,768]{1,0:T(8,128)(2,1)}, u32[]{:S(2)}, u32[]{:S(2)}) collective-permute-start(bf16[512,768]{1,0:T(8,128)(2,1)} %shard_map.208), channel_id=1, source_target_pairs={{0,2},{2,0},{4,6},{6,4},{8,10},{10,8},{12,14},{14,12},{16,18},{18,... | collective-permute-start | bytes 2359304 | tf_op jit(solution)/shard_map/ppermute | solution.py:373
  312.4 56.2 %collective-permute-start.22 = (bf16[512,768]{1,0:T(8,128)(2,1)}, bf16[512,768]{1,0:T(8,128)(2,1)}, u32[]{:S(2)}, u32[]{:S(2)}) collective-permute-start(bf16[512,768]{1,0:T(8,128)(2,1)} %shard_map.209), channel_id=1, source_target_pairs={{0,2},{2,0},{4,6},{6,4},{8,10},{10,8},{12,14},{14,12},{16,18},{18,... | collective-permute-start | bytes 2359304 | tf_op jit(solution)/shard_map/ppermute | solution.py:373
  317.9 55.0 %collective-permute-start.23 = (bf16[512,768]{1,0:T(8,128)(2,1)}, bf16[512,768]{1,0:T(8,128)(2,1)}, u32[]{:S(2)}, u32[]{:S(2)}) collective-permute-start(bf16[512,768]{1,0:T(8,128)(2,1)} %shard_map.210), channel_id=1, source_target_pairs={{0,2},{2,0},{4,6},{6,4},{8,10},{10,8},{12,14},{14,12},{16,18},{18,... | collective-permute-start | bytes 2359304 | tf_op jit(solution)/shard_map/ppermute | solution.py:373
  318.4 28.6 %all-to-all-start.6 = ((bf16[4,128,2048]{2,1,0:T(8,128)(2,1)}), bf16[4,128,2048]{2,1,0:T(8,128)(2,1)S(1)}, u32[]{:S(2)}, u32[]{:S(2)}) async-start(bf16[4,128,2048]{2,1,0:T(8,128)(2,1)} %bitcast.79), calls=%async_computation.6 | async-start | bytes 4194304 | tf_op jit(solution)/shard_map/all_to_all | solution.py:413
  330.7 16.7 %copy-start.25 = (f32[1,2,2,2,2,128]{5,4,3,2,1,0:T(2,128)S(1)}, f32[1,2,2,2,2,128]{5,4,3,2,1,0:T(2,128)}, u32[]{:S(2)}) copy-start(f32[1,2,2,2,2,128]{5,4,3,2,1,0:T(2,128)} %copy-done.24) | copy-start | bytes 24580
  330.7 16.7 %copy-start.34 = (f32[128]{0:T(128)S(1)}, f32[128]{0:T(128)}, u32[]{:S(2)}) copy-start(f32[128]{0:T(128)} %copy-done.33) | copy-start | bytes 1540
  330.7 16.7 %copy-start.40 = (f32[128]{0:T(128)S(1)}, f32[128]{0:T(128)}, u32[]{:S(2)}) copy-start(f32[128]{0:T(128)} %copy-done.39) | copy-start | bytes 1540
  330.7 77.5 %collective-permute-start.25 = (bf16[512,2304]{1,0:T(8,128)(2,1)}, bf16[512,2304]{1,0:T(8,128)(2,1)}, u32[]{:S(2)}, u32[]{:S(2)}) collective-permute-start(bf16[512,2304]{1,0:T(8,128)(2,1)} %shard_map.211), channel_id=1, source_target_pairs={{0,2},{2,0},{4,6},{6,4},{8,10},{10,8},{12,14},{14,12},{16,18},{18,... | collective-permute-start | bytes 7077896 | tf_op jit(solution)/shard_map/ppermute | solution.py:373
  355.8 52.3 %collective-permute-start.24 = (bf16[512,768]{1,0:T(8,128)(2,1)}, bf16[512,768]{1,0:T(8,128)(2,1)S(1)}, u32[]{:S(2)}, u32[]{:S(2)}) collective-permute-start(bf16[512,768]{1,0:T(8,128)(2,1)} %shard_map.213), channel_id=1, source_target_pairs={{0,16},{2,18},{4,20},{6,22},{8,24},{10,26},{12,28},{14,30},{16,0},... | collective-permute-start | bytes 2359304 | tf_op jit(solution)/shard_map/ppermute | solution.py:373
  365.0 12.0 %collective-permute-start.21 = (bf16[512,2048]{1,0:T(8,128)(2,1)}, bf16[512,2048]{1,0:T(8,128)(2,1)}, u32[]{:S(2)}, u32[]{:S(2)}) collective-permute-start(bf16[512,2048]{1,0:T(8,128)(2,1)} %get-tuple-element.121), channel_id=1, source_target_pairs={{0,1},{1,0},{2,3},{3,2},{4,5},{5,4},{6,7},{7,6},{8,9},{9,8},{10,11... | collective-permute-start | bytes 6291464 | tf_op jit(solution)/shard_map/ppermute | solution.py:376
  365.0 44.3 %all-to-all-start.7 = ((bf16[4,128,2048]{2,1,0:T(8,128)(2,1)}), bf16[4,128,2048]{2,1,0:T(8,128)(2,1)S(1)}, u32[]{:S(2)}, u32[]{:S(2)}) async-start(bf16[4,128,2048]{2,1,0:T(8,128)(2,1)} %broadcast_in_dim.75), calls=%async_computation.7 | async-start | bytes 4194304 | tf_op jit(solution)/shard_map/all_to_all | solution.py:413
  409.3 6.1 collective-permute-start.26
  409.3 37.9 %collective-permute-start.27 = (bf16[512,768]{1,0:T(8,128)(2,1)}, bf16[512,768]{1,0:T(8,128)(2,1)}, u32[]{:S(2)}, u32[]{:S(2)}) collective-permute-start(bf16[512,768]{1,0:T(8,128)(2,1)} %shard_map.214), channel_id=1, source_target_pairs={{0,16},{2,18},{4,20},{6,22},{8,24},{10,26},{12,28},{14,30},{16,0},... | collective-permute-start | bytes 2359304 | tf_op jit(solution)/shard_map/ppermute | solution.py:373
  410.8 48.4 %all-to-all-start.8 = ((bf16[4,128,2048]{2,1,0:T(8,128)(2,1)}), bf16[4,128,2048]{2,1,0:T(8,128)(2,1)}, u32[]{:S(2)}, u32[]{:S(2)}) async-start(bf16[4,128,2048]{2,1,0:T(8,128)(2,1)} %bitcast.27), calls=%async_computation.8 | async-start | bytes 4194304 | tf_op jit(solution)/shard_map/all_to_all | solution.py:413
  415.4 31.8 %copy-start.44 = (bf16[512,768]{1,0:T(8,128)(2,1)S(1)}, bf16[512,768]{1,0:T(8,128)(2,1)}, u32[]{:S(2)}) copy-start(bf16[512,768]{1,0:T(8,128)(2,1)} %shard_map.215) | copy-start | bytes 2359300
  447.3 17.3 %collective-permute-start.28 = (bf16[512,2048]{1,0:T(8,128)(2,1)}, bf16[512,2048]{1,0:T(8,128)(2,1)}, u32[]{:S(2)}, u32[]{:S(2)}) collective-permute-start(bf16[512,2048]{1,0:T(8,128)(2,1)} %bitcast.133), channel_id=1, source_target_pairs={{0,1},{1,0},{2,3},{3,2},{4,5},{5,4},{6,7},{7,6},{8,9},{9,8},{10,11... | collective-permute-start | bytes 6291464 | tf_op jit(solution)/shard_map/ppermute | solution.py:376
  447.3 62.4 %collective-permute-start.29 = (bf16[512,768]{1,0:T(8,128)(2,1)S(1)}, bf16[512,768]{1,0:T(8,128)(2,1)}, u32[]{:S(2)}, u32[]{:S(2)}) collective-permute-start(bf16[512,768]{1,0:T(8,128)(2,1)S(1)} %copy-done.44), channel_id=1, source_target_pairs={{0,16},{2,18},{4,20},{6,22},{8,24},{10,26},{12,28},{14,30},{16,0},... | collective-permute-start | bytes 2359304 | tf_op jit(solution)/shard_map/ppermute | solution.py:373
  451.7 58.5 %collective-permute-start.38 = (bf16[512,1024]{1,0:T(8,128)(2,1)}, bf16[512,1024]{1,0:T(8,128)(2,1)}, u32[]{:S(2)}, u32[]{:S(2)}) collective-permute-start(bf16[512,1024]{1,0:T(8,128)(2,1)} %shard_map.217), channel_id=1, source_target_pairs={{0,2},{2,0},{4,6},{6,4},{8,10},{10,8},{12,14},{14,12},{16,18},{18,... | collective-permute-start | bytes 3145736 | tf_op jit(solution)/shard_map/ppermute | solution.py:373
  468.3 39.3 %all-to-all-start.9 = ((bf16[4,128,2048]{2,1,0:T(8,128)(2,1)}), bf16[4,128,2048]{2,1,0:T(8,128)(2,1)}, u32[]{:S(2)}, u32[]{:S(2)}) async-start(bf16[4,128,2048]{2,1,0:T(8,128)(2,1)} %fusion), calls=%async_computation.9 | async-start | bytes 4194304 | tf_op jit(solution)/shard_map/all_to_all | solution.py:413
  479.6 30.1 %copy-start.7 = (f32[128,2048]{1,0:T(8,128)S(1)}, f32[128,2048]{1,0:T(8,128)}, u32[]{:S(2)}) copy-start(f32[128,2048]{1,0:T(8,128)} %copy-done.6) | copy-start | bytes 3145732
  479.6 30.2 %copy-start.23 = (f32[1,2,2,2,2,128]{5,4,3,2,1,0:T(2,128)S(1)}, f32[1,2,2,2,2,128]{5,4,3,2,1,0:T(2,128)}, u32[]{:S(2)}) copy-start(f32[1,2,2,2,2,128]{5,4,3,2,1,0:T(2,128)} %copy-done.22) | copy-start | bytes 24580
  479.6 30.2 %copy-start.36 = (f32[128]{0:T(128)S(1)}, f32[128]{0:T(128)}, u32[]{:S(2)}) copy-start(f32[128]{0:T(128)} %copy-done.35) | copy-start | bytes 1540
  479.6 30.2 %copy-start.38 = (f32[128]{0:T(128)S(1)}, f32[128]{0:T(128)}, u32[]{:S(2)}) copy-start(f32[128]{0:T(128)} %copy-done.37) | copy-start | bytes 1540
  479.6 89.5 %collective-permute-start.37 = (bf16[512,1024]{1,0:T(8,128)(2,1)}, bf16[512,1024]{1,0:T(8,128)(2,1)}, u32[]{:S(2)}, u32[]{:S(2)}) collective-permute-start(bf16[512,1024]{1,0:T(8,128)(2,1)} %shard_map.218), channel_id=1, source_target_pairs={{0,2},{2,0},{4,6},{6,4},{8,10},{10,8},{12,14},{14,12},{16,18},{18,... | collective-permute-start | bytes 3145736 | tf_op jit(solution)/shard_map/ppermute | solution.py:373
  515.0 54.1 %collective-permute-start.39 = (bf16[512,1024]{1,0:T(8,128)(2,1)}, bf16[512,1024]{1,0:T(8,128)(2,1)}, u32[]{:S(2)}, u32[]{:S(2)}) collective-permute-start(bf16[512,1024]{1,0:T(8,128)(2,1)} %shard_map.219), channel_id=1, source_target_pairs={{0,16},{2,18},{4,20},{6,22},{8,24},{10,26},{12,28},{14,30},{16,0},... | collective-permute-start | bytes 3145736 | tf_op jit(solution)/shard_map/ppermute | solution.py:373
  515.4 10.2 %collective-permute-start.30 = (f32[7,2048]{1,0:T(8,128)S(1)}, f32[7,2048]{1,0:T(8,128)S(1)}, u32[]{:S(2)}, u32[]{:S(2)}) collective-permute-start(f32[7,2048]{1,0:T(8,128)S(1)} %pad_maximum_fusion.5), channel_id=1, source_target_pairs={{0,1},{1,0},{2,3},{3,2},{4,5},{5,4},{6,7},{7,6},{8,9},{9,8},{10,11... | collective-permute-start | bytes 172040 | tf_op jit(solution)/shard_map/ppermute | solution.py:376
  525.6 14.7 %collective-permute-start.33 = (f32[7,2048]{1,0:T(8,128)S(1)}, f32[7,2048]{1,0:T(8,128)S(1)}, u32[]{:S(2)}, u32[]{:S(2)}) collective-permute-start(f32[7,2048]{1,0:T(8,128)S(1)} %fusion.20), channel_id=1, source_target_pairs={{0,12},{2,14},{4,8},{6,10},{8,4},{10,6},{12,0},{14,2},{16,28},{18,... | collective-permute-start | bytes 172040 | tf_op jit(solution)/shard_map/ppermute | solution.py:373
  529.3 12.4 %collective-permute-start.32 = (f32[7,2048]{1,0:T(8,128)S(1)}, f32[7,2048]{1,0:T(8,128)S(1)}, u32[]{:S(2)}, u32[]{:S(2)}) collective-permute-start(f32[7,2048]{1,0:T(8,128)S(1)} %fusion.20), channel_id=1, source_target_pairs={{0,8},{2,10},{4,12},{6,14},{8,0},{10,2},{12,4},{14,6},{16,24},{18,... | collective-permute-start | bytes 172040 | tf_op jit(solution)/shard_map/ppermute | solution.py:373
  529.3 12.4 %collective-permute-start.31 = (f32[7,2048]{1,0:T(8,128)S(1)}, f32[7,2048]{1,0:T(8,128)S(1)}, u32[]{:S(2)}, u32[]{:S(2)}) collective-permute-start(f32[7,2048]{1,0:T(8,128)S(1)} %fusion.20), channel_id=1, source_target_pairs={{0,4},{2,6},{4,0},{6,2},{8,12},{10,14},{12,8},{14,10},{16,20},{18,... | collective-permute-start | bytes 172040 | tf_op jit(solution)/shard_map/ppermute | solution.py:373
  530.0 57.8 %all-to-all-start.10 = ((bf16[4,128,2304]{2,1,0:T(8,128)(2,1)}), bf16[4,128,2304]{2,1,0:T(8,128)(2,1)}, u32[]{:S(2)}, u32[]{:S(2)}) async-start(bf16[4,128,2304]{2,1,0:T(8,128)(2,1)} %bitcast.84), calls=%async_computation.10 | async-start | bytes 4718592 | tf_op jit(solution)/shard_map/all_to_all | solution.py:413
  541.8 26.5 %collective-permute-start.36 = (f32[7,2048]{1,0:T(8,128)S(1)}, f32[7,2048]{1,0:T(8,128)S(1)}, u32[]{:S(2)}, u32[]{:S(2)}) collective-permute-start(f32[7,2048]{1,0:T(8,128)S(1)} %add_add_fusion.1), channel_id=1, source_target_pairs={{0,18},{2,16},{4,22},{6,20},{8,26},{10,24},{12,30},{14,28},{16,2},... | collective-permute-start | bytes 172040 | tf_op jit(solution)/shard_map/ppermute | solution.py:373
  545.5 22.8 %collective-permute-start.35 = (f32[7,2048]{1,0:T(8,128)S(1)}, f32[7,2048]{1,0:T(8,128)S(1)}, u32[]{:S(2)}, u32[]{:S(2)}) collective-permute-start(f32[7,2048]{1,0:T(8,128)S(1)} %add_add_fusion.1), channel_id=1, source_target_pairs={{0,2},{2,0},{4,6},{6,4},{8,10},{10,8},{12,14},{14,12},{16,18},{18,... | collective-permute-start | bytes 172040 | tf_op jit(solution)/shard_map/ppermute | solution.py:373
  546.2 22.8 %collective-permute-start.34 = (f32[7,2048]{1,0:T(8,128)S(1)}, f32[7,2048]{1,0:T(8,128)S(1)}, u32[]{:S(2)}, u32[]{:S(2)}) collective-permute-start(f32[7,2048]{1,0:T(8,128)S(1)} %add_add_fusion.1), channel_id=1, source_target_pairs={{0,16},{2,18},{4,20},{6,22},{8,24},{10,26},{12,28},{14,30},{16,0},... | collective-permute-start | bytes 172040 | tf_op jit(solution)/shard_map/ppermute | solution.py:373
  587.7 18.3 %all-to-all-start.11 = ((bf16[4,128,1024]{2,1,0:T(8,128)(2,1)}), bf16[4,128,1024]{2,1,0:T(8,128)(2,1)S(1)}, u32[]{:S(2)}, u32[]{:S(2)}) async-start(bf16[4,128,1024]{2,1,0:T(8,128)(2,1)} %bitcast.106), calls=%async_computation.11 | async-start | bytes 2097152 | tf_op jit(solution)/shard_map/all_to_all | solution.py:413
  (33 other events, 151.9 us)

commit v4 on v3

--- a/solution.py
+++ b/solution.py
@@ -218,7 +218,7 @@
     mixed_sib[...] = mixed_ref[rows:]
     for at, w in spans(weights):
         term = dot(mixed_ref[...], w[:, 3 * cols :], 1, 1)
-        mine_ref[:, at] = term[:rows]
+        mine_ref[:, at] = term[:rows].astype(BF)
         other_ref[:, at] = term[rows:].astype(BF)
 
 
@@ -258,7 +258,7 @@
     sums_ref[...] = jnp.sum(lin_ref[...].astype(F32), axis=0, keepdims=True)
     for at, w in spans(weights):
         term = dot(lin_ref[...], w[:, : 3 * cols], 1, 1)
-        mine_ref[:, at] = term[:rows]
+        mine_ref[:, at] = term[:rows].astype(BF)
         other_ref[:, at] = term[rows:].astype(BF)
 
 
@@ -442,7 +442,7 @@
 
     def merge(mine, other, after=()):
         other = sibling(tie(other, *after))
-        return (by_block(mine) + by_block(other).astype(F32)).astype(BF)
+        return (by_block(mine).astype(F32) + by_block(other).astype(F32)).astype(BF)
 
     def collect(both, after=()):
         return jnp.sum(exchange(tie(both, *after)).astype(F32), axis=0)
@@ -453,7 +453,7 @@
         bits_left = range(i.bit_length(), len(far_bits))
         return [c for b in bits_left for c in below(i | 1 << b) + [i | 1 << b]]
 
-    def block_grad(i, kinds, adds, after=()):
+    def block_grad(i, kinds, adds, after=(), cost=LONG):
         cols = sum(c[0].shape[1] for _, sets in kinds for c in sets)
         ins, specs = [], []
         for left, sets in kinds:
@@ -471,6 +471,7 @@
             [shaped((shard_rows, cols), BF)],
             2 * group * seq_len * shard_rows * cols,
             in_specs=specs,
+            cost=cost,
         )[0]
 
     def send(i, part):
@@ -517,11 +518,11 @@
         shard = mlp_shard[:, t * 3 * TILE : (t + 1) * 3 * TILE]
         w_mlp.append(gather(shard, after, after_own))
         after, after_own = [w_mlp[t][1]], [w_mlp[t][2]]
-    grad_local = to_rel(out_grad)
+    grad_local = to_rel(tie(out_grad))
     grad_copies = copies(grad_local)
     heard = spread(
         tie(copies(seq_local), grad_copies, cosine, lead, tail, mask),
-        [mlp_shard] + w_attn[1:3],
+        [mlp_shard] + w_attn[1:2] + w_attn[2:3],
         w_attn[3:] + w_mlp[0][1:2],
     )
     seq_in = [half(h) for h in heard]
@@ -531,14 +532,14 @@
     facts = [mask, cosine, lead, tail]
     lines = pltpu.VMEM((seq_len, width), BF)
     mine, other = shaped((group * rows, width), F32), shaped((group * rows, width), BF)
-    mine3, other3 = (shaped((group, rows, width), t) for t in (F32, BF))
+    term3 = shaped((group, rows, width), BF)
     qkv_shape = shaped((group, seq_len, 3 * head_cols), BF)
     mixed_shape = shaped((group, rows, head_cols), BF)
     lin_shape = shaped((group, rows, 3 * head_cols), BF)
     attn_flops = 2 * group * seq_len * width * 4 * head_cols
 
     ins = [*heard, bias] + facts + w_attn
-    outs = [qkv_shape, mixed_shape, mixed_shape, mine3, other3]
+    outs = [qkv_shape, mixed_shape, mixed_shape, term3, term3]
     qkv, mixed_own, mixed_sib, *terms = call(
         functools.partial(attend_kernel, len(w_attn)),
         ins,
@@ -553,11 +554,13 @@
         scratch=[lines, pltpu.VMEM((seq_len, head_cols), BF)],
     )
     mixed = [half(mixed_own), half(mixed_sib)]
-    both = merge(*map(half, terms), w_mlp[0][2:3])
-    attn_sum = collect(both, [grad_rows[0]])
-    resid_two = resid + tie(attn_sum, *w_mlp[0][3:], *w_mlp[1][1:3])
+    both = merge(*map(half, terms), w_mlp[0][2:3] + [])
+    attn_sum = collect(both, [grad_rows[0]] + [])
+    resid_two = resid + tie(
+        attn_sum, *w_mlp[0][3:], *w_mlp[1][1:2], *w_mlp[1][2:3]
+    )
     normed_mid, normed_two, inv_two = norm_parts(resid_two, gains[2], gains[3])
-    seq_mid = [half(h) for h in spread(copies(normed_mid.astype(BF)), (), w_mlp[1][3:] + [p for w in w_mlp[2:] for p in w[1:3]])]
+    seq_mid = [half(h) for h in spread(copies(normed_mid.astype(BF)), (), w_mlp[1][3:] + w_mlp[2][1:2] + w_mlp[2][2:3])]
     grad_rows = [half(h) for h in grad_rows]
 
     row_spec = pl.BlockSpec((rows, width), lambda k: (k, 0))
@@ -571,7 +574,7 @@
         *found, mid_own, mid_sib = call(
             functools.partial(mlp_kernel, far, len(batch), not mid),
             ins + [w for t in batch for w in weights[t]],
-            ([pair_shape] * 2 + [hidden_shape] * 2) * len(batch) + [mine, other if final else mine],
+            ([pair_shape] * 2 + [hidden_shape] * 2) * len(batch) + [other if final else mine] * 2,
             10 * group * seq_len * width * TILE * len(batch),
             in_specs=[row_spec] * len(ins)
             + [
@@ -601,7 +604,7 @@
 
     def batch_step(n, i, after):
         part = block_grad(i, batch_kinds[n], [(v, 0) for v in batch_adds[n][i]], after)
-        if i == 1 and n > 1:
+        if i == 1 and n >= 2:
             held.append((n, i, part))
             return part, None
         came = send(i, part)
@@ -613,9 +616,9 @@
         part, came = batch_step(n, steps[0], [both] + first_parts if n else [])
         first_parts.append(part)
         first_came.append(came)
-    last_part = block_grad(last, all_kinds, [], first_parts)
+    last_part = block_grad(last, all_kinds, [], first_parts, cost=LONG)
     last_came = send(last, last_part)
-    mid_local = tie(collect(both), last_part, first_came[0])
+    mid_local = tie(collect(both), last_part, *first_came[:1])
     resid_grad = grad_local.astype(F32) + norm_back(mid_local, normed_two, inv_two, gains[2])
     resid_back = resid_grad.astype(BF)
     copied = copies(resid_back)
@@ -629,7 +632,7 @@
     out_terms = call(
         functools.partial(mlp_out_kernel, far, tiles),
         out_ins + weights,
-        [mine, other],
+        [other, other],
         2 * group * seq_len * width * hidden_cols,
         in_specs=[whole(v.shape) for v in out_ins]
         + [
@@ -639,9 +642,9 @@
         cost=SHORT,
     )
     out_both = merge(*out_terms)
-    attn_grad = spread(copied, [], [out_both, *later, later_came[0], last_came])
+    attn_grad = spread(copied, [], [out_both] + later + later_came[:1] + [])
     ins = [*attn_grad, qkv] + facts + w_attn
-    outs = [lin_shape, lin_shape, shaped((group, 1, 3 * head_cols), F32), mine3, other3]
+    outs = [lin_shape, lin_shape, shaped((group, 1, 3 * head_cols), F32), term3, term3]
     lin_own, lin_sib, bias_sums, *terms = call(
         functools.partial(attend_back_kernel, len(w_attn)),
         ins,
@@ -658,7 +661,7 @@
         batch_adds[n][parent(i)].append(came)
         later_came.append(came)
     later_came = [came for came in later_came if came is not None]
-    both = merge(*map(half, terms), later_came[1:2])
+    both = merge(*map(half, terms), [])
     out_sum = collect(out_both, [attn_grad[0]])
     in_grad = tie(collect(both, [out_sum]), *later_came[2:3])
     attn_kinds = [
@@ -668,7 +671,7 @@
     attn_adds = [[] for _ in range(far)]
     parts, attn_sent = [], []
     for n, i in enumerate(wide):
-        after = ([in_grad] if attn_adds[i] else [both]) + parts if n else []
+        after = (([] + parts) if attn_adds[i] else [both] + parts) if n else []
         part = block_grad(i, attn_kinds, [(v, 0) for v in attn_adds[i]], after)
         parts.append(part)
         attn_sent.append(send(i, part))
@@ -699,8 +702,11 @@
     result = from_rel((resid_two + out_sum).astype(BF))
     adds = [(v, 3 * TILE * b[0]) for b, into in zip(batches, batch_adds) for v in into[0]]
     adds.append((last_came, 0))
-    mlp_came = exchange(tie(block_grad(0, all_kinds, adds, parts), in_grad))
-    attn_mine = block_grad(0, attn_kinds, [(v, 0) for v in attn_adds[0]], sums[1:])
+    mlp_after = parts
+    mlp_mine = block_grad(0, all_kinds, adds, mlp_after)
+    attn_after = sums[1:] + [result]
+    attn_mine = block_grad(0, attn_kinds, [(v, 0) for v in attn_adds[0]], attn_after)
+    mlp_came = exchange(tie(mlp_mine, in_grad, out_sum))
     attn_came = exchange(tie(attn_mine, mlp_came))
     gate_up_grad, down_grad = finish(
         finish_mlp_kernel, [mlp_came], (gate_up_weight.shape, down_weight.shape)

time: 621 us -> 604 us (0.973)
  waiting for transfers between devices: 286 us -> 268 us
    ppermute x31, waiting for transfers between devices: 171 us -> 138 us  [swap(): return lax.ppermute(array, 'dp', [(d, d ^ mask) for d in range(dp_size)])]
    all_to_all x12, waiting for transfers between devices: 106 us -> 122 us  [exchange(): lax.all_to_all(rows_by_rank, 'dp', 0, 0, axis_index_groups=bands, tiled=T...]
  transfers between devices with their start and end apart: 52 -> 52, of which waited for: 23 -> 21; matrix products, arithmetic and copies ran while one was open for 12% -> 12% of each run, Pallas kernels for 22% -> 22%
where the time goes in v4:
time: 604 us; the launch traced here: 594 us
  waiting for transfers between devices  268 us (44%)
  Pallas kernels  151 us (25%)
  starting transfers between devices  91.9 us (15%)
  other arithmetic  50.2 us (8%)
  local copies, waits for them, and re-layouts  30.4 us (5%)
    pallas_call x21, Pallas kernels, call(): pl.pallas_call(kernel, grid=grid, in_specs=in_specs or [whole(v.shape) fo...  151 us
    ppermute x31, waiting for transfers between devices, swap(): return lax.ppermute(array, 'dp', [(d, d ^ mask) for d in range(dp_size)])  138 us
    all_to_all x12, waiting for transfers between devices, exchange(): lax.all_to_all(rows_by_rank, 'dp', 0, 0, axis_index_groups=bands, tiled=T...  122 us
    all_to_all x12, starting transfers between devices, exchange(): lax.all_to_all(rows_by_rank, 'dp', 0, 0, axis_index_groups=bands, tiled=T...  53.5 us
    ppermute x31, starting transfers between devices, swap(): return lax.ppermute(array, 'dp', [(d, d ^ mask) for d in range(dp_size)])  38 us
    convert_element_type x4, other arithmetic, merge(): return (by_block(mine).astype(F32) + by_block(other).astype(F32)).astype(BF)  15.2 us
  transfers between devices with their start and end apart: 52, of which 21 were waited for; matrix products, arithmetic and copies ran while one was open for 12% of the time, Pallas kernels for 22%

profile of v4, /device:TPU:0, one launch (start us, length us, event | category | flops | bytes accessed | tf_op | source)
XLA Modules:
  0.0 593.8 jit_solution(12759758106625612658)
XLA Ops:
  0.7 2.4 shard_map.203
  3.0 3.0 collective-permute-start.2
  7.6 4.2 all-to-all-start
  25.3 3.5 shard_map.204
  28.8 4.0 all-to-all-start.1
  33.9 2.2 copy.42
  36.1 2.2 reshape.456
  40.2 3.0 collective-permute-start.3
  45.9 3.1 fusion.2
  52.4 35.4 %collective-permute-done.3.refs_1_ = bf16[512,1024]{1,0:T(8,128)(2,1)S(1)} collective-permute-done((bf16[512,1024]{1,0:T(8,128)(2,1)}, bf16[512,1024]{1,0:T(8,128)(2,1)S(1)}, u32[]{:S(2)}, u32[]{:S(2)}) %collective-permute-start.3) | collective-permute-done | bytes 1048608 | tf_op jit(solution)/shard_map/ppermute | solution.py:373
  88.7 4.5 all-to-all-start.2
  99.0 17.5 %collective-permute-done.5.refs_3_ = bf16[512,1024]{1,0:T(8,128)(2,1)} collective-permute-done((bf16[512,1024]{1,0:T(8,128)(2,1)}, bf16[512,1024]{1,0:T(8,128)(2,1)}, u32[]{:S(2)}, u32[]{:S(2)}) %collective-permute-start.5) | collective-permute-done | bytes 1048608 | tf_op jit(solution)/shard_map/ppermute | solution.py:373
  116.5 14.5 %collective-permute-done.6.refs_5_.refs_7_ = bf16[512,768]{1,0:T(8,128)(2,1)} collective-permute-done((bf16[512,768]{1,0:T(8,128)(2,1)S(1)}, bf16[512,768]{1,0:T(8,128)(2,1)}, u32[]{:S(2)}, u32[]{:S(2)}) %collective-permute-start.6) | collective-permute-done | bytes 786464 | tf_op jit(solution)/shard_map/ppermute | solution.py:373
  131.1 2.3 all-to-all-done.2.own_ref
  135.5 4.6 all-to-all-start.3
  140.1 16.9 %shard_map.205 = (bf16[4,256,768]{2,1,0:T(8,128)(2,1)}, bf16[4,128,256]{2,1,0:T(8,128)(2,1)}, bf16[4,128,256]{2,1,0:T(8,128)(2,1)}, bf16[4,128,2048]{2,1,0:T(8,128)(2,1)}, bf16[4,128,2048]{2,1,0:T(8,128)(2,1)}) custom-call(bf16[4,128,2048]{2,1,0:T(8,128)(2,1)} %all-to-all-done.2.own_ref, bf16[4,128,2048]{2,1,0:T(8,128)(2,1)} %collective-permute-done.7.sib_ref, ...), custom_call_target="tpu_custom_call" | custom-call | flops 128849018880 | bytes 519137280 | tf_op jit(solution)/shard_map/pallas_call | solution.py:75
  157.0 4.4 collective-permute-done.9
  161.4 3.8 fusion.1
  167.5 3.6 all-to-all-start.4
  173.4 39.8 %all-to-all-done.4 = bf16[4,128,2048]{2,1,0:T(8,128)(2,1)S(1)} async-done(((bf16[4,128,2048]{2,1,0:T(8,128)(2,1)}), bf16[4,128,2048]{2,1,0:T(8,128)(2,1)S(1)}, u32[]{:S(2)}, u32[]{:S(2)}) %all-to-all-start.4) | async-done | bytes 2097184 | tf_op jit(solution)/shard_map/all_to_all | solution.py:413
  216.8 5.1 all-to-all-start.5
  224.8 18.7 %collective-permute-done.13.refs_11_.refs_13_ = bf16[512,768]{1,0:T(8,128)(2,1)S(1)} collective-permute-done((bf16[512,768]{1,0:T(8,128)(2,1)}, bf16[512,768]{1,0:T(8,128)(2,1)S(1)}, u32[]{:S(2)}, u32[]{:S(2)}) %collective-permute-start.13) | collective-permute-done | bytes 786464 | tf_op jit(solution)/shard_map/ppermute | solution.py:373
  243.4 17.5 %collective-permute-done.14.refs_7_.refs_15_ = bf16[512,768]{1,0:T(8,128)(2,1)S(1)} collective-permute-done((bf16[512,768]{1,0:T(8,128)(2,1)S(1)}, bf16[512,768]{1,0:T(8,128)(2,1)S(1)}, u32[]{:S(2)}, u32[]{:S(2)}) %collective-permute-start.14) | collective-permute-done | bytes 786464 | tf_op jit(solution)/shard_map/ppermute | solution.py:373
  263.7 4.0 collective-permute-done.16
  267.7 17.1 %shard_map.206 = (bf16[512,512]{1,0:T(8,128)(2,1)}, bf16[512,512]{1,0:T(8,128)(2,1)}, bf16[512,256]{1,0:T(8,128)(2,1)}, bf16[512,256]{1,0:T(8,128)(2,1)}, bf16[5...) custom-call(bf16[512,2048]{1,0:T(8,128)(2,1)} %bitcast.22.refs_0_.re, ...), custom_call_target="tpu_custom_call" | custom-call | flops 322122547200 | bytes 880803840 | tf_op jit(solution)/shard_map/pallas_call | solution.py:75
  284.8 13.6 %shard_map.207 = (bf16[512,512]{1,0:T(8,128)(2,1)}, bf16[512,512]{1,0:T(8,128)(2,1)}, bf16[512,256]{1,0:T(8,128)(2,1)}, bf16[512,256]{1,0:T(8,128)(2,1)}, bf16[5...) custom-call(bf16[512,2048]{1,0:T(8,128)(2,1)} %bitcast.22.refs_0_.refs_8_.refs_16_, ...), custom_call_target="tpu_custom_call" | custom-call | flops 161061273600 | bytes 817889280 | tf_op jit(solution)/shard_map/pallas_call | solution.py:75
  298.7 4.1 shard_map.208
  303.3 3.9 add_convert_fusion.1
  307.2 3.9 shard_map.209
  312.6 3.9 shard_map.210
  317.0 4.0 all-to-all-start.6
  321.0 8.7 %shard_map.211 = bf16[512,2304]{1,0:T(8,128)(2,1)} custom-call(bf16[512,2048]{1,0:T(8,128)(2,1)} %bitcast.22.refs_0_.refs_8_.refs_16_, bf16[512,2048]{1,0:T(8,128)(2,1)} %bitcast.23.refs_1_.refs_9_.refs_17_, bf16[512,512]{1,0:T(8,128)(2,1)} %get-tuple-element.103.refs_2_, bf16[512,512]{1,0:T(8,128)(2,1)} %get-tuple-element.104.refs_3_, ...), custom_call_target="tpu_custom_call" | custom-call | flops 72477573120 | bytes 967311360 | tf_op jit(solution)/shard_map/pallas_call | solution.py:75
  329.7 15.9 %all-to-all-done.6 = bf16[4,128,2048]{2,1,0:T(8,128)(2,1)S(1)} async-done(((bf16[4,128,2048]{2,1,0:T(8,128)(2,1)}), bf16[4,128,2048]{2,1,0:T(8,128)(2,1)S(1)}, u32[]{:S(2)}, u32[]{:S(2)}) %all-to-all-start.6) | async-done | bytes 2097184 | tf_op jit(solution)/shard_map/all_to_all | solution.py:413
  350.3 4.2 shard_map.213
  354.5 2.1 collective-permute-start.24
  356.6 7.1 %shard_map.212 = (bf16[512,2048]{1,0:T(8,128)(2,1)}, bf16[512,2048]{1,0:T(8,128)(2,1)}) custom-call(bf16[512,256]{1,0:T(8,128)(2,1)} %get-tuple-element.118.refs_6_.refs_0_, bf16[512,256]{1,0:T(8,128)(2,1)} %get-tuple-element.105.refs_7_.refs_1_, bf16[512,256]{1,0:T(8,128)(2,1)} %get-tuple-element.109.refs_6_.refs_14_.refs_2_, ...), custom_call_target="tpu_custom_call" | custom-call | tf_op jit(solution)/shard_map/pallas_call | solution.py:75
  363.7 4.5 all-to-all-start.7
  368.2 4.2 shard_map.214
  372.4 4.3 shard_map.215
  376.7 3.8 add_convert_fusion
  380.5 10.6 %collective-permute-done.24.refs_24_ = bf16[512,768]{1,0:T(8,128)(2,1)S(1)} collective-permute-done((bf16[512,768]{1,0:T(8,128)(2,1)}, bf16[512,768]{1,0:T(8,128)(2,1)S(1)}, u32[]{:S(2)}, u32[]{:S(2)}) %collective-permute-start.24) | collective-permute-done | bytes 786464 | tf_op jit(solution)/shard_map/ppermute | solution.py:373
  391.1 17.8 %all-to-all-done.7.own_ref = bf16[4,128,2048]{2,1,0:T(8,128)(2,1)} async-done(((bf16[4,128,2048]{2,1,0:T(8,128)(2,1)}), bf16[4,128,2048]{2,1,0:T(8,128)(2,1)}, u32[]{:S(2)}, u32[]{:S(2)}) %all-to-all-start.7) | async-done | bytes 2097184 | tf_op jit(solution)/shard_map/all_to_all | solution.py:413
  411.0 5.1 all-to-all-start.8
  417.4 21.3 %shard_map.216 = (bf16[4,128,768]{2,1,0:T(8,128)(2,1)}, bf16[4,128,768]{2,1,0:T(8,128)(2,1)}, f32[4,1,768]{2,1,0:T(1,128)}, bf16[4,128,2048]{2,1,0:T(8,128)(2,1)}, bf16[4,128,2048]{2,1,0:T(8,128)(2,1)}) custom-call(bf16[4,128,2048]{2,1,0:T(8,128)(2,1)} %all-to-all-done.7.own_ref, bf16[4,128,2048]{2,1,0:T(8,128)(2,1)} %copy-done.43, ...), custom_call_target="tpu_custom_call" | custom-call | flops 128849018880 | bytes 550871040 | tf_op jit(solution)/shard_map/pallas_call | solution.py:75
  440.8 4.4 shard_map.217
  445.9 18.3 %all-to-all-done.8 = bf16[4,128,2048]{2,1,0:T(8,128)(2,1)} async-done(((bf16[4,128,2048]{2,1,0:T(8,128)(2,1)}), bf16[4,128,2048]{2,1,0:T(8,128)(2,1)}, u32[]{:S(2)}, u32[]{:S(2)}) %all-to-all-start.8) | async-done | bytes 2097184 | tf_op jit(solution)/shard_map/all_to_all | solution.py:413
  464.2 2.1 convert_reduce_fusion.1
  471.7 3.7 fusion
  475.4 4.7 all-to-all-start.9
  480.1 4.4 shard_map.218
  485.4 4.8 shard_map.219
  490.8 25.0 %all-to-all-done.9 = bf16[4,128,2048]{2,1,0:T(8,128)(2,1)} async-done(((bf16[4,128,2048]{2,1,0:T(8,128)(2,1)}), bf16[4,128,2048]{2,1,0:T(8,128)(2,1)}, u32[]{:S(2)}, u32[]{:S(2)}) %all-to-all-start.9) | async-done | bytes 2097184 | tf_op jit(solution)/shard_map/all_to_all | solution.py:413
  518.7 10.1 %shard_map.221 = bf16[512,2304]{1,0:T(8,128)(2,1)} custom-call(bf16[512,2048]{1,0:T(8,128)(2,1)} %bitcast.22.refs_0_.refs_8_.refs_16_, bf16[512,2048]{1,0:T(8,128)(2,1)} %bitcast.23.refs_1_.refs_9_.refs_17_, bf16[512,512]{1,0:T(8,128)(2,1)} %get-tuple-element.103.refs_2_, bf16[512,512]{1,0:T(8,128)(2,1)} %get-tuple-element.104.refs_3_, ...), custom_call_target="tpu_custom_call" | custom-call | flops 72477573120 | bytes 1108869120 | tf_op jit(solution)/shard_map/pallas_call | solution.py:75
  529.3 2.5 collective-permute-start.30
  532.4 4.5 all-to-all-start.10
  536.9 4.8 collective-permute-done.31
  543.7 2.4 collective-permute-start.32
  546.1 18.4 %collective-permute-done.34 = f32[7,2048]{1,0:T(8,128)S(1)} collective-permute-done((f32[7,2048]{1,0:T(8,128)S(1)}, f32[7,2048]{1,0:T(8,128)S(1)}, u32[]{:S(2)}, u32[]{:S(2)}) %collective-permute-start.34) | collective-permute-done | bytes 57376 | tf_op jit(solution)/shard_map/ppermute | solution.py:373
  565.2 5.1 shard_map.220
  570.3 4.8 all-to-all-start.11
  575.1 2.7 multiply_add_fusion
  577.8 2.1 reshape.469
  585.6 4.1 shard_map.223
  590.6 2.7 shard_map.222
  (268 shorter events, 80.0 us)
Async XLA Ops:
  0.6 132.8 %copy-start = (f32[3,1024]{1,0:T(4,128)S(1)}, f32[3,1024]{1,0:T(4,128)}, u32[]{:S(2)}) copy-start(f32[3,1024]{1,0:T(4,128)} %param.17) | copy-start | bytes 36868
  3.0 35.3 %collective-permute-start.2 = (s32[256]{0:T(256)S(1)}, s32[256]{0:T(256)S(1)}, u32[]{:S(2)}, u32[]{:S(2)}) collective-permute-start(s32[256]{0:T(256)S(1)} %copy-done.42), channel_id=1, source_target_pairs={{0,4},{2,6},{4,0},{6,2},{8,12},{10,14},{12,8},{14,10},{16,20},{18,... | collective-permute-start | bytes 3080 | tf_op jit(solution)/shard_map/ppermute | solution.py:373
  6.0 32.3 %collective-permute-start.1 = (s32[256]{0:T(256)S(1)}, s32[256]{0:T(256)S(1)}, u32[]{:S(2)}, u32[]{:S(2)}) collective-permute-start(s32[256]{0:T(256)S(1)} %copy-done.42), channel_id=1, source_target_pairs={{0,12},{2,14},{4,8},{6,10},{8,4},{10,6},{12,0},{14,2},{16,28},{18,... | collective-permute-start | bytes 3080 | tf_op jit(solution)/shard_map/ppermute | solution.py:373
  7.5 30.8 %collective-permute-start = (s32[256]{0:T(256)S(1)}, s32[256]{0:T(256)S(1)}, u32[]{:S(2)}, u32[]{:S(2)}) collective-permute-start(s32[256]{0:T(256)S(1)} %copy-done.42), channel_id=1, source_target_pairs={{0,8},{2,10},{4,12},{6,14},{8,0},{10,2},{12,4},{14,6},{16,24},{18,... | collective-permute-start | bytes 3080 | tf_op jit(solution)/shard_map/ppermute | solution.py:373
  7.6 17.7 %all-to-all-start = ((bf16[4,128,1024]{2,1,0:T(8,128)(2,1)}), bf16[4,128,1024]{2,1,0:T(8,128)(2,1)}, u32[]{:S(2)}, u32[]{:S(2)}) async-start(bf16[4,128,1024]{2,1,0:T(8,128)(2,1)} %bitcast.81), calls=%async_computation | async-start | bytes 2097152 | tf_op jit(solution)/shard_map/all_to_all | solution.py:413
  20.2 193.3 %copy-start.6 = (f32[128,2048]{1,0:T(8,128)}, f32[128,2048]{1,0:T(8,128)S(1)}, u32[]{:S(2)}) copy-start(f32[128,2048]{1,0:T(8,128)S(1)} %reshape.481) | copy-start | bytes 3145732
  28.8 59.9 %all-to-all-start.1 = ((bf16[4,128,2304]{2,1,0:T(8,128)(2,1)}), bf16[4,128,2304]{2,1,0:T(8,128)(2,1)S(1)}, u32[]{:S(2)}, u32[]{:S(2)}) async-start(bf16[4,128,2304]{2,1,0:T(8,128)(2,1)} %bitcast.78), calls=%async_computation.1 | async-start | bytes 4718592 | tf_op jit(solution)/shard_map/all_to_all | solution.py:413
  40.2 47.5 %collective-permute-start.3 = (bf16[512,1024]{1,0:T(8,128)(2,1)}, bf16[512,1024]{1,0:T(8,128)(2,1)S(1)}, u32[]{:S(2)}, u32[]{:S(2)}) collective-permute-start(bf16[512,1024]{1,0:T(8,128)(2,1)} %bitcast.15.refs_0_), channel_id=1, source_target_pairs={{0,16},{2,18},{4,20},{6,22},{8,24},{10,26},{12,28},{14,30},{16,0},... | collective-permute-start | bytes 3145736 | tf_op jit(solution)/shard_map/ppermute | solution.py:373
  43.2 45.5 %collective-permute-start.4 = (bf16[512,1024]{1,0:T(8,128)(2,1)}, bf16[512,1024]{1,0:T(8,128)(2,1)}, u32[]{:S(2)}, u32[]{:S(2)}) collective-permute-start(bf16[512,1024]{1,0:T(8,128)(2,1)} %bitcast.15.refs_0_), channel_id=1, source_target_pairs={{0,2},{2,0},{4,6},{6,4},{8,10},{10,8},{12,14},{14,12},{16,18},{18,... | collective-permute-start | bytes 3145736 | tf_op jit(solution)/shard_map/ppermute | solution.py:373
  88.7 44.7 %all-to-all-start.2 = ((bf16[4,128,2048]{2,1,0:T(8,128)(2,1)}), bf16[4,128,2048]{2,1,0:T(8,128)(2,1)}, u32[]{:S(2)}, u32[]{:S(2)}) async-start(bf16[4,128,2048]{2,1,0:T(8,128)(2,1)} %broadcast_in_dim.64), calls=%async_computation.2 | async-start | bytes 4194304 | tf_op jit(solution)/shard_map/all_to_all | solution.py:413
  93.2 23.4 %collective-permute-start.5 = (bf16[512,1024]{1,0:T(8,128)(2,1)}, bf16[512,1024]{1,0:T(8,128)(2,1)}, u32[]{:S(2)}, u32[]{:S(2)}) collective-permute-start(bf16[512,1024]{1,0:T(8,128)(2,1)} %copy-done.44), channel_id=1, source_target_pairs={{0,2},{2,0},{4,6},{6,4},{8,10},{10,8},{12,14},{14,12},{16,18},{18,... | collective-permute-start | bytes 3145736 | tf_op jit(solution)/shard_map/ppermute | solution.py:373
  97.1 34.0 %collective-permute-start.6 = (bf16[512,768]{1,0:T(8,128)(2,1)S(1)}, bf16[512,768]{1,0:T(8,128)(2,1)}, u32[]{:S(2)}, u32[]{:S(2)}) collective-permute-start(bf16[512,768]{1,0:T(8,128)(2,1)S(1)} %get-tuple-element.88), channel_id=1, source_target_pairs={{0,16},{2,18},{4,20},{6,22},{8,24},{10,26},{12,28},{14,30},{16,0},... | collective-permute-start | bytes 2359304 | tf_op jit(solution)/shard_map/ppermute | solution.py:373
  133.4 6.6 %collective-permute-start.7 = (bf16[4,128,2048]{2,1,0:T(8,128)(2,1)}, bf16[4,128,2048]{2,1,0:T(8,128)(2,1)}, u32[]{:S(2)}, u32[]{:S(2)}) collective-permute-start(bf16[4,128,2048]{2,1,0:T(8,128)(2,1)} %all-to-all-done.2.own_ref), channel_id=1, source_target_pairs={{0,1},{1,0},{2,3},{3,2},{4,5},{5,4},{6,7},{7,6},{8,9},{9,8},{10,11... | collective-permute-start | bytes 6291464 | tf_op jit(solution)/shard_map/ppermute | solution.py:376
  134.0 22.9 %collective-permute-start.8 = (bf16[512,768]{1,0:T(8,128)(2,1)}, bf16[512,768]{1,0:T(8,128)(2,1)}, u32[]{:S(2)}, u32[]{:S(2)}) collective-permute-start(bf16[512,768]{1,0:T(8,128)(2,1)} %copy-done.18), channel_id=1, source_target_pairs={{0,2},{2,0},{4,6},{6,4},{8,10},{10,8},{12,14},{14,12},{16,18},{18,... | collective-permute-start | bytes 2359304 | tf_op jit(solution)/shard_map/ppermute | solution.py:373
  135.5 30.7 %all-to-all-start.3 = ((bf16[4,128,2048]{2,1,0:T(8,128)(2,1)}), bf16[4,128,2048]{2,1,0:T(8,128)(2,1)S(1)}, u32[]{:S(2)}, u32[]{:S(2)}) async-start(bf16[4,128,2048]{2,1,0:T(8,128)(2,1)} %broadcast_in_dim.65), calls=%async_computation.3 | async-start | bytes 4194304 | tf_op jit(solution)/shard_map/all_to_all | solution.py:413
  156.9 4.4 collective-permute-start.9
  167.5 45.6 %all-to-all-start.4 = ((bf16[4,128,2048]{2,1,0:T(8,128)(2,1)}), bf16[4,128,2048]{2,1,0:T(8,128)(2,1)S(1)}, u32[]{:S(2)}, u32[]{:S(2)}) async-start(bf16[4,128,2048]{2,1,0:T(8,128)(2,1)} %fusion.1), calls=%async_computation.4 | async-start | bytes 4194304 | tf_op jit(solution)/shard_map/all_to_all | solution.py:413
  171.2 42.3 %collective-permute-start.11 = (bf16[512,768]{1,0:T(8,128)(2,1)}, bf16[512,768]{1,0:T(8,128)(2,1)}, u32[]{:S(2)}, u32[]{:S(2)}) collective-permute-start(bf16[512,768]{1,0:T(8,128)(2,1)} %get-tuple-element.93), channel_id=1, source_target_pairs={{0,16},{2,18},{4,20},{6,22},{8,24},{10,26},{12,28},{14,30},{16,0},... | collective-permute-start | bytes 2359304 | tf_op jit(solution)/shard_map/ppermute | solution.py:373
  171.2 42.3 %collective-permute-start.10 = (bf16[512,768]{1,0:T(8,128)(2,1)}, bf16[512,768]{1,0:T(8,128)(2,1)}, u32[]{:S(2)}, u32[]{:S(2)}) collective-permute-start(bf16[512,768]{1,0:T(8,128)(2,1)} %collective-permute-done.6.refs_5_.refs_7_), channel_id=1, source_target_pairs={{0,2},{2,0},{4,6},{6,4},{8,10},{10,8},{12,14},{14,12},{16,18},{18,... | collective-permute-start | bytes 2359304 | tf_op jit(solution)/shard_map/ppermute | solution.py:373
  172.1 41.4 %collective-permute-start.12 = (bf16[512,768]{1,0:T(8,128)(2,1)}, bf16[512,768]{1,0:T(8,128)(2,1)}, u32[]{:S(2)}, u32[]{:S(2)}) collective-permute-start(bf16[512,768]{1,0:T(8,128)(2,1)} %get-tuple-element.93), channel_id=1, source_target_pairs={{0,2},{2,0},{4,6},{6,4},{8,10},{10,8},{12,14},{14,12},{16,18},{18,... | collective-permute-start | bytes 2359304 | tf_op jit(solution)/shard_map/ppermute | solution.py:373
  173.3 40.7 %copy-start.25 = (f32[1,2,2,2,2,128]{5,4,3,2,1,0:T(2,128)}, f32[1,2,2,2,2,128]{5,4,3,2,1,0:T(2,128)S(1)}, u32[]{:S(2)}) copy-start(f32[1,2,2,2,2,128]{5,4,3,2,1,0:T(2,128)S(1)} %copy.45) | copy-start | bytes 24580
  216.8 46.4 %all-to-all-start.5 = ((bf16[4,128,2048]{2,1,0:T(8,128)(2,1)}), bf16[4,128,2048]{2,1,0:T(8,128)(2,1)}, u32[]{:S(2)}, u32[]{:S(2)}) async-start(bf16[4,128,2048]{2,1,0:T(8,128)(2,1)} %broadcast_in_dim.74), calls=%async_computation.5 | async-start | bytes 4194304 | tf_op jit(solution)/shard_map/all_to_all | solution.py:413
  221.9 39.1 %collective-permute-start.14 = (bf16[512,768]{1,0:T(8,128)(2,1)S(1)}, bf16[512,768]{1,0:T(8,128)(2,1)S(1)}, u32[]{:S(2)}, u32[]{:S(2)}) collective-permute-start(bf16[512,768]{1,0:T(8,128)(2,1)S(1)} %copy-done.17), channel_id=1, source_target_pairs={{0,16},{2,18},{4,20},{6,22},{8,24},{10,26},{12,28},{14,30},{16,0},... | collective-permute-start | bytes 2359304 | tf_op jit(solution)/shard_map/ppermute | solution.py:373
  222.7 20.7 %collective-permute-start.13 = (bf16[512,768]{1,0:T(8,128)(2,1)}, bf16[512,768]{1,0:T(8,128)(2,1)S(1)}, u32[]{:S(2)}, u32[]{:S(2)}) collective-permute-start(bf16[512,768]{1,0:T(8,128)(2,1)} %collective-permute-done.11.refs_9_.refs_11_), channel_id=1, source_target_pairs={{0,2},{2,0},{4,6},{6,4},{8,10},{10,8},{12,14},{14,12},{16,18},{18,... | collective-permute-start | bytes 2359304 | tf_op jit(solution)/shard_map/ppermute | solution.py:373
  223.3 38.6 %collective-permute-start.15 = (bf16[512,768]{1,0:T(8,128)(2,1)S(1)}, bf16[512,768]{1,0:T(8,128)(2,1)}, u32[]{:S(2)}, u32[]{:S(2)}) collective-permute-start(bf16[512,768]{1,0:T(8,128)(2,1)S(1)} %copy-done.17), channel_id=1, source_target_pairs={{0,2},{2,0},{4,6},{6,4},{8,10},{10,8},{12,14},{14,12},{16,18},{18,... | collective-permute-start | bytes 2359304 | tf_op jit(solution)/shard_map/ppermute | solution.py:373
  224.8 39.0 %collective-permute-start.17 = (bf16[4,128,2048]{2,1,0:T(8,128)(2,1)S(1)}, bf16[4,128,2048]{2,1,0:T(8,128)(2,1)}, u32[]{:S(2)}, u32[]{:S(2)}) collective-permute-start(bf16[4,128,2048]{2,1,0:T(8,128)(2,1)S(1)} %copy-done.15), channel_id=1, source_target_pairs={{0,1},{1,0},{2,3},{3,2},{4,5},{5,4},{6,7},{7,6},{8,9},{9,8},{10,11... | collective-permute-start | bytes 6291464 | tf_op jit(solution)/shard_map/ppermute | solution.py:376
  243.4 17.5 %copy-start.20 = (bf16[512,768]{1,0:T(8,128)(2,1)}, bf16[512,768]{1,0:T(8,128)(2,1)S(1)}, u32[]{:S(2)}) copy-start(bf16[512,768]{1,0:T(8,128)(2,1)S(1)} %collective-permute-done.13.refs_11_.refs_13_) | copy-start | bytes 2359300
  263.2 4.5 collective-permute-start.16
  263.2 21.6 %collective-permute-start.18 = (bf16[512,768]{1,0:T(8,128)(2,1)}, bf16[512,768]{1,0:T(8,128)(2,1)}, u32[]{:S(2)}, u32[]{:S(2)}) collective-permute-start(bf16[512,768]{1,0:T(8,128)(2,1)} %copy-done.19), channel_id=1, source_target_pairs={{0,2},{2,0},{4,6},{6,4},{8,10},{10,8},{12,14},{14,12},{16,18},{18,... | collective-permute-start | bytes 2359304 | tf_op jit(solution)/shard_map/ppermute | solution.py:373
  298.5 4.8 collective-permute-start.19
  302.8 43.2 %collective-permute-start.20 = (bf16[512,768]{1,0:T(8,128)(2,1)}, bf16[512,768]{1,0:T(8,128)(2,1)}, u32[]{:S(2)}, u32[]{:S(2)}) collective-permute-start(bf16[512,768]{1,0:T(8,128)(2,1)} %shard_map.208), channel_id=1, source_target_pairs={{0,2},{2,0},{4,6},{6,4},{8,10},{10,8},{12,14},{14,12},{16,18},{18,... | collective-permute-start | bytes 2359304 | tf_op jit(solution)/shard_map/ppermute | solution.py:373
  311.1 57.1 %collective-permute-start.22 = (bf16[512,768]{1,0:T(8,128)(2,1)}, bf16[512,768]{1,0:T(8,128)(2,1)}, u32[]{:S(2)}, u32[]{:S(2)}) collective-permute-start(bf16[512,768]{1,0:T(8,128)(2,1)} %shard_map.209), channel_id=1, source_target_pairs={{0,2},{2,0},{4,6},{6,4},{8,10},{10,8},{12,14},{14,12},{16,18},{18,... | collective-permute-start | bytes 2359304 | tf_op jit(solution)/shard_map/ppermute | solution.py:373
  316.5 55.9 %collective-permute-start.23 = (bf16[512,768]{1,0:T(8,128)(2,1)}, bf16[512,768]{1,0:T(8,128)(2,1)}, u32[]{:S(2)}, u32[]{:S(2)}) collective-permute-start(bf16[512,768]{1,0:T(8,128)(2,1)} %shard_map.210), channel_id=1, source_target_pairs={{0,2},{2,0},{4,6},{6,4},{8,10},{10,8},{12,14},{14,12},{16,18},{18,... | collective-permute-start | bytes 2359304 | tf_op jit(solution)/shard_map/ppermute | solution.py:373
  317.0 28.6 %all-to-all-start.6 = ((bf16[4,128,2048]{2,1,0:T(8,128)(2,1)}), bf16[4,128,2048]{2,1,0:T(8,128)(2,1)S(1)}, u32[]{:S(2)}, u32[]{:S(2)}) async-start(bf16[4,128,2048]{2,1,0:T(8,128)(2,1)} %bitcast.26), calls=%async_computation.6 | async-start | bytes 4194304 | tf_op jit(solution)/shard_map/all_to_all | solution.py:413
  354.5 36.6 %collective-permute-start.24 = (bf16[512,768]{1,0:T(8,128)(2,1)}, bf16[512,768]{1,0:T(8,128)(2,1)S(1)}, u32[]{:S(2)}, u32[]{:S(2)}) collective-permute-start(bf16[512,768]{1,0:T(8,128)(2,1)} %shard_map.213), channel_id=1, source_target_pairs={{0,16},{2,18},{4,20},{6,22},{8,24},{10,26},{12,28},{14,30},{16,0},... | collective-permute-start | bytes 2359304 | tf_op jit(solution)/shard_map/ppermute | solution.py:373
  363.7 13.0 %collective-permute-start.21 = (bf16[512,2048]{1,0:T(8,128)(2,1)}, bf16[512,2048]{1,0:T(8,128)(2,1)}, u32[]{:S(2)}, u32[]{:S(2)}) collective-permute-start(bf16[512,2048]{1,0:T(8,128)(2,1)} %get-tuple-element.120), channel_id=1, source_target_pairs={{0,1},{1,0},{2,3},{3,2},{4,5},{5,4},{6,7},{7,6},{8,9},{9,8},{10,11... | collective-permute-start | bytes 6291464 | tf_op jit(solution)/shard_map/ppermute | solution.py:376
  363.7 45.2 %all-to-all-start.7 = ((bf16[4,128,2048]{2,1,0:T(8,128)(2,1)}), bf16[4,128,2048]{2,1,0:T(8,128)(2,1)}, u32[]{:S(2)}, u32[]{:S(2)}) async-start(bf16[4,128,2048]{2,1,0:T(8,128)(2,1)} %broadcast_in_dim.75), calls=%async_computation.7 | async-start | bytes 4194304 | tf_op jit(solution)/shard_map/all_to_all | solution.py:413
  391.1 17.8 %copy-start.45 = (bf16[512,768]{1,0:T(8,128)(2,1)}, bf16[512,768]{1,0:T(8,128)(2,1)S(1)}, u32[]{:S(2)}) copy-start(bf16[512,768]{1,0:T(8,128)(2,1)S(1)} %collective-permute-done.24.refs_24_) | copy-start | bytes 2359300
  408.9 7.2 %collective-permute-start.25 = (bf16[4,128,2048]{2,1,0:T(8,128)(2,1)}, bf16[4,128,2048]{2,1,0:T(8,128)(2,1)S(1)}, u32[]{:S(2)}, u32[]{:S(2)}) collective-permute-start(bf16[4,128,2048]{2,1,0:T(8,128)(2,1)} %all-to-all-done.7.own_ref), channel_id=1, source_target_pairs={{0,1},{1,0},{2,3},{3,2},{4,5},{5,4},{6,7},{7,6},{8,9},{9,8},{10,11... | collective-permute-start | bytes 6291464 | tf_op jit(solution)/shard_map/ppermute | solution.py:376
  408.9 109.7 %collective-permute-start.39 = (bf16[512,2304]{1,0:T(8,128)(2,1)}, bf16[512,2304]{1,0:T(8,128)(2,1)}, u32[]{:S(2)}, u32[]{:S(2)}) collective-permute-start(bf16[512,2304]{1,0:T(8,128)(2,1)} %shard_map.211), channel_id=1, source_target_pairs={{0,2},{2,0},{4,6},{6,4},{8,10},{10,8},{12,14},{14,12},{16,18},{18,... | collective-permute-start | bytes 7077896 | tf_op jit(solution)/shard_map/ppermute | solution.py:373
  410.4 108.2 %collective-permute-start.38 = (bf16[512,768]{1,0:T(8,128)(2,1)}, bf16[512,768]{1,0:T(8,128)(2,1)}, u32[]{:S(2)}, u32[]{:S(2)}) collective-permute-start(bf16[512,768]{1,0:T(8,128)(2,1)} %shard_map.214), channel_id=1, source_target_pairs={{0,16},{2,18},{4,20},{6,22},{8,24},{10,26},{12,28},{14,30},{16,0},... | collective-permute-start | bytes 2359304 | tf_op jit(solution)/shard_map/ppermute | solution.py:373
  411.0 53.2 %all-to-all-start.8 = ((bf16[4,128,2048]{2,1,0:T(8,128)(2,1)}), bf16[4,128,2048]{2,1,0:T(8,128)(2,1)}, u32[]{:S(2)}, u32[]{:S(2)}) async-start(bf16[4,128,2048]{2,1,0:T(8,128)(2,1)} %bitcast.27), calls=%async_computation.8 | async-start | bytes 4194304 | tf_op jit(solution)/shard_map/all_to_all | solution.py:413
  438.7 33.0 %collective-permute-start.26 = (bf16[512,2048]{1,0:T(8,128)(2,1)}, bf16[512,2048]{1,0:T(8,128)(2,1)}, u32[]{:S(2)}, u32[]{:S(2)}) collective-permute-start(bf16[512,2048]{1,0:T(8,128)(2,1)} %bitcast.132), channel_id=1, source_target_pairs={{0,1},{1,0},{2,3},{3,2},{4,5},{5,4},{6,7},{7,6},{8,9},{9,8},{10,11... | collective-permute-start | bytes 6291464 | tf_op jit(solution)/shard_map/ppermute | solution.py:376
  438.8 79.1 %collective-permute-start.27 = (bf16[512,768]{1,0:T(8,128)(2,1)}, bf16[512,768]{1,0:T(8,128)(2,1)}, u32[]{:S(2)}, u32[]{:S(2)}) collective-permute-start(bf16[512,768]{1,0:T(8,128)(2,1)} %shard_map.215), channel_id=1, source_target_pairs={{0,16},{2,18},{4,20},{6,22},{8,24},{10,26},{12,28},{14,30},{16,0},... | collective-permute-start | bytes 2359304 | tf_op jit(solution)/shard_map/ppermute | solution.py:373
  445.2 21.1 %copy-start.5 = (f32[128,2048]{1,0:T(8,128)S(1)}, f32[128,2048]{1,0:T(8,128)}, u32[]{:S(2)}) copy-start(f32[128,2048]{1,0:T(8,128)} %copy-done.3) | copy-start | bytes 3145732
  445.3 40.1 %collective-permute-start.36 = (bf16[512,1024]{1,0:T(8,128)(2,1)}, bf16[512,1024]{1,0:T(8,128)(2,1)}, u32[]{:S(2)}, u32[]{:S(2)}) collective-permute-start(bf16[512,1024]{1,0:T(8,128)(2,1)} %shard_map.217), channel_id=1, source_target_pairs={{0,2},{2,0},{4,6},{6,4},{8,10},{10,8},{12,14},{14,12},{16,18},{18,... | collective-permute-start | bytes 3145736 | tf_op jit(solution)/shard_map/ppermute | solution.py:373
  475.4 40.3 %all-to-all-start.9 = ((bf16[4,128,2048]{2,1,0:T(8,128)(2,1)}), bf16[4,128,2048]{2,1,0:T(8,128)(2,1)}, u32[]{:S(2)}, u32[]{:S(2)}) async-start(bf16[4,128,2048]{2,1,0:T(8,128)(2,1)} %fusion), calls=%async_computation.9 | async-start | bytes 4194304 | tf_op jit(solution)/shard_map/all_to_all | solution.py:413
  484.6 80.7 %collective-permute-start.35 = (bf16[512,1024]{1,0:T(8,128)(2,1)}, bf16[512,1024]{1,0:T(8,128)(2,1)}, u32[]{:S(2)}, u32[]{:S(2)}) collective-permute-start(bf16[512,1024]{1,0:T(8,128)(2,1)} %shard_map.218), channel_id=1, source_target_pairs={{0,2},{2,0},{4,6},{6,4},{8,10},{10,8},{12,14},{14,12},{16,18},{18,... | collective-permute-start | bytes 3145736 | tf_op jit(solution)/shard_map/ppermute | solution.py:373
  490.2 27.7 %copy-start.7 = (f32[128,2048]{1,0:T(8,128)S(1)}, f32[128,2048]{1,0:T(8,128)}, u32[]{:S(2)}) copy-start(f32[128,2048]{1,0:T(8,128)} %copy-done.6) | copy-start | bytes 3145732
  490.2 27.7 %copy-start.24 = (f32[1,2,2,2,2,128]{5,4,3,2,1,0:T(2,128)S(1)}, f32[1,2,2,2,2,128]{5,4,3,2,1,0:T(2,128)}, u32[]{:S(2)}) copy-start(f32[1,2,2,2,2,128]{5,4,3,2,1,0:T(2,128)} %copy-done.23) | copy-start | bytes 24580
  490.2 27.7 %copy-start.37 = (f32[128]{0:T(128)S(1)}, f32[128]{0:T(128)}, u32[]{:S(2)}) copy-start(f32[128]{0:T(128)} %copy-done.36) | copy-start | bytes 1540
  490.2 27.7 %copy-start.39 = (f32[128]{0:T(128)S(1)}, f32[128]{0:T(128)}, u32[]{:S(2)}) copy-start(f32[128]{0:T(128)} %copy-done.38) | copy-start | bytes 1540
  490.2 28.2 %copy-start.28 = (f32[2048]{0:T(1024)S(1)}, f32[2048]{0:T(1024)}, u32[]{:S(2)}) copy-start(f32[2048]{0:T(1024)} %get-tuple-element.147) | copy-start | bytes 24580
  490.2 28.2 %copy-start.27 = (f32[2048]{0:T(1024)S(1)}, f32[2048]{0:T(1024)}, u32[]{:S(2)}) copy-start(f32[2048]{0:T(1024)} %get-tuple-element.153) | copy-start | bytes 24580
  490.2 75.0 %collective-permute-start.37 = (bf16[512,1024]{1,0:T(8,128)(2,1)}, bf16[512,1024]{1,0:T(8,128)(2,1)}, u32[]{:S(2)}, u32[]{:S(2)}) collective-permute-start(bf16[512,1024]{1,0:T(8,128)(2,1)} %shard_map.219), channel_id=1, source_target_pairs={{0,16},{2,18},{4,20},{6,22},{8,24},{10,26},{12,28},{14,30},{16,0},... | collective-permute-start | bytes 3145736 | tf_op jit(solution)/shard_map/ppermute | solution.py:373
  518.6 10.2 %collective-permute-start.28 = (f32[7,2048]{1,0:T(8,128)S(1)}, f32[7,2048]{1,0:T(8,128)S(1)}, u32[]{:S(2)}, u32[]{:S(2)}) collective-permute-start(f32[7,2048]{1,0:T(8,128)S(1)} %pad_maximum_fusion.5), channel_id=1, source_target_pairs={{0,1},{1,0},{2,3},{3,2},{4,5},{5,4},{6,7},{7,6},{8,9},{9,8},{10,11... | collective-permute-start | bytes 172040 | tf_op jit(solution)/shard_map/ppermute | solution.py:376
  528.8 12.8 %collective-permute-start.31 = (f32[7,2048]{1,0:T(8,128)S(1)}, f32[7,2048]{1,0:T(8,128)S(1)}, u32[]{:S(2)}, u32[]{:S(2)}) collective-permute-start(f32[7,2048]{1,0:T(8,128)S(1)} %fusion.20), channel_id=1, source_target_pairs={{0,12},{2,14},{4,8},{6,10},{8,4},{10,6},{12,0},{14,2},{16,28},{18,... | collective-permute-start | bytes 172040 | tf_op jit(solution)/shard_map/ppermute | solution.py:373
  529.3 12.3 %collective-permute-start.30 = (f32[7,2048]{1,0:T(8,128)S(1)}, f32[7,2048]{1,0:T(8,128)S(1)}, u32[]{:S(2)}, u32[]{:S(2)}) collective-permute-start(f32[7,2048]{1,0:T(8,128)S(1)} %fusion.20), channel_id=1, source_target_pairs={{0,8},{2,10},{4,12},{6,14},{8,0},{10,2},{12,4},{14,6},{16,24},{18,... | collective-permute-start | bytes 172040 | tf_op jit(solution)/shard_map/ppermute | solution.py:373
  531.8 9.9 %collective-permute-start.29 = (f32[7,2048]{1,0:T(8,128)S(1)}, f32[7,2048]{1,0:T(8,128)S(1)}, u32[]{:S(2)}, u32[]{:S(2)}) collective-permute-start(f32[7,2048]{1,0:T(8,128)S(1)} %fusion.20), channel_id=1, source_target_pairs={{0,4},{2,6},{4,0},{6,2},{8,12},{10,14},{12,8},{14,10},{16,20},{18,... | collective-permute-start | bytes 172040 | tf_op jit(solution)/shard_map/ppermute | solution.py:373
  532.4 38.0 %all-to-all-start.10 = ((bf16[4,128,2304]{2,1,0:T(8,128)(2,1)}), bf16[4,128,2304]{2,1,0:T(8,128)(2,1)}, u32[]{:S(2)}, u32[]{:S(2)}) async-start(bf16[4,128,2304]{2,1,0:T(8,128)(2,1)} %bitcast.83), calls=%async_computation.10 | async-start | bytes 4718592 | tf_op jit(solution)/shard_map/all_to_all | solution.py:413
  541.7 22.8 %collective-permute-start.34 = (f32[7,2048]{1,0:T(8,128)S(1)}, f32[7,2048]{1,0:T(8,128)S(1)}, u32[]{:S(2)}, u32[]{:S(2)}) collective-permute-start(f32[7,2048]{1,0:T(8,128)S(1)} %add_add_fusion.1), channel_id=1, source_target_pairs={{0,18},{2,16},{4,22},{6,20},{8,26},{10,24},{12,30},{14,28},{16,2},... | collective-permute-start | bytes 172040 | tf_op jit(solution)/shard_map/ppermute | solution.py:373
  543.1 21.4 %collective-permute-start.33 = (f32[7,2048]{1,0:T(8,128)S(1)}, f32[7,2048]{1,0:T(8,128)S(1)}, u32[]{:S(2)}, u32[]{:S(2)}) collective-permute-start(f32[7,2048]{1,0:T(8,128)S(1)} %add_add_fusion.1), channel_id=1, source_target_pairs={{0,2},{2,0},{4,6},{6,4},{8,10},{10,8},{12,14},{14,12},{16,18},{18,... | collective-permute-start | bytes 172040 | tf_op jit(solution)/shard_map/ppermute | solution.py:373
  543.7 21.5 %collective-permute-start.32 = (f32[7,2048]{1,0:T(8,128)S(1)}, f32[7,2048]{1,0:T(8,128)S(1)}, u32[]{:S(2)}, u32[]{:S(2)}) collective-permute-start(f32[7,2048]{1,0:T(8,128)S(1)} %add_add_fusion.1), channel_id=1, source_target_pairs={{0,16},{2,18},{4,20},{6,22},{8,24},{10,26},{12,28},{14,30},{16,0},... | collective-permute-start | bytes 172040 | tf_op jit(solution)/shard_map/ppermute | solution.py:373
  570.3 19.3 %all-to-all-start.11 = ((bf16[4,128,1024]{2,1,0:T(8,128)(2,1)}), bf16[4,128,1024]{2,1,0:T(8,128)(2,1)S(1)}, u32[]{:S(2)}, u32[]{:S(2)}) async-start(bf16[4,128,1024]{2,1,0:T(8,128)(2,1)} %bitcast.101), calls=%async_computation.11 | async-start | bytes 2097152 | tf_op jit(solution)/shard_map/all_to_all | solution.py:413
  (34 other events, 188.7 us)

commit v5 on v4

--- a/solution.py
+++ b/solution.py
@@ -20,13 +20,6 @@
 BF = jnp.bfloat16
 F32 = jnp.float32
 VMEM_LIMIT = 60 * 1024 * 1024
-
-
-def doc_positions(segment):
-    token_index = jnp.arange(segment.shape[0], dtype=jnp.int32)
-    begins = jnp.concatenate([jnp.ones((1,), dtype=jnp.bool_), segment[1:] != segment[:-1]])
-    starts = lax.cummax(jnp.where(begins, token_index, jnp.zeros_like(token_index)), axis=0)
-    return token_index - starts
 
 
 def norm_parts(values, gain, shift):
@@ -177,10 +170,10 @@
     return value * cosine + (ahead * lead + behind * tail) * sign
 
 
-def soft(queries, keys, mask):
-    scores = dot(queries, keys, 1, 1) * score_scale + mask
-    weights = jnp.exp(scores - jnp.max(scores, axis=-1, keepdims=True))
-    return weights * (1.0 / jnp.sum(weights, axis=-1, keepdims=True))
+def soft(left, right, mask, axis):
+    scores = dot(left, right, 1, 1) * score_scale + mask
+    weights = jnp.exp(scores - jnp.max(scores, axis=axis, keepdims=True))
+    return weights * (1.0 / jnp.sum(weights, axis=axis, keepdims=True))
 
 
 def own_head(half):
@@ -210,7 +203,7 @@
         mixed = None
         for half in range(LANES // HD):
             here = own_head(half)
-            probs = soft(jnp.where(here, queries, 0).astype(BF), keys, mask).astype(BF)
+            probs = soft(jnp.where(here, queries, 0).astype(BF), keys, mask, 1).astype(BF)
             part = dot(probs, values, 1, 0)
             mixed = part if mixed is None else jnp.where(here, part, mixed)
         mixed_ref[:, i * LANES : (i + 1) * LANES] = mixed.astype(BF)
@@ -240,14 +233,14 @@
         found = [None] * 3
         for half in range(LANES // HD):
             here = own_head(half)
-            probs = soft(jnp.where(here, queries, 0).astype(BF), keys, mask)
-            value_grad = dot(probs.astype(BF), grad, 0, 0)
-            prob_grad = dot(jnp.where(here, grad, 0).astype(BF), values, 1, 1)
+            probs = soft(keys, jnp.where(here, queries, 0).astype(BF), mask, 0)
+            value_grad = dot(probs.astype(BF), grad, 1, 0)
+            prob_grad = dot(values, jnp.where(here, grad, 0).astype(BF), 1, 1)
             score_grad = (
-                probs * (prob_grad - jnp.sum(probs * prob_grad, axis=-1, keepdims=True))
+                probs * (prob_grad - jnp.sum(probs * prob_grad, axis=0, keepdims=True))
             ).astype(BF)
-            query_grad = dot(score_grad, keys, 1, 0)
-            key_grad = dot(score_grad, queries, 0, 0)
+            query_grad = dot(score_grad, keys, 0, 0)
+            key_grad = dot(score_grad, queries, 1, 0)
             parts = (query_grad, key_grad, value_grad)
             found = [p if f is None else jnp.where(here, p, f) for p, f in zip(parts, found)]
         lin_ref[:, at[0]] = turn(found[0] * score_scale, tables, -1.0).astype(BF)
@@ -498,12 +491,15 @@
     mlp_shard = exchange(tie(mlp_pack, attn_shard))
     w_attn = gather(attn_shard)
     tiles = hidden_cols // TILE
-    spots = jax.vmap(doc_positions)(segs)
-    segs, spots = (jnp.where(core == 1, jnp.roll(v, rows, axis=1), v) for v in (segs, spots))
+    segs = tie(segs, w_attn[2])
+    segs = jnp.where(core == 1, jnp.roll(segs, rows, axis=1), segs)
     index = jnp.arange(seq_len, dtype=jnp.int32)
     index = jnp.where(core == 1, jnp.roll(index, rows), index)
+    spots = index - jnp.sum(segs[:, None, :] < segs[:, :, None], axis=2, dtype=jnp.int32)
     allowed = (segs[:, :, None] == segs[:, None, :]) & (index[None, :] <= index[:, None])
     mask = jnp.where(allowed, 0.0, masked_score).astype(F32)
+    allowed_back = (segs[:, :, None] == segs[:, None, :]) & (index[None, :] >= index[:, None])
+    mask_back = jnp.where(allowed_back, 0.0, masked_score).astype(F32)
     dim = jnp.arange(LANES, dtype=jnp.int32) % HD
     pair = (dim % (ROT // 2)).astype(F32)
     speed = jnp.where(dim < ROT, rope_base ** (-2.0 * pair / ROT), 0.0)
@@ -518,7 +514,7 @@
         shard = mlp_shard[:, t * 3 * TILE : (t + 1) * 3 * TILE]
         w_mlp.append(gather(shard, after, after_own))
         after, after_own = [w_mlp[t][1]], [w_mlp[t][2]]
-    grad_local = to_rel(tie(out_grad))
+    grad_local = to_rel(tie(out_grad, w_attn[2]))
     grad_copies = copies(grad_local)
     heard = spread(
         tie(copies(seq_local), grad_copies, cosine, lead, tail, mask),
@@ -554,8 +550,8 @@
         scratch=[lines, pltpu.VMEM((seq_len, head_cols), BF)],
     )
     mixed = [half(mixed_own), half(mixed_sib)]
-    both = merge(*map(half, terms), w_mlp[0][2:3] + [])
-    attn_sum = collect(both, [grad_rows[0]] + [])
+    both = merge(*map(half, terms), w_mlp[0][2:3])
+    attn_sum = collect(both, [grad_rows[0]])
     resid_two = resid + tie(
         attn_sum, *w_mlp[0][3:], *w_mlp[1][1:2], *w_mlp[1][2:3]
     )
@@ -642,8 +638,8 @@
         cost=SHORT,
     )
     out_both = merge(*out_terms)
-    attn_grad = spread(copied, [], [out_both] + later + later_came[:1] + [])
-    ins = [*attn_grad, qkv] + facts + w_attn
+    attn_grad = spread(copied, [], [out_both] + later + later_came[:1])
+    ins = [*attn_grad, qkv, mask_back] + facts[1:] + w_attn
     outs = [lin_shape, lin_shape, shaped((group, 1, 3 * head_cols), F32), term3, term3]
     lin_own, lin_sib, bias_sums, *terms = call(
         functools.partial(attend_back_kernel, len(w_attn)),
@@ -671,7 +667,7 @@
     attn_adds = [[] for _ in range(far)]
     parts, attn_sent = [], []
     for n, i in enumerate(wide):
-        after = (([] + parts) if attn_adds[i] else [both] + parts) if n else []
+        after = (parts if attn_adds[i] else [both] + parts) if n else []
         part = block_grad(i, attn_kinds, [(v, 0) for v in attn_adds[i]], after)
         parts.append(part)
         attn_sent.append(send(i, part))

time: 604 us -> 596 us (0.987)
  waiting for transfers between devices: 268 us -> 259 us
    ppermute x31, waiting for transfers between devices: 138 us -> 114 us  [swap(): return lax.ppermute(array, 'dp', [(d, d ^ mask) for d in range(dp_size)])]
    all_to_all x12, waiting for transfers between devices: 122 us -> 138 us  [exchange(): lax.all_to_all(rows_by_rank, 'dp', 0, 0, axis_index_groups=bands, tiled=T...]
  transfers between devices with their start and end apart: 52 -> 52, of which waited for: 21 -> 22; matrix products, arithmetic and copies ran while one was open for 12% -> 13% of each run, Pallas kernels for 22% -> 22%
where the time goes in v5:
time: 596 us; the launch traced here: 590 us
  waiting for transfers between devices  259 us (43%)
  Pallas kernels  149 us (25%)
  starting transfers between devices  91.8 us (15%)
  other arithmetic  53.7 us (9%)
  local copies, waits for them, and re-layouts  34.9 us (6%)
    pallas_call x21, Pallas kernels, call(): pl.pallas_call(kernel, grid=grid, in_specs=in_specs or [whole(v.shape) fo...  149 us
    all_to_all x12, waiting for transfers between devices, exchange(): lax.all_to_all(rows_by_rank, 'dp', 0, 0, axis_index_groups=bands, tiled=T...  138 us
    ppermute x31, waiting for transfers between devices, swap(): return lax.ppermute(array, 'dp', [(d, d ^ mask) for d in range(dp_size)])  114 us
    all_to_all x12, starting transfers between devices, exchange(): lax.all_to_all(rows_by_rank, 'dp', 0, 0, axis_index_groups=bands, tiled=T...  53.9 us
    ppermute x31, starting transfers between devices, swap(): return lax.ppermute(array, 'dp', [(d, d ^ mask) for d in range(dp_size)])  37.3 us
    convert_element_type x4, other arithmetic, merge(): return (by_block(mine).astype(F32) + by_block(other).astype(F32)).astype(BF)  15 us
  transfers between devices with their start and end apart: 52, of which 22 were waited for; matrix products, arithmetic and copies ran while one was open for 13% of the time, Pallas kernels for 22%

profile of v5, /device:TPU:0, one launch (start us, length us, event | category | flops | bytes accessed | tf_op | source)
XLA Modules:
  0.0 590.4 jit_solution(7293952667875769292)
XLA Ops:
  0.7 2.4 shard_map.203
  3.1 5.4 all-to-all-start
  14.4 8.3 %all-to-all-done = bf16[4,128,1024]{2,1,0:T(8,128)(2,1)} async-done(((bf16[4,128,1024]{2,1,0:T(8,128)(2,1)}), bf16[4,128,1024]{2,1,0:T(8,128)(2,1)}, u32[]{:S(2)}, u32[]{:S(2)}) %all-to-all-start) | async-done | bytes 1048608 | tf_op jit(solution)/shard_map/all_to_all | solution.py:406
  29.7 2.6 collective-permute-start.4
  32.3 3.3 shard_map.204
  35.6 3.8 all-to-all-start.1
  39.4 7.9 %collective-permute-done.refs_2_ = bf16[512,1024]{1,0:T(8,128)(2,1)} collective-permute-done((bf16[512,1024]{1,0:T(8,128)(2,1)}, bf16[512,1024]{1,0:T(8,128)(2,1)}, u32[]{:S(2)}, u32[]{:S(2)}) %collective-permute-start) | collective-permute-done | bytes 1048608 | tf_op jit(solution)/shard_map/ppermute | solution.py:366
  62.7 2.6 copy.38
  65.3 2.3 reshape.422
  67.5 3.9 fusion.4
  71.4 2.4 fusion.3
  77.4 9.8 %all-to-all-done.1 = bf16[4,128,2304]{2,1,0:T(8,128)(2,1)S(1)} async-done(((bf16[4,128,2304]{2,1,0:T(8,128)(2,1)}), bf16[4,128,2304]{2,1,0:T(8,128)(2,1)S(1)}, u32[]{:S(2)}, u32[]{:S(2)}) %all-to-all-start.1) | async-done | bytes 2359328 | tf_op jit(solution)/shard_map/all_to_all | solution.py:406
  87.2 4.4 all-to-all-start.2
  94.6 20.8 %collective-permute-done.5.refs_3_ = bf16[512,1024]{1,0:T(8,128)(2,1)} collective-permute-done((bf16[512,1024]{1,0:T(8,128)(2,1)}, bf16[512,1024]{1,0:T(8,128)(2,1)}, u32[]{:S(2)}, u32[]{:S(2)}) %collective-permute-start.5) | collective-permute-done | bytes 1048608 | tf_op jit(solution)/shard_map/ppermute | solution.py:366
  115.3 14.5 %collective-permute-done.6.refs_5_.refs_7_ = bf16[512,768]{1,0:T(8,128)(2,1)} collective-permute-done((bf16[512,768]{1,0:T(8,128)(2,1)S(1)}, bf16[512,768]{1,0:T(8,128)(2,1)}, u32[]{:S(2)}, u32[]{:S(2)}) %collective-permute-start.6) | collective-permute-done | bytes 786464 | tf_op jit(solution)/shard_map/ppermute | solution.py:366
  129.8 2.3 all-to-all-done.2.own_ref
  133.4 4.1 all-to-all-start.3
  137.4 16.9 %shard_map.205 = (bf16[4,256,768]{2,1,0:T(8,128)(2,1)}, bf16[4,128,256]{2,1,0:T(8,128)(2,1)}, bf16[4,128,256]{2,1,0:T(8,128)(2,1)}, bf16[4,128,2048]{2,1,0:T(8,128)(2,1)}, bf16[4,128,2048]{2,1,0:T(8,128)(2,1)}) custom-call(bf16[4,128,2048]{2,1,0:T(8,128)(2,1)} %all-to-all-done.2.own_ref, bf16[4,128,2048]{2,1,0:T(8,128)(2,1)} %collective-permute-done.7.sib_ref, ...), custom_call_target="tpu_custom_call" | custom-call | flops 128849018880 | bytes 519137280 | tf_op jit(solution)/shard_map/pallas_call | solution.py:68
  154.6 4.1 collective-permute-done.9
  158.8 3.7 fusion.1
  164.3 3.7 all-to-all-start.4
  171.3 38.7 %all-to-all-done.4 = bf16[4,128,2048]{2,1,0:T(8,128)(2,1)S(1)} async-done(((bf16[4,128,2048]{2,1,0:T(8,128)(2,1)}), bf16[4,128,2048]{2,1,0:T(8,128)(2,1)S(1)}, u32[]{:S(2)}, u32[]{:S(2)}) %all-to-all-start.4) | async-done | bytes 2097184 | tf_op jit(solution)/shard_map/all_to_all | solution.py:406
  213.5 4.7 all-to-all-start.5
  221.3 18.7 %collective-permute-done.13.refs_11_.refs_13_ = bf16[512,768]{1,0:T(8,128)(2,1)S(1)} collective-permute-done((bf16[512,768]{1,0:T(8,128)(2,1)}, bf16[512,768]{1,0:T(8,128)(2,1)S(1)}, u32[]{:S(2)}, u32[]{:S(2)}) %collective-permute-start.13) | collective-permute-done | bytes 786464 | tf_op jit(solution)/shard_map/ppermute | solution.py:366
  239.9 17.4 %collective-permute-done.14.refs_7_.refs_15_ = bf16[512,768]{1,0:T(8,128)(2,1)S(1)} collective-permute-done((bf16[512,768]{1,0:T(8,128)(2,1)S(1)}, bf16[512,768]{1,0:T(8,128)(2,1)S(1)}, u32[]{:S(2)}, u32[]{:S(2)}) %collective-permute-start.14) | collective-permute-done | bytes 786464 | tf_op jit(solution)/shard_map/ppermute | solution.py:366
  260.9 3.1 collective-permute-done.16
  264.0 17.1 %shard_map.206 = (bf16[512,512]{1,0:T(8,128)(2,1)}, bf16[512,512]{1,0:T(8,128)(2,1)}, bf16[512,256]{1,0:T(8,128)(2,1)}, bf16[512,256]{1,0:T(8,128)(2,1)}, bf16[5...) custom-call(bf16[512,2048]{1,0:T(8,128)(2,1)} %bitcast.21.refs_0_.re, ...), custom_call_target="tpu_custom_call" | custom-call | flops 322122547200 | bytes 880803840 | tf_op jit(solution)/shard_map/pallas_call | solution.py:68
  281.1 13.7 %shard_map.207 = (bf16[512,512]{1,0:T(8,128)(2,1)}, bf16[512,512]{1,0:T(8,128)(2,1)}, bf16[512,256]{1,0:T(8,128)(2,1)}, bf16[512,256]{1,0:T(8,128)(2,1)}, bf16[5...) custom-call(bf16[512,2048]{1,0:T(8,128)(2,1)} %bitcast.21.refs_0_.refs_8_.refs_16_, ...), custom_call_target="tpu_custom_call" | custom-call | flops 161061273600 | bytes 817889280 | tf_op jit(solution)/shard_map/pallas_call | solution.py:68
  295.0 4.1 shard_map.208
  300.5 3.8 add_convert_fusion.1
  304.4 3.9 shard_map.209
  308.9 3.9 shard_map.210
  314.2 4.3 all-to-all-start.6
  318.5 8.7 %shard_map.211 = bf16[512,2304]{1,0:T(8,128)(2,1)} custom-call(bf16[512,2048]{1,0:T(8,128)(2,1)} %bitcast.21.refs_0_.refs_8_.refs_16_, bf16[512,2048]{1,0:T(8,128)(2,1)} %bitcast.22.refs_1_.refs_9_.refs_17_, bf16[512,512]{1,0:T(8,128)(2,1)} %get-tuple-element.107.refs_2_, bf16[512,512]{1,0:T(8,128)(2,1)} %get-tuple-element.108.refs_3_, ...), custom_call_target="tpu_custom_call" | custom-call | flops 72477573120 | bytes 967311360 | tf_op jit(solution)/shard_map/pallas_call | solution.py:68
  327.3 15.8 %all-to-all-done.6 = bf16[4,128,2048]{2,1,0:T(8,128)(2,1)S(1)} async-done(((bf16[4,128,2048]{2,1,0:T(8,128)(2,1)}), bf16[4,128,2048]{2,1,0:T(8,128)(2,1)S(1)}, u32[]{:S(2)}, u32[]{:S(2)}) %all-to-all-start.6) | async-done | bytes 2097184 | tf_op jit(solution)/shard_map/all_to_all | solution.py:406
  347.8 4.2 shard_map.213
  353.8 7.1 %shard_map.212 = (bf16[512,2048]{1,0:T(8,128)(2,1)}, bf16[512,2048]{1,0:T(8,128)(2,1)}) custom-call(bf16[512,256]{1,0:T(8,128)(2,1)} %get-tuple-element.122.refs_6_.refs_0_, bf16[512,256]{1,0:T(8,128)(2,1)} %get-tuple-element.109.refs_7_.refs_1_, bf16[512,256]{1,0:T(8,128)(2,1)} %get-tuple-element.113.refs_6_.refs_14_.refs_2_, ...), custom_call_target="tpu_custom_call" | custom-call | tf_op jit(solution)/shard_map/pallas_call | solution.py:68
  360.9 4.4 all-to-all-start.7
  365.3 4.2 shard_map.214
  369.6 4.3 shard_map.215
  373.9 3.8 add_convert_fusion
  377.7 10.9 %collective-permute-done.24.refs_24_ = bf16[512,768]{1,0:T(8,128)(2,1)S(1)} collective-permute-done((bf16[512,768]{1,0:T(8,128)(2,1)}, bf16[512,768]{1,0:T(8,128)(2,1)S(1)}, u32[]{:S(2)}, u32[]{:S(2)}) %collective-permute-start.24) | collective-permute-done | bytes 786464 | tf_op jit(solution)/shard_map/ppermute | solution.py:366
  388.6 17.5 %all-to-all-done.7.own_ref = bf16[4,128,2048]{2,1,0:T(8,128)(2,1)} async-done(((bf16[4,128,2048]{2,1,0:T(8,128)(2,1)}), bf16[4,128,2048]{2,1,0:T(8,128)(2,1)}, u32[]{:S(2)}, u32[]{:S(2)}) %all-to-all-start.7) | async-done | bytes 2097184 | tf_op jit(solution)/shard_map/all_to_all | solution.py:406
  407.6 5.1 all-to-all-start.8
  414.0 19.5 %shard_map.216 = (bf16[4,128,768]{2,1,0:T(8,128)(2,1)}, bf16[4,128,768]{2,1,0:T(8,128)(2,1)}, f32[4,1,768]{2,1,0:T(1,128)}, bf16[4,128,2048]{2,1,0:T(8,128)(2,1)}, bf16[4,128,2048]{2,1,0:T(8,128)(2,1)}) custom-call(bf16[4,128,2048]{2,1,0:T(8,128)(2,1)} %all-to-all-done.7.own_ref, bf16[4,128,2048]{2,1,0:T(8,128)(2,1)} %copy-done.51, ...), custom_call_target="tpu_custom_call" | custom-call | flops 128849018880 | bytes 550871040 | tf_op jit(solution)/shard_map/pallas_call | solution.py:68
  435.4 4.4 shard_map.217
  441.3 19.5 %all-to-all-done.8 = bf16[4,128,2048]{2,1,0:T(8,128)(2,1)} async-done(((bf16[4,128,2048]{2,1,0:T(8,128)(2,1)}), bf16[4,128,2048]{2,1,0:T(8,128)(2,1)}, u32[]{:S(2)}, u32[]{:S(2)}) %all-to-all-start.8) | async-done | bytes 2097184 | tf_op jit(solution)/shard_map/all_to_all | solution.py:406
  468.4 3.7 fusion
  472.0 4.7 all-to-all-start.9
  476.8 4.4 shard_map.218
  482.6 4.8 shard_map.219
  488.5 23.0 %all-to-all-done.9 = bf16[4,128,2048]{2,1,0:T(8,128)(2,1)} async-done(((bf16[4,128,2048]{2,1,0:T(8,128)(2,1)}), bf16[4,128,2048]{2,1,0:T(8,128)(2,1)}, u32[]{:S(2)}, u32[]{:S(2)}) %all-to-all-start.9) | async-done | bytes 2097184 | tf_op jit(solution)/shard_map/all_to_all | solution.py:406
  514.4 10.1 %shard_map.221 = bf16[512,2304]{1,0:T(8,128)(2,1)} custom-call(bf16[512,2048]{1,0:T(8,128)(2,1)} %bitcast.21.refs_0_.refs_8_.refs_16_, bf16[512,2048]{1,0:T(8,128)(2,1)} %bitcast.22.refs_1_.refs_9_.refs_17_, bf16[512,512]{1,0:T(8,128)(2,1)} %get-tuple-element.107.refs_2_, bf16[512,512]{1,0:T(8,128)(2,1)} %get-tuple-element.108.refs_3_, ...), custom_call_target="tpu_custom_call" | custom-call | flops 72477573120 | bytes 1108869120 | tf_op jit(solution)/shard_map/pallas_call | solution.py:68
  525.0 2.5 collective-permute-start.30
  528.1 4.5 all-to-all-start.10
  532.6 6.2 %collective-permute-done.31 = f32[7,2048]{1,0:T(8,128)S(1)} collective-permute-done((f32[7,2048]{1,0:T(8,128)S(1)}, f32[7,2048]{1,0:T(8,128)S(1)}, u32[]{:S(2)}, u32[]{:S(2)}) %collective-permute-start.31) | collective-permute-done | bytes 57376 | tf_op jit(solution)/shard_map/ppermute | solution.py:366
  541.1 2.1 collective-permute-start.32
  543.3 17.0 %collective-permute-done.34 = f32[7,2048]{1,0:T(8,128)S(1)} collective-permute-done((f32[7,2048]{1,0:T(8,128)S(1)}, f32[7,2048]{1,0:T(8,128)S(1)}, u32[]{:S(2)}, u32[]{:S(2)}) %collective-permute-start.34) | collective-permute-done | bytes 57376 | tf_op jit(solution)/shard_map/ppermute | solution.py:366
  561.0 5.1 shard_map.220
  567.0 4.7 all-to-all-start.11
  571.7 2.7 multiply_add_fusion
  574.4 2.1 reshape.433
  582.1 4.1 shard_map.223
  587.1 2.7 shard_map.222
  (271 shorter events, 91.8 us)
Async XLA Ops:
  0.6 131.5 %copy-start = (f32[3,1024]{1,0:T(4,128)S(1)}, f32[3,1024]{1,0:T(4,128)}, u32[]{:S(2)}) copy-start(f32[3,1024]{1,0:T(4,128)} %param.17) | copy-start | bytes 36868
  3.1 19.7 %all-to-all-start = ((bf16[4,128,1024]{2,1,0:T(8,128)(2,1)}), bf16[4,128,1024]{2,1,0:T(8,128)(2,1)}, u32[]{:S(2)}, u32[]{:S(2)}) async-start(bf16[4,128,1024]{2,1,0:T(8,128)(2,1)} %bitcast.75), calls=%async_computation | async-start | bytes 2097152 | tf_op jit(solution)/shard_map/all_to_all | solution.py:406
  8.4 20.6 %collective-permute-start.3 = (s32[256]{0:T(256)S(1)}, s32[256]{0:T(256)S(1)}, u32[]{:S(2)}, u32[]{:S(2)}) collective-permute-start(s32[256]{0:T(256)S(1)} %copy-done.50), channel_id=1, source_target_pairs={{0,4},{2,6},{4,0},{6,2},{8,12},{10,14},{12,8},{14,10},{16,20},{18,... | collective-permute-start | bytes 3080 | tf_op jit(solution)/shard_map/ppermute | solution.py:366
  10.5 18.5 %collective-permute-start.2 = (s32[256]{0:T(256)S(1)}, s32[256]{0:T(256)S(1)}, u32[]{:S(2)}, u32[]{:S(2)}) collective-permute-start(s32[256]{0:T(256)S(1)} %copy-done.50), channel_id=1, source_target_pairs={{0,12},{2,14},{4,8},{6,10},{8,4},{10,6},{12,0},{14,2},{16,28},{18,... | collective-permute-start | bytes 3080 | tf_op jit(solution)/shard_map/ppermute | solution.py:366
  12.0 17.0 %collective-permute-start.1 = (s32[256]{0:T(256)S(1)}, s32[256]{0:T(256)S(1)}, u32[]{:S(2)}, u32[]{:S(2)}) collective-permute-start(s32[256]{0:T(256)S(1)} %copy-done.50), channel_id=1, source_target_pairs={{0,8},{2,10},{4,12},{6,14},{8,0},{10,2},{12,4},{14,6},{16,24},{18,... | collective-permute-start | bytes 3080 | tf_op jit(solution)/shard_map/ppermute | solution.py:366
  22.7 24.6 %collective-permute-start = (bf16[512,1024]{1,0:T(8,128)(2,1)}, bf16[512,1024]{1,0:T(8,128)(2,1)}, u32[]{:S(2)}, u32[]{:S(2)}) collective-permute-start(bf16[512,1024]{1,0:T(8,128)(2,1)} %bitcast.9.refs_0_), channel_id=1, source_target_pairs={{0,2},{2,0},{4,6},{6,4},{8,10},{10,8},{12,14},{14,12},{16,18},{18,... | collective-permute-start | bytes 3145736 | tf_op jit(solution)/shard_map/ppermute | solution.py:366
  29.7 47.7 %collective-permute-start.4 = (bf16[512,1024]{1,0:T(8,128)(2,1)}, bf16[512,1024]{1,0:T(8,128)(2,1)}, u32[]{:S(2)}, u32[]{:S(2)}) collective-permute-start(bf16[512,1024]{1,0:T(8,128)(2,1)} %bitcast.9.refs_0_), channel_id=1, source_target_pairs={{0,16},{2,18},{4,20},{6,22},{8,24},{10,26},{12,28},{14,30},{16,0},... | collective-permute-start | bytes 3145736 | tf_op jit(solution)/shard_map/ppermute | solution.py:366
  35.6 51.6 %all-to-all-start.1 = ((bf16[4,128,2304]{2,1,0:T(8,128)(2,1)}), bf16[4,128,2304]{2,1,0:T(8,128)(2,1)S(1)}, u32[]{:S(2)}, u32[]{:S(2)}) async-start(bf16[4,128,2304]{2,1,0:T(8,128)(2,1)} %bitcast.71), calls=%async_computation.1 | async-start | bytes 4718592 | tf_op jit(solution)/shard_map/all_to_all | solution.py:406
  62.7 147.7 %copy-start.6 = (f32[128,2048]{1,0:T(8,128)}, f32[128,2048]{1,0:T(8,128)S(1)}, u32[]{:S(2)}) copy-start(f32[128,2048]{1,0:T(8,128)S(1)} %reshape.445) | copy-start | bytes 3145732
  87.2 44.9 %all-to-all-start.2 = ((bf16[4,128,2048]{2,1,0:T(8,128)(2,1)}), bf16[4,128,2048]{2,1,0:T(8,128)(2,1)}, u32[]{:S(2)}, u32[]{:S(2)}) async-start(bf16[4,128,2048]{2,1,0:T(8,128)(2,1)} %broadcast_in_dim.36), calls=%async_computation.2 | async-start | bytes 4194304 | tf_op jit(solution)/shard_map/all_to_all | solution.py:406
  91.6 23.7 %collective-permute-start.5 = (bf16[512,1024]{1,0:T(8,128)(2,1)}, bf16[512,1024]{1,0:T(8,128)(2,1)}, u32[]{:S(2)}, u32[]{:S(2)}) collective-permute-start(bf16[512,1024]{1,0:T(8,128)(2,1)} %collective-permute-done.4.refs_1_), channel_id=1, source_target_pairs={{0,2},{2,0},{4,6},{6,4},{8,10},{10,8},{12,14},{14,12},{16,18},{18,... | collective-permute-start | bytes 3145736 | tf_op jit(solution)/shard_map/ppermute | solution.py:366
  94.6 35.3 %collective-permute-start.6 = (bf16[512,768]{1,0:T(8,128)(2,1)S(1)}, bf16[512,768]{1,0:T(8,128)(2,1)}, u32[]{:S(2)}, u32[]{:S(2)}) collective-permute-start(bf16[512,768]{1,0:T(8,128)(2,1)S(1)} %get-tuple-element.92), channel_id=1, source_target_pairs={{0,16},{2,18},{4,20},{6,22},{8,24},{10,26},{12,28},{14,30},{16,0},... | collective-permute-start | bytes 2359304 | tf_op jit(solution)/shard_map/ppermute | solution.py:366
  132.1 5.3 collective-permute-start.7
  132.7 21.6 %collective-permute-start.8 = (bf16[512,768]{1,0:T(8,128)(2,1)}, bf16[512,768]{1,0:T(8,128)(2,1)}, u32[]{:S(2)}, u32[]{:S(2)}) collective-permute-start(bf16[512,768]{1,0:T(8,128)(2,1)} %copy-done.19), channel_id=1, source_target_pairs={{0,2},{2,0},{4,6},{6,4},{8,10},{10,8},{12,14},{14,12},{16,18},{18,... | collective-permute-start | bytes 2359304 | tf_op jit(solution)/shard_map/ppermute | solution.py:366
  133.4 29.6 %all-to-all-start.3 = ((bf16[4,128,2048]{2,1,0:T(8,128)(2,1)}), bf16[4,128,2048]{2,1,0:T(8,128)(2,1)S(1)}, u32[]{:S(2)}, u32[]{:S(2)}) async-start(bf16[4,128,2048]{2,1,0:T(8,128)(2,1)} %broadcast_in_dim.37), calls=%async_computation.3 | async-start | bytes 4194304 | tf_op jit(solution)/shard_map/all_to_all | solution.py:406
  154.3 4.4 collective-permute-start.9
  164.3 45.6 %all-to-all-start.4 = ((bf16[4,128,2048]{2,1,0:T(8,128)(2,1)}), bf16[4,128,2048]{2,1,0:T(8,128)(2,1)S(1)}, u32[]{:S(2)}, u32[]{:S(2)}) async-start(bf16[4,128,2048]{2,1,0:T(8,128)(2,1)} %fusion.1), calls=%async_computation.4 | async-start | bytes 4194304 | tf_op jit(solution)/shard_map/all_to_all | solution.py:406
  168.0 42.4 %collective-permute-start.11 = (bf16[512,768]{1,0:T(8,128)(2,1)}, bf16[512,768]{1,0:T(8,128)(2,1)}, u32[]{:S(2)}, u32[]{:S(2)}) collective-permute-start(bf16[512,768]{1,0:T(8,128)(2,1)} %get-tuple-element.97), channel_id=1, source_target_pairs={{0,16},{2,18},{4,20},{6,22},{8,24},{10,26},{12,28},{14,30},{16,0},... | collective-permute-start | bytes 2359304 | tf_op jit(solution)/shard_map/ppermute | solution.py:366
  169.2 41.1 %collective-permute-start.10 = (bf16[512,768]{1,0:T(8,128)(2,1)}, bf16[512,768]{1,0:T(8,128)(2,1)}, u32[]{:S(2)}, u32[]{:S(2)}) collective-permute-start(bf16[512,768]{1,0:T(8,128)(2,1)} %collective-permute-done.6.refs_5_.refs_7_), channel_id=1, source_target_pairs={{0,2},{2,0},{4,6},{6,4},{8,10},{10,8},{12,14},{14,12},{16,18},{18,... | collective-permute-start | bytes 2359304 | tf_op jit(solution)/shard_map/ppermute | solution.py:366
  170.6 39.8 %collective-permute-start.12 = (bf16[512,768]{1,0:T(8,128)(2,1)}, bf16[512,768]{1,0:T(8,128)(2,1)}, u32[]{:S(2)}, u32[]{:S(2)}) collective-permute-start(bf16[512,768]{1,0:T(8,128)(2,1)} %get-tuple-element.97), channel_id=1, source_target_pairs={{0,2},{2,0},{4,6},{6,4},{8,10},{10,8},{12,14},{14,12},{16,18},{18,... | collective-permute-start | bytes 2359304 | tf_op jit(solution)/shard_map/ppermute | solution.py:366
  171.2 39.7 %copy-start.25 = (f32[1,2,2,2,2,128]{5,4,3,2,1,0:T(2,128)}, f32[1,2,2,2,2,128]{5,4,3,2,1,0:T(2,128)S(1)}, u32[]{:S(2)}) copy-start(f32[1,2,2,2,2,128]{5,4,3,2,1,0:T(2,128)S(1)} %copy.39) | copy-start | bytes 24580
  213.5 46.0 %all-to-all-start.5 = ((bf16[4,128,2048]{2,1,0:T(8,128)(2,1)}), bf16[4,128,2048]{2,1,0:T(8,128)(2,1)}, u32[]{:S(2)}, u32[]{:S(2)}) async-start(bf16[4,128,2048]{2,1,0:T(8,128)(2,1)} %broadcast_in_dim.72), calls=%async_computation.5 | async-start | bytes 4194304 | tf_op jit(solution)/shard_map/all_to_all | solution.py:406
  218.3 39.0 %collective-permute-start.14 = (bf16[512,768]{1,0:T(8,128)(2,1)S(1)}, bf16[512,768]{1,0:T(8,128)(2,1)S(1)}, u32[]{:S(2)}, u32[]{:S(2)}) collective-permute-start(bf16[512,768]{1,0:T(8,128)(2,1)S(1)} %copy-done.18), channel_id=1, source_target_pairs={{0,16},{2,18},{4,20},{6,22},{8,24},{10,26},{12,28},{14,30},{16,0},... | collective-permute-start | bytes 2359304 | tf_op jit(solution)/shard_map/ppermute | solution.py:366
  219.2 20.7 %collective-permute-start.13 = (bf16[512,768]{1,0:T(8,128)(2,1)}, bf16[512,768]{1,0:T(8,128)(2,1)S(1)}, u32[]{:S(2)}, u32[]{:S(2)}) collective-permute-start(bf16[512,768]{1,0:T(8,128)(2,1)} %collective-permute-done.11.refs_9_.refs_11_), channel_id=1, source_target_pairs={{0,2},{2,0},{4,6},{6,4},{8,10},{10,8},{12,14},{14,12},{16,18},{18,... | collective-permute-start | bytes 2359304 | tf_op jit(solution)/shard_map/ppermute | solution.py:366
  220.6 37.6 %collective-permute-start.15 = (bf16[512,768]{1,0:T(8,128)(2,1)S(1)}, bf16[512,768]{1,0:T(8,128)(2,1)}, u32[]{:S(2)}, u32[]{:S(2)}) collective-permute-start(bf16[512,768]{1,0:T(8,128)(2,1)S(1)} %copy-done.18), channel_id=1, source_target_pairs={{0,2},{2,0},{4,6},{6,4},{8,10},{10,8},{12,14},{14,12},{16,18},{18,... | collective-permute-start | bytes 2359304 | tf_op jit(solution)/shard_map/ppermute | solution.py:366
  221.3 39.7 %collective-permute-start.17 = (bf16[4,128,2048]{2,1,0:T(8,128)(2,1)S(1)}, bf16[4,128,2048]{2,1,0:T(8,128)(2,1)}, u32[]{:S(2)}, u32[]{:S(2)}) collective-permute-start(bf16[4,128,2048]{2,1,0:T(8,128)(2,1)S(1)} %copy-done.15), channel_id=1, source_target_pairs={{0,1},{1,0},{2,3},{3,2},{4,5},{5,4},{6,7},{7,6},{8,9},{9,8},{10,11... | collective-permute-start | bytes 6291464 | tf_op jit(solution)/shard_map/ppermute | solution.py:369
  239.9 17.4 %copy-start.21 = (bf16[512,768]{1,0:T(8,128)(2,1)}, bf16[512,768]{1,0:T(8,128)(2,1)S(1)}, u32[]{:S(2)}) copy-start(bf16[512,768]{1,0:T(8,128)(2,1)S(1)} %collective-permute-done.13.refs_11_.refs_13_) | copy-start | bytes 2359300
  259.5 4.5 collective-permute-start.16
  259.5 21.6 %collective-permute-start.18 = (bf16[512,768]{1,0:T(8,128)(2,1)}, bf16[512,768]{1,0:T(8,128)(2,1)}, u32[]{:S(2)}, u32[]{:S(2)}) collective-permute-start(bf16[512,768]{1,0:T(8,128)(2,1)} %copy-done.20), channel_id=1, source_target_pairs={{0,2},{2,0},{4,6},{6,4},{8,10},{10,8},{12,14},{14,12},{16,18},{18,... | collective-permute-start | bytes 2359304 | tf_op jit(solution)/shard_map/ppermute | solution.py:366
  294.8 5.7 collective-permute-start.19
  299.1 44.3 %collective-permute-start.20 = (bf16[512,768]{1,0:T(8,128)(2,1)}, bf16[512,768]{1,0:T(8,128)(2,1)}, u32[]{:S(2)}, u32[]{:S(2)}) collective-permute-start(bf16[512,768]{1,0:T(8,128)(2,1)} %shard_map.208), channel_id=1, source_target_pairs={{0,2},{2,0},{4,6},{6,4},{8,10},{10,8},{12,14},{14,12},{16,18},{18,... | collective-permute-start | bytes 2359304 | tf_op jit(solution)/shard_map/ppermute | solution.py:366
  308.3 57.0 %collective-permute-start.22 = (bf16[512,768]{1,0:T(8,128)(2,1)}, bf16[512,768]{1,0:T(8,128)(2,1)}, u32[]{:S(2)}, u32[]{:S(2)}) collective-permute-start(bf16[512,768]{1,0:T(8,128)(2,1)} %shard_map.209), channel_id=1, source_target_pairs={{0,2},{2,0},{4,6},{6,4},{8,10},{10,8},{12,14},{14,12},{16,18},{18,... | collective-permute-start | bytes 2359304 | tf_op jit(solution)/shard_map/ppermute | solution.py:366
  312.8 56.7 %collective-permute-start.23 = (bf16[512,768]{1,0:T(8,128)(2,1)}, bf16[512,768]{1,0:T(8,128)(2,1)}, u32[]{:S(2)}, u32[]{:S(2)}) collective-permute-start(bf16[512,768]{1,0:T(8,128)(2,1)} %shard_map.210), channel_id=1, source_target_pairs={{0,2},{2,0},{4,6},{6,4},{8,10},{10,8},{12,14},{14,12},{16,18},{18,... | collective-permute-start | bytes 2359304 | tf_op jit(solution)/shard_map/ppermute | solution.py:366
  314.2 28.8 %all-to-all-start.6 = ((bf16[4,128,2048]{2,1,0:T(8,128)(2,1)}), bf16[4,128,2048]{2,1,0:T(8,128)(2,1)S(1)}, u32[]{:S(2)}, u32[]{:S(2)}) async-start(bf16[4,128,2048]{2,1,0:T(8,128)(2,1)} %bitcast.25), calls=%async_computation.6 | async-start | bytes 4194304 | tf_op jit(solution)/shard_map/all_to_all | solution.py:406
  352.0 36.6 %collective-permute-start.24 = (bf16[512,768]{1,0:T(8,128)(2,1)}, bf16[512,768]{1,0:T(8,128)(2,1)S(1)}, u32[]{:S(2)}, u32[]{:S(2)}) collective-permute-start(bf16[512,768]{1,0:T(8,128)(2,1)} %shard_map.213), channel_id=1, source_target_pairs={{0,16},{2,18},{4,20},{6,22},{8,24},{10,26},{12,28},{14,30},{16,0},... | collective-permute-start | bytes 2359304 | tf_op jit(solution)/shard_map/ppermute | solution.py:366
  360.9 13.0 %collective-permute-start.21 = (bf16[512,2048]{1,0:T(8,128)(2,1)}, bf16[512,2048]{1,0:T(8,128)(2,1)}, u32[]{:S(2)}, u32[]{:S(2)}) collective-permute-start(bf16[512,2048]{1,0:T(8,128)(2,1)} %get-tuple-element.124), channel_id=1, source_target_pairs={{0,1},{1,0},{2,3},{3,2},{4,5},{5,4},{6,7},{7,6},{8,9},{9,8},{10,11... | collective-permute-start | bytes 6291464 | tf_op jit(solution)/shard_map/ppermute | solution.py:369
  360.9 45.2 %all-to-all-start.7 = ((bf16[4,128,2048]{2,1,0:T(8,128)(2,1)}), bf16[4,128,2048]{2,1,0:T(8,128)(2,1)}, u32[]{:S(2)}, u32[]{:S(2)}) async-start(bf16[4,128,2048]{2,1,0:T(8,128)(2,1)} %broadcast_in_dim.73), calls=%async_computation.7 | async-start | bytes 4194304 | tf_op jit(solution)/shard_map/all_to_all | solution.py:406
  388.6 17.5 %copy-start.52 = (bf16[512,768]{1,0:T(8,128)(2,1)}, bf16[512,768]{1,0:T(8,128)(2,1)S(1)}, u32[]{:S(2)}) copy-start(bf16[512,768]{1,0:T(8,128)(2,1)S(1)} %collective-permute-done.24.refs_24_) | copy-start | bytes 2359300
  406.1 6.6 %collective-permute-start.25 = (bf16[4,128,2048]{2,1,0:T(8,128)(2,1)}, bf16[4,128,2048]{2,1,0:T(8,128)(2,1)S(1)}, u32[]{:S(2)}, u32[]{:S(2)}) collective-permute-start(bf16[4,128,2048]{2,1,0:T(8,128)(2,1)} %all-to-all-done.7.own_ref), channel_id=1, source_target_pairs={{0,1},{1,0},{2,3},{3,2},{4,5},{5,4},{6,7},{7,6},{8,9},{9,8},{10,11... | collective-permute-start | bytes 6291464 | tf_op jit(solution)/shard_map/ppermute | solution.py:369
  406.1 108.3 %collective-permute-start.39 = (bf16[512,2304]{1,0:T(8,128)(2,1)}, bf16[512,2304]{1,0:T(8,128)(2,1)}, u32[]{:S(2)}, u32[]{:S(2)}) collective-permute-start(bf16[512,2304]{1,0:T(8,128)(2,1)} %shard_map.211), channel_id=1, source_target_pairs={{0,2},{2,0},{4,6},{6,4},{8,10},{10,8},{12,14},{14,12},{16,18},{18,... | collective-permute-start | bytes 7077896 | tf_op jit(solution)/shard_map/ppermute | solution.py:366
  406.7 107.7 %collective-permute-start.38 = (bf16[512,768]{1,0:T(8,128)(2,1)}, bf16[512,768]{1,0:T(8,128)(2,1)}, u32[]{:S(2)}, u32[]{:S(2)}) collective-permute-start(bf16[512,768]{1,0:T(8,128)(2,1)} %shard_map.214), channel_id=1, source_target_pairs={{0,16},{2,18},{4,20},{6,22},{8,24},{10,26},{12,28},{14,30},{16,0},... | collective-permute-start | bytes 2359304 | tf_op jit(solution)/shard_map/ppermute | solution.py:366
  407.6 53.2 %all-to-all-start.8 = ((bf16[4,128,2048]{2,1,0:T(8,128)(2,1)}), bf16[4,128,2048]{2,1,0:T(8,128)(2,1)}, u32[]{:S(2)}, u32[]{:S(2)}) async-start(bf16[4,128,2048]{2,1,0:T(8,128)(2,1)} %bitcast.26), calls=%async_computation.8 | async-start | bytes 4194304 | tf_op jit(solution)/shard_map/all_to_all | solution.py:406
  433.6 34.8 %collective-permute-start.26 = (bf16[512,2048]{1,0:T(8,128)(2,1)}, bf16[512,2048]{1,0:T(8,128)(2,1)}, u32[]{:S(2)}, u32[]{:S(2)}) collective-permute-start(bf16[512,2048]{1,0:T(8,128)(2,1)} %bitcast.124), channel_id=1, source_target_pairs={{0,1},{1,0},{2,3},{3,2},{4,5},{5,4},{6,7},{7,6},{8,9},{9,8},{10,11... | collective-permute-start | bytes 6291464 | tf_op jit(solution)/shard_map/ppermute | solution.py:369
  433.6 80.0 %collective-permute-start.27 = (bf16[512,768]{1,0:T(8,128)(2,1)}, bf16[512,768]{1,0:T(8,128)(2,1)}, u32[]{:S(2)}, u32[]{:S(2)}) collective-permute-start(bf16[512,768]{1,0:T(8,128)(2,1)} %shard_map.215), channel_id=1, source_target_pairs={{0,16},{2,18},{4,20},{6,22},{8,24},{10,26},{12,28},{14,30},{16,0},... | collective-permute-start | bytes 2359304 | tf_op jit(solution)/shard_map/ppermute | solution.py:366
  439.8 23.1 %copy-start.5 = (f32[128,2048]{1,0:T(8,128)S(1)}, f32[128,2048]{1,0:T(8,128)}, u32[]{:S(2)}) copy-start(f32[128,2048]{1,0:T(8,128)} %copy-done.3) | copy-start | bytes 3145732
  439.8 42.7 %collective-permute-start.36 = (bf16[512,1024]{1,0:T(8,128)(2,1)}, bf16[512,1024]{1,0:T(8,128)(2,1)}, u32[]{:S(2)}, u32[]{:S(2)}) collective-permute-start(bf16[512,1024]{1,0:T(8,128)(2,1)} %shard_map.217), channel_id=1, source_target_pairs={{0,2},{2,0},{4,6},{6,4},{8,10},{10,8},{12,14},{14,12},{16,18},{18,... | collective-permute-start | bytes 3145736 | tf_op jit(solution)/shard_map/ppermute | solution.py:366
  472.0 39.5 %all-to-all-start.9 = ((bf16[4,128,2048]{2,1,0:T(8,128)(2,1)}), bf16[4,128,2048]{2,1,0:T(8,128)(2,1)}, u32[]{:S(2)}, u32[]{:S(2)}) async-start(bf16[4,128,2048]{2,1,0:T(8,128)(2,1)} %fusion), calls=%async_computation.9 | async-start | bytes 4194304 | tf_op jit(solution)/shard_map/all_to_all | solution.py:406
  481.2 79.8 %collective-permute-start.35 = (bf16[512,1024]{1,0:T(8,128)(2,1)}, bf16[512,1024]{1,0:T(8,128)(2,1)}, u32[]{:S(2)}, u32[]{:S(2)}) collective-permute-start(bf16[512,1024]{1,0:T(8,128)(2,1)} %shard_map.218), channel_id=1, source_target_pairs={{0,2},{2,0},{4,6},{6,4},{8,10},{10,8},{12,14},{14,12},{16,18},{18,... | collective-permute-start | bytes 3145736 | tf_op jit(solution)/shard_map/ppermute | solution.py:366
  487.3 26.3 %copy-start.7 = (f32[128,2048]{1,0:T(8,128)S(1)}, f32[128,2048]{1,0:T(8,128)}, u32[]{:S(2)}) copy-start(f32[128,2048]{1,0:T(8,128)} %copy-done.6) | copy-start | bytes 3145732
  487.3 26.3 %copy-start.24 = (f32[1,2,2,2,2,128]{5,4,3,2,1,0:T(2,128)S(1)}, f32[1,2,2,2,2,128]{5,4,3,2,1,0:T(2,128)}, u32[]{:S(2)}) copy-start(f32[1,2,2,2,2,128]{5,4,3,2,1,0:T(2,128)} %copy.36) | copy-start | bytes 24580
  487.3 26.3 %copy-start.45 = (f32[128]{0:T(128)S(1)}, f32[128]{0:T(128)}, u32[]{:S(2)}) copy-start(f32[128]{0:T(128)} %copy-done.43) | copy-start | bytes 1540
  487.3 26.3 %copy-start.47 = (f32[128]{0:T(128)S(1)}, f32[128]{0:T(128)}, u32[]{:S(2)}) copy-start(f32[128]{0:T(128)} %add_rsqrt_fusion.1) | copy-start | bytes 1540
  487.4 26.8 %copy-start.30 = (f32[2048]{0:T(1024)S(1)}, f32[2048]{0:T(1024)}, u32[]{:S(2)}) copy-start(f32[2048]{0:T(1024)} %get-tuple-element.151) | copy-start | bytes 24580
  487.4 26.8 %copy-start.29 = (f32[2048]{0:T(1024)S(1)}, f32[2048]{0:T(1024)}, u32[]{:S(2)}) copy-start(f32[2048]{0:T(1024)} %get-tuple-element.157) | copy-start | bytes 24580
  487.4 73.6 %collective-permute-start.37 = (bf16[512,1024]{1,0:T(8,128)(2,1)}, bf16[512,1024]{1,0:T(8,128)(2,1)}, u32[]{:S(2)}, u32[]{:S(2)}) collective-permute-start(bf16[512,1024]{1,0:T(8,128)(2,1)} %shard_map.219), channel_id=1, source_target_pairs={{0,16},{2,18},{4,20},{6,22},{8,24},{10,26},{12,28},{14,30},{16,0},... | collective-permute-start | bytes 3145736 | tf_op jit(solution)/shard_map/ppermute | solution.py:366
  514.3 10.2 %collective-permute-start.28 = (f32[7,2048]{1,0:T(8,128)S(1)}, f32[7,2048]{1,0:T(8,128)S(1)}, u32[]{:S(2)}, u32[]{:S(2)}) collective-permute-start(f32[7,2048]{1,0:T(8,128)S(1)} %pad_maximum_fusion.5), channel_id=1, source_target_pairs={{0,1},{1,0},{2,3},{3,2},{4,5},{5,4},{6,7},{7,6},{8,9},{9,8},{10,11... | collective-permute-start | bytes 172040 | tf_op jit(solution)/shard_map/ppermute | solution.py:369
  524.6 14.2 %collective-permute-start.31 = (f32[7,2048]{1,0:T(8,128)S(1)}, f32[7,2048]{1,0:T(8,128)S(1)}, u32[]{:S(2)}, u32[]{:S(2)}) collective-permute-start(f32[7,2048]{1,0:T(8,128)S(1)} %fusion.21), channel_id=1, source_target_pairs={{0,12},{2,14},{4,8},{6,10},{8,4},{10,6},{12,0},{14,2},{16,28},{18,... | collective-permute-start | bytes 172040 | tf_op jit(solution)/shard_map/ppermute | solution.py:366
  525.0 13.8 %collective-permute-start.30 = (f32[7,2048]{1,0:T(8,128)S(1)}, f32[7,2048]{1,0:T(8,128)S(1)}, u32[]{:S(2)}, u32[]{:S(2)}) collective-permute-start(f32[7,2048]{1,0:T(8,128)S(1)} %fusion.21), channel_id=1, source_target_pairs={{0,8},{2,10},{4,12},{6,14},{8,0},{10,2},{12,4},{14,6},{16,24},{18,... | collective-permute-start | bytes 172040 | tf_op jit(solution)/shard_map/ppermute | solution.py:366
  527.5 11.3 %collective-permute-start.29 = (f32[7,2048]{1,0:T(8,128)S(1)}, f32[7,2048]{1,0:T(8,128)S(1)}, u32[]{:S(2)}, u32[]{:S(2)}) collective-permute-start(f32[7,2048]{1,0:T(8,128)S(1)} %fusion.21), channel_id=1, source_target_pairs={{0,4},{2,6},{4,0},{6,2},{8,12},{10,14},{12,8},{14,10},{16,20},{18,... | collective-permute-start | bytes 172040 | tf_op jit(solution)/shard_map/ppermute | solution.py:366
  528.1 38.9 %all-to-all-start.10 = ((bf16[4,128,2304]{2,1,0:T(8,128)(2,1)}), bf16[4,128,2304]{2,1,0:T(8,128)(2,1)}, u32[]{:S(2)}, u32[]{:S(2)}) async-start(bf16[4,128,2304]{2,1,0:T(8,128)(2,1)} %bitcast.76), calls=%async_computation.10 | async-start | bytes 4718592 | tf_op jit(solution)/shard_map/all_to_all | solution.py:406
  538.8 21.5 %collective-permute-start.34 = (f32[7,2048]{1,0:T(8,128)S(1)}, f32[7,2048]{1,0:T(8,128)S(1)}, u32[]{:S(2)}, u32[]{:S(2)}) collective-permute-start(f32[7,2048]{1,0:T(8,128)S(1)} %add_add_fusion.1), channel_id=1, source_target_pairs={{0,18},{2,16},{4,22},{6,20},{8,26},{10,24},{12,30},{14,28},{16,2},... | collective-permute-start | bytes 172040 | tf_op jit(solution)/shard_map/ppermute | solution.py:366
  539.7 20.5 %collective-permute-start.33 = (f32[7,2048]{1,0:T(8,128)S(1)}, f32[7,2048]{1,0:T(8,128)S(1)}, u32[]{:S(2)}, u32[]{:S(2)}) collective-permute-start(f32[7,2048]{1,0:T(8,128)S(1)} %add_add_fusion.1), channel_id=1, source_target_pairs={{0,2},{2,0},{4,6},{6,4},{8,10},{10,8},{12,14},{14,12},{16,18},{18,... | collective-permute-start | bytes 172040 | tf_op jit(solution)/shard_map/ppermute | solution.py:366
  541.1 19.8 %collective-permute-start.32 = (f32[7,2048]{1,0:T(8,128)S(1)}, f32[7,2048]{1,0:T(8,128)S(1)}, u32[]{:S(2)}, u32[]{:S(2)}) collective-permute-start(f32[7,2048]{1,0:T(8,128)S(1)} %add_add_fusion.1), channel_id=1, source_target_pairs={{0,16},{2,18},{4,20},{6,22},{8,24},{10,26},{12,28},{14,30},{16,0},... | collective-permute-start | bytes 172040 | tf_op jit(solution)/shard_map/ppermute | solution.py:366
  567.0 19.2 %all-to-all-start.11 = ((bf16[4,128,1024]{2,1,0:T(8,128)(2,1)}), bf16[4,128,1024]{2,1,0:T(8,128)(2,1)S(1)}, u32[]{:S(2)}, u32[]{:S(2)}) async-start(bf16[4,128,1024]{2,1,0:T(8,128)(2,1)} %bitcast.94), calls=%async_computation.11 | async-start | bytes 2097152 | tf_op jit(solution)/shard_map/all_to_all | solution.py:406
  (41 other events, 253.5 us)

commit v6 on v5

--- a/solution.py
+++ b/solution.py
@@ -448,15 +448,17 @@
 
     def block_grad(i, kinds, adds, after=(), cost=LONG):
         cols = sum(c[0].shape[1] for _, sets in kinds for c in sets)
+        steps = 2 if shard_rows % (2 * LANES) == 0 else 1
+        depth = shard_rows // steps
         ins, specs = [], []
         for left, sets in kinds:
             ins += left
-            specs += [pl.BlockSpec((v.shape[0], shard_rows), lambda *_: (0, i)) for v in left]
+            specs += [pl.BlockSpec((v.shape[0], depth), lambda s: (0, steps * i + s)) for v in left]
             for s in sets:
                 ins += s
                 specs += [whole(v.shape) for v in s]
         ins += [v for v, _ in adds]
-        specs += [whole(v.shape) for v, _ in adds]
+        specs += [pl.BlockSpec((depth, v.shape[1]), lambda s: (s, 0)) for v, _ in adds]
         ins[0] = tie(ins[0], *after)
         return call(
             functools.partial(grad_kernel, [len(s) for _, s in kinds], [at for _, at in adds]),
@@ -464,6 +466,8 @@
             [shaped((shard_rows, cols), BF)],
             2 * group * seq_len * shard_rows * cols,
             in_specs=specs,
+            out_specs=[pl.BlockSpec((depth, cols), lambda s: (s, 0))],
+            grid=(steps,),
             cost=cost,
         )[0]
 

time: 596 us -> 594 us (level)
  transfers between devices with their start and end apart: 52 -> 52, of which waited for: 22 -> 23; matrix products, arithmetic and copies ran while one was open for 13% -> 13% of each run, Pallas kernels for 22% -> 21%
where the time goes in v6:
time: 594 us; the launch traced here: 588 us
  waiting for transfers between devices  263 us (44%)
  Pallas kernels  144 us (24%)
  starting transfers between devices  90.6 us (15%)
  other arithmetic  53.7 us (9%)
  local copies, waits for them, and re-layouts  34.9 us (6%)
    pallas_call x21, Pallas kernels, call(): pl.pallas_call(kernel, grid=grid, in_specs=in_specs or [whole(v.shape) fo...  144 us
    all_to_all x12, waiting for transfers between devices, exchange(): lax.all_to_all(rows_by_rank, 'dp', 0, 0, axis_index_groups=bands, tiled=T...  141 us
    ppermute x31, waiting for transfers between devices, swap(): return lax.ppermute(array, 'dp', [(d, d ^ mask) for d in range(dp_size)])  115 us
    all_to_all x12, starting transfers between devices, exchange(): lax.all_to_all(rows_by_rank, 'dp', 0, 0, axis_index_groups=bands, tiled=T...  52.5 us
    ppermute x31, starting transfers between devices, swap(): return lax.ppermute(array, 'dp', [(d, d ^ mask) for d in range(dp_size)])  37.4 us
    convert_element_type x4, other arithmetic, merge(): return (by_block(mine).astype(F32) + by_block(other).astype(F32)).astype(BF)  15 us
  transfers between devices with their start and end apart: 52, of which 23 were waited for; matrix products, arithmetic and copies ran while one was open for 13% of the time, Pallas kernels for 21%

profile of v6, /device:TPU:0, one launch (start us, length us, event | category | flops | bytes accessed | tf_op | source)
XLA Modules:
  0.0 588.0 jit_solution(7430136786957281107)
XLA Ops:
  0.7 2.4 shard_map.203
  3.1 5.4 all-to-all-start
  14.4 8.3 %all-to-all-done = bf16[4,128,1024]{2,1,0:T(8,128)(2,1)} async-done(((bf16[4,128,1024]{2,1,0:T(8,128)(2,1)}), bf16[4,128,1024]{2,1,0:T(8,128)(2,1)}, u32[]{:S(2)}, u32[]{:S(2)}) %all-to-all-start) | async-done | bytes 1048608 | tf_op jit(solution)/shard_map/all_to_all | solution.py:406
  29.7 2.6 collective-permute-start.4
  32.3 3.3 shard_map.204
  35.6 3.8 all-to-all-start.1
  39.4 8.0 %collective-permute-done.refs_2_ = bf16[512,1024]{1,0:T(8,128)(2,1)} collective-permute-done((bf16[512,1024]{1,0:T(8,128)(2,1)}, bf16[512,1024]{1,0:T(8,128)(2,1)}, u32[]{:S(2)}, u32[]{:S(2)}) %collective-permute-start) | collective-permute-done | bytes 1048608 | tf_op jit(solution)/shard_map/ppermute | solution.py:366
  62.7 2.6 copy.38
  65.3 2.3 reshape.422
  67.5 3.9 fusion.4
  71.4 2.4 fusion.3
  77.4 9.8 %all-to-all-done.1 = bf16[4,128,2304]{2,1,0:T(8,128)(2,1)S(1)} async-done(((bf16[4,128,2304]{2,1,0:T(8,128)(2,1)}), bf16[4,128,2304]{2,1,0:T(8,128)(2,1)S(1)}, u32[]{:S(2)}, u32[]{:S(2)}) %all-to-all-start.1) | async-done | bytes 2359328 | tf_op jit(solution)/shard_map/all_to_all | solution.py:406
  87.1 4.4 all-to-all-start.2
  94.5 20.8 %collective-permute-done.5.refs_3_ = bf16[512,1024]{1,0:T(8,128)(2,1)} collective-permute-done((bf16[512,1024]{1,0:T(8,128)(2,1)}, bf16[512,1024]{1,0:T(8,128)(2,1)}, u32[]{:S(2)}, u32[]{:S(2)}) %collective-permute-start.5) | collective-permute-done | bytes 1048608 | tf_op jit(solution)/shard_map/ppermute | solution.py:366
  115.3 14.5 %collective-permute-done.6.refs_5_.refs_7_ = bf16[512,768]{1,0:T(8,128)(2,1)} collective-permute-done((bf16[512,768]{1,0:T(8,128)(2,1)S(1)}, bf16[512,768]{1,0:T(8,128)(2,1)}, u32[]{:S(2)}, u32[]{:S(2)}) %collective-permute-start.6) | collective-permute-done | bytes 786464 | tf_op jit(solution)/shard_map/ppermute | solution.py:366
  129.8 2.3 all-to-all-done.2.own_ref
  133.3 3.8 all-to-all-start.3
  137.2 16.9 %shard_map.205 = (bf16[4,256,768]{2,1,0:T(8,128)(2,1)}, bf16[4,128,256]{2,1,0:T(8,128)(2,1)}, bf16[4,128,256]{2,1,0:T(8,128)(2,1)}, bf16[4,128,2048]{2,1,0:T(8,128)(2,1)}, bf16[4,128,2048]{2,1,0:T(8,128)(2,1)}) custom-call(bf16[4,128,2048]{2,1,0:T(8,128)(2,1)} %all-to-all-done.2.own_ref, bf16[4,128,2048]{2,1,0:T(8,128)(2,1)} %collective-permute-done.7.sib_ref, ...), custom_call_target="tpu_custom_call" | custom-call | flops 128849018880 | bytes 519137280 | tf_op jit(solution)/shard_map/pallas_call | solution.py:68
  154.3 4.1 collective-permute-done.9
  158.5 3.7 fusion.1
  164.0 3.7 all-to-all-start.4
  171.0 38.7 %all-to-all-done.4 = bf16[4,128,2048]{2,1,0:T(8,128)(2,1)S(1)} async-done(((bf16[4,128,2048]{2,1,0:T(8,128)(2,1)}), bf16[4,128,2048]{2,1,0:T(8,128)(2,1)S(1)}, u32[]{:S(2)}, u32[]{:S(2)}) %all-to-all-start.4) | async-done | bytes 2097184 | tf_op jit(solution)/shard_map/all_to_all | solution.py:406
  213.2 4.7 all-to-all-start.5
  221.0 18.7 %collective-permute-done.13.refs_11_.refs_13_ = bf16[512,768]{1,0:T(8,128)(2,1)S(1)} collective-permute-done((bf16[512,768]{1,0:T(8,128)(2,1)}, bf16[512,768]{1,0:T(8,128)(2,1)S(1)}, u32[]{:S(2)}, u32[]{:S(2)}) %collective-permute-start.13) | collective-permute-done | bytes 786464 | tf_op jit(solution)/shard_map/ppermute | solution.py:366
  239.6 17.4 %collective-permute-done.14.refs_7_.refs_15_ = bf16[512,768]{1,0:T(8,128)(2,1)S(1)} collective-permute-done((bf16[512,768]{1,0:T(8,128)(2,1)S(1)}, bf16[512,768]{1,0:T(8,128)(2,1)S(1)}, u32[]{:S(2)}, u32[]{:S(2)}) %collective-permute-start.14) | collective-permute-done | bytes 786464 | tf_op jit(solution)/shard_map/ppermute | solution.py:366
  260.6 3.1 collective-permute-done.16
  263.7 17.1 %shard_map.206 = (bf16[512,512]{1,0:T(8,128)(2,1)}, bf16[512,512]{1,0:T(8,128)(2,1)}, bf16[512,256]{1,0:T(8,128)(2,1)}, bf16[512,256]{1,0:T(8,128)(2,1)}, bf16[5...) custom-call(bf16[512,2048]{1,0:T(8,128)(2,1)} %bitcast.21.refs_0_.re, ...), custom_call_target="tpu_custom_call" | custom-call | flops 322122547200 | bytes 880803840 | tf_op jit(solution)/shard_map/pallas_call | solution.py:68
  280.9 13.7 %shard_map.207 = (bf16[512,512]{1,0:T(8,128)(2,1)}, bf16[512,512]{1,0:T(8,128)(2,1)}, bf16[512,256]{1,0:T(8,128)(2,1)}, bf16[512,256]{1,0:T(8,128)(2,1)}, bf16[5...) custom-call(bf16[512,2048]{1,0:T(8,128)(2,1)} %bitcast.21.refs_0_.refs_8_.refs_16_, ...), custom_call_target="tpu_custom_call" | custom-call | flops 161061273600 | bytes 817889280 | tf_op jit(solution)/shard_map/pallas_call | solution.py:68
  294.7 4.0 shard_map.208
  300.1 3.8 add_convert_fusion.1
  303.9 3.8 shard_map.209
  308.4 3.8 shard_map.210
  313.6 4.5 all-to-all-start.6
  318.1 7.5 %shard_map.211 = bf16[512,2304]{1,0:T(8,128)(2,1)} custom-call(bf16[512,2048]{1,0:T(8,128)(2,1)} %bitcast.21.refs_0_.refs_8_.refs_16_, bf16[512,2048]{1,0:T(8,128)(2,1)} %bitcast.22.refs_1_.refs_9_.refs_17_, bf16[512,512]{1,0:T(8,128)(2,1)} %get-tuple-element.107.refs_2_, bf16[512,512]{1,0:T(8,128)(2,1)} %get-tuple-element.108.refs_3_, ...), custom_call_target="tpu_custom_call" | custom-call | flops 72477573120 | bytes 967311360 | tf_op jit(solution)/shard_map/pallas_call | solution.py:68
  325.6 17.0 %all-to-all-done.6 = bf16[4,128,2048]{2,1,0:T(8,128)(2,1)S(1)} async-done(((bf16[4,128,2048]{2,1,0:T(8,128)(2,1)}), bf16[4,128,2048]{2,1,0:T(8,128)(2,1)S(1)}, u32[]{:S(2)}, u32[]{:S(2)}) %all-to-all-start.6) | async-done | bytes 2097184 | tf_op jit(solution)/shard_map/all_to_all | solution.py:406
  347.3 4.0 shard_map.213
  353.2 7.1 %shard_map.212 = (bf16[512,2048]{1,0:T(8,128)(2,1)}, bf16[512,2048]{1,0:T(8,128)(2,1)}) custom-call(bf16[512,256]{1,0:T(8,128)(2,1)} %get-tuple-element.122.refs_6_.refs_0_, bf16[512,256]{1,0:T(8,128)(2,1)} %get-tuple-element.109.refs_7_.refs_1_, bf16[512,256]{1,0:T(8,128)(2,1)} %get-tuple-element.113.refs_6_.refs_14_.refs_2_, ...), custom_call_target="tpu_custom_call" | custom-call | tf_op jit(solution)/shard_map/pallas_call | solution.py:68
  360.3 4.4 all-to-all-start.7
  364.7 4.1 shard_map.214
  368.8 4.2 shard_map.215
  373.0 3.8 add_convert_fusion
  376.8 11.2 %collective-permute-done.24.refs_24_ = bf16[512,768]{1,0:T(8,128)(2,1)S(1)} collective-permute-done((bf16[512,768]{1,0:T(8,128)(2,1)}, bf16[512,768]{1,0:T(8,128)(2,1)S(1)}, u32[]{:S(2)}, u32[]{:S(2)}) %collective-permute-start.24) | collective-permute-done | bytes 786464 | tf_op jit(solution)/shard_map/ppermute | solution.py:366
  388.0 17.5 %all-to-all-done.7.own_ref = bf16[4,128,2048]{2,1,0:T(8,128)(2,1)} async-done(((bf16[4,128,2048]{2,1,0:T(8,128)(2,1)}), bf16[4,128,2048]{2,1,0:T(8,128)(2,1)}, u32[]{:S(2)}, u32[]{:S(2)}) %all-to-all-start.7) | async-done | bytes 2097184 | tf_op jit(solution)/shard_map/all_to_all | solution.py:406
  407.0 5.1 all-to-all-start.8
  413.4 19.5 %shard_map.216 = (bf16[4,128,768]{2,1,0:T(8,128)(2,1)}, bf16[4,128,768]{2,1,0:T(8,128)(2,1)}, f32[4,1,768]{2,1,0:T(1,128)}, bf16[4,128,2048]{2,1,0:T(8,128)(2,1)}, bf16[4,128,2048]{2,1,0:T(8,128)(2,1)}) custom-call(bf16[4,128,2048]{2,1,0:T(8,128)(2,1)} %all-to-all-done.7.own_ref, bf16[4,128,2048]{2,1,0:T(8,128)(2,1)} %copy-done.51, ...), custom_call_target="tpu_custom_call" | custom-call | flops 128849018880 | bytes 550871040 | tf_op jit(solution)/shard_map/pallas_call | solution.py:68
  434.8 4.3 shard_map.217
  440.5 19.6 %all-to-all-done.8 = bf16[4,128,2048]{2,1,0:T(8,128)(2,1)} async-done(((bf16[4,128,2048]{2,1,0:T(8,128)(2,1)}), bf16[4,128,2048]{2,1,0:T(8,128)(2,1)}, u32[]{:S(2)}, u32[]{:S(2)}) %all-to-all-start.8) | async-done | bytes 2097184 | tf_op jit(solution)/shard_map/all_to_all | solution.py:406
  467.7 3.7 fusion
  471.4 4.7 all-to-all-start.9
  476.1 4.3 shard_map.218
  482.0 4.5 shard_map.219
  487.8 23.3 %all-to-all-done.9 = bf16[4,128,2048]{2,1,0:T(8,128)(2,1)} async-done(((bf16[4,128,2048]{2,1,0:T(8,128)(2,1)}), bf16[4,128,2048]{2,1,0:T(8,128)(2,1)}, u32[]{:S(2)}, u32[]{:S(2)}) %all-to-all-start.9) | async-done | bytes 2097184 | tf_op jit(solution)/shard_map/all_to_all | solution.py:406
  514.0 8.4 %shard_map.221 = bf16[512,2304]{1,0:T(8,128)(2,1)} custom-call(bf16[512,2048]{1,0:T(8,128)(2,1)} %bitcast.21.refs_0_.refs_8_.refs_16_, bf16[512,2048]{1,0:T(8,128)(2,1)} %bitcast.22.refs_1_.refs_9_.refs_17_, bf16[512,512]{1,0:T(8,128)(2,1)} %get-tuple-element.107.refs_2_, bf16[512,512]{1,0:T(8,128)(2,1)} %get-tuple-element.108.refs_3_, ...), custom_call_target="tpu_custom_call" | custom-call | flops 72477573120 | bytes 1108869120 | tf_op jit(solution)/shard_map/pallas_call | solution.py:68
  522.8 2.5 collective-permute-start.30
  526.0 4.5 all-to-all-start.10
  530.5 7.5 %collective-permute-done.31 = f32[7,2048]{1,0:T(8,128)S(1)} collective-permute-done((f32[7,2048]{1,0:T(8,128)S(1)}, f32[7,2048]{1,0:T(8,128)S(1)}, u32[]{:S(2)}, u32[]{:S(2)}) %collective-permute-start.31) | collective-permute-done | bytes 57376 | tf_op jit(solution)/shard_map/ppermute | solution.py:366
  540.3 2.1 collective-permute-start.32
  542.4 15.7 %collective-permute-done.34 = f32[7,2048]{1,0:T(8,128)S(1)} collective-permute-done((f32[7,2048]{1,0:T(8,128)S(1)}, f32[7,2048]{1,0:T(8,128)S(1)}, u32[]{:S(2)}, u32[]{:S(2)}) %collective-permute-start.34) | collective-permute-done | bytes 57376 | tf_op jit(solution)/shard_map/ppermute | solution.py:366
  558.8 4.7 shard_map.220
  563.6 2.5 all-to-all-done.10
  566.1 3.5 all-to-all-start.11
  569.7 2.7 multiply_add_fusion
  580.1 4.1 shard_map.223
  585.1 2.7 shard_map.222
  (271 shorter events, 93.4 us)
Async XLA Ops:
  0.6 131.4 %copy-start = (f32[3,1024]{1,0:T(4,128)S(1)}, f32[3,1024]{1,0:T(4,128)}, u32[]{:S(2)}) copy-start(f32[3,1024]{1,0:T(4,128)} %param.17) | copy-start | bytes 36868
  3.1 19.7 %all-to-all-start = ((bf16[4,128,1024]{2,1,0:T(8,128)(2,1)}), bf16[4,128,1024]{2,1,0:T(8,128)(2,1)}, u32[]{:S(2)}, u32[]{:S(2)}) async-start(bf16[4,128,1024]{2,1,0:T(8,128)(2,1)} %bitcast.75), calls=%async_computation | async-start | bytes 2097152 | tf_op jit(solution)/shard_map/all_to_all | solution.py:406
  8.4 20.6 %collective-permute-start.3 = (s32[256]{0:T(256)S(1)}, s32[256]{0:T(256)S(1)}, u32[]{:S(2)}, u32[]{:S(2)}) collective-permute-start(s32[256]{0:T(256)S(1)} %copy-done.50), channel_id=1, source_target_pairs={{0,4},{2,6},{4,0},{6,2},{8,12},{10,14},{12,8},{14,10},{16,20},{18,... | collective-permute-start | bytes 3080 | tf_op jit(solution)/shard_map/ppermute | solution.py:366
  10.5 18.5 %collective-permute-start.2 = (s32[256]{0:T(256)S(1)}, s32[256]{0:T(256)S(1)}, u32[]{:S(2)}, u32[]{:S(2)}) collective-permute-start(s32[256]{0:T(256)S(1)} %copy-done.50), channel_id=1, source_target_pairs={{0,12},{2,14},{4,8},{6,10},{8,4},{10,6},{12,0},{14,2},{16,28},{18,... | collective-permute-start | bytes 3080 | tf_op jit(solution)/shard_map/ppermute | solution.py:366
  12.0 17.0 %collective-permute-start.1 = (s32[256]{0:T(256)S(1)}, s32[256]{0:T(256)S(1)}, u32[]{:S(2)}, u32[]{:S(2)}) collective-permute-start(s32[256]{0:T(256)S(1)} %copy-done.50), channel_id=1, source_target_pairs={{0,8},{2,10},{4,12},{6,14},{8,0},{10,2},{12,4},{14,6},{16,24},{18,... | collective-permute-start | bytes 3080 | tf_op jit(solution)/shard_map/ppermute | solution.py:366
  22.7 24.6 %collective-permute-start = (bf16[512,1024]{1,0:T(8,128)(2,1)}, bf16[512,1024]{1,0:T(8,128)(2,1)}, u32[]{:S(2)}, u32[]{:S(2)}) collective-permute-start(bf16[512,1024]{1,0:T(8,128)(2,1)} %bitcast.9.refs_0_), channel_id=1, source_target_pairs={{0,2},{2,0},{4,6},{6,4},{8,10},{10,8},{12,14},{14,12},{16,18},{18,... | collective-permute-start | bytes 3145736 | tf_op jit(solution)/shard_map/ppermute | solution.py:366
  29.7 47.7 %collective-permute-start.4 = (bf16[512,1024]{1,0:T(8,128)(2,1)}, bf16[512,1024]{1,0:T(8,128)(2,1)}, u32[]{:S(2)}, u32[]{:S(2)}) collective-permute-start(bf16[512,1024]{1,0:T(8,128)(2,1)} %bitcast.9.refs_0_), channel_id=1, source_target_pairs={{0,16},{2,18},{4,20},{6,22},{8,24},{10,26},{12,28},{14,30},{16,0},... | collective-permute-start | bytes 3145736 | tf_op jit(solution)/shard_map/ppermute | solution.py:366
  35.6 51.6 %all-to-all-start.1 = ((bf16[4,128,2304]{2,1,0:T(8,128)(2,1)}), bf16[4,128,2304]{2,1,0:T(8,128)(2,1)S(1)}, u32[]{:S(2)}, u32[]{:S(2)}) async-start(bf16[4,128,2304]{2,1,0:T(8,128)(2,1)} %bitcast.71), calls=%async_computation.1 | async-start | bytes 4718592 | tf_op jit(solution)/shard_map/all_to_all | solution.py:406
  62.7 147.4 %copy-start.6 = (f32[128,2048]{1,0:T(8,128)}, f32[128,2048]{1,0:T(8,128)S(1)}, u32[]{:S(2)}) copy-start(f32[128,2048]{1,0:T(8,128)S(1)} %reshape.445) | copy-start | bytes 3145732
  87.1 44.9 %all-to-all-start.2 = ((bf16[4,128,2048]{2,1,0:T(8,128)(2,1)}), bf16[4,128,2048]{2,1,0:T(8,128)(2,1)}, u32[]{:S(2)}, u32[]{:S(2)}) async-start(bf16[4,128,2048]{2,1,0:T(8,128)(2,1)} %broadcast_in_dim.36), calls=%async_computation.2 | async-start | bytes 4194304 | tf_op jit(solution)/shard_map/all_to_all | solution.py:406
  91.6 23.7 %collective-permute-start.5 = (bf16[512,1024]{1,0:T(8,128)(2,1)}, bf16[512,1024]{1,0:T(8,128)(2,1)}, u32[]{:S(2)}, u32[]{:S(2)}) collective-permute-start(bf16[512,1024]{1,0:T(8,128)(2,1)} %collective-permute-done.4.refs_1_), channel_id=1, source_target_pairs={{0,2},{2,0},{4,6},{6,4},{8,10},{10,8},{12,14},{14,12},{16,18},{18,... | collective-permute-start | bytes 3145736 | tf_op jit(solution)/shard_map/ppermute | solution.py:366
  94.5 35.3 %collective-permute-start.6 = (bf16[512,768]{1,0:T(8,128)(2,1)S(1)}, bf16[512,768]{1,0:T(8,128)(2,1)}, u32[]{:S(2)}, u32[]{:S(2)}) collective-permute-start(bf16[512,768]{1,0:T(8,128)(2,1)S(1)} %get-tuple-element.92), channel_id=1, source_target_pairs={{0,16},{2,18},{4,20},{6,22},{8,24},{10,26},{12,28},{14,30},{16,0},... | collective-permute-start | bytes 2359304 | tf_op jit(solution)/shard_map/ppermute | solution.py:366
  132.1 5.1 collective-permute-start.7
  132.7 21.4 %collective-permute-start.8 = (bf16[512,768]{1,0:T(8,128)(2,1)}, bf16[512,768]{1,0:T(8,128)(2,1)}, u32[]{:S(2)}, u32[]{:S(2)}) collective-permute-start(bf16[512,768]{1,0:T(8,128)(2,1)} %copy-done.19), channel_id=1, source_target_pairs={{0,2},{2,0},{4,6},{6,4},{8,10},{10,8},{12,14},{14,12},{16,18},{18,... | collective-permute-start | bytes 2359304 | tf_op jit(solution)/shard_map/ppermute | solution.py:366
  133.3 29.3 %all-to-all-start.3 = ((bf16[4,128,2048]{2,1,0:T(8,128)(2,1)}), bf16[4,128,2048]{2,1,0:T(8,128)(2,1)S(1)}, u32[]{:S(2)}, u32[]{:S(2)}) async-start(bf16[4,128,2048]{2,1,0:T(8,128)(2,1)} %broadcast_in_dim.37), calls=%async_computation.3 | async-start | bytes 4194304 | tf_op jit(solution)/shard_map/all_to_all | solution.py:406
  154.0 4.4 collective-permute-start.9
  164.0 45.6 %all-to-all-start.4 = ((bf16[4,128,2048]{2,1,0:T(8,128)(2,1)}), bf16[4,128,2048]{2,1,0:T(8,128)(2,1)S(1)}, u32[]{:S(2)}, u32[]{:S(2)}) async-start(bf16[4,128,2048]{2,1,0:T(8,128)(2,1)} %fusion.1), calls=%async_computation.4 | async-start | bytes 4194304 | tf_op jit(solution)/shard_map/all_to_all | solution.py:406
  167.7 42.4 %collective-permute-start.11 = (bf16[512,768]{1,0:T(8,128)(2,1)}, bf16[512,768]{1,0:T(8,128)(2,1)}, u32[]{:S(2)}, u32[]{:S(2)}) collective-permute-start(bf16[512,768]{1,0:T(8,128)(2,1)} %get-tuple-element.97), channel_id=1, source_target_pairs={{0,16},{2,18},{4,20},{6,22},{8,24},{10,26},{12,28},{14,30},{16,0},... | collective-permute-start | bytes 2359304 | tf_op jit(solution)/shard_map/ppermute | solution.py:366
  168.9 41.1 %collective-permute-start.10 = (bf16[512,768]{1,0:T(8,128)(2,1)}, bf16[512,768]{1,0:T(8,128)(2,1)}, u32[]{:S(2)}, u32[]{:S(2)}) collective-permute-start(bf16[512,768]{1,0:T(8,128)(2,1)} %collective-permute-done.6.refs_5_.refs_7_), channel_id=1, source_target_pairs={{0,2},{2,0},{4,6},{6,4},{8,10},{10,8},{12,14},{14,12},{16,18},{18,... | collective-permute-start | bytes 2359304 | tf_op jit(solution)/shard_map/ppermute | solution.py:366
  170.3 39.8 %collective-permute-start.12 = (bf16[512,768]{1,0:T(8,128)(2,1)}, bf16[512,768]{1,0:T(8,128)(2,1)}, u32[]{:S(2)}, u32[]{:S(2)}) collective-permute-start(bf16[512,768]{1,0:T(8,128)(2,1)} %get-tuple-element.97), channel_id=1, source_target_pairs={{0,2},{2,0},{4,6},{6,4},{8,10},{10,8},{12,14},{14,12},{16,18},{18,... | collective-permute-start | bytes 2359304 | tf_op jit(solution)/shard_map/ppermute | solution.py:366
  170.9 39.7 %copy-start.25 = (f32[1,2,2,2,2,128]{5,4,3,2,1,0:T(2,128)}, f32[1,2,2,2,2,128]{5,4,3,2,1,0:T(2,128)S(1)}, u32[]{:S(2)}) copy-start(f32[1,2,2,2,2,128]{5,4,3,2,1,0:T(2,128)S(1)} %copy.39) | copy-start | bytes 24580
  213.2 46.0 %all-to-all-start.5 = ((bf16[4,128,2048]{2,1,0:T(8,128)(2,1)}), bf16[4,128,2048]{2,1,0:T(8,128)(2,1)}, u32[]{:S(2)}, u32[]{:S(2)}) async-start(bf16[4,128,2048]{2,1,0:T(8,128)(2,1)} %broadcast_in_dim.72), calls=%async_computation.5 | async-start | bytes 4194304 | tf_op jit(solution)/shard_map/all_to_all | solution.py:406
  218.0 39.0 %collective-permute-start.14 = (bf16[512,768]{1,0:T(8,128)(2,1)S(1)}, bf16[512,768]{1,0:T(8,128)(2,1)S(1)}, u32[]{:S(2)}, u32[]{:S(2)}) collective-permute-start(bf16[512,768]{1,0:T(8,128)(2,1)S(1)} %copy-done.18), channel_id=1, source_target_pairs={{0,16},{2,18},{4,20},{6,22},{8,24},{10,26},{12,28},{14,30},{16,0},... | collective-permute-start | bytes 2359304 | tf_op jit(solution)/shard_map/ppermute | solution.py:366
  218.9 20.7 %collective-permute-start.13 = (bf16[512,768]{1,0:T(8,128)(2,1)}, bf16[512,768]{1,0:T(8,128)(2,1)S(1)}, u32[]{:S(2)}, u32[]{:S(2)}) collective-permute-start(bf16[512,768]{1,0:T(8,128)(2,1)} %collective-permute-done.11.refs_9_.refs_11_), channel_id=1, source_target_pairs={{0,2},{2,0},{4,6},{6,4},{8,10},{10,8},{12,14},{14,12},{16,18},{18,... | collective-permute-start | bytes 2359304 | tf_op jit(solution)/shard_map/ppermute | solution.py:366
  220.3 37.6 %collective-permute-start.15 = (bf16[512,768]{1,0:T(8,128)(2,1)S(1)}, bf16[512,768]{1,0:T(8,128)(2,1)}, u32[]{:S(2)}, u32[]{:S(2)}) collective-permute-start(bf16[512,768]{1,0:T(8,128)(2,1)S(1)} %copy-done.18), channel_id=1, source_target_pairs={{0,2},{2,0},{4,6},{6,4},{8,10},{10,8},{12,14},{14,12},{16,18},{18,... | collective-permute-start | bytes 2359304 | tf_op jit(solution)/shard_map/ppermute | solution.py:366
  221.0 39.7 %collective-permute-start.17 = (bf16[4,128,2048]{2,1,0:T(8,128)(2,1)S(1)}, bf16[4,128,2048]{2,1,0:T(8,128)(2,1)}, u32[]{:S(2)}, u32[]{:S(2)}) collective-permute-start(bf16[4,128,2048]{2,1,0:T(8,128)(2,1)S(1)} %copy-done.15), channel_id=1, source_target_pairs={{0,1},{1,0},{2,3},{3,2},{4,5},{5,4},{6,7},{7,6},{8,9},{9,8},{10,11... | collective-permute-start | bytes 6291464 | tf_op jit(solution)/shard_map/ppermute | solution.py:369
  259.2 4.5 collective-permute-start.16
  259.2 21.6 %collective-permute-start.18 = (bf16[512,768]{1,0:T(8,128)(2,1)}, bf16[512,768]{1,0:T(8,128)(2,1)}, u32[]{:S(2)}, u32[]{:S(2)}) collective-permute-start(bf16[512,768]{1,0:T(8,128)(2,1)} %copy-done.20), channel_id=1, source_target_pairs={{0,2},{2,0},{4,6},{6,4},{8,10},{10,8},{12,14},{14,12},{16,18},{18,... | collective-permute-start | bytes 2359304 | tf_op jit(solution)/shard_map/ppermute | solution.py:366
  294.5 5.6 collective-permute-start.19
  298.7 44.3 %collective-permute-start.20 = (bf16[512,768]{1,0:T(8,128)(2,1)}, bf16[512,768]{1,0:T(8,128)(2,1)}, u32[]{:S(2)}, u32[]{:S(2)}) collective-permute-start(bf16[512,768]{1,0:T(8,128)(2,1)} %shard_map.208), channel_id=1, source_target_pairs={{0,2},{2,0},{4,6},{6,4},{8,10},{10,8},{12,14},{14,12},{16,18},{18,... | collective-permute-start | bytes 2359304 | tf_op jit(solution)/shard_map/ppermute | solution.py:366
  307.7 57.0 %collective-permute-start.22 = (bf16[512,768]{1,0:T(8,128)(2,1)}, bf16[512,768]{1,0:T(8,128)(2,1)}, u32[]{:S(2)}, u32[]{:S(2)}) collective-permute-start(bf16[512,768]{1,0:T(8,128)(2,1)} %shard_map.209), channel_id=1, source_target_pairs={{0,2},{2,0},{4,6},{6,4},{8,10},{10,8},{12,14},{14,12},{16,18},{18,... | collective-permute-start | bytes 2359304 | tf_op jit(solution)/shard_map/ppermute | solution.py:366
  312.2 56.6 %collective-permute-start.23 = (bf16[512,768]{1,0:T(8,128)(2,1)}, bf16[512,768]{1,0:T(8,128)(2,1)}, u32[]{:S(2)}, u32[]{:S(2)}) collective-permute-start(bf16[512,768]{1,0:T(8,128)(2,1)} %shard_map.210), channel_id=1, source_target_pairs={{0,2},{2,0},{4,6},{6,4},{8,10},{10,8},{12,14},{14,12},{16,18},{18,... | collective-permute-start | bytes 2359304 | tf_op jit(solution)/shard_map/ppermute | solution.py:366
  313.6 29.1 %all-to-all-start.6 = ((bf16[4,128,2048]{2,1,0:T(8,128)(2,1)}), bf16[4,128,2048]{2,1,0:T(8,128)(2,1)S(1)}, u32[]{:S(2)}, u32[]{:S(2)}) async-start(bf16[4,128,2048]{2,1,0:T(8,128)(2,1)} %bitcast.25), calls=%async_computation.6 | async-start | bytes 4194304 | tf_op jit(solution)/shard_map/all_to_all | solution.py:406
  325.6 17.5 %copy-start.4 = (f32[128,2048]{1,0:T(8,128)S(1)}, f32[128,2048]{1,0:T(8,128)}, u32[]{:S(2)}) copy-start(f32[128,2048]{1,0:T(8,128)} %copy-done.3) | copy-start | bytes 3145732
  351.4 36.6 %collective-permute-start.24 = (bf16[512,768]{1,0:T(8,128)(2,1)}, bf16[512,768]{1,0:T(8,128)(2,1)S(1)}, u32[]{:S(2)}, u32[]{:S(2)}) collective-permute-start(bf16[512,768]{1,0:T(8,128)(2,1)} %shard_map.213), channel_id=1, source_target_pairs={{0,16},{2,18},{4,20},{6,22},{8,24},{10,26},{12,28},{14,30},{16,0},... | collective-permute-start | bytes 2359304 | tf_op jit(solution)/shard_map/ppermute | solution.py:366
  360.3 12.7 %collective-permute-start.21 = (bf16[512,2048]{1,0:T(8,128)(2,1)}, bf16[512,2048]{1,0:T(8,128)(2,1)}, u32[]{:S(2)}, u32[]{:S(2)}) collective-permute-start(bf16[512,2048]{1,0:T(8,128)(2,1)} %get-tuple-element.124), channel_id=1, source_target_pairs={{0,1},{1,0},{2,3},{3,2},{4,5},{5,4},{6,7},{7,6},{8,9},{9,8},{10,11... | collective-permute-start | bytes 6291464 | tf_op jit(solution)/shard_map/ppermute | solution.py:369
  360.3 45.2 %all-to-all-start.7 = ((bf16[4,128,2048]{2,1,0:T(8,128)(2,1)}), bf16[4,128,2048]{2,1,0:T(8,128)(2,1)}, u32[]{:S(2)}, u32[]{:S(2)}) async-start(bf16[4,128,2048]{2,1,0:T(8,128)(2,1)} %broadcast_in_dim.73), calls=%async_computation.7 | async-start | bytes 4194304 | tf_op jit(solution)/shard_map/all_to_all | solution.py:406
  388.0 17.5 %copy-start.52 = (bf16[512,768]{1,0:T(8,128)(2,1)}, bf16[512,768]{1,0:T(8,128)(2,1)S(1)}, u32[]{:S(2)}) copy-start(bf16[512,768]{1,0:T(8,128)(2,1)S(1)} %collective-permute-done.24.refs_24_) | copy-start | bytes 2359300
  405.5 6.6 %collective-permute-start.25 = (bf16[4,128,2048]{2,1,0:T(8,128)(2,1)}, bf16[4,128,2048]{2,1,0:T(8,128)(2,1)S(1)}, u32[]{:S(2)}, u32[]{:S(2)}) collective-permute-start(bf16[4,128,2048]{2,1,0:T(8,128)(2,1)} %all-to-all-done.7.own_ref), channel_id=1, source_target_pairs={{0,1},{1,0},{2,3},{3,2},{4,5},{5,4},{6,7},{7,6},{8,9},{9,8},{10,11... | collective-permute-start | bytes 6291464 | tf_op jit(solution)/shard_map/ppermute | solution.py:369
  405.5 108.4 %collective-permute-start.39 = (bf16[512,2304]{1,0:T(8,128)(2,1)}, bf16[512,2304]{1,0:T(8,128)(2,1)}, u32[]{:S(2)}, u32[]{:S(2)}) collective-permute-start(bf16[512,2304]{1,0:T(8,128)(2,1)} %shard_map.211), channel_id=1, source_target_pairs={{0,2},{2,0},{4,6},{6,4},{8,10},{10,8},{12,14},{14,12},{16,18},{18,... | collective-permute-start | bytes 7077896 | tf_op jit(solution)/shard_map/ppermute | solution.py:366
  406.2 107.8 %collective-permute-start.38 = (bf16[512,768]{1,0:T(8,128)(2,1)}, bf16[512,768]{1,0:T(8,128)(2,1)}, u32[]{:S(2)}, u32[]{:S(2)}) collective-permute-start(bf16[512,768]{1,0:T(8,128)(2,1)} %shard_map.214), channel_id=1, source_target_pairs={{0,16},{2,18},{4,20},{6,22},{8,24},{10,26},{12,28},{14,30},{16,0},... | collective-permute-start | bytes 2359304 | tf_op jit(solution)/shard_map/ppermute | solution.py:366
  407.0 53.2 %all-to-all-start.8 = ((bf16[4,128,2048]{2,1,0:T(8,128)(2,1)}), bf16[4,128,2048]{2,1,0:T(8,128)(2,1)}, u32[]{:S(2)}, u32[]{:S(2)}) async-start(bf16[4,128,2048]{2,1,0:T(8,128)(2,1)} %bitcast.26), calls=%async_computation.8 | async-start | bytes 4194304 | tf_op jit(solution)/shard_map/all_to_all | solution.py:406
  432.9 34.8 %collective-permute-start.26 = (bf16[512,2048]{1,0:T(8,128)(2,1)}, bf16[512,2048]{1,0:T(8,128)(2,1)}, u32[]{:S(2)}, u32[]{:S(2)}) collective-permute-start(bf16[512,2048]{1,0:T(8,128)(2,1)} %bitcast.124), channel_id=1, source_target_pairs={{0,1},{1,0},{2,3},{3,2},{4,5},{5,4},{6,7},{7,6},{8,9},{9,8},{10,11... | collective-permute-start | bytes 6291464 | tf_op jit(solution)/shard_map/ppermute | solution.py:369
  433.0 80.1 %collective-permute-start.27 = (bf16[512,768]{1,0:T(8,128)(2,1)}, bf16[512,768]{1,0:T(8,128)(2,1)}, u32[]{:S(2)}, u32[]{:S(2)}) collective-permute-start(bf16[512,768]{1,0:T(8,128)(2,1)} %shard_map.215), channel_id=1, source_target_pairs={{0,16},{2,18},{4,20},{6,22},{8,24},{10,26},{12,28},{14,30},{16,0},... | collective-permute-start | bytes 2359304 | tf_op jit(solution)/shard_map/ppermute | solution.py:366
  439.0 23.2 %copy-start.5 = (f32[128,2048]{1,0:T(8,128)S(1)}, f32[128,2048]{1,0:T(8,128)}, u32[]{:S(2)}) copy-start(f32[128,2048]{1,0:T(8,128)} %copy-done.3) | copy-start | bytes 3145732
  439.1 42.9 %collective-permute-start.36 = (bf16[512,1024]{1,0:T(8,128)(2,1)}, bf16[512,1024]{1,0:T(8,128)(2,1)}, u32[]{:S(2)}, u32[]{:S(2)}) collective-permute-start(bf16[512,1024]{1,0:T(8,128)(2,1)} %shard_map.217), channel_id=1, source_target_pairs={{0,2},{2,0},{4,6},{6,4},{8,10},{10,8},{12,14},{14,12},{16,18},{18,... | collective-permute-start | bytes 3145736 | tf_op jit(solution)/shard_map/ppermute | solution.py:366
  471.4 39.7 %all-to-all-start.9 = ((bf16[4,128,2048]{2,1,0:T(8,128)(2,1)}), bf16[4,128,2048]{2,1,0:T(8,128)(2,1)}, u32[]{:S(2)}, u32[]{:S(2)}) async-start(bf16[4,128,2048]{2,1,0:T(8,128)(2,1)} %fusion), calls=%async_computation.9 | async-start | bytes 4194304 | tf_op jit(solution)/shard_map/all_to_all | solution.py:406
  480.4 78.5 %collective-permute-start.35 = (bf16[512,1024]{1,0:T(8,128)(2,1)}, bf16[512,1024]{1,0:T(8,128)(2,1)}, u32[]{:S(2)}, u32[]{:S(2)}) collective-permute-start(bf16[512,1024]{1,0:T(8,128)(2,1)} %shard_map.218), channel_id=1, source_target_pairs={{0,2},{2,0},{4,6},{6,4},{8,10},{10,8},{12,14},{14,12},{16,18},{18,... | collective-permute-start | bytes 3145736 | tf_op jit(solution)/shard_map/ppermute | solution.py:366
  486.5 26.7 %copy-start.7 = (f32[128,2048]{1,0:T(8,128)S(1)}, f32[128,2048]{1,0:T(8,128)}, u32[]{:S(2)}) copy-start(f32[128,2048]{1,0:T(8,128)} %copy-done.6) | copy-start | bytes 3145732
  486.5 26.7 %copy-start.24 = (f32[1,2,2,2,2,128]{5,4,3,2,1,0:T(2,128)S(1)}, f32[1,2,2,2,2,128]{5,4,3,2,1,0:T(2,128)}, u32[]{:S(2)}) copy-start(f32[1,2,2,2,2,128]{5,4,3,2,1,0:T(2,128)} %copy.36) | copy-start | bytes 24580
  486.5 26.7 %copy-start.45 = (f32[128]{0:T(128)S(1)}, f32[128]{0:T(128)}, u32[]{:S(2)}) copy-start(f32[128]{0:T(128)} %copy-done.43) | copy-start | bytes 1540
  486.5 26.7 %copy-start.47 = (f32[128]{0:T(128)S(1)}, f32[128]{0:T(128)}, u32[]{:S(2)}) copy-start(f32[128]{0:T(128)} %add_rsqrt_fusion.1) | copy-start | bytes 1540
  486.5 27.1 %copy-start.30 = (f32[2048]{0:T(1024)S(1)}, f32[2048]{0:T(1024)}, u32[]{:S(2)}) copy-start(f32[2048]{0:T(1024)} %get-tuple-element.151) | copy-start | bytes 24580
  486.5 27.2 %copy-start.29 = (f32[2048]{0:T(1024)S(1)}, f32[2048]{0:T(1024)}, u32[]{:S(2)}) copy-start(f32[2048]{0:T(1024)} %get-tuple-element.157) | copy-start | bytes 24580
  486.5 72.3 %collective-permute-start.37 = (bf16[512,1024]{1,0:T(8,128)(2,1)}, bf16[512,1024]{1,0:T(8,128)(2,1)}, u32[]{:S(2)}, u32[]{:S(2)}) collective-permute-start(bf16[512,1024]{1,0:T(8,128)(2,1)} %shard_map.219), channel_id=1, source_target_pairs={{0,16},{2,18},{4,20},{6,22},{8,24},{10,26},{12,28},{14,30},{16,0},... | collective-permute-start | bytes 3145736 | tf_op jit(solution)/shard_map/ppermute | solution.py:366
  513.9 8.5 %collective-permute-start.28 = (f32[7,2048]{1,0:T(8,128)S(1)}, f32[7,2048]{1,0:T(8,128)S(1)}, u32[]{:S(2)}, u32[]{:S(2)}) collective-permute-start(f32[7,2048]{1,0:T(8,128)S(1)} %pad_maximum_fusion.5), channel_id=1, source_target_pairs={{0,1},{1,0},{2,3},{3,2},{4,5},{5,4},{6,7},{7,6},{8,9},{9,8},{10,11... | collective-permute-start | bytes 172040 | tf_op jit(solution)/shard_map/ppermute | solution.py:369
  522.4 15.5 %collective-permute-start.31 = (f32[7,2048]{1,0:T(8,128)S(1)}, f32[7,2048]{1,0:T(8,128)S(1)}, u32[]{:S(2)}, u32[]{:S(2)}) collective-permute-start(f32[7,2048]{1,0:T(8,128)S(1)} %fusion.21), channel_id=1, source_target_pairs={{0,12},{2,14},{4,8},{6,10},{8,4},{10,6},{12,0},{14,2},{16,28},{18,... | collective-permute-start | bytes 172040 | tf_op jit(solution)/shard_map/ppermute | solution.py:366
  522.8 15.2 %collective-permute-start.30 = (f32[7,2048]{1,0:T(8,128)S(1)}, f32[7,2048]{1,0:T(8,128)S(1)}, u32[]{:S(2)}, u32[]{:S(2)}) collective-permute-start(f32[7,2048]{1,0:T(8,128)S(1)} %fusion.21), channel_id=1, source_target_pairs={{0,8},{2,10},{4,12},{6,14},{8,0},{10,2},{12,4},{14,6},{16,24},{18,... | collective-permute-start | bytes 172040 | tf_op jit(solution)/shard_map/ppermute | solution.py:366
  525.3 12.7 %collective-permute-start.29 = (f32[7,2048]{1,0:T(8,128)S(1)}, f32[7,2048]{1,0:T(8,128)S(1)}, u32[]{:S(2)}, u32[]{:S(2)}) collective-permute-start(f32[7,2048]{1,0:T(8,128)S(1)} %fusion.21), channel_id=1, source_target_pairs={{0,4},{2,6},{4,0},{6,2},{8,12},{10,14},{12,8},{14,10},{16,20},{18,... | collective-permute-start | bytes 172040 | tf_op jit(solution)/shard_map/ppermute | solution.py:366
  526.0 40.2 %all-to-all-start.10 = ((bf16[4,128,2304]{2,1,0:T(8,128)(2,1)}), bf16[4,128,2304]{2,1,0:T(8,128)(2,1)}, u32[]{:S(2)}, u32[]{:S(2)}) async-start(bf16[4,128,2304]{2,1,0:T(8,128)(2,1)} %bitcast.76), calls=%async_computation.10 | async-start | bytes 4718592 | tf_op jit(solution)/shard_map/all_to_all | solution.py:406
  538.0 20.1 %collective-permute-start.34 = (f32[7,2048]{1,0:T(8,128)S(1)}, f32[7,2048]{1,0:T(8,128)S(1)}, u32[]{:S(2)}, u32[]{:S(2)}) collective-permute-start(f32[7,2048]{1,0:T(8,128)S(1)} %add_add_fusion.1), channel_id=1, source_target_pairs={{0,18},{2,16},{4,22},{6,20},{8,26},{10,24},{12,30},{14,28},{16,2},... | collective-permute-start | bytes 172040 | tf_op jit(solution)/shard_map/ppermute | solution.py:366
  538.9 19.2 %collective-permute-start.33 = (f32[7,2048]{1,0:T(8,128)S(1)}, f32[7,2048]{1,0:T(8,128)S(1)}, u32[]{:S(2)}, u32[]{:S(2)}) collective-permute-start(f32[7,2048]{1,0:T(8,128)S(1)} %add_add_fusion.1), channel_id=1, source_target_pairs={{0,2},{2,0},{4,6},{6,4},{8,10},{10,8},{12,14},{14,12},{16,18},{18,... | collective-permute-start | bytes 172040 | tf_op jit(solution)/shard_map/ppermute | solution.py:366
  540.3 18.5 %collective-permute-start.32 = (f32[7,2048]{1,0:T(8,128)S(1)}, f32[7,2048]{1,0:T(8,128)S(1)}, u32[]{:S(2)}, u32[]{:S(2)}) collective-permute-start(f32[7,2048]{1,0:T(8,128)S(1)} %add_add_fusion.1), channel_id=1, source_target_pairs={{0,16},{2,18},{4,20},{6,22},{8,24},{10,26},{12,28},{14,30},{16,0},... | collective-permute-start | bytes 172040 | tf_op jit(solution)/shard_map/ppermute | solution.py:366
  566.1 18.0 %all-to-all-start.11 = ((bf16[4,128,1024]{2,1,0:T(8,128)(2,1)}), bf16[4,128,1024]{2,1,0:T(8,128)(2,1)S(1)}, u32[]{:S(2)}, u32[]{:S(2)}) async-start(bf16[4,128,1024]{2,1,0:T(8,128)(2,1)} %bitcast.94), calls=%async_computation.11 | async-start | bytes 2097152 | tf_op jit(solution)/shard_map/all_to_all | solution.py:406
  (41 other events, 258.0 us)
